TPU v7x, 128 devices: a whole 4x4x4 slice. The times are simulated.
128 devices in a mesh: dp: 8 (over x, core), seq: 16 (over y, z).
Axes of the slice: x: 4, y: 4, z: 4, core: 2. Of those that a mesh axis runs over, the one named last changes fastest.
Arguments:
- events: bfloat16 [8, 4096, 1024], P('dp', 'seq'), may hold values from -6 to 6
- cotangent: bfloat16 [8, 4096, 1024], P('dp', 'seq'), may hold values from -6 to 6
- hist_lengths: int32 [8, 8], P('dp'), may hold values from 1 to 1024, 4096 in all within a row
- w_in: bfloat16 [1024, 4096], replicated, may hold values from -0.1875 to 0.1875
- w_out: bfloat16 [1024, 1024], replicated, may hold values from -0.1875 to 0.1875
Outputs:
- grad_events: bfloat16 [8, 4096, 1024], P('dp', 'seq')
- grad_w_in: bfloat16 [1024, 4096], P(('dp', 'seq'))
- grad_w_out: bfloat16 [1024, 1024], P(('dp', 'seq'))
Inputs may be any that keep to these rules, and one draw needn't show every extreme that they name: `hist_lengths`: each row sums to 4096; some history in each row has exactly 1024 events.
All inputs are finite; a program needn't handle non-finite values.
Results may differ from a plain program's by a relative error of at most 0.014.
Values may be sent and summed in bfloat16 or wider, within the bound.
No kernel may reach another device: no remote copies, remote signals or barrier semaphores. Data moves between devices by JAX's collectives and lax.ppermute only.
A program may use at most 128 MiB of HBM per device.

v0:
```python
import jax
import jax.numpy as jnp
from jax import lax
from jax.sharding import PartitionSpec as P

HEADS = 8
SPAN = 4


def passed_along(block, axis, distance):
    devices = range(lax.axis_size(axis))
    route = [(i - distance, i) for i in devices if i - distance in devices]
    return lax.ppermute(block, axis, route)


def segment_ids(positions, doc_ends):
    return jnp.sum((positions[:, None] >= doc_ends[None, :]).astype(jnp.int32), axis=1)


def pair_keep(query_pos, key_pos, doc_ends):
    same = segment_ids(query_pos, doc_ends)[:, None] == segment_ids(key_pos, doc_ends)[None, :]
    keep = same & (key_pos[None, :] <= query_pos[:, None]) & (key_pos[None, :] >= 0)
    return keep.astype(jnp.float32)[None]


def pair_output(query_rows, key_rows, value_rows, query_pos, key_pos, doc_ends, row_count):
    keep = pair_keep(query_pos, key_pos, doc_ends)
    scores = jnp.einsum("qhd,khd->hqk", query_rows, key_rows, preferred_element_type=jnp.float32)
    weights_bf = (scores * jax.nn.sigmoid(scores) * keep / row_count).astype(jnp.bfloat16)
    return jnp.einsum("hqk,khd->qhd", weights_bf, value_rows, preferred_element_type=jnp.float32)


def pair_grads(
    query_rows, grad_rows, key_rows, value_rows, query_pos, key_pos, doc_ends, row_count
):
    keep = pair_keep(query_pos, key_pos, doc_ends)
    scores = jnp.einsum("qhd,khd->hqk", query_rows, key_rows, preferred_element_type=jnp.float32)
    sigma = jax.nn.sigmoid(scores)
    weights_bf = (scores * sigma * keep / row_count).astype(jnp.bfloat16)
    grad_weights = jnp.einsum(
        "qhd,khd->hqk", grad_rows, value_rows, preferred_element_type=jnp.float32
    )
    grad_scores = (grad_weights * sigma * (1.0 + scores * (1.0 - sigma)) * keep / row_count).astype(
        jnp.bfloat16
    )
    grad_query = jnp.einsum(
        "hqk,khd->qhd", grad_scores, key_rows, preferred_element_type=jnp.float32
    )
    grad_key = jnp.einsum(
        "hqk,qhd->khd", grad_scores, query_rows, preferred_element_type=jnp.float32
    )
    grad_value = jnp.einsum(
        "hqk,qhd->khd", weights_bf, grad_rows, preferred_element_type=jnp.float32
    )
    return (grad_query, grad_key, grad_value)


def earlier(tensors, offset):
    return passed_along((tensors[0], tensors[1]), "seq", offset)


def later(tensors, offset):
    return passed_along((tensors[0], tensors[1]), "seq", -offset)


def shards(events, cotangent, hist_lengths, w_in, w_out):
    row_count = events.shape[1]
    model_width = events.shape[2]
    head_dim = model_width // HEADS
    tokens = events[0]
    upstream = cotangent[0]
    doc_ends = jnp.cumsum(hist_lengths[0])
    own_pos = lax.axis_index("seq") * row_count + jnp.arange(row_count, dtype=jnp.int32)
    proj = jnp.dot(tokens, w_in, preferred_element_type=jnp.float32)
    sigma_proj = jax.nn.sigmoid(proj)
    act_bf = (proj * sigma_proj).astype(jnp.bfloat16)
    parts = act_bf.reshape(row_count, 4, HEADS, head_dim)
    gate_rows = parts[:, 0].reshape(row_count, model_width).astype(jnp.float32)
    value_rows = parts[:, 1]
    query_rows = parts[:, 2]
    key_rows = parts[:, 3]
    earlier_pieces = []
    for offset in range(1, SPAN + 1):
        key_prev, value_prev = earlier((key_rows, value_rows), offset)
        earlier_pieces.append((offset, key_prev, value_prev, own_pos - offset * row_count))
    attended = pair_output(query_rows, key_rows, value_rows, own_pos, own_pos, doc_ends, row_count)
    for offset, key_prev, value_prev, key_pos in earlier_pieces:
        attended = attended + pair_output(
            query_rows, key_prev, value_prev, own_pos, key_pos, doc_ends, row_count
        )
    attended = attended.reshape(row_count, model_width)
    center = attended - jnp.mean(attended, axis=1, keepdims=True)
    inv_std = lax.rsqrt(jnp.mean(center * center, axis=1, keepdims=True) + 1e-06)
    normed = center * inv_std
    gated_bf = (normed * gate_rows).astype(jnp.bfloat16)
    grad_wout = lax.dot_general(
        gated_bf, upstream, (((0,), (0,)), ((), ())), preferred_element_type=jnp.float32
    )
    grad_gated = lax.dot_general(
        upstream, w_out, (((1,), (1,)), ((), ())), preferred_element_type=jnp.float32
    )
    grad_gate = grad_gated * normed
    grad_normed = grad_gated * gate_rows
    grad_att = inv_std * (
        grad_normed
        - jnp.mean(grad_normed, axis=1, keepdims=True)
        - normed * jnp.mean(grad_normed * normed, axis=1, keepdims=True)
    )
    grad_att_bf = grad_att.astype(jnp.bfloat16).reshape(row_count, HEADS, head_dim)
    grad_q_sum, grad_k_sum, grad_v_sum = pair_grads(
        query_rows, grad_att_bf, key_rows, value_rows, own_pos, own_pos, doc_ends, row_count
    )
    for offset, key_prev, value_prev, key_pos in earlier_pieces:
        prev_q, prev_k, prev_v = pair_grads(
            query_rows, grad_att_bf, key_prev, value_prev, own_pos, key_pos, doc_ends, row_count
        )
        grad_q_sum = grad_q_sum + prev_q
    for offset in range(1, SPAN + 1):
        query_next, grad_next = later((query_rows, grad_att_bf), offset)
        unused_query, next_k, next_v = pair_grads(
            query_next,
            grad_next,
            key_rows,
            value_rows,
            own_pos + offset * row_count,
            own_pos,
            doc_ends,
            row_count,
        )
        grad_k_sum = grad_k_sum + next_k
        grad_v_sum = grad_v_sum + next_v
    grad_query = grad_q_sum.reshape(row_count, model_width)
    grad_key = grad_k_sum.reshape(row_count, model_width)
    grad_value = grad_v_sum.reshape(row_count, model_width)
    grad_act = jnp.concatenate([grad_gate, grad_value, grad_query, grad_key], axis=1)
    grad_proj_bf = (grad_act * sigma_proj * (1.0 + proj * (1.0 - sigma_proj))).astype(jnp.bfloat16)
    grad_win = lax.dot_general(
        tokens, grad_proj_bf, (((0,), (0,)), ((), ())), preferred_element_type=jnp.float32
    )
    grad_tokens = (
        lax.dot_general(
            grad_proj_bf, w_in, (((1,), (1,)), ((), ())), preferred_element_type=jnp.float32
        )
        + upstream.astype(jnp.float32)
    ).astype(jnp.bfloat16)
    summed_in, summed_out = (
        lax.psum_scatter(grad_win, ("dp", "seq"), scatter_dimension=0, tiled=True),
        lax.psum_scatter(grad_wout, ("dp", "seq"), scatter_dimension=0, tiled=True),
    )
    return (grad_tokens[None], summed_in.astype(jnp.bfloat16), summed_out.astype(jnp.bfloat16))


def solution(mesh):
    return jax.shard_map(
        shards,
        mesh=mesh,
        in_specs=(P("dp", "seq", None), P("dp", "seq", None), P("dp", None), P(), P()),
        out_specs=(P("dp", "seq", None), P(("dp", "seq"), None), P(("dp", "seq"), None)),
        check_vma=False,
    )
```

profile of v0, /device:TPU:0, one launch (start us, length us, event | category | flops | bytes accessed | tf_op | source)
XLA Modules:
  0.0 1480.0 jit_solution(7331288664296428669)
XLA Ops:
  7.2 6.0 fusion.56
  17.9 6.9 collective-permute-start.5
  24.8 3.7 collective-permute-start.3
  49.5 24.1 %collective-permute-start.4 = (bf16[256,8,128]{0,2,1:T(8,128)(2,1)S(1)}, bf16[256,8,128]{0,2,1:T(8,128)(2,1)S(1)}, u32[]{:S(2)}, u32[]{:S(2)}) collective-permute-start(bf16[256,8,128]{0,2,1:T(8,128)(2,1)S(1)} %bitcast.141), channel_id=1, source_target_pairs={{0,3},{1,4},{2,5},{3,6},{4,7},{5,8},{6,9},{7,10},{8,11},{9,12},{10... | collective-permute-start | bytes 1572872 | tf_op jit(solution)/shard_map/ppermute | solution.py:13
  84.8 4.6 collective-permute-start
  90.9 11.6 collective-permute-start.2
  104.0 6.9 collective-permute-done
  113.1 8.9 collective-permute-done.2
  127.5 3.6 fusion.125
  153.7 4.3 fusion.12
  160.9 4.3 fusion.11
  165.2 4.4 convolution_add_fusion.3
  169.6 5.3 fusion.6
  181.8 17.2 %collective-permute-done.14 = bf16[256,8,128]{0,2,1:T(8,128)(2,1)} collective-permute-done((bf16[256,8,128]{0,2,1:T(8,128)(2,1)}, bf16[256,8,128]{0,2,1:T(8,128)(2,1)}, u32[]{:S(2)}, u32[]{:S(2)}) %collective-permute-start.14) | collective-permute-done | bytes 524320 | tf_op jit(solution)/shard_map/ppermute | solution.py:13
  208.7 4.3 fusion.13
  213.0 4.6 fusion.14
  217.6 4.3 convolution_add_fusion.1
  221.8 4.1 fusion.4
  227.3 4.0 fusion.1
  231.3 8.1 convolution_bitcast_fusion
  239.5 17.5 %copy.133 = f32[1024,4096]{1,0:T(8,128)} copy(f32[1024,4096]{0,1:T(8,128)} %convolution_bitcast_fusion) | data formatting | bytes 33554432
  258.0 7.4 fusion.16
  265.4 540.3 %reduce-scatter.5.cloned.1.call-done = f32[8,1024]{1,0:T(8,128)} async-done(((f32[1024,1024]{1,0:T(8,128)}), f32[8,1024]{1,0:T(8,128)}) %reduce-scatter.5.cloned.1.call-update) | async-done | bytes 32784 | tf_op jit(solution)/shard_map/reduce_scatter | solution.py:148
  807.0 663.3 %reduce-scatter.7.cloned.1.call-done = f32[8,4096]{1,0:T(8,128)} async-done(((f32[1024,4096]{1,0:T(8,128)}), f32[8,4096]{1,0:T(8,128)}) %reduce-scatter.7.cloned.1.call-update) | async-done | bytes 131088
  (172 shorter events, 95.2 us)
Async XLA Ops:
  7.2 120.3 %copy-start = (bf16[1024,1024]{1,0:T(8,128)(2,1)S(1)}, bf16[1024,1024]{1,0:T(8,128)(2,1)}, u32[]{:S(2)}) copy-start(bf16[1024,1024]{1,0:T(8,128)(2,1)} %param.9) | copy-start | bytes 6291460
  7.2 798.5 %reduce-scatter.5.cloned.1.call-start = ((), (), s32[]{:S(2)}) async-start(), calls=%async_computation.2 | async-start | bytes 4227072 | tf_op jit(solution)/shard_map/reduce_scatter | solution.py:148
  17.9 60.4 %collective-permute-start.5 = (bf16[256,8,128]{2,0,1:T(8,128)(2,1)}, bf16[256,8,128]{2,0,1:T(8,128)(2,1)}, u32[]{:S(2)}, u32[]{:S(2)}) collective-permute-start(bf16[256,8,128]{2,0,1:T(8,128)(2,1)} %bitcast.134), channel_id=1, source_target_pairs={{0,3},{1,4},{2,5},{3,6},{4,7},{5,8},{6,9},{7,10},{8,11},{9,12},{10... | collective-permute-start | bytes 1572872 | tf_op jit(solution)/shard_map/ppermute | solution.py:13
  24.8 66.1 %collective-permute-start.3 = (bf16[256,8,128]{2,0,1:T(8,128)(2,1)}, bf16[256,8,128]{2,0,1:T(8,128)(2,1)}, u32[]{:S(2)}, u32[]{:S(2)}) collective-permute-start(bf16[256,8,128]{2,0,1:T(8,128)(2,1)} %bitcast.134), channel_id=1, source_target_pairs={{0,2},{1,3},{2,4},{3,5},{4,6},{5,7},{6,8},{7,9},{8,10},{9,11},{10,... | collective-permute-start | bytes 1572872 | tf_op jit(solution)/shard_map/ppermute | solution.py:13
  28.5 56.3 %collective-permute-start.1 = (bf16[256,8,128]{2,0,1:T(8,128)(2,1)}, bf16[256,8,128]{2,0,1:T(8,128)(2,1)}, u32[]{:S(2)}, u32[]{:S(2)}) collective-permute-start(bf16[256,8,128]{2,0,1:T(8,128)(2,1)} %bitcast.134), channel_id=1, source_target_pairs={{0,1},{1,2},{2,3},{3,4},{4,5},{5,6},{6,7},{7,8},{8,9},{9,10},{10,1... | collective-permute-start | bytes 1572872 | tf_op jit(solution)/shard_map/ppermute | solution.py:13
  31.7 17.8 %collective-permute-start.7 = (bf16[256,8,128]{2,0,1:T(8,128)(2,1)}, bf16[256,8,128]{2,0,1:T(8,128)(2,1)}, u32[]{:S(2)}, u32[]{:S(2)}) collective-permute-start(bf16[256,8,128]{2,0,1:T(8,128)(2,1)} %bitcast.134), channel_id=1, source_target_pairs={{0,4},{1,5},{2,6},{3,7},{4,8},{5,9},{6,10},{7,11},{8,12},{9,13},{1... | collective-permute-start | bytes 1572872 | tf_op jit(solution)/shard_map/ppermute | solution.py:13
  36.5 38.6 %collective-permute-start.6 = (bf16[256,8,128]{0,2,1:T(8,128)(2,1)}, bf16[256,8,128]{0,2,1:T(8,128)(2,1)}, u32[]{:S(2)}, u32[]{:S(2)}) collective-permute-start(bf16[256,8,128]{0,2,1:T(8,128)(2,1)} %bitcast.140), channel_id=1, source_target_pairs={{0,4},{1,5},{2,6},{3,7},{4,8},{5,9},{6,10},{7,11},{8,12},{9,13},{1... | collective-permute-start | bytes 1572872 | tf_op jit(solution)/shard_map/ppermute | solution.py:13
  46.7 29.7 %copy-start.36 = (f32[256,256]{1,0:T(8,128)}, f32[256,256]{1,0:T(8,128)S(1)}, u32[]{:S(2)}) copy-start(f32[256,256]{1,0:T(8,128)S(1)} %get-tuple-element.34) | copy-start | bytes 786436
  46.8 75.3 %copy-start.34 = (f32[256,256]{1,0:T(8,128)}, f32[256,256]{1,0:T(8,128)S(1)}, u32[]{:S(2)}) copy-start(f32[256,256]{1,0:T(8,128)S(1)} %get-tuple-element.35) | copy-start | bytes 786436
  48.8 26.3 %copy-start.7 = (bf16[8,256,256]{2,1,0:T(8,128)(2,1)}, bf16[8,256,256]{2,1,0:T(8,128)(2,1)S(1)}, u32[]{:S(2)}) copy-start(bf16[8,256,256]{2,1,0:T(8,128)(2,1)S(1)} %get-tuple-element.38) | copy-start | bytes 3145732
  49.5 34.5 %copy-start.26 = (f32[256,256]{1,0:T(8,128)}, f32[256,256]{1,0:T(8,128)S(1)}, u32[]{:S(2)}) copy-start(f32[256,256]{1,0:T(8,128)S(1)} %get-tuple-element.37) | copy-start | bytes 786436
  49.5 33.2 %collective-permute-start.4 = (bf16[256,8,128]{0,2,1:T(8,128)(2,1)S(1)}, bf16[256,8,128]{0,2,1:T(8,128)(2,1)S(1)}, u32[]{:S(2)}, u32[]{:S(2)}) collective-permute-start(bf16[256,8,128]{0,2,1:T(8,128)(2,1)S(1)} %bitcast.141), channel_id=1, source_target_pairs={{0,3},{1,4},{2,5},{3,6},{4,7},{5,8},{6,9},{7,10},{8,11},{9,12},{10... | collective-permute-start | bytes 1572872 | tf_op jit(solution)/shard_map/ppermute | solution.py:13
  75.1 82.9 %collective-permute-start.13 = (bf16[256,8,128]{2,0,1:T(8,128)(2,1)}, bf16[256,8,128]{2,0,1:T(8,128)(2,1)}, u32[]{:S(2)}, u32[]{:S(2)}) collective-permute-start(bf16[256,8,128]{2,0,1:T(8,128)(2,1)} %bitcast.135), channel_id=1, source_target_pairs={{3,0},{4,1},{5,2},{6,3},{7,4},{8,5},{9,6},{10,7},{11,8},{12,9},{13... | collective-permute-start | bytes 1572872 | tf_op jit(solution)/shard_map/ppermute | solution.py:13
  78.3 71.1 %collective-permute-start.11 = (bf16[256,8,128]{2,0,1:T(8,128)(2,1)}, bf16[256,8,128]{2,0,1:T(8,128)(2,1)}, u32[]{:S(2)}, u32[]{:S(2)}) collective-permute-start(bf16[256,8,128]{2,0,1:T(8,128)(2,1)} %bitcast.135), channel_id=1, source_target_pairs={{2,0},{3,1},{4,2},{5,3},{6,4},{7,5},{8,6},{9,7},{10,8},{11,9},{12,... | collective-permute-start | bytes 1572872 | tf_op jit(solution)/shard_map/ppermute | solution.py:13
  82.7 62.5 %collective-permute-start.9 = (bf16[256,8,128]{2,0,1:T(8,128)(2,1)}, bf16[256,8,128]{2,0,1:T(8,128)(2,1)}, u32[]{:S(2)}, u32[]{:S(2)}) collective-permute-start(bf16[256,8,128]{2,0,1:T(8,128)(2,1)} %bitcast.135), channel_id=1, source_target_pairs={{1,0},{2,1},{3,2},{4,3},{5,4},{6,5},{7,6},{8,7},{9,8},{10,9},{11,1... | collective-permute-start | bytes 1572872 | tf_op jit(solution)/shard_map/ppermute | solution.py:13
  84.8 26.0 %collective-permute-start = (bf16[256,8,128]{0,2,1:T(8,128)(2,1)S(1)}, bf16[256,8,128]{0,2,1:T(8,128)(2,1)S(1)}, u32[]{:S(2)}, u32[]{:S(2)}) collective-permute-start(bf16[256,8,128]{0,2,1:T(8,128)(2,1)S(1)} %bitcast.142), channel_id=1, source_target_pairs={{0,1},{1,2},{2,3},{3,4},{4,5},{5,6},{6,7},{7,8},{8,9},{9,10},{10,1... | collective-permute-start | bytes 1572872 | tf_op jit(solution)/shard_map/ppermute | solution.py:13
  90.9 31.1 %collective-permute-start.2 = (bf16[256,8,128]{0,2,1:T(8,128)(2,1)S(1)}, bf16[256,8,128]{0,2,1:T(8,128)(2,1)S(1)}, u32[]{:S(2)}, u32[]{:S(2)}) collective-permute-start(bf16[256,8,128]{0,2,1:T(8,128)(2,1)S(1)} %bitcast.143), channel_id=1, source_target_pairs={{0,2},{1,3},{2,4},{3,5},{4,6},{5,7},{6,8},{7,9},{8,10},{9,11},{10,... | collective-permute-start | bytes 1572872 | tf_op jit(solution)/shard_map/ppermute | solution.py:13
  110.9 29.7 %collective-permute-start.15 = (bf16[256,8,128]{2,0,1:T(8,128)(2,1)}, bf16[256,8,128]{2,0,1:T(8,128)(2,1)}, u32[]{:S(2)}, u32[]{:S(2)}) collective-permute-start(bf16[256,8,128]{2,0,1:T(8,128)(2,1)} %bitcast.135), channel_id=1, source_target_pairs={{4,0},{5,1},{6,2},{7,3},{8,4},{9,5},{10,6},{11,7},{12,8},{13,9},{1... | collective-permute-start | bytes 1572872 | tf_op jit(solution)/shard_map/ppermute | solution.py:13
  132.5 46.6 %collective-permute-start.12 = (bf16[256,8,128]{0,2,1:T(8,128)(2,1)}, bf16[256,8,128]{0,2,1:T(8,128)(2,1)}, u32[]{:S(2)}, u32[]{:S(2)}) collective-permute-start(bf16[256,8,128]{0,2,1:T(8,128)(2,1)} %bitcast.25), channel_id=1, source_target_pairs={{3,0},{4,1},{5,2},{6,3},{7,4},{8,5},{9,6},{10,7},{11,8},{12,9},{13... | collective-permute-start | bytes 1572872 | tf_op jit(solution)/shard_map/ppermute | solution.py:13
  136.6 1333.7 %reduce-scatter.7.cloned.1.call-start = ((), (), s32[]{:S(2)}) async-start(), calls=%async_computation.3 | async-start | bytes 16908288
  140.6 62.6 %collective-permute-start.10 = (bf16[256,8,128]{0,2,1:T(8,128)(2,1)}, bf16[256,8,128]{0,2,1:T(8,128)(2,1)}, u32[]{:S(2)}, u32[]{:S(2)}) collective-permute-start(bf16[256,8,128]{0,2,1:T(8,128)(2,1)} %bitcast.25), channel_id=1, source_target_pairs={{2,0},{3,1},{4,2},{5,3},{6,4},{7,5},{8,6},{9,7},{10,8},{11,9},{12,... | collective-permute-start | bytes 1572872 | tf_op jit(solution)/shard_map/ppermute | solution.py:13
  145.2 55.9 %collective-permute-start.8 = (bf16[256,8,128]{0,2,1:T(8,128)(2,1)}, bf16[256,8,128]{0,2,1:T(8,128)(2,1)}, u32[]{:S(2)}, u32[]{:S(2)}) collective-permute-start(bf16[256,8,128]{0,2,1:T(8,128)(2,1)} %bitcast.25), channel_id=1, source_target_pairs={{1,0},{2,1},{3,2},{4,3},{5,4},{6,5},{7,6},{8,7},{9,8},{10,9},{11,1... | collective-permute-start | bytes 1572872 | tf_op jit(solution)/shard_map/ppermute | solution.py:13
  149.4 49.7 %collective-permute-start.14 = (bf16[256,8,128]{0,2,1:T(8,128)(2,1)}, bf16[256,8,128]{0,2,1:T(8,128)(2,1)}, u32[]{:S(2)}, u32[]{:S(2)}) collective-permute-start(bf16[256,8,128]{0,2,1:T(8,128)(2,1)} %bitcast.25), channel_id=1, source_target_pairs={{4,0},{5,1},{6,2},{7,3},{8,4},{9,5},{10,6},{11,7},{12,8},{13,9},{1... | collective-permute-start | bytes 1572872 | tf_op jit(solution)/shard_map/ppermute | solution.py:13
  258.0 1214.7 %copy-start.1 = (bf16[1024,1024]{1,0:T(8,128)(2,1)S(1)}, bf16[1024,1024]{1,0:T(8,128)(2,1)}, u32[]{:S(2)}) copy-start(bf16[1024,1024]{1,0:T(8,128)(2,1)} %param.9) | copy-start | bytes 6291460
  (37 other events, 173.9 us)
Sparse Core Ops, SparseCore 0:
  136.7 668.8 reduce-scatter.4
  808.2 662.1 reduce-scatter.6
where the time goes:
time: 1490 us; the launch traced here: 1480 us
  waiting for transfers between devices  1240 us (83%)
  matrix products  104 us (7%)
  starting transfers between devices  70.8 us (5%)
  local copies, waits for them, and re-layouts  41.6 us (3%)
  between operations  15.1 us (1%)
    unnamed x3, waiting for transfers between devices  663 us
    reduce_scatter x1, waiting for transfers between devices, shards(): lax.psum_scatter(grad_wout, ('dp', 'seq'), scatter_dimension=0, tiled=True)  540 us
    ppermute x16, starting transfers between devices, passed_along(): return lax.ppermute(block, axis, route)  70.7 us
    ppermute x16, waiting for transfers between devices, passed_along(): return lax.ppermute(block, axis, route)  34.6 us
    unnamed x94, local copies, waits for them, and re-layouts  30.1 us
  transfers between devices with their start and end apart: 18, of which 6 were waited for; matrix products, arithmetic and copies ran while one was open for 9% of the time, Pallas kernels for 0%

commit v1 on v0

v1 whole, which is shorter than its diff:
```python
import jax
import jax.numpy as jnp
from jax import lax
from jax.experimental import pallas as pl
from jax.experimental.pallas import tpu as pltpu
from jax.sharding import Mesh
from jax.sharding import PartitionSpec as P

BLK = 256
NB = 4
DH = 128
GRP = NB * BLK
D = 1024
F32 = jnp.float32
BF16 = jnp.bfloat16
SCALE = 1.0 / 256.0
VMEM = pl.BlockSpec(memory_space=pltpu.VMEM)
SMEM = pl.BlockSpec(memory_space=pltpu.SMEM)


def call(body, outs, n_in, flops, nbytes, scratch=()):
    return pl.pallas_call(
        body,
        out_shape=outs,
        in_specs=[SMEM] + [VMEM] * n_in,
        out_specs=jax.tree.map(lambda _: VMEM, outs),
        scratch_shapes=scratch,
        compiler_params=pltpu.CompilerParams(vmem_limit_bytes=48 * 1024 * 1024),
        cost_estimate=pl.CostEstimate(flops=flops, bytes_accessed=nbytes, transcendentals=0),
    )


def nt(a, b):
    return lax.dot_general(a, b, (((1,), (1,)), ((), ())), preferred_element_type=F32)


def nn(a, b):
    return lax.dot_general(a, b, (((1,), (0,)), ((), ())), preferred_element_type=F32)


def tn(a, b):
    return lax.dot_general(a, b, (((0,), (0,)), ((), ())), preferred_element_type=F32)


def history_ends(info):
    ends, total = [], jnp.int32(0)
    for k in range(8):
        total = total + info[k]
        ends.append(total)
    return ends


def start_of(pos, ends):
    start = jnp.zeros_like(pos)
    for e in ends:
        start = jnp.where(pos >= e, e, start)
    return start


def end_of(pos, ends):
    end = ends[-1]
    for e in reversed(ends):
        end = jnp.where(e > pos, e, end)
    return end


def rows(i):
    return pl.ds(pl.multiple_of(i * BLK, BLK), BLK)


def head(h, base=0):
    return slice(base + h * DH, base + (h + 1) * DH)


def project_body(info, ev, wk, wv, wq, wg, kv, q, g, dsig):
    x = ev[...]
    for p, w in enumerate((wg, wv, wq, wk)):
        proj = nn(x, w[...])
        sig = 0.5 + 0.5 * jnp.tanh(0.5 * proj)
        act = (proj * sig).astype(BF16)
        if p == 0:
            g[...] = act
        elif p == 1:
            kv[:, BLK:] = act
        elif p == 2:
            q[...] = (0.5 * act.astype(F32)).astype(BF16)
        else:
            kv[:, :BLK] = act
        dsig[:, p * BLK : (p + 1) * BLK] = (sig * (1.0 + proj * (1.0 - sig))).astype(BF16)


def keep_rows(qpos, kpos, ends):
    r = qpos + lax.broadcasted_iota(jnp.int32, (BLK, 1), 0)
    c = kpos + lax.broadcasted_iota(jnp.int32, (1, BLK), 1)
    return jnp.where((c >= start_of(r, ends)) & (c <= r), SCALE, 0.0)


def keep_cols(qpos, kpos, ends):
    r = qpos + lax.broadcasted_iota(jnp.int32, (1, BLK), 1)
    c = kpos + lax.broadcasted_iota(jnp.int32, (BLK, 1), 0)
    return jnp.where((c >= start_of(r, ends)) & (c <= r), SCALE, 0.0)


def attend(q, kv, att, i, j, keep):
    for h in range(2):
        u = nt(q[rows(i), head(h)], kv[rows(j), head(h)])
        w = (u * (1.0 + jnp.tanh(u)) * keep).astype(BF16)
        att[rows(i), head(h)] += nn(w, kv[rows(j), head(h, BLK)])


def forward_local_body(info, *refs):
    q_in, kv_in = refs[0:4], refs[4:8]
    q, kv, att = refs[8:]
    ends = history_ends(info)
    base = info[8] * GRP
    for k in range(NB):
        at = rows(lax.rem(info[9] + k, NB))
        q[at, :] = q_in[k][...]
        kv[at, :] = kv_in[k][...]
    att[...] = jnp.zeros_like(att)

    def over_i(i, _):
        qpos = base + i * BLK
        first = jnp.maximum(start_of(qpos, ends) - base, 0) // BLK

        def over_j(j, _):
            attend(q, kv, att, i, j, keep_rows(qpos, base + j * BLK, ends))
            return 0

        return lax.fori_loop(first, i + 1, over_j, 0)

    lax.fori_loop(0, NB, over_i, 0)


def halo_first(i, qpos, prev, ends):
    start = start_of(qpos, ends)
    return jnp.where(start >= prev + GRP, NB, jnp.maximum((start - prev) // BLK, i))


def forward_halo_body(info, *refs):
    q, att_in, wout = refs[0:3]
    kv_in, cot, gate_in = refs[3:7], refs[7:11], refs[11:15]
    att, kv, gg, gate, stats = refs[15:20]
    ends = history_ends(info)
    base = info[8] * GRP
    prev = base - GRP
    att[...] = att_in[...]
    for k in range(NB):
        at = rows(lax.rem(info[9] + k, NB))
        kv[at, :] = kv_in[k][...]
        gate[at, :] = gate_in[k][...]
        gg[at, :] = nt(cot[k][...], wout[...])

    def over_i(i, _):
        qpos = base + i * BLK

        def over_j(j, _):
            attend(q, kv, att, i, j, keep_rows(qpos, prev + j * BLK, ends))
            return 0

        return lax.fori_loop(halo_first(i, qpos, prev, ends), NB, over_j, 0)

    lax.fori_loop(0, NB, over_i, 0)
    a = att[...]
    gn = gg[...] * gate[...].astype(F32)
    mean = jnp.sum(a, axis=1, keepdims=True) / BLK
    cent = a - mean
    m2 = jnp.sum(cent * cent, axis=1, keepdims=True)
    g1 = jnp.sum(gn, axis=1, keepdims=True)
    ga = jnp.sum(gn * cent, axis=1, keepdims=True)
    lane = lax.broadcasted_iota(jnp.int32, (GRP, DH), 1)
    packed = jnp.where(lane == 0, mean, jnp.where(lane == 1, m2, jnp.where(lane == 2, g1, ga)))
    stats[...] = packed.T[:8, :]


def norm_body(info, *refs):
    att, gg, gate = refs[0:3]
    stats, dsig = refs[3:7], refs[7:11]
    gatt, gated, gp, table = refs[11:15]
    parts = [s[...] for s in stats]
    mean = (parts[0][0:1] + parts[1][0:1] + parts[2][0:1] + parts[3][0:1]) * 0.25
    m2 = jnp.zeros_like(mean)
    g1 = jnp.zeros_like(mean)
    ga = jnp.zeros_like(mean)
    for p in parts:
        off = p[0:1] - mean
        m2 = m2 + p[1:2] + BLK * off * off
        g1 = g1 + p[2:3]
        ga = ga + p[3:4] + off * p[2:3]
    inv = lax.rsqrt(m2 / D + 1e-6)
    row = lax.broadcasted_iota(jnp.int32, (DH, GRP), 0)
    cols = jnp.where(row == 0, mean, jnp.where(row == 1, inv, jnp.where(row == 2, g1 / D, ga * inv / D)))
    table[...] = cols.T
    for k in range(NB):
        at = rows(lax.rem(info[9] + k, NB))
        t = table[at, :]
        mean_c, inv_c, g1_c, ga_c = (t[:, n : n + 1] for n in range(4))
        normed = (att[at, :] - mean_c) * inv_c
        g = gate[at, :].astype(F32)
        grad_gated = gg[at, :]
        gatt[at, :] = (inv_c * (grad_gated * g - g1_c - normed * ga_c)).astype(BF16)
        gated[at, :] = (normed * g).astype(BF16)
        gp[at, :] = (grad_gated * normed * dsig[k][:, 0:BLK].astype(F32)).astype(BF16)


def early_weights_body(info, *refs):
    ev, cot = refs[0:4], refs[4:8]
    gated, gp = refs[8:10]
    send, keep, acc_in, acc_out = refs[10:14]
    for k in range(NB):
        at = rows(lax.rem(info[9] + k, NB))
        part_in = tn(ev[k][...], gp[at, :])
        part_out = tn(gated[at, :], cot[k][...])
        if k:
            part_in += acc_in[...]
            part_out += acc_out[...]
        acc_in[...] = part_in
        acc_out[...] = part_out
    for x in range(4):
        for out, c, kind in ((send, 1 - info[10], BF16), (keep, info[10], F32)):
            big = pl.multiple_of((x * 2 + c) * 128, 128)
            small = pl.multiple_of((x * 2 + c) * 32, 32)
            out[x, 0:128, :] = acc_in[pl.ds(big, 128), :].astype(kind)
            for n in range(4):
                out[x, 128 + 32 * n : 160 + 32 * n, :] = acc_out[
                    pl.ds(small, 32), n * BLK : (n + 1) * BLK
                ].astype(kind)


def late_weights_body(info, *refs):
    ev = refs[0:4]
    gp_q, gp_kv = refs[4:6]
    send, keep, acc = refs[6:9]
    for k in range(NB):
        at = rows(lax.rem(info[9] + k, NB))
        x = ev[k][...]
        for n, gp, lanes in ((0, gp_kv, slice(BLK, 2 * BLK)), (1, gp_q, slice(0, BLK)), (2, gp_kv, slice(0, BLK))):
            part = tn(x, gp[at, lanes])
            cols = slice(n * BLK, (n + 1) * BLK)
            acc[:, cols] = part if k == 0 else acc[:, cols] + part
    for x in range(4):
        for out, c, kind in ((send, 1 - info[10], BF16), (keep, info[10], F32)):
            at = pl.multiple_of((x * 2 + c) * 128, 128)
            out[x, :, :] = acc[pl.ds(at, 128), :].astype(kind)


def silu_parts(u):
    t = jnp.tanh(u)
    a = 1.0 + t
    ut = u * t
    return u + ut, a * ((1.0 + u) - ut)


def key_side(q, g, kv, dkv, dq, i, j, keep):
    half = keep * 0.5
    for h in range(2):
        qi, gi = q[rows(i), head(h)], g[rows(i), head(h)]
        kj, vj = kv[rows(j), head(h)], kv[rows(j), head(h, BLK)]
        silu, slope = silu_parts(nt(kj, qi))
        w = (silu * keep).astype(BF16)
        ds = (nt(vj, gi) * slope * half).astype(BF16)
        dkv[rows(j), head(h, BLK)] += nn(w, gi)
        dkv[rows(j), head(h)] += nn(ds, qi)
        if dq is not None:
            dq[rows(i), head(h)] += tn(ds, kj)


def query_side(q, g, kv, dq, i, j, keep):
    half = keep * 0.5
    for h in range(2):
        kj, vj = kv[rows(j), head(h)], kv[rows(j), head(h, BLK)]
        slope = silu_parts(nt(q[rows(i), head(h)], kj))[1]
        ds = (nt(g[rows(i), head(h)], vj) * slope * half).astype(BF16)
        dq[rows(i), head(h)] += nn(ds, kj)


def backward_local_body(info, *refs):
    q, g, kv, kv_prev = refs[0:4]
    dsig = refs[4:8]
    gp_q, dkv, dq = refs[8:11]
    ends = history_ends(info)
    base = info[8] * GRP
    prev = base - GRP
    dq[...] = jnp.zeros_like(dq)
    dkv[...] = jnp.zeros_like(dkv)

    def over_j(j, _):
        kpos = base + j * BLK
        last = jnp.minimum((end_of(kpos + BLK - 1, ends) - 1 - base) // BLK, NB - 1)

        def over_i(i, _):
            key_side(q, g, kv, dkv, dq, i, j, keep_cols(base + i * BLK, kpos, ends))
            return 0

        return lax.fori_loop(j, last + 1, over_i, 0)

    lax.fori_loop(0, NB, over_j, 0)

    def halo_i(i, _):
        qpos = base + i * BLK

        def halo_j(j, _):
            query_side(q, g, kv_prev, dq, i, j, keep_rows(qpos, prev + j * BLK, ends))
            return 0

        return lax.fori_loop(halo_first(i, qpos, prev, ends), NB, halo_j, 0)

    lax.fori_loop(0, NB, halo_i, 0)
    for k in range(NB):
        at = rows(lax.rem(info[9] + k, NB))
        gp_q[at, :] = (dq[at, :] * dsig[k][:, 2 * BLK : 3 * BLK].astype(F32)).astype(BF16)


def backward_later_body(info, *refs):
    q, g, kv, dkv_in = refs[0:4]
    dsig = refs[4:8]
    gp_kv, dkv = refs[8:10]
    ends = history_ends(info)
    base = info[8] * GRP
    later = base + GRP
    dkv[...] = dkv_in[...]

    def over_j(j, _):
        kpos = base + j * BLK
        end = end_of(kpos + BLK - 1, ends)
        count = jnp.where(end > later, jnp.minimum((end - 1 - later) // BLK, j) + 1, 0)

        def over_i(i, _):
            key_side(q, g, kv, dkv, None, i, j, keep_cols(later + i * BLK, kpos, ends))
            return 0

        return lax.fori_loop(0, count, over_i, 0)

    lax.fori_loop(0, NB, over_j, 0)
    for k in range(NB):
        at = rows(lax.rem(info[9] + k, NB))
        dk = 2.0 * dkv[at, 0:BLK]
        gp_kv[at, 0:BLK] = (dk * dsig[k][:, 3 * BLK :].astype(F32)).astype(BF16)
        gp_kv[at, BLK:] = (dkv[at, BLK:] * dsig[k][:, BLK : 2 * BLK].astype(F32)).astype(BF16)


def input_early_body(gp_g, gp_q, w_g, w_q, cot, out):
    part = nt(gp_g[0], w_g[...]) + nt(gp_q[0], w_q[...])

    @pl.when(pl.program_id(0) == 0)
    def _():
        out[...] = part + cot[...].astype(F32)

    @pl.when(pl.program_id(0) > 0)
    def _():
        out[...] += part


def input_late_body(gp_kv, w_k, w_v, early, out, acc):
    part = nt(gp_kv[0, :, :BLK], w_k[...]) + nt(gp_kv[0, :, BLK:], w_v[...])

    @pl.when(pl.program_id(0) == 0)
    def _():
        acc[...] = part + early[...]

    @pl.when(pl.program_id(0) > 0)
    def _():
        acc[...] += part

    @pl.when(pl.program_id(0) == 3)
    def _():
        out[...] = acc[...].astype(BF16)


def along(x, axis, d):
    return lax.ppermute(x, axis, [(i, (i + d) % 4) for i in range(4)])


def swap(x):
    return lax.ppermute(x, "c", [(0, 1), (1, 0)])


def gather_z(x):
    return [x, along(x, "z", -1), along(x, "z", 2), along(x, "z", 1)]


def to_owner(x):
    route = []
    for xc in range(8):
        for y in range(4):
            for z in range(4):
                src = (xc * 4 + y) * 4 + z
                dst = ((2 * z + xc // 4) * 4 + xc % 4) * 4 + y
                route.append((src, dst))
    return lax.ppermute(x, ("x", "c", "y", "z"), route)


def f32(shape):
    return jax.ShapeDtypeStruct(shape, F32)


def bf16(shape):
    return jax.ShapeDtypeStruct(shape, BF16)


def reduce_xc(send, keep):
    summed = (keep + swap(send).astype(F32)).astype(BF16)
    got = lax.all_to_all(summed, "x", 0, 0)
    return jnp.sum(got.astype(F32), axis=0)


def body(events, cotangent, hist, w_in, w_out):
    z = lax.axis_index("z")
    info = jnp.concatenate(
        [hist[0], jnp.stack([lax.axis_index("y"), z, lax.axis_index("c")]).astype(jnp.int32)]
    )
    ev, cot = events[0], cotangent[0]
    evs = gather_z(ev)
    wg, wv, wq, wk = (lax.dynamic_slice(w_in, (0, p * D + z * BLK), (D, BLK)) for p in range(4))
    wout = lax.dynamic_slice(w_out, (z * BLK, 0), (BLK, D))
    kvs, qs, gs, dsigs, kv_prevs = [], [], [], [], []
    for k in range(NB):
        kv, q, g, dsig = call(
            project_body,
            (bf16((BLK, 2 * BLK)), bf16((BLK, BLK)), bf16((BLK, BLK)), bf16((BLK, 4 * BLK))),
            5, 2 * BLK * D * D, 4 << 20,
        )(info, evs[k], wk, wv, wq, wg)
        kvs.append(kv)
        qs.append(q)
        gs.append(g)
        dsigs.append(dsig)
        kv_prevs.append(along(kv, "y", 1))
    cots = gather_z(cot)
    q, kv, att = call(
        forward_local_body, (bf16((GRP, BLK)), bf16((GRP, 2 * BLK)), f32((GRP, BLK))), 8, 5 << 30, 4 << 20
    )(info, *qs, *kvs)
    q_next = along(q, "y", -1)
    att, kv_prev, gg, gate, stats = call(
        forward_halo_body,
        (f32((GRP, BLK)), bf16((GRP, 2 * BLK)), f32((GRP, BLK)), bf16((GRP, BLK)), f32((8, GRP))),
        15, 5 << 30, 4 << 20,
    )(info, q, att, wout, *kv_prevs, *cots, *gs)
    gatt, gated, gp_g = call(
        norm_body, (bf16((GRP, BLK)),) * 3, 11, 1 << 30, 4 << 20, [pltpu.VMEM((GRP, DH), F32)]
    )(info, att, gg, gate, *gather_z(stats), *dsigs)
    g_next = along(gatt, "y", -1)
    send_1, keep_1 = call(
        early_weights_body,
        (bf16((4, BLK, BLK)), f32((4, BLK, BLK))), 10, 1 << 30, 4 << 20,
        [pltpu.VMEM((D, BLK), F32), pltpu.VMEM((BLK, D), F32)],
    )(info, *evs, *cots, gated, gp_g)
    gp_q, dkv = call(
        backward_local_body, (bf16((GRP, BLK)), f32((GRP, 2 * BLK))), 8, 10 << 30, 4 << 20,
        [pltpu.VMEM((GRP, BLK), F32)],
    )(info, q, gatt, kv, kv_prev, *dsigs)
    gp_kv = call(
        backward_later_body, bf16((GRP, 2 * BLK)), 8, 5 << 30, 4 << 20, [pltpu.VMEM((GRP, 2 * BLK), F32)]
    )(info, q_next, g_next, kv, dkv, *dsigs)
    send_2, keep_2 = call(
        late_weights_body,
        (bf16((4, 128, 768)), f32((4, 128, 768))), 6, 2 << 30, 4 << 20,
        [pltpu.VMEM((D, 768), F32)],
    )(info, *evs, gp_q, gp_kv)

    rows_g = lax.all_to_all(gp_g.reshape(NB, BLK, BLK), "z", 0, 0)
    rows_q = lax.all_to_all(gp_q.reshape(NB, BLK, BLK), "z", 0, 0)
    rows_kv = lax.all_to_all(gp_kv.reshape(NB, BLK, 2 * BLK), "z", 0, 0)
    early = pl.pallas_call(
        input_early_body,
        grid=(4,),
        out_shape=f32((BLK, D)),
        in_specs=[
            pl.BlockSpec((1, BLK, BLK), lambda s: (s, 0, 0)),
            pl.BlockSpec((1, BLK, BLK), lambda s: (s, 0, 0)),
            pl.BlockSpec((D, BLK), lambda s: (0, s)),
            pl.BlockSpec((D, BLK), lambda s: (0, 8 + s)),
            pl.BlockSpec((BLK, D), lambda s: (0, 0)),
        ],
        out_specs=pl.BlockSpec((BLK, D), lambda s: (0, 0)),
        cost_estimate=pl.CostEstimate(flops=1 << 30, bytes_accessed=6 << 20, transcendentals=0),
    )(rows_g, rows_q, w_in, w_in, cot)
    grad_events = pl.pallas_call(
        input_late_body,
        grid=(4,),
        out_shape=bf16((BLK, D)),
        in_specs=[
            pl.BlockSpec((1, BLK, 2 * BLK), lambda s: (s, 0, 0)),
            pl.BlockSpec((D, BLK), lambda s: (0, 12 + s)),
            pl.BlockSpec((D, BLK), lambda s: (0, 4 + s)),
            pl.BlockSpec((BLK, D), lambda s: (0, 0)),
        ],
        out_specs=pl.BlockSpec((BLK, D), lambda s: (0, 0)),
        scratch_shapes=[pltpu.VMEM((BLK, D), F32)],
        cost_estimate=pl.CostEstimate(flops=1 << 30, bytes_accessed=6 << 20, transcendentals=0),
    )(rows_kv, w_in, w_in, early)

    first = reduce_xc(send_1, keep_1)
    out_rows = first[128:].reshape(4, 32, BLK).transpose(1, 0, 2).reshape(4, 8, D).astype(BF16)
    out_rows = jnp.sum(lax.all_to_all(out_rows, "y", 0, 0).astype(F32), axis=0)
    grad_w_out = to_owner(out_rows.astype(BF16))

    def reduce_yz(part):
        chunks = part.astype(BF16).reshape(16, 8, part.shape[1])
        got = lax.all_to_all(chunks, ("y", "z"), 0, 0)
        return jnp.sum(got.reshape(4, 4, 8, part.shape[1]).astype(F32), axis=0)

    gate_part = reduce_yz(first[:128])
    late = reduce_yz(reduce_xc(send_2, keep_2))
    pieces = [gate_part] + [late[:, :, n * BLK : (n + 1) * BLK] for n in range(3)]
    grad_w_in = jnp.stack(pieces).transpose(2, 0, 1, 3).reshape(8, 4 * D).astype(BF16)
    return grad_events[None], grad_w_in, grad_w_out


def solution(mesh):
    axes = ("x", "c", "y", "z")
    split = Mesh(mesh.devices.reshape(4, 2, 4, 4), axes)
    dp, seq = ("x", "c"), ("y", "z")
    return jax.shard_map(
        body,
        mesh=split,
        in_specs=(P(dp, seq, None), P(dp, seq, None), P(dp, None), P(), P()),
        out_specs=(P(dp, seq, None), P(axes, None), P(axes, None)),
        check_vma=False,
    )
```

time: 1490 us -> 205 us (0.14)
  waiting for transfers between devices: 1240 us -> 34.7 us
  matrix products: 104 us -> 0 us
  Pallas kernels: 0 us -> 58.3 us
  local copies, waits for them, and re-layouts: 41.6 us -> 15.6 us
  blocking collectives: 0 us -> 23.8 us
    unnamed x3 -> x0, waiting for transfers between devices: 663 us -> none
    reduce_scatter x1 -> x0, waiting for transfers between devices: 540 us -> none  [shards(): lax.psum_scatter(grad_wout, ('dp', 'seq'), scatter_dimension=0, tiled=True)]
    dot_general x35 -> x0, matrix products: 104 us -> none  [the longest x5 18.9 us: pair_grads(): jnp.einsum('hqk,khd->qhd', grad_scores, key_rows, preferred_element_type=...]
    pallas_call x0 -> x13, Pallas kernels: none -> 58.3 us  [the longest x1 11.1 us: body(): call(backward_local_body, (bf16((GRP, BLK)), f32((GRP, 2 * BLK))), 8, 10...]
    ppermute x16 -> x18, starting transfers between devices: 70.7 us -> 35.6 us  [the longest x15 35 us: along(): return lax.ppermute(x, axis, [(i, (i + d) % 4) for i in range(4)])]
    all_to_all x0 -> x6, starting transfers between devices: none -> 25.8 us  [the longest x1 7.56 us: reduce_xc(): got = lax.all_to_all(summed, 'x', 0, 0)]
    all_to_all x0 -> x2, blocking collectives: none -> 23.8 us  [the longest x1 14.2 us: reduce_xc(): got = lax.all_to_all(summed, 'x', 0, 0)]
    all_to_all x0 -> x6, waiting for transfers between devices: none -> 23.7 us  [the longest x1 8.23 us: body(): rows_kv = lax.all_to_all(gp_kv.reshape(NB, BLK, 2 * BLK), 'z', 0, 0)]
  transfers between devices with their start and end apart: 18 -> 24, of which waited for: 6 -> 9; matrix products, arithmetic and copies ran while one was open for 9% -> 5% of each run, Pallas kernels for 0% -> 27%
where the time goes in v1:
time: 205 us; the launch traced here: 204 us
  starting transfers between devices  61.4 us (30%)
  Pallas kernels  58.3 us (28%)
  waiting for transfers between devices  34.7 us (17%)
  blocking collectives  23.8 us (12%)
  local copies, waits for them, and re-layouts  15.6 us (8%)
  other arithmetic  8.7 us (4%)
    ppermute x15, starting transfers between devices, along(): return lax.ppermute(x, axis, [(i, (i + d) % 4) for i in range(4)])  35 us
    all_to_all x1, blocking collectives, reduce_xc(): got = lax.all_to_all(summed, 'x', 0, 0)  14.2 us
    unnamed x61, local copies, waits for them, and re-layouts  13.1 us
    pallas_call x1, Pallas kernels, body(): call(backward_local_body, (bf16((GRP, BLK)), f32((GRP, 2 * BLK))), 8, 10...  11.1 us
    ppermute x15, waiting for transfers between devices, along(): return lax.ppermute(x, axis, [(i, (i + d) % 4) for i in range(4)])  11 us
    all_to_all x1, blocking collectives, body(): out_rows = jnp.sum(lax.all_to_all(out_rows, 'y', 0, 0).astype(F32), axis=0)  9.65 us
    all_to_all x1, waiting for transfers between devices, body(): rows_kv = lax.all_to_all(gp_kv.reshape(NB, BLK, 2 * BLK), 'z', 0, 0)  8.23 us
    pallas_call x4, Pallas kernels, body(): call(project_body, (bf16((BLK, 2 * BLK)), bf16((BLK, BLK)), bf16((BLK, BL...  8.09 us
  transfers between devices with their start and end apart: 24, of which 9 were waited for; matrix products, arithmetic and copies ran while one was open for 5% of the time, Pallas kernels for 27%

profile of v1, /device:TPU:0, one launch (start us, length us, event | category | flops | bytes accessed | tf_op | source)
XLA Modules:
  0.0 203.6 jit_solution(6178274595684797759)
XLA Ops:
  2.7 3.6 %collective-permute-start.1 = (bf16[256,1024]{1,0:T(8,128)(2,1)}, bf16[256,1024]{1,0:T(8,128)(2,1)}, u32[]{:S(2)}, u32[]{:S(2)}) collective-permute-start(bf16[256,1024]{1,0:T(8,128)(2,1)} %bitcast.35), channel_id=1, source_target_pairs={{0,2},{1,3},{2,0},{3,1},{4,6},{5,7},{6,4},{7,5},{8,10},{9,11},{10,... | collective-permute-start | bytes 1572872 | tf_op jit(solution)/shard_map/ppermute | solution.py:371
  24.0 6.6 %collective-permute-done.1.ev.refs_2_ = bf16[256,1024]{1,0:T(8,128)(2,1)} collective-permute-done((bf16[256,1024]{1,0:T(8,128)(2,1)}, bf16[256,1024]{1,0:T(8,128)(2,1)}, u32[]{:S(2)}, u32[]{:S(2)}) %collective-permute-start.1) | collective-permute-done | bytes 524320 | tf_op jit(solution)/shard_map/ppermute | solution.py:371
  30.7 4.5 %collective-permute-start.9 = (bf16[256,1024]{1,0:T(8,128)(2,1)S(1)}, bf16[256,1024]{1,0:T(8,128)(2,1)S(1)}, u32[]{:S(2)}, u32[]{:S(2)}) collective-permute-start(bf16[256,1024]{1,0:T(8,128)(2,1)S(1)} %bitcast.31), channel_id=1, source_target_pairs={{0,2},{1,3},{2,0},{3,1},{4,6},{5,7},{6,4},{7,5},{8,10},{9,11},{10,... | collective-permute-start | bytes 1572872 | tf_op jit(solution)/shard_map/ppermute | solution.py:371
  43.8 7.5 %shard_map.80 = (bf16[1024,256]{1,0:T(8,128)(2,1)}, bf16[1024,512]{1,0:T(8,128)(2,1)S(1)}, f32[1024,256]{1,0:T(8,128)S(1)}) custom-call(s32[11]{0:T(128)S(1)} %pad_add_fusion.info, bf16[256,256]{1,0:T(8,128)(2,1)S(1)} %copy-done.21, bf16[256,256]{1,0:T(8,128)(2,1)S(1)} %get-tuple-element.37.refs_1_, bf16[256,256]{1,0:T(8,128)(2,1)S(1)} %get-tuple-element.38.refs_2_, ...), custom_call_target="tpu_custom_call" | custom-call | flops 5368709120 | bytes 4194304 | tf_op jit(solution)/shard_map/pallas_call | solution.py:429
  53.3 4.3 %shard_map.81 = (f32[1024,256]{1,0:T(8,128)}, bf16[1024,512]{1,0:T(8,128)(2,1)}, f32[1024,256]{1,0:T(8,128)}, bf16[1024,256]{1,0:T(8,128)(2,1)S(1)}, f32[8,1024]{1,0:T(8,128)S(1)}) custom-call(s32[11]{0:T(128)S(1)} %pad_add_fusion.info, bf16[1024,256]{1,0:T(8,128)(2,1)} %get-tuple-element.44.refs_0_, f32[1024,256]{1,0:T(8,128)} %copy-done.25, ...), custom_call_target="tpu_custom_call" | custom-call | flops 5368709120 | bytes 4194304 | tf_op jit(solution)/shard_map/pallas_call | solution.py:433
  58.4 8.7 %collective-permute-start.12 = (f32[8,1024]{1,0:T(8,128)S(1)}, f32[8,1024]{1,0:T(8,128)S(1)}, u32[]{:S(2)}, u32[]{:S(2)}) collective-permute-start(f32[8,1024]{1,0:T(8,128)S(1)} %get-tuple-element.53.refs_3_), channel_id=1, source_target_pairs={{0,2},{1,3},{2,0},{3,1},{4,6},{5,7},{6,4},{7,5},{8,10},{9,11},{10,... | collective-permute-start | bytes 98312 | tf_op jit(solution)/shard_map/ppermute | solution.py:371
  73.5 3.3 %shard_map.82 = (bf16[1024,256]{1,0:T(8,128)(2,1)}, bf16[1024,256]{1,0:T(8,128)(2,1)S(1)}, bf16[1024,256]{1,0:T(8,128)(2,1)}) custom-call(s32[11]{0:T(128)S(1)} %pad_add_fusion.info, f32[1024,256]{1,0:T(8,128)S(1)} %copy-done.9, f32[1024,256]{1,0:T(8,128)} %get-tuple-element.51.refs_1_, bf16[1024,256]{1,0:T(8,128)(2,1)S(1)} %get-tuple-element.52.refs_2_, ...), custom_call_target="tpu_custom_call" | custom-call | flops 1073741824 | bytes 4194304 | tf_op jit(solution)/shard_map/pallas_call | solution.py:438
  76.8 4.3 %shard_map.87 = (bf16[4,256,256]{2,1,0:T(8,128)(2,1)}, f32[4,256,256]{2,1,0:T(8,128)}) custom-call(s32[11]{0:T(128)S(1)} %pad_add_fusion.info, bf16[256,1024]{1,0:T(8,128)(2,1)S(1)} %bitcast.38, bf16[256,1024]{1,0:T(8,128)(2,1)} %collective-permute-done.ev.refs_1_, bf16[256,1024]{1,0:T(8,128)(2,1)} %collective-permute-done.1.ev.refs_2_, ...), custom_call_target="tpu_custom_call" | custom-call | flops 1073741824 | bytes 4194304 | tf_op jit(solution)/shard_map/pallas_call | solution.py:442
  83.4 11.1 %shard_map.83 = (bf16[1024,256]{1,0:T(8,128)(2,1)S(1)}, f32[1024,512]{1,0:T(8,128)}) custom-call(s32[11]{0:T(128)S(1)} %pad_add_fusion.info, bf16[1024,256]{1,0:T(8,128)(2,1)} %get-tuple-element.44.refs_0_, bf16[1024,256]{1,0:T(8,128)(2,1)} %get-tuple-element.58.refs_1_, bf16[1024,512]{1,0:T(8,128)(2,1)S(1)} %get-tuple-element.59.refs_2_, ...), custom_call_target="tpu_custom_call" | custom-call | flops 10737418240 | bytes 4194304 | tf_op jit(solution)/shard_map/pallas_call | solution.py:447
  95.4 4.1 %all-to-all-start.2 = ((bf16[4,256,256]{2,1,0:T(8,128)(2,1)}), bf16[4,256,256]{2,1,0:T(8,128)(2,1)}, u32[]{:S(2)}, u32[]{:S(2)}) async-start(bf16[4,256,256]{2,1,0:T(8,128)(2,1)} %bitcast.40), calls=%async_computation.2 | async-start | bytes 1048576 | tf_op jit(solution)/shard_map/all_to_all | solution.py:461
  103.2 3.4 %shard_map.84.refs_5_ = bf16[1024,512]{1,0:T(8,128)(2,1)} custom-call(s32[11]{0:T(128)S(1)} %pad_add_fusion.info, bf16[1024,256]{1,0:T(8,128)(2,1)} %collective-permute-done.3.refs_0_, bf16[1024,256]{1,0:T(8,128)(2,1)} %collective-permute-done.14.refs_1_, bf16[1024,512]{1,0:T(8,128)(2,1)S(1)} %copy-done.23, f32[1024,512]{1,0:T(8,128)} %get-tuple-element.61.refs_3_, ...), custom_call_target="tpu_custom_call" | custom-call | flops 5368709120 | bytes 4194304 | tf_op jit(solution)/shard_map/pallas_call | solution.py:451
  108.1 7.6 %all-to-all-start.3 = ((bf16[4,256,256]{2,1,0:T(8,128)(2,1)}), bf16[4,256,256]{2,1,0:T(8,128)(2,1)S(1)}, u32[]{:S(2)}, u32[]{:S(2)}) async-start(bf16[4,256,256]{2,1,0:T(8,128)(2,1)} %add_convert_fusion.1), calls=%async_computation.3 | async-start | bytes 1048576 | tf_op jit(solution)/shard_map/all_to_all | solution.py:403
  116.7 4.7 %shard_map.88 = (bf16[4,128,768]{2,1,0:T(8,128)(2,1)}, f32[4,128,768]{2,1,0:T(8,128)S(1)}) custom-call(s32[11]{0:T(128)S(1)} %pad_add_fusion.info, bf16[256,1024]{1,0:T(8,128)(2,1)S(1)} %bitcast.39, bf16[256,1024]{1,0:T(8,128)(2,1)} %collective-permute-done.ev.refs_1_, bf16[256,1024]{1,0:T(8,128)(2,1)} %collective-permute-done.1.ev.refs_2_, ...), custom_call_target="tpu_custom_call" | custom-call | flops 2147483648 | bytes 4194304 | tf_op jit(solution)/shard_map/pallas_call | solution.py:454
  125.5 3.5 %all-to-all-start.1 = ((bf16[4,256,256]{2,1,0:T(8,128)(2,1)}), bf16[4,256,256]{2,1,0:T(8,128)(2,1)S(1)}, u32[]{:S(2)}, u32[]{:S(2)}) async-start(bf16[4,256,256]{2,1,0:T(8,128)(2,1)} %bitcast.7), calls=%async_computation.1 | async-start | bytes 1048576 | tf_op jit(solution)/shard_map/all_to_all | solution.py:460
  130.8 6.9 %all-to-all-done.1.gp_g = bf16[4,256,256]{2,1,0:T(8,128)(2,1)S(1)} async-done(((bf16[4,256,256]{2,1,0:T(8,128)(2,1)}), bf16[4,256,256]{2,1,0:T(8,128)(2,1)S(1)}, u32[]{:S(2)}, u32[]{:S(2)}) %all-to-all-start.1) | async-done | bytes 524320 | tf_op jit(solution)/shard_map/all_to_all | solution.py:460
  137.8 9.7 %all_to_all.40 = bf16[4,8,1024]{2,1,0:T(8,128)(2,1)S(1)} all-to-all(bf16[4,8,1024]{2,1,0:T(8,128)(2,1)S(1)} %convert_element_type.62), channel_id=1, replica_groups=mesh['x'=4,'c'=2,'y'=4,'z'=4] {'y'}, dimensions={0} | all-to-all | bytes 131072 | tf_op jit(solution)/shard_map/all_to_all | solution.py:494
  147.4 3.5 %all-to-all-start.4 = ((bf16[16,8,256]{2,1,0:T(8,128)(2,1)}), bf16[16,8,256]{2,1,0:T(8,128)(2,1)S(1)}, u32[]{:S(2)}, u32[]{:S(2)}) async-start(bf16[16,8,256]{2,1,0:T(8,128)(2,1)} %get-tuple-element.74), calls=%async_computation.4 | async-start | bytes 131072 | tf_op jit(solution)/shard_map/all_to_all | solution.py:499
  153.6 4.9 %all-to-all-done.4 = bf16[16,8,256]{2,1,0:T(8,128)(2,1)S(1)} async-done(((bf16[16,8,256]{2,1,0:T(8,128)(2,1)}), bf16[16,8,256]{2,1,0:T(8,128)(2,1)S(1)}, u32[]{:S(2)}, u32[]{:S(2)}) %all-to-all-start.4) | async-done | bytes 65568 | tf_op jit(solution)/shard_map/all_to_all | solution.py:499
  158.5 14.2 %all_to_all.41 = bf16[4,128,768]{2,1,0:T(8,128)(2,1)} all-to-all(bf16[4,128,768]{2,1,0:T(8,128)(2,1)S(1)} %add_convert_fusion), channel_id=1, replica_groups=mesh['x'=4,'c'=2,'y'=4,'z'=4] {'x'}, dimensions={0} | all-to-all | bytes 1572864 | tf_op jit(solution)/shard_map/all_to_all | solution.py:403
  172.7 3.5 %all-to-all-start = ((bf16[4,256,512]{2,1,0:T(8,128)(2,1)}), bf16[4,256,512]{2,1,0:T(8,128)(2,1)S(1)}, u32[]{:S(2)}, u32[]{:S(2)}) async-start(bf16[4,256,512]{2,1,0:T(8,128)(2,1)} %bitcast.6), calls=%async_computation | async-start | bytes 2097152 | tf_op jit(solution)/shard_map/all_to_all | solution.py:462
  178.9 8.2 %all-to-all-done.gp_kv = bf16[4,256,512]{2,1,0:T(8,128)(2,1)S(1)} async-done(((bf16[4,256,512]{2,1,0:T(8,128)(2,1)}), bf16[4,256,512]{2,1,0:T(8,128)(2,1)S(1)}, u32[]{:S(2)}, u32[]{:S(2)}) %all-to-all-start) | async-done | bytes 1048608 | tf_op jit(solution)/shard_map/all_to_all | solution.py:462
  187.2 3.6 %all-to-all-start.6 = ((bf16[16,8,768]{2,1,0:T(8,128)(2,1)}), bf16[16,8,768]{2,1,0:T(8,128)(2,1)S(1)}, u32[]{:S(2)}, u32[]{:S(2)}) async-start(bf16[16,8,768]{2,1,0:T(8,128)(2,1)} %bitcast.13), calls=%async_computation.6 | async-start | bytes 393216 | tf_op jit(solution)/shard_map/all_to_all | solution.py:499
  190.7 5.7 %shard_map.85.early = f32[256,1024]{1,0:T(8,128)} custom-call(bf16[4,256,256]{2,1,0:T(8,128)(2,1)} %copy-done.27, bf16[4,256,256]{2,1,0:T(8,128)(2,1)} %all-to-all-done.2.gp_q, bf16[1024,4096]{1,0:T(8,128)(2,1)} %w_v.1, bf16[1024,4096]{1,0:T(8,128)(2,1)} %w_v.1, bf16[256,1024]{1,0:T(8,128)(2,1)} %bitcast.30), custom_call_target="tpu_custom_call" | custom-call | flops 1073741824 | bytes 6291456 | tf_op jit(solution)/shard_map/pallas_call | solution.py:463
  196.5 5.8 %shard_map.86 = bf16[256,1024]{1,0:T(8,128)(2,1)} custom-call(bf16[4,256,512]{2,1,0:T(8,128)(2,1)} %copy-done.26, bf16[1024,4096]{1,0:T(8,128)(2,1)} %w_v.1, bf16[1024,4096]{1,0:T(8,128)(2,1)} %w_v.1, f32[256,1024]{1,0:T(8,128)} %shard_map.85.early), custom_call_target="tpu_custom_call" | custom-call | flops 1073741824 | bytes 6291456 | tf_op jit(solution)/shard_map/pallas_call | solution.py:477
  (115 shorter events, 59.2 us)
Async XLA Ops:
  0.6 18.1 %collective-permute-start.2 = (bf16[256,1024]{1,0:T(8,128)(2,1)}, bf16[256,1024]{1,0:T(8,128)(2,1)}, u32[]{:S(2)}, u32[]{:S(2)}) collective-permute-start(bf16[256,1024]{1,0:T(8,128)(2,1)} %bitcast.34), channel_id=1, source_target_pairs={{0,1},{1,2},{2,3},{3,0},{4,5},{5,6},{6,7},{7,4},{8,9},{9,10},{10,1... | collective-permute-start | bytes 1572872 | tf_op jit(solution)/shard_map/ppermute | solution.py:371
  2.7 28.0 %collective-permute-start.1 = (bf16[256,1024]{1,0:T(8,128)(2,1)}, bf16[256,1024]{1,0:T(8,128)(2,1)}, u32[]{:S(2)}, u32[]{:S(2)}) collective-permute-start(bf16[256,1024]{1,0:T(8,128)(2,1)} %bitcast.35), channel_id=1, source_target_pairs={{0,2},{1,3},{2,0},{3,1},{4,6},{5,7},{6,4},{7,5},{8,10},{9,11},{10,... | collective-permute-start | bytes 1572872 | tf_op jit(solution)/shard_map/ppermute | solution.py:371
  6.3 30.9 %collective-permute-start = (bf16[256,1024]{1,0:T(8,128)(2,1)}, bf16[256,1024]{1,0:T(8,128)(2,1)}, u32[]{:S(2)}, u32[]{:S(2)}) collective-permute-start(bf16[256,1024]{1,0:T(8,128)(2,1)} %bitcast.36), channel_id=1, source_target_pairs={{0,3},{1,0},{2,1},{3,2},{4,7},{5,4},{6,5},{7,6},{8,11},{9,8},{10,9... | collective-permute-start | bytes 1572872 | tf_op jit(solution)/shard_map/ppermute | solution.py:371
  7.3 35.2 %collective-permute-start.10 = (bf16[256,1024]{1,0:T(8,128)(2,1)}, bf16[256,1024]{1,0:T(8,128)(2,1)}, u32[]{:S(2)}, u32[]{:S(2)}) collective-permute-start(bf16[256,1024]{1,0:T(8,128)(2,1)} %bitcast.28), channel_id=1, source_target_pairs={{0,1},{1,2},{2,3},{3,0},{4,5},{5,6},{6,7},{7,4},{8,9},{9,10},{10,1... | collective-permute-start | bytes 1572872 | tf_op jit(solution)/shard_map/ppermute | solution.py:371
  15.2 25.6 %collective-permute-start.4 = (bf16[256,512]{1,0:T(8,128)(2,1)}, bf16[256,512]{1,0:T(8,128)(2,1)S(1)}, u32[]{:S(2)}, u32[]{:S(2)}) collective-permute-start(bf16[256,512]{1,0:T(8,128)(2,1)} %get-tuple-element.40.refs_4_), channel_id=1, source_target_pairs={{0,4},{4,8},{8,12},{12,0},{1,5},{5,9},{9,13},{13,1},{2,6},{6,10},{... | collective-permute-start | bytes 786440 | tf_op jit(solution)/shard_map/ppermute | solution.py:371
  18.7 33.6 %collective-permute-start.8 = (bf16[256,1024]{1,0:T(8,128)(2,1)}, bf16[256,1024]{1,0:T(8,128)(2,1)S(1)}, u32[]{:S(2)}, u32[]{:S(2)}) collective-permute-start(bf16[256,1024]{1,0:T(8,128)(2,1)} %bitcast.29), channel_id=1, source_target_pairs={{0,3},{1,0},{2,1},{3,2},{4,7},{5,4},{6,5},{7,6},{8,11},{9,8},{10,9... | collective-permute-start | bytes 1572872 | tf_op jit(solution)/shard_map/ppermute | solution.py:371
  30.7 21.6 %collective-permute-start.9 = (bf16[256,1024]{1,0:T(8,128)(2,1)S(1)}, bf16[256,1024]{1,0:T(8,128)(2,1)S(1)}, u32[]{:S(2)}, u32[]{:S(2)}) collective-permute-start(bf16[256,1024]{1,0:T(8,128)(2,1)S(1)} %bitcast.31), channel_id=1, source_target_pairs={{0,2},{1,3},{2,0},{3,1},{4,6},{5,7},{6,4},{7,5},{8,10},{9,11},{10,... | collective-permute-start | bytes 1572872 | tf_op jit(solution)/shard_map/ppermute | solution.py:371
  37.2 15.1 %collective-permute-start.7 = (bf16[256,512]{1,0:T(8,128)(2,1)S(1)}, bf16[256,512]{1,0:T(8,128)(2,1)S(1)}, u32[]{:S(2)}, u32[]{:S(2)}) collective-permute-start(bf16[256,512]{1,0:T(8,128)(2,1)S(1)} %get-tuple-element.43.refs_7_), channel_id=1, source_target_pairs={{0,4},{4,8},{8,12},{12,0},{1,5},{5,9},{9,13},{13,1},{2,6},{6,10},{... | collective-permute-start | bytes 786440 | tf_op jit(solution)/shard_map/ppermute | solution.py:371
  40.9 11.5 %collective-permute-start.6 = (bf16[256,512]{1,0:T(8,128)(2,1)S(1)}, bf16[256,512]{1,0:T(8,128)(2,1)S(1)}, u32[]{:S(2)}, u32[]{:S(2)}) collective-permute-start(bf16[256,512]{1,0:T(8,128)(2,1)S(1)} %get-tuple-element.42.refs_6_), channel_id=1, source_target_pairs={{0,4},{4,8},{8,12},{12,0},{1,5},{5,9},{9,13},{13,1},{2,6},{6,10},{... | collective-permute-start | bytes 786440 | tf_op jit(solution)/shard_map/ppermute | solution.py:371
  42.5 10.8 %collective-permute-start.5 = (bf16[256,512]{1,0:T(8,128)(2,1)S(1)}, bf16[256,512]{1,0:T(8,128)(2,1)S(1)}, u32[]{:S(2)}, u32[]{:S(2)}) collective-permute-start(bf16[256,512]{1,0:T(8,128)(2,1)S(1)} %get-tuple-element.41.refs_5_), channel_id=1, source_target_pairs={{0,4},{4,8},{8,12},{12,0},{1,5},{5,9},{9,13},{13,1},{2,6},{6,10},{... | collective-permute-start | bytes 786440 | tf_op jit(solution)/shard_map/ppermute | solution.py:371
  57.6 13.1 %collective-permute-start.11 = (f32[8,1024]{1,0:T(8,128)S(1)}, f32[8,1024]{1,0:T(8,128)S(1)}, u32[]{:S(2)}, u32[]{:S(2)}) collective-permute-start(f32[8,1024]{1,0:T(8,128)S(1)} %get-tuple-element.53.refs_3_), channel_id=1, source_target_pairs={{0,3},{1,0},{2,1},{3,2},{4,7},{5,4},{6,5},{7,6},{8,11},{9,8},{10,9... | collective-permute-start | bytes 98312 | tf_op jit(solution)/shard_map/ppermute | solution.py:371
  58.4 12.4 %collective-permute-start.12 = (f32[8,1024]{1,0:T(8,128)S(1)}, f32[8,1024]{1,0:T(8,128)S(1)}, u32[]{:S(2)}, u32[]{:S(2)}) collective-permute-start(f32[8,1024]{1,0:T(8,128)S(1)} %get-tuple-element.53.refs_3_), channel_id=1, source_target_pairs={{0,2},{1,3},{2,0},{3,1},{4,6},{5,7},{6,4},{7,5},{8,10},{9,11},{10,... | collective-permute-start | bytes 98312 | tf_op jit(solution)/shard_map/ppermute | solution.py:371
  67.1 5.1 %collective-permute-start.13 = (f32[8,1024]{1,0:T(8,128)S(1)}, f32[8,1024]{1,0:T(8,128)S(1)}, u32[]{:S(2)}, u32[]{:S(2)}) collective-permute-start(f32[8,1024]{1,0:T(8,128)S(1)} %get-tuple-element.53.refs_3_), channel_id=1, source_target_pairs={{0,1},{1,2},{2,3},{3,0},{4,5},{5,6},{6,7},{7,4},{8,9},{9,10},{10,1... | collective-permute-start | bytes 98312 | tf_op jit(solution)/shard_map/ppermute | solution.py:371
  68.5 33.4 %collective-permute-start.3 = (bf16[1024,256]{1,0:T(8,128)(2,1)}, bf16[1024,256]{1,0:T(8,128)(2,1)}, u32[]{:S(2)}, u32[]{:S(2)}) collective-permute-start(bf16[1024,256]{1,0:T(8,128)(2,1)} %get-tuple-element.44.refs_0_), channel_id=1, source_target_pairs={{0,12},{4,0},{8,4},{12,8},{1,13},{5,1},{9,5},{13,9},{2,14},{6,2},{... | collective-permute-start | bytes 1572872 | tf_op jit(solution)/shard_map/ppermute | solution.py:371
  81.2 18.4 %collective-permute-start.15 = (bf16[4,256,256]{2,1,0:T(8,128)(2,1)}, bf16[4,256,256]{2,1,0:T(8,128)(2,1)}, u32[]{:S(2)}, u32[]{:S(2)}) collective-permute-start(bf16[4,256,256]{2,1,0:T(8,128)(2,1)} %get-tuple-element.66), channel_id=1, source_target_pairs={{0,16},{16,0},{1,17},{17,1},{2,18},{18,2},{3,19},{19,3},{4,20},{20... | collective-permute-start | bytes 1572872 | tf_op jit(solution)/shard_map/ppermute | solution.py:375
  81.2 20.8 %collective-permute-start.14 = (bf16[1024,256]{1,0:T(8,128)(2,1)}, bf16[1024,256]{1,0:T(8,128)(2,1)}, u32[]{:S(2)}, u32[]{:S(2)}) collective-permute-start(bf16[1024,256]{1,0:T(8,128)(2,1)} %get-tuple-element.58.refs_1_), channel_id=1, source_target_pairs={{0,12},{4,0},{8,4},{12,8},{1,13},{5,1},{9,5},{13,9},{2,14},{6,2},{... | collective-permute-start | bytes 1572872 | tf_op jit(solution)/shard_map/ppermute | solution.py:371
  95.4 12.7 %all-to-all-start.2 = ((bf16[4,256,256]{2,1,0:T(8,128)(2,1)}), bf16[4,256,256]{2,1,0:T(8,128)(2,1)}, u32[]{:S(2)}, u32[]{:S(2)}) async-start(bf16[4,256,256]{2,1,0:T(8,128)(2,1)} %bitcast.40), calls=%async_computation.2 | async-start | bytes 1048576 | tf_op jit(solution)/shard_map/all_to_all | solution.py:461
  108.1 16.6 %all-to-all-start.3 = ((bf16[4,256,256]{2,1,0:T(8,128)(2,1)}), bf16[4,256,256]{2,1,0:T(8,128)(2,1)S(1)}, u32[]{:S(2)}, u32[]{:S(2)}) async-start(bf16[4,256,256]{2,1,0:T(8,128)(2,1)} %add_convert_fusion.1), calls=%async_computation.3 | async-start | bytes 1048576 | tf_op jit(solution)/shard_map/all_to_all | solution.py:403
  122.6 28.4 %collective-permute-start.16 = (bf16[4,128,768]{2,1,0:T(8,128)(2,1)}, bf16[4,128,768]{2,1,0:T(8,128)(2,1)S(1)}, u32[]{:S(2)}, u32[]{:S(2)}) collective-permute-start(bf16[4,128,768]{2,1,0:T(8,128)(2,1)} %get-tuple-element.68), channel_id=1, source_target_pairs={{0,16},{16,0},{1,17},{17,1},{2,18},{18,2},{3,19},{19,3},{4,20},{20... | collective-permute-start | bytes 2359304 | tf_op jit(solution)/shard_map/ppermute | solution.py:375
  125.5 12.3 %all-to-all-start.1 = ((bf16[4,256,256]{2,1,0:T(8,128)(2,1)}), bf16[4,256,256]{2,1,0:T(8,128)(2,1)S(1)}, u32[]{:S(2)}, u32[]{:S(2)}) async-start(bf16[4,256,256]{2,1,0:T(8,128)(2,1)} %bitcast.7), calls=%async_computation.1 | async-start | bytes 1048576 | tf_op jit(solution)/shard_map/all_to_all | solution.py:460
  147.4 11.1 %all-to-all-start.4 = ((bf16[16,8,256]{2,1,0:T(8,128)(2,1)}), bf16[16,8,256]{2,1,0:T(8,128)(2,1)S(1)}, u32[]{:S(2)}, u32[]{:S(2)}) async-start(bf16[16,8,256]{2,1,0:T(8,128)(2,1)} %get-tuple-element.74), calls=%async_computation.4 | async-start | bytes 131072 | tf_op jit(solution)/shard_map/all_to_all | solution.py:499
  172.7 14.4 %all-to-all-start = ((bf16[4,256,512]{2,1,0:T(8,128)(2,1)}), bf16[4,256,512]{2,1,0:T(8,128)(2,1)S(1)}, u32[]{:S(2)}, u32[]{:S(2)}) async-start(bf16[4,256,512]{2,1,0:T(8,128)(2,1)} %bitcast.6), calls=%async_computation | async-start | bytes 2097152 | tf_op jit(solution)/shard_map/all_to_all | solution.py:462
  176.3 20.2 %collective-permute-start.17 = (bf16[8,1024]{1,0:T(8,128)(2,1)S(1)}, bf16[8,1024]{1,0:T(8,128)(2,1)S(1)}, u32[]{:S(2)}, u32[]{:S(2)}) collective-permute-start(bf16[8,1024]{1,0:T(8,128)(2,1)S(1)} %reduce_sum.55), channel_id=1, source_target_pairs={{0,0},{1,32},{2,64},{3,96},{4,1},{5,33},{6,65},{7,97},{8,2},{9,34}... | collective-permute-start | bytes 49160 | tf_op jit(solution)/shard_map/ppermute | solution.py:390
  187.2 15.1 %all-to-all-start.6 = ((bf16[16,8,768]{2,1,0:T(8,128)(2,1)}), bf16[16,8,768]{2,1,0:T(8,128)(2,1)S(1)}, u32[]{:S(2)}, u32[]{:S(2)}) async-start(bf16[16,8,768]{2,1,0:T(8,128)(2,1)} %bitcast.13), calls=%async_computation.6 | async-start | bytes 393216 | tf_op jit(solution)/shard_map/all_to_all | solution.py:499
  (30 other events, 304.0 us)

commit v2 on v1

--- a/solution.py
+++ b/solution.py
@@ -25,7 +25,7 @@
         in_specs=[SMEM] + [VMEM] * n_in,
         out_specs=jax.tree.map(lambda _: VMEM, outs),
         scratch_shapes=scratch,
-        compiler_params=pltpu.CompilerParams(vmem_limit_bytes=48 * 1024 * 1024),
+        compiler_params=pltpu.CompilerParams(vmem_limit_bytes=20 * 1024 * 1024),
         cost_estimate=pl.CostEstimate(flops=flops, bytes_accessed=nbytes, transcendentals=0),
     )
 
@@ -204,13 +204,11 @@
 
 
 def early_weights_body(info, *refs):
-    ev, cot = refs[0:4], refs[4:8]
-    gated, gp = refs[8:10]
-    send, keep, acc_in, acc_out = refs[10:14]
-    for k in range(NB):
-        at = rows(lax.rem(info[9] + k, NB))
-        part_in = tn(ev[k][...], gp[at, :])
-        part_out = tn(gated[at, :], cot[k][...])
+    ev, cot, gp = refs[0:4], refs[4:8], refs[8:12]
+    gated, send, keep, acc_in, acc_out = refs[12:17]
+    for k in range(NB):
+        part_in = tn(ev[k][...], gp[k][...])
+        part_out = tn(gated[rows(lax.rem(info[9] + k, NB)), :], cot[k][...])
         if k:
             part_in += acc_in[...]
             part_out += acc_out[...]
@@ -220,28 +218,44 @@
         for out, c, kind in ((send, 1 - info[10], BF16), (keep, info[10], F32)):
             big = pl.multiple_of((x * 2 + c) * 128, 128)
             small = pl.multiple_of((x * 2 + c) * 32, 32)
-            out[x, 0:128, :] = acc_in[pl.ds(big, 128), :].astype(kind)
+            out[x, :, 0:512] = acc_in[pl.ds(big, 128), :].astype(kind)
             for n in range(4):
-                out[x, 128 + 32 * n : 160 + 32 * n, :] = acc_out[
+                out[x, 32 * n : 32 * n + 32, 512:768] = acc_out[
                     pl.ds(small, 32), n * BLK : (n + 1) * BLK
                 ].astype(kind)
 
 
 def late_weights_body(info, *refs):
-    ev = refs[0:4]
-    gp_q, gp_kv = refs[4:6]
-    send, keep, acc = refs[6:9]
-    for k in range(NB):
-        at = rows(lax.rem(info[9] + k, NB))
-        x = ev[k][...]
-        for n, gp, lanes in ((0, gp_kv, slice(BLK, 2 * BLK)), (1, gp_q, slice(0, BLK)), (2, gp_kv, slice(0, BLK))):
-            part = tn(x, gp[at, lanes])
-            cols = slice(n * BLK, (n + 1) * BLK)
-            acc[:, cols] = part if k == 0 else acc[:, cols] + part
+    ev, gp = refs[0:4], refs[4:8]
+    send, keep, acc = refs[8:11]
+    for k in range(NB):
+        part = tn(ev[k][...], gp[k][...])
+        if k:
+            part += acc[...]
+        acc[...] = part
     for x in range(4):
         for out, c, kind in ((send, 1 - info[10], BF16), (keep, info[10], F32)):
             at = pl.multiple_of((x * 2 + c) * 128, 128)
             out[x, :, :] = acc[pl.ds(at, 128), :].astype(kind)
+
+
+def add_core_body(info, keep, got, to_1, to_2, to_3, own):
+    own[...] = keep[info[11]] + got[info[11]].astype(F32)
+    for d, out in ((1, to_1), (2, to_2), (3, to_3)):
+        at = lax.rem(info[11] + d, 4)
+        out[...] = (keep[at] + got[at].astype(F32)).astype(BF16)
+
+
+def add_early_body(info, own, got_1, got_2, got_3, part_in, part_out):
+    total = own[...] + got_1[...].astype(F32) + got_2[...].astype(F32) + got_3[...].astype(F32)
+    part_in[...] = total[:, 0:512].astype(BF16)
+    part_out[...] = total[:, 512:768]
+
+
+def add_late_body(info, own, got_1, got_2, got_3, early, part_in):
+    total = own[...] + got_1[...].astype(F32) + got_2[...].astype(F32) + got_3[...].astype(F32)
+    part_in[:, 0:512] = early[...]
+    part_in[:, 512:1024] = total.astype(BF16)
 
 
 def silu_parts(u):
@@ -275,9 +289,9 @@
 
 
 def backward_local_body(info, *refs):
-    q, g, kv, kv_prev = refs[0:4]
-    dsig = refs[4:8]
-    gp_q, dkv, dq = refs[8:11]
+    q, g, kv, kv_prev, gp_g = refs[0:5]
+    dsig, gp = refs[5:9], refs[9:13]
+    dkv, dq = refs[13:15]
     ends = history_ends(info)
     base = info[8] * GRP
     prev = base - GRP
@@ -308,13 +322,14 @@
     lax.fori_loop(0, NB, halo_i, 0)
     for k in range(NB):
         at = rows(lax.rem(info[9] + k, NB))
-        gp_q[at, :] = (dq[at, :] * dsig[k][:, 2 * BLK : 3 * BLK].astype(F32)).astype(BF16)
+        gp[k][:, :BLK] = gp_g[at, :]
+        gp[k][:, BLK:] = (dq[at, :] * dsig[k][:, 2 * BLK : 3 * BLK].astype(F32)).astype(BF16)
 
 
 def backward_later_body(info, *refs):
     q, g, kv, dkv_in = refs[0:4]
-    dsig = refs[4:8]
-    gp_kv, dkv = refs[8:10]
+    dsig, gp = refs[4:8], refs[8:12]
+    dkv = refs[12]
     ends = history_ends(info)
     base = info[8] * GRP
     later = base + GRP
@@ -335,36 +350,27 @@
     for k in range(NB):
         at = rows(lax.rem(info[9] + k, NB))
         dk = 2.0 * dkv[at, 0:BLK]
-        gp_kv[at, 0:BLK] = (dk * dsig[k][:, 3 * BLK :].astype(F32)).astype(BF16)
-        gp_kv[at, BLK:] = (dkv[at, BLK:] * dsig[k][:, BLK : 2 * BLK].astype(F32)).astype(BF16)
-
-
-def input_early_body(gp_g, gp_q, w_g, w_q, cot, out):
-    part = nt(gp_g[0], w_g[...]) + nt(gp_q[0], w_q[...])
-
-    @pl.when(pl.program_id(0) == 0)
-    def _():
-        out[...] = part + cot[...].astype(F32)
-
-    @pl.when(pl.program_id(0) > 0)
-    def _():
-        out[...] += part
-
-
-def input_late_body(gp_kv, w_k, w_v, early, out, acc):
-    part = nt(gp_kv[0, :, :BLK], w_k[...]) + nt(gp_kv[0, :, BLK:], w_v[...])
-
-    @pl.when(pl.program_id(0) == 0)
-    def _():
-        acc[...] = part + early[...]
-
-    @pl.when(pl.program_id(0) > 0)
-    def _():
-        acc[...] += part
-
-    @pl.when(pl.program_id(0) == 3)
-    def _():
-        out[...] = acc[...].astype(BF16)
+        gp[k][:, :BLK] = (dkv[at, BLK:] * dsig[k][:, BLK : 2 * BLK].astype(F32)).astype(BF16)
+        gp[k][:, BLK:] = (dk * dsig[k][:, 3 * BLK :].astype(F32)).astype(BF16)
+
+
+def input_rows(info, gp, w, parts, total):
+    for d in range(NB):
+        owner = lax.rem(info[9] + NB - d, NB)
+        for n, part in enumerate(parts):
+            lanes = pl.ds(pl.multiple_of(part * D + owner * BLK, BLK), BLK)
+            total = total + nt(gp[d][:, n * BLK : (n + 1) * BLK], w[:, lanes])
+    return total
+
+
+def input_early_body(info, *refs):
+    gp, (w, cot, out) = refs[0:4], refs[4:7]
+    out[...] = input_rows(info, gp, w, (0, 2), cot[...].astype(F32))
+
+
+def input_late_body(info, *refs):
+    gp, (w, early, out) = refs[0:4], refs[4:7]
+    out[...] = input_rows(info, gp, w, (1, 3), early[...]).astype(BF16)
 
 
 def along(x, axis, d):
@@ -379,15 +385,23 @@
     return [x, along(x, "z", -1), along(x, "z", 2), along(x, "z", 1)]
 
 
-def to_owner(x):
-    route = []
-    for xc in range(8):
-        for y in range(4):
-            for z in range(4):
-                src = (xc * 4 + y) * 4 + z
-                dst = ((2 * z + xc // 4) * 4 + xc % 4) * 4 + y
-                route.append((src, dst))
-    return lax.ppermute(x, ("x", "c", "y", "z"), route)
+def to_owners(pieces, y):
+    got = []
+    for step in range(4):
+        route = []
+        for xc in range(8):
+            for ys in range(4):
+                for z in range(4):
+                    src = (xc * 4 + ys) * 4 + z
+                    dst = ((2 * z + xc // 4) * 4 + xc % 4) * 4 + (ys + step) % 4
+                    route.append((src, dst))
+        piece = lax.dynamic_index_in_dim(pieces, lax.rem(y + step, 4), 0, keepdims=False)
+        got.append(lax.ppermute(piece, ("x", "c", "y", "z"), route).astype(F32))
+    return got[0] + got[1] + got[2] + got[3]
+
+
+def exchange(parts, axis):
+    return [parts[0]] + [along(parts[d], axis, d) for d in (1, 2, 3)]
 
 
 def f32(shape):
@@ -396,18 +410,12 @@
 
 def bf16(shape):
     return jax.ShapeDtypeStruct(shape, BF16)
-
-
-def reduce_xc(send, keep):
-    summed = (keep + swap(send).astype(F32)).astype(BF16)
-    got = lax.all_to_all(summed, "x", 0, 0)
-    return jnp.sum(got.astype(F32), axis=0)
 
 
 def body(events, cotangent, hist, w_in, w_out):
     z = lax.axis_index("z")
     info = jnp.concatenate(
-        [hist[0], jnp.stack([lax.axis_index("y"), z, lax.axis_index("c")]).astype(jnp.int32)]
+        [hist[0], jnp.stack([lax.axis_index("y"), z, lax.axis_index("c"), lax.axis_index("x")]).astype(jnp.int32)]
     )
     ev, cot = events[0], cotangent[0]
     evs = gather_z(ev)
@@ -439,71 +447,49 @@
         norm_body, (bf16((GRP, BLK)),) * 3, 11, 1 << 30, 4 << 20, [pltpu.VMEM((GRP, DH), F32)]
     )(info, att, gg, gate, *gather_z(stats), *dsigs)
     g_next = along(gatt, "y", -1)
+    *gp_gq, dkv = call(
+        backward_local_body, (bf16((BLK, 2 * BLK)),) * 4 + (f32((GRP, 2 * BLK)),), 9, 10 << 30, 4 << 20,
+        [pltpu.VMEM((GRP, BLK), F32)],
+    )(info, q, gatt, kv, kv_prev, gp_g, *dsigs)
+    rows_gq = exchange(gp_gq, "z")
     send_1, keep_1 = call(
         early_weights_body,
-        (bf16((4, BLK, BLK)), f32((4, BLK, BLK))), 10, 1 << 30, 4 << 20,
-        [pltpu.VMEM((D, BLK), F32), pltpu.VMEM((BLK, D), F32)],
-    )(info, *evs, *cots, gated, gp_g)
-    gp_q, dkv = call(
-        backward_local_body, (bf16((GRP, BLK)), f32((GRP, 2 * BLK))), 8, 10 << 30, 4 << 20,
-        [pltpu.VMEM((GRP, BLK), F32)],
-    )(info, q, gatt, kv, kv_prev, *dsigs)
-    gp_kv = call(
-        backward_later_body, bf16((GRP, 2 * BLK)), 8, 5 << 30, 4 << 20, [pltpu.VMEM((GRP, 2 * BLK), F32)]
+        (bf16((4, 128, 768)), f32((4, 128, 768))), 13, 2 << 30, 4 << 20,
+        [pltpu.VMEM((D, 2 * BLK), F32), pltpu.VMEM((BLK, D), F32)],
+    )(info, *evs, *cots, *gp_gq, gated)
+    got_1 = swap(send_1)
+    q_next, g_next, keep_1 = lax.optimization_barrier((q_next, g_next, keep_1))
+    gp_vk = call(
+        backward_later_body, (bf16((BLK, 2 * BLK)),) * 4, 8, 5 << 30, 4 << 20, [pltpu.VMEM((GRP, 2 * BLK), F32)]
     )(info, q_next, g_next, kv, dkv, *dsigs)
+    rows_vk = exchange(gp_vk, "z")
     send_2, keep_2 = call(
         late_weights_body,
-        (bf16((4, 128, 768)), f32((4, 128, 768))), 6, 2 << 30, 4 << 20,
-        [pltpu.VMEM((D, 768), F32)],
-    )(info, *evs, gp_q, gp_kv)
-
-    rows_g = lax.all_to_all(gp_g.reshape(NB, BLK, BLK), "z", 0, 0)
-    rows_q = lax.all_to_all(gp_q.reshape(NB, BLK, BLK), "z", 0, 0)
-    rows_kv = lax.all_to_all(gp_kv.reshape(NB, BLK, 2 * BLK), "z", 0, 0)
-    early = pl.pallas_call(
-        input_early_body,
-        grid=(4,),
-        out_shape=f32((BLK, D)),
-        in_specs=[
-            pl.BlockSpec((1, BLK, BLK), lambda s: (s, 0, 0)),
-            pl.BlockSpec((1, BLK, BLK), lambda s: (s, 0, 0)),
-            pl.BlockSpec((D, BLK), lambda s: (0, s)),
-            pl.BlockSpec((D, BLK), lambda s: (0, 8 + s)),
-            pl.BlockSpec((BLK, D), lambda s: (0, 0)),
-        ],
-        out_specs=pl.BlockSpec((BLK, D), lambda s: (0, 0)),
-        cost_estimate=pl.CostEstimate(flops=1 << 30, bytes_accessed=6 << 20, transcendentals=0),
-    )(rows_g, rows_q, w_in, w_in, cot)
-    grad_events = pl.pallas_call(
-        input_late_body,
-        grid=(4,),
-        out_shape=bf16((BLK, D)),
-        in_specs=[
-            pl.BlockSpec((1, BLK, 2 * BLK), lambda s: (s, 0, 0)),
-            pl.BlockSpec((D, BLK), lambda s: (0, 12 + s)),
-            pl.BlockSpec((D, BLK), lambda s: (0, 4 + s)),
-            pl.BlockSpec((BLK, D), lambda s: (0, 0)),
-        ],
-        out_specs=pl.BlockSpec((BLK, D), lambda s: (0, 0)),
-        scratch_shapes=[pltpu.VMEM((BLK, D), F32)],
-        cost_estimate=pl.CostEstimate(flops=1 << 30, bytes_accessed=6 << 20, transcendentals=0),
-    )(rows_kv, w_in, w_in, early)
-
-    first = reduce_xc(send_1, keep_1)
-    out_rows = first[128:].reshape(4, 32, BLK).transpose(1, 0, 2).reshape(4, 8, D).astype(BF16)
-    out_rows = jnp.sum(lax.all_to_all(out_rows, "y", 0, 0).astype(F32), axis=0)
-    grad_w_out = to_owner(out_rows.astype(BF16))
-
-    def reduce_yz(part):
-        chunks = part.astype(BF16).reshape(16, 8, part.shape[1])
-        got = lax.all_to_all(chunks, ("y", "z"), 0, 0)
-        return jnp.sum(got.reshape(4, 4, 8, part.shape[1]).astype(F32), axis=0)
-
-    gate_part = reduce_yz(first[:128])
-    late = reduce_yz(reduce_xc(send_2, keep_2))
-    pieces = [gate_part] + [late[:, :, n * BLK : (n + 1) * BLK] for n in range(3)]
-    grad_w_in = jnp.stack(pieces).transpose(2, 0, 1, 3).reshape(8, 4 * D).astype(BF16)
-    return grad_events[None], grad_w_in, grad_w_out
+        (bf16((4, 128, 512)), f32((4, 128, 512))), 8, 1 << 30, 4 << 20,
+        [pltpu.VMEM((D, 2 * BLK), F32)],
+    )(info, *evs, *gp_vk)
+    got_2 = swap(send_2)
+
+    def add_core(keep, got):
+        n = keep.shape[2]
+        *away, own = call(
+            add_core_body, (bf16((128, n)),) * 3 + (f32((128, n)),), 2, 1 << 20, 4 << 20
+        )(info, keep, got)
+        return exchange([own] + away, "x")
+
+    first = add_core(keep_1, got_1)
+    second = add_core(keep_2, got_2)
+    part_gq, part_out = call(add_early_body, (bf16((128, 512)), f32((128, BLK))), 4, 1 << 20, 1 << 20)(info, *first)
+    pieces = part_out.reshape(4, 4, 8, BLK).transpose(1, 2, 0, 3).reshape(4, 8, D).astype(BF16)
+    grad_w_out = to_owners(pieces, lax.axis_index("y")).astype(BF16)
+    early = call(input_early_body, f32((BLK, D)), 6, 1 << 30, 8 << 20)(info, *rows_gq, w_in, cot)
+    part_in = call(add_late_body, bf16((128, D)), 5, 1 << 20, 1 << 20)(info, *second, part_gq)
+    got = lax.all_to_all(part_in.reshape(16, 8, D), ("y", "z"), 0, 0)
+    grad_events = call(input_late_body, bf16((BLK, D)), 6, 1 << 30, 8 << 20)(info, *rows_vk, w_in, early)
+    got = jnp.sum(got.reshape(4, 4, 8, 4, BLK).astype(F32), axis=0)
+    got = got.transpose(1, 2, 0, 3)
+    got = jnp.stack([got[:, 0], got[:, 2], got[:, 1], got[:, 3]], axis=1)
+    return grad_events[None], got.reshape(8, 4 * D).astype(BF16), grad_w_out
 
 
 def solution(mesh):

time: 205 us -> 179 us (0.87)
  the two profiles are of different devices: /device:TPU:0 before, /device:TPU:40 now
where the time goes in v2:
time: 179 us; the launch traced here: 177 us
  starting transfers between devices  68.1 us (38%)
  Pallas kernels  49.9 us (28%)
  local copies, waits for them, and re-layouts  28.4 us (16%)
  waiting for transfers between devices  28.4 us (16%)
    ppermute x27, starting transfers between devices, along(): return lax.ppermute(x, axis, [(i, (i + d) % 4) for i in range(4)])  42.8 us
    ppermute x27, waiting for transfers between devices, along(): return lax.ppermute(x, axis, [(i, (i + d) % 4) for i in range(4)])  28.3 us
    unnamed x74, local copies, waits for them, and re-layouts  25.1 us
    ppermute x4, starting transfers between devices, to_owners(): got.append(lax.ppermute(piece, ('x', 'c', 'y', 'z'), route).astype(F32))  18.3 us
    pallas_call x1, Pallas kernels, body(): call(backward_local_body, (bf16((BLK, 2 * BLK)),) * 4 + (f32((GRP, 2 * BL...  8.78 us
    pallas_call x4, Pallas kernels, body(): call(project_body, (bf16((BLK, 2 * BLK)), bf16((BLK, BLK)), bf16((BLK, BL...  8.08 us
    all_to_all x1, starting transfers between devices, body(): got = lax.all_to_all(part_in.reshape(16, 8, D), ('y', 'z'), 0, 0)  6.78 us
    pallas_call x1, Pallas kernels, body(): call(backward_later_body, (bf16((BLK, 2 * BLK)),) * 4, 8, 5 << 30, 4 << 2...  5.63 us
  transfers between devices with their start and end apart: 34, of which 7 were waited for; matrix products, arithmetic and copies ran while one was open for 2% of the time, Pallas kernels for 26%

profile of v2, /device:TPU:40, one launch (start us, length us, event | category | flops | bytes accessed | tf_op | source)
XLA Modules:
  0.0 176.5 jit_solution(9817995124353136138)
XLA Ops:
  0.6 2.0 %collective-permute-start.2 = (bf16[256,1024]{1,0:T(8,128)(2,1)}, bf16[256,1024]{1,0:T(8,128)(2,1)}, u32[]{:S(2)}, u32[]{:S(2)}) collective-permute-start(bf16[256,1024]{1,0:T(8,128)(2,1)} %bitcast.32), channel_id=1, source_target_pairs={{0,1},{1,2},{2,3},{3,0},{4,5},{5,6},{6,7},{7,4},{8,9},{9,10},{10,1... | collective-permute-start | bytes 1572872 | tf_op jit(solution)/shard_map/ppermute | solution.py:377
  3.8 2.5 %collective-permute-start = (bf16[256,1024]{1,0:T(8,128)(2,1)}, bf16[256,1024]{1,0:T(8,128)(2,1)}, u32[]{:S(2)}, u32[]{:S(2)}) collective-permute-start(bf16[256,1024]{1,0:T(8,128)(2,1)} %bitcast.34), channel_id=1, source_target_pairs={{0,3},{1,0},{2,1},{3,2},{4,7},{5,4},{6,5},{7,6},{8,11},{9,8},{10,9... | collective-permute-start | bytes 1572872 | tf_op jit(solution)/shard_map/ppermute | solution.py:377
  8.8 2.2 %shard_map.76 = (bf16[256,512]{1,0:T(8,128)(2,1)}, bf16[256,256]{1,0:T(8,128)(2,1)S(1)}, bf16[256,256]{1,0:T(8,128)(2,1)S(1)}, bf16[256,1024]{1,0:T(8,128)(2,1)S(1)}) custom-call(s32[12]{0:T(128)S(1)} %concatenate.3.info, bf16[256,1024]{1,0:T(8,128)(2,1)S(1)} %bitcast.35, bf16[1024,256]{1,0:T(8,128)(2,1)S(1)} %get-tuple-element.112.wk, ...), custom_call_target="tpu_custom_call" | custom-call | flops 536870912 | bytes 4194304 | tf_op jit(solution)/shard_map/pallas_call | solution.py:426
  14.9 11.5 %collective-permute-done.2.ev.refs_3_ = bf16[256,1024]{1,0:T(8,128)(2,1)} collective-permute-done((bf16[256,1024]{1,0:T(8,128)(2,1)}, bf16[256,1024]{1,0:T(8,128)(2,1)}, u32[]{:S(2)}, u32[]{:S(2)}) %collective-permute-start.2) | collective-permute-done | bytes 524320 | tf_op jit(solution)/shard_map/ppermute | solution.py:377
  30.5 4.2 %collective-permute-start.9 = (bf16[256,1024]{1,0:T(8,128)(2,1)S(1)}, bf16[256,1024]{1,0:T(8,128)(2,1)S(1)}, u32[]{:S(2)}, u32[]{:S(2)}) collective-permute-start(bf16[256,1024]{1,0:T(8,128)(2,1)S(1)} %bitcast.28), channel_id=1, source_target_pairs={{0,2},{1,3},{2,0},{3,1},{4,6},{5,7},{6,4},{7,5},{8,10},{9,11},{10,... | collective-permute-start | bytes 1572872 | tf_op jit(solution)/shard_map/ppermute | solution.py:377
  41.6 6.3 %collective-permute-done.10.refs_10_.refs_7_ = bf16[256,1024]{1,0:T(8,128)(2,1)} collective-permute-done((bf16[256,1024]{1,0:T(8,128)(2,1)}, bf16[256,1024]{1,0:T(8,128)(2,1)}, u32[]{:S(2)}, u32[]{:S(2)}) %collective-permute-start.10) | collective-permute-done | bytes 524320 | tf_op jit(solution)/shard_map/ppermute | solution.py:377
  49.4 5.6 %shard_map.80 = (bf16[1024,256]{1,0:T(8,128)(2,1)S(1)}, bf16[1024,512]{1,0:T(8,128)(2,1)S(1)}, f32[1024,256]{1,0:T(8,128)S(1)}) custom-call(s32[12]{0:T(128)S(1)} %concatenate.3.info, bf16[256,256]{1,0:T(8,128)(2,1)S(1)} %copy-done.36, bf16[256,256]{1,0:T(8,128)(2,1)S(1)} %get-tuple-element.57.refs_1_, bf16[256,256]{1,0:T(8,128)(2,1)S(1)} %get-tuple-element.58.refs_2_, ...), custom_call_target="tpu_custom_call" | custom-call | flops 5368709120 | bytes 4194304 | tf_op jit(solution)/shard_map/pallas_call | solution.py:437
  55.1 4.0 %shard_map.81 = (f32[1024,256]{1,0:T(8,128)S(1)}, bf16[1024,512]{1,0:T(8,128)(2,1)S(1)}, f32[1024,256]{1,0:T(8,128)S(1)}, bf16[1024,256]{1,0:T(8,128)(2,1)S(1)}, f32[8,1024]{1,0:T(8,128)S(1)}) custom-call(s32[12]{0:T(128)S(1)} %concatenate.3.info, bf16[1024,256]{1,0:T(8,128)(2,1)S(1)} %get-tuple-element.64.refs_0_, ...), custom_call_target="tpu_custom_call" | custom-call | flops 5368709120 | bytes 4194304 | tf_op jit(solution)/shard_map/pallas_call | solution.py:441
  59.2 3.9 %collective-permute-start.12 = (f32[8,1024]{1,0:T(8,128)S(1)}, f32[8,1024]{1,0:T(8,128)S(1)}, u32[]{:S(2)}, u32[]{:S(2)}) collective-permute-start(f32[8,1024]{1,0:T(8,128)S(1)} %get-tuple-element.73.refs_3_), channel_id=1, source_target_pairs={{0,2},{1,3},{2,0},{3,1},{4,6},{5,7},{6,4},{7,5},{8,10},{9,11},{10,... | collective-permute-start | bytes 98312 | tf_op jit(solution)/shard_map/ppermute | solution.py:377
  68.7 8.8 %shard_map.83 = (bf16[256,512]{1,0:T(8,128)(2,1)S(1)}, bf16[256,512]{1,0:T(8,128)(2,1)S(1)}, bf16[256,512]{1,0:T(8,128)(2,1)S(1)}, bf16[256,512]{1,0:T(8,128)(2,1)S(1)}, f32[1024,512]{1,0:T(8,128)S(1)}) custom-call(s32[12]{0:T(128)S(1)} %concatenate.3.info, bf16[1024,256]{1,0:T(8,128)(2,1)S(1)} %get-tuple-element.64.refs_0_, ...), custom_call_target="tpu_custom_call" | custom-call | flops 10737418240 | bytes 4194304 | tf_op jit(solution)/shard_map/pallas_call | solution.py:450
  77.5 3.6 %shard_map.84 = (bf16[4,128,768]{2,1,0:T(8,128)(2,1)S(1)}, f32[4,128,768]{2,1,0:T(8,128)S(1)}) custom-call(s32[12]{0:T(128)S(1)} %concatenate.3.info, bf16[256,1024]{1,0:T(8,128)(2,1)S(1)} %bitcast.36, bf16[256,1024]{1,0:T(8,128)(2,1)} %collective-permute-done.ev.refs_1_, bf16[256,1024]{1,0:T(8,128)(2,1)} %collective-permute-done.1.ev.refs_2_, ...), custom_call_target="tpu_custom_call" | custom-call | flops 2147483648 | bytes 4194304 | tf_op jit(solution)/shard_map/pallas_call | solution.py:455
  81.2 3.7 %collective-permute-done.14.refs_1_ = bf16[1024,256]{1,0:T(8,128)(2,1)S(1)} collective-permute-done((bf16[1024,256]{1,0:T(8,128)(2,1)S(1)}, bf16[1024,256]{1,0:T(8,128)(2,1)S(1)}, u32[]{:S(2)}, u32[]{:S(2)}) %collective-permute-start.14) | collective-permute-done | bytes 524320 | tf_op jit(solution)/shard_map/ppermute | solution.py:377
  84.9 5.6 %shard_map.85 = (bf16[256,512]{1,0:T(8,128)(2,1)S(1)}, bf16[256,512]{1,0:T(8,128)(2,1)}, bf16[256,512]{1,0:T(8,128)(2,1)}, bf16[256,512]{1,0:T(8,128)(2,1)}) custom-call(s32[12]{0:T(128)S(1)} %concatenate.3.info, bf16[1024,256]{1,0:T(8,128)(2,1)S(1)} %collective-permute-done.3.refs_0_, bf16[1024,256]{1,0:T(8,128)(2,1)S(1)} %collective-permute-done.14.refs_1_, ...), custom_call_target="tpu_custom_call" | custom-call | flops 5368709120 | bytes 4194304 | tf_op jit(solution)/shard_map/pallas_call | solution.py:462
  90.6 3.1 %shard_map.88 = (bf16[4,128,512]{2,1,0:T(8,128)(2,1)S(1)}, f32[4,128,512]{2,1,0:T(8,128)S(1)}) custom-call(s32[12]{0:T(128)S(1)} %concatenate.3.info, bf16[256,1024]{1,0:T(8,128)(2,1)S(1)} %bitcast.37, bf16[256,1024]{1,0:T(8,128)(2,1)} %collective-permute-done.ev.refs_1_, bf16[256,1024]{1,0:T(8,128)(2,1)} %collective-permute-done.1.ev.refs_2_, ...), custom_call_target="tpu_custom_call" | custom-call | flops 1073741824 | bytes 4194304 | tf_op jit(solution)/shard_map/pallas_call | solution.py:466
  98.0 2.0 %collective-permute-start.26 = (bf16[128,768]{1,0:T(8,128)(2,1)S(1)}, bf16[128,768]{1,0:T(8,128)(2,1)S(1)}, u32[]{:S(2)}, u32[]{:S(2)}) collective-permute-start(bf16[128,768]{1,0:T(8,128)(2,1)S(1)} %get-tuple-element.104), channel_id=1, source_target_pairs={{0,32},{32,64},{64,96},{96,0},{1,33},{33,65},{65,97},{97,1},{2,34}... | collective-permute-start | bytes 589832 | tf_op jit(solution)/shard_map/ppermute | solution.py:377
  100.0 2.9 %collective-permute-done.18.refs_1_ = bf16[256,512]{1,0:T(8,128)(2,1)S(1)} collective-permute-done((bf16[256,512]{1,0:T(8,128)(2,1)S(1)}, bf16[256,512]{1,0:T(8,128)(2,1)S(1)}, u32[]{:S(2)}, u32[]{:S(2)}) %collective-permute-start.18) | collective-permute-done | bytes 262176 | tf_op jit(solution)/shard_map/ppermute | solution.py:377
  104.8 2.2 %collective-permute-start.28 = (bf16[128,768]{1,0:T(8,128)(2,1)S(1)}, bf16[128,768]{1,0:T(8,128)(2,1)S(1)}, u32[]{:S(2)}, u32[]{:S(2)}) collective-permute-start(bf16[128,768]{1,0:T(8,128)(2,1)S(1)} %get-tuple-element.106), channel_id=1, source_target_pairs={{0,96},{32,0},{64,32},{96,64},{1,97},{33,1},{65,33},{97,65},{2,98}... | collective-permute-start | bytes 589832 | tf_op jit(solution)/shard_map/ppermute | solution.py:377
  112.8 8.6 %collective-permute-start.16 = (bf16[256,512]{1,0:T(8,128)(2,1)}, bf16[256,512]{1,0:T(8,128)(2,1)}, u32[]{:S(2)}, u32[]{:S(2)}) collective-permute-start(bf16[256,512]{1,0:T(8,128)(2,1)} %get-tuple-element.93.refs_6_), channel_id=1, source_target_pairs={{0,2},{1,3},{2,0},{3,1},{4,6},{5,7},{6,4},{7,5},{8,10},{9,11},{10,... | collective-permute-start | bytes 786440 | tf_op jit(solution)/shard_map/ppermute | solution.py:377
  126.3 3.4 %copy-done.1 = bf16[1024,4096]{1,0:T(8,128)(2,1)S(1)} copy-done((bf16[1024,4096]{1,0:T(8,128)(2,1)S(1)}, bf16[1024,4096]{1,0:T(8,128)(2,1)}, u32[]{:S(2)}) %copy-start.1) | copy-done | bytes 8388632
  139.8 7.6 %collective-permute-start.30 = (bf16[8,1024]{1,0:T(8,128)(2,1)S(1)}, bf16[8,1024]{1,0:T(8,128)(2,1)S(1)}, u32[]{:S(2)}, u32[]{:S(2)}) collective-permute-start(bf16[8,1024]{1,0:T(8,128)(2,1)S(1)} %get-tuple-element.116), channel_id=1, source_target_pairs={{0,1},{1,33},{2,65},{3,97},{4,2},{5,34},{6,66},{7,98},{8,3},{9,35}... | collective-permute-start | bytes 49160 | tf_op jit(solution)/shard_map/ppermute | solution.py:399
  151.9 6.8 %all-to-all-start = ((bf16[16,8,1024]{2,1,0:T(8,128)(2,1)}), bf16[16,8,1024]{2,1,0:T(8,128)(2,1)S(1)}, u32[]{:S(2)}, u32[]{:S(2)}) async-start(bf16[16,8,1024]{2,1,0:T(8,128)(2,1)} %bitcast.8), calls=%async_computation | async-start | bytes 524288 | tf_op jit(solution)/shard_map/all_to_all | solution.py:487
  159.4 8.1 %collective-permute-start.32 = (bf16[8,1024]{1,0:T(8,128)(2,1)S(1)}, bf16[8,1024]{1,0:T(8,128)(2,1)S(1)}, u32[]{:S(2)}, u32[]{:S(2)}) collective-permute-start(bf16[8,1024]{1,0:T(8,128)(2,1)S(1)} %get-tuple-element.114), channel_id=1, source_target_pairs={{0,3},{1,35},{2,67},{3,99},{4,0},{5,32},{6,64},{7,96},{8,1},{9,33}... | collective-permute-start | bytes 49160 | tf_op jit(solution)/shard_map/ppermute | solution.py:399
  167.5 3.4 %copy-done.2 = bf16[1024,4096]{1,0:T(8,128)(2,1)S(1)} copy-done((bf16[1024,4096]{1,0:T(8,128)(2,1)S(1)}, bf16[1024,4096]{1,0:T(8,128)(2,1)}, u32[]{:S(2)}) %copy-start.2) | copy-done | bytes 8388632
  171.9 3.2 %shard_map.87 = bf16[256,1024]{1,0:T(8,128)(2,1)} custom-call(s32[12]{0:T(128)S(1)} %concatenate.3.info, bf16[256,512]{1,0:T(8,128)(2,1)S(1)} %copy-done.14, bf16[256,512]{1,0:T(8,128)(2,1)} %collective-permute-done.15.refs_1_, bf16[256,512]{1,0:T(8,128)(2,1)} %collective-permute-done.16.refs_2_, bf16[256,512]{1,0:T(8,128)(2,1)} %collective-permute-done.17.refs_3_, ...), custom_call_target="tpu_custom_call" | custom-call | flops 1073741824 | bytes 8388608 | tf_op jit(solution)/shard_map/pallas_call | solution.py:488
  (148 shorter events, 60.4 us)
Async XLA Ops:
  0.6 25.7 %collective-permute-start.2 = (bf16[256,1024]{1,0:T(8,128)(2,1)}, bf16[256,1024]{1,0:T(8,128)(2,1)}, u32[]{:S(2)}, u32[]{:S(2)}) collective-permute-start(bf16[256,1024]{1,0:T(8,128)(2,1)} %bitcast.32), channel_id=1, source_target_pairs={{0,1},{1,2},{2,3},{3,0},{4,5},{5,6},{6,7},{7,4},{8,9},{9,10},{10,1... | collective-permute-start | bytes 1572872 | tf_op jit(solution)/shard_map/ppermute | solution.py:377
  2.6 27.8 %collective-permute-start.1 = (bf16[256,1024]{1,0:T(8,128)(2,1)}, bf16[256,1024]{1,0:T(8,128)(2,1)}, u32[]{:S(2)}, u32[]{:S(2)}) collective-permute-start(bf16[256,1024]{1,0:T(8,128)(2,1)} %bitcast.33), channel_id=1, source_target_pairs={{0,2},{1,3},{2,0},{3,1},{4,6},{5,7},{6,4},{7,5},{8,10},{9,11},{10,... | collective-permute-start | bytes 1572872 | tf_op jit(solution)/shard_map/ppermute | solution.py:377
  3.8 32.8 %collective-permute-start = (bf16[256,1024]{1,0:T(8,128)(2,1)}, bf16[256,1024]{1,0:T(8,128)(2,1)}, u32[]{:S(2)}, u32[]{:S(2)}) collective-permute-start(bf16[256,1024]{1,0:T(8,128)(2,1)} %bitcast.34), channel_id=1, source_target_pairs={{0,3},{1,0},{2,1},{3,2},{4,7},{5,4},{6,5},{7,6},{8,11},{9,8},{10,9... | collective-permute-start | bytes 1572872 | tf_op jit(solution)/shard_map/ppermute | solution.py:377
  6.3 41.5 %collective-permute-start.10 = (bf16[256,1024]{1,0:T(8,128)(2,1)}, bf16[256,1024]{1,0:T(8,128)(2,1)}, u32[]{:S(2)}, u32[]{:S(2)}) collective-permute-start(bf16[256,1024]{1,0:T(8,128)(2,1)} %bitcast.26), channel_id=1, source_target_pairs={{0,1},{1,2},{2,3},{3,0},{4,5},{5,6},{6,7},{7,4},{8,9},{9,10},{10,1... | collective-permute-start | bytes 1572872 | tf_op jit(solution)/shard_map/ppermute | solution.py:377
  13.2 27.0 %collective-permute-start.4 = (bf16[256,512]{1,0:T(8,128)(2,1)}, bf16[256,512]{1,0:T(8,128)(2,1)S(1)}, u32[]{:S(2)}, u32[]{:S(2)}) collective-permute-start(bf16[256,512]{1,0:T(8,128)(2,1)} %get-tuple-element.60.refs_4_), channel_id=1, source_target_pairs={{0,4},{4,8},{8,12},{12,0},{1,5},{5,9},{9,13},{13,1},{2,6},{6,10},{... | collective-permute-start | bytes 786440 | tf_op jit(solution)/shard_map/ppermute | solution.py:377
  26.4 28.7 %collective-permute-start.8 = (bf16[256,1024]{1,0:T(8,128)(2,1)}, bf16[256,1024]{1,0:T(8,128)(2,1)S(1)}, u32[]{:S(2)}, u32[]{:S(2)}) collective-permute-start(bf16[256,1024]{1,0:T(8,128)(2,1)} %bitcast.27), channel_id=1, source_target_pairs={{0,3},{1,0},{2,1},{3,2},{4,7},{5,4},{6,5},{7,6},{8,11},{9,8},{10,9... | collective-permute-start | bytes 1572872 | tf_op jit(solution)/shard_map/ppermute | solution.py:377
  30.5 24.6 %collective-permute-start.9 = (bf16[256,1024]{1,0:T(8,128)(2,1)S(1)}, bf16[256,1024]{1,0:T(8,128)(2,1)S(1)}, u32[]{:S(2)}, u32[]{:S(2)}) collective-permute-start(bf16[256,1024]{1,0:T(8,128)(2,1)S(1)} %bitcast.28), channel_id=1, source_target_pairs={{0,2},{1,3},{2,0},{3,1},{4,6},{5,7},{6,4},{7,5},{8,10},{9,11},{10,... | collective-permute-start | bytes 1572872 | tf_op jit(solution)/shard_map/ppermute | solution.py:377
  36.6 18.5 %collective-permute-start.7 = (bf16[256,512]{1,0:T(8,128)(2,1)S(1)}, bf16[256,512]{1,0:T(8,128)(2,1)S(1)}, u32[]{:S(2)}, u32[]{:S(2)}) collective-permute-start(bf16[256,512]{1,0:T(8,128)(2,1)S(1)} %get-tuple-element.63.refs_7_), channel_id=1, source_target_pairs={{0,4},{4,8},{8,12},{12,0},{1,5},{5,9},{9,13},{13,1},{2,6},{6,10},{... | collective-permute-start | bytes 786440 | tf_op jit(solution)/shard_map/ppermute | solution.py:377
  40.2 14.9 %collective-permute-start.6 = (bf16[256,512]{1,0:T(8,128)(2,1)S(1)}, bf16[256,512]{1,0:T(8,128)(2,1)S(1)}, u32[]{:S(2)}, u32[]{:S(2)}) collective-permute-start(bf16[256,512]{1,0:T(8,128)(2,1)S(1)} %get-tuple-element.62.refs_6_), channel_id=1, source_target_pairs={{0,4},{4,8},{8,12},{12,0},{1,5},{5,9},{9,13},{13,1},{2,6},{6,10},{... | collective-permute-start | bytes 786440 | tf_op jit(solution)/shard_map/ppermute | solution.py:377
  63.1 18.1 %collective-permute-start.3 = (bf16[1024,256]{1,0:T(8,128)(2,1)S(1)}, bf16[1024,256]{1,0:T(8,128)(2,1)S(1)}, u32[]{:S(2)}, u32[]{:S(2)}) collective-permute-start(bf16[1024,256]{1,0:T(8,128)(2,1)S(1)} %get-tuple-element.64.refs_0_), channel_id=1, source_target_pairs={{0,12},{4,0},{8,4},{12,8},{1,13},{5,1},{9,5},{13,9},{2,14},{6,2},{... | collective-permute-start | bytes 1572872 | tf_op jit(solution)/shard_map/ppermute | solution.py:377
  68.6 16.3 %collective-permute-start.14 = (bf16[1024,256]{1,0:T(8,128)(2,1)S(1)}, bf16[1024,256]{1,0:T(8,128)(2,1)S(1)}, u32[]{:S(2)}, u32[]{:S(2)}) collective-permute-start(bf16[1024,256]{1,0:T(8,128)(2,1)S(1)} %get-tuple-element.78.refs_1_), channel_id=1, source_target_pairs={{0,12},{4,0},{8,4},{12,8},{1,13},{5,1},{9,5},{13,9},{2,14},{6,2},{... | collective-permute-start | bytes 1572872 | tf_op jit(solution)/shard_map/ppermute | solution.py:377
  81.1 16.2 %collective-permute-start.25 = (bf16[4,128,768]{2,1,0:T(8,128)(2,1)S(1)}, bf16[4,128,768]{2,1,0:T(8,128)(2,1)S(1)}, u32[]{:S(2)}, u32[]{:S(2)}) collective-permute-start(bf16[4,128,768]{2,1,0:T(8,128)(2,1)S(1)} %get-tuple-element.102), channel_id=1, source_target_pairs={{0,16},{16,0},{1,17},{17,1},{2,18},{18,2},{3,19},{19,3},{4,20},{20... | collective-permute-start | bytes 2359304 | tf_op jit(solution)/shard_map/ppermute | solution.py:381
  102.9 18.4 %collective-permute-start.27 = (bf16[128,768]{1,0:T(8,128)(2,1)S(1)}, bf16[128,768]{1,0:T(8,128)(2,1)S(1)}, u32[]{:S(2)}, u32[]{:S(2)}) collective-permute-start(bf16[128,768]{1,0:T(8,128)(2,1)S(1)} %get-tuple-element.105), channel_id=1, source_target_pairs={{0,64},{32,96},{64,0},{96,32},{1,65},{33,97},{65,1},{97,33},{2,66}... | collective-permute-start | bytes 589832 | tf_op jit(solution)/shard_map/ppermute | solution.py:377
  104.8 17.2 %collective-permute-start.28 = (bf16[128,768]{1,0:T(8,128)(2,1)S(1)}, bf16[128,768]{1,0:T(8,128)(2,1)S(1)}, u32[]{:S(2)}, u32[]{:S(2)}) collective-permute-start(bf16[128,768]{1,0:T(8,128)(2,1)S(1)} %get-tuple-element.106), channel_id=1, source_target_pairs={{0,96},{32,0},{64,32},{96,64},{1,97},{33,1},{65,33},{97,65},{2,98}... | collective-permute-start | bytes 589832 | tf_op jit(solution)/shard_map/ppermute | solution.py:377
  110.4 48.3 %collective-permute-start.15 = (bf16[256,512]{1,0:T(8,128)(2,1)}, bf16[256,512]{1,0:T(8,128)(2,1)}, u32[]{:S(2)}, u32[]{:S(2)}) collective-permute-start(bf16[256,512]{1,0:T(8,128)(2,1)} %get-tuple-element.92.refs_5_), channel_id=1, source_target_pairs={{0,1},{1,2},{2,3},{3,0},{4,5},{5,6},{6,7},{7,4},{8,9},{9,10},{10,1... | collective-permute-start | bytes 786440 | tf_op jit(solution)/shard_map/ppermute | solution.py:377
  112.8 46.7 %collective-permute-start.16 = (bf16[256,512]{1,0:T(8,128)(2,1)}, bf16[256,512]{1,0:T(8,128)(2,1)}, u32[]{:S(2)}, u32[]{:S(2)}) collective-permute-start(bf16[256,512]{1,0:T(8,128)(2,1)} %get-tuple-element.93.refs_6_), channel_id=1, source_target_pairs={{0,2},{1,3},{2,0},{3,1},{4,6},{5,7},{6,4},{7,5},{8,10},{9,11},{10,... | collective-permute-start | bytes 786440 | tf_op jit(solution)/shard_map/ppermute | solution.py:377
  122.0 45.5 %collective-permute-start.17 = (bf16[256,512]{1,0:T(8,128)(2,1)}, bf16[256,512]{1,0:T(8,128)(2,1)}, u32[]{:S(2)}, u32[]{:S(2)}) collective-permute-start(bf16[256,512]{1,0:T(8,128)(2,1)} %get-tuple-element.94.refs_7_), channel_id=1, source_target_pairs={{0,3},{1,0},{2,1},{3,2},{4,7},{5,4},{6,5},{7,6},{8,11},{9,8},{10,9... | collective-permute-start | bytes 786440 | tf_op jit(solution)/shard_map/ppermute | solution.py:377
  122.7 15.2 %collective-permute-start.23 = (bf16[128,512]{1,0:T(8,128)(2,1)}, bf16[128,512]{1,0:T(8,128)(2,1)}, u32[]{:S(2)}, u32[]{:S(2)}) collective-permute-start(bf16[128,512]{1,0:T(8,128)(2,1)} %get-tuple-element.99), channel_id=1, source_target_pairs={{0,64},{32,96},{64,0},{96,32},{1,65},{33,97},{65,1},{97,33},{2,66}... | collective-permute-start | bytes 393224 | tf_op jit(solution)/shard_map/ppermute | solution.py:377
  124.6 15.2 %collective-permute-start.24 = (bf16[128,512]{1,0:T(8,128)(2,1)}, bf16[128,512]{1,0:T(8,128)(2,1)}, u32[]{:S(2)}, u32[]{:S(2)}) collective-permute-start(bf16[128,512]{1,0:T(8,128)(2,1)} %get-tuple-element.100), channel_id=1, source_target_pairs={{0,96},{32,0},{64,32},{96,64},{1,97},{33,1},{65,33},{97,65},{2,98}... | collective-permute-start | bytes 393224 | tf_op jit(solution)/shard_map/ppermute | solution.py:377
  137.9 37.2 %collective-permute-start.29 = (bf16[8,1024]{1,0:T(8,128)(2,1)S(1)}, bf16[8,1024]{1,0:T(8,128)(2,1)S(1)}, u32[]{:S(2)}, u32[]{:S(2)}) collective-permute-start(bf16[8,1024]{1,0:T(8,128)(2,1)S(1)} %get-tuple-element.113), channel_id=1, source_target_pairs={{0,0},{1,32},{2,64},{3,96},{4,1},{5,33},{6,65},{7,97},{8,2},{9,34}... | collective-permute-start | bytes 49160 | tf_op jit(solution)/shard_map/ppermute | solution.py:399
  139.8 35.3 %collective-permute-start.30 = (bf16[8,1024]{1,0:T(8,128)(2,1)S(1)}, bf16[8,1024]{1,0:T(8,128)(2,1)S(1)}, u32[]{:S(2)}, u32[]{:S(2)}) collective-permute-start(bf16[8,1024]{1,0:T(8,128)(2,1)S(1)} %get-tuple-element.116), channel_id=1, source_target_pairs={{0,1},{1,33},{2,65},{3,97},{4,2},{5,34},{6,66},{7,98},{8,3},{9,35}... | collective-permute-start | bytes 49160 | tf_op jit(solution)/shard_map/ppermute | solution.py:399
  151.9 23.8 %all-to-all-start = ((bf16[16,8,1024]{2,1,0:T(8,128)(2,1)}), bf16[16,8,1024]{2,1,0:T(8,128)(2,1)S(1)}, u32[]{:S(2)}, u32[]{:S(2)}) async-start(bf16[16,8,1024]{2,1,0:T(8,128)(2,1)} %bitcast.8), calls=%async_computation | async-start | bytes 524288 | tf_op jit(solution)/shard_map/all_to_all | solution.py:487
  158.7 16.4 %collective-permute-start.31 = (bf16[8,1024]{1,0:T(8,128)(2,1)S(1)}, bf16[8,1024]{1,0:T(8,128)(2,1)S(1)}, u32[]{:S(2)}, u32[]{:S(2)}) collective-permute-start(bf16[8,1024]{1,0:T(8,128)(2,1)S(1)} %get-tuple-element.115), channel_id=1, source_target_pairs={{0,2},{1,34},{2,66},{3,98},{4,3},{5,35},{6,67},{7,99},{8,0},{9,32}... | collective-permute-start | bytes 49160 | tf_op jit(solution)/shard_map/ppermute | solution.py:399
  159.4 15.6 %collective-permute-start.32 = (bf16[8,1024]{1,0:T(8,128)(2,1)S(1)}, bf16[8,1024]{1,0:T(8,128)(2,1)S(1)}, u32[]{:S(2)}, u32[]{:S(2)}) collective-permute-start(bf16[8,1024]{1,0:T(8,128)(2,1)S(1)} %get-tuple-element.114), channel_id=1, source_target_pairs={{0,3},{1,35},{2,67},{3,99},{4,0},{5,32},{6,64},{7,96},{8,1},{9,33}... | collective-permute-start | bytes 49160 | tf_op jit(solution)/shard_map/ppermute | solution.py:399
  (47 other events, 219.6 us)

commit v3 on v2

--- a/solution.py
+++ b/solution.py
@@ -72,21 +72,31 @@
     return slice(base + h * DH, base + (h + 1) * DH)
 
 
-def project_body(info, ev, wk, wv, wq, wg, kv, q, g, dsig):
-    x = ev[...]
-    for p, w in enumerate((wg, wv, wq, wk)):
-        proj = nn(x, w[...])
-        sig = 0.5 + 0.5 * jnp.tanh(0.5 * proj)
-        act = (proj * sig).astype(BF16)
-        if p == 0:
-            g[...] = act
-        elif p == 1:
-            kv[:, BLK:] = act
-        elif p == 2:
-            q[...] = (0.5 * act.astype(F32)).astype(BF16)
-        else:
-            kv[:, :BLK] = act
-        dsig[:, p * BLK : (p + 1) * BLK] = (sig * (1.0 + proj * (1.0 - sig))).astype(BF16)
+def project_body(info, *refs):
+    n = (len(refs) - 4) // 2
+    ev, (w, kv, q, g), dsig = refs[:n], refs[n : n + 4], refs[n + 4 :]
+    for b in range(n):
+        x, at = ev[b][...], slice(b * BLK, (b + 1) * BLK)
+        for p in range(4):
+            lanes = pl.ds(pl.multiple_of(p * D + info[9] * BLK, BLK), BLK)
+            proj = nn(x, w[:, lanes])
+            sig = 0.5 + 0.5 * jnp.tanh(0.5 * proj)
+            act = (proj * sig).astype(BF16)
+            if p == 0:
+                g[at, :] = act
+            elif p == 1:
+                kv[at, BLK:] = act
+            elif p == 2:
+                q[at, :] = (0.5 * act.astype(F32)).astype(BF16)
+            else:
+                kv[at, :BLK] = act
+            dsig[b][:, p * BLK : (p + 1) * BLK] = (sig * (1.0 + proj * (1.0 - sig))).astype(BF16)
+
+
+def grad_gated_body(info, cot, w, *outs):
+    for d in range(NB):
+        out_rows = rows(lax.rem(info[9] + d, NB))
+        outs[d][...] = nt(cot[...], w[out_rows, :]).astype(BF16)
 
 
 def keep_rows(qpos, kpos, ends):
@@ -108,15 +118,20 @@
         att[rows(i), head(h)] += nn(w, kv[rows(j), head(h, BLK)])
 
 
+def block_of(parts, k):
+    part, at = ((0, 0), (1, 0), (2, 0), (1, BLK))[k]
+    return parts[part][at : at + BLK, :]
+
+
 def forward_local_body(info, *refs):
-    q_in, kv_in = refs[0:4], refs[4:8]
-    q, kv, att = refs[8:]
+    q_in, kv_in = refs[0:3], refs[3:6]
+    q, kv, att = refs[6:]
     ends = history_ends(info)
     base = info[8] * GRP
     for k in range(NB):
         at = rows(lax.rem(info[9] + k, NB))
-        q[at, :] = q_in[k][...]
-        kv[at, :] = kv_in[k][...]
+        q[at, :] = block_of(q_in, k)
+        kv[at, :] = block_of(kv_in, k)
     att[...] = jnp.zeros_like(att)
 
     def over_i(i, _):
@@ -138,18 +153,18 @@
 
 
 def forward_halo_body(info, *refs):
-    q, att_in, wout = refs[0:3]
-    kv_in, cot, gate_in = refs[3:7], refs[7:11], refs[11:15]
-    att, kv, gg, gate, stats = refs[15:20]
+    q, att_in = refs[0:2]
+    kv_in, gg_in, gate_in = refs[2:5], refs[5:9], refs[9:12]
+    att, kv, gg, gate, stats = refs[12:17]
     ends = history_ends(info)
     base = info[8] * GRP
     prev = base - GRP
     att[...] = att_in[...]
     for k in range(NB):
         at = rows(lax.rem(info[9] + k, NB))
-        kv[at, :] = kv_in[k][...]
-        gate[at, :] = gate_in[k][...]
-        gg[at, :] = nt(cot[k][...], wout[...])
+        kv[at, :] = block_of(kv_in, k)
+        gate[at, :] = block_of(gate_in, k)
+        gg[at, :] = gg_in[(4 - k) % 4][...]
 
     def over_i(i, _):
         qpos = base + i * BLK
@@ -162,7 +177,7 @@
 
     lax.fori_loop(0, NB, over_i, 0)
     a = att[...]
-    gn = gg[...] * gate[...].astype(F32)
+    gn = gg[...].astype(F32) * gate[...].astype(F32)
     mean = jnp.sum(a, axis=1, keepdims=True) / BLK
     cent = a - mean
     m2 = jnp.sum(cent * cent, axis=1, keepdims=True)
@@ -197,42 +212,38 @@
         mean_c, inv_c, g1_c, ga_c = (t[:, n : n + 1] for n in range(4))
         normed = (att[at, :] - mean_c) * inv_c
         g = gate[at, :].astype(F32)
-        grad_gated = gg[at, :]
+        grad_gated = gg[at, :].astype(F32)
         gatt[at, :] = (inv_c * (grad_gated * g - g1_c - normed * ga_c)).astype(BF16)
         gated[at, :] = (normed * g).astype(BF16)
         gp[at, :] = (grad_gated * normed * dsig[k][:, 0:BLK].astype(F32)).astype(BF16)
 
 
 def early_weights_body(info, *refs):
-    ev, cot, gp = refs[0:4], refs[4:8], refs[8:12]
-    gated, send, keep, acc_in, acc_out = refs[12:17]
-    for k in range(NB):
-        part_in = tn(ev[k][...], gp[k][...])
-        part_out = tn(gated[rows(lax.rem(info[9] + k, NB)), :], cot[k][...])
+    ev, cot = refs[0:4], refs[4:8]
+    gated, gp, out, acc_in, acc_out = refs[8:13]
+    for k in range(NB):
+        at = rows(lax.rem(info[9] + k, NB))
+        part_in = tn(ev[k][...], gp[at, :])
+        part_out = tn(gated[at, :], cot[k][...])
         if k:
             part_in += acc_in[...]
             part_out += acc_out[...]
         acc_in[...] = part_in
         acc_out[...] = part_out
-    for x in range(4):
-        for out, c, kind in ((send, 1 - info[10], BF16), (keep, info[10], F32)):
-            big = pl.multiple_of((x * 2 + c) * 128, 128)
-            small = pl.multiple_of((x * 2 + c) * 32, 32)
-            out[x, :, 0:512] = acc_in[pl.ds(big, 128), :].astype(kind)
-            for n in range(4):
-                out[x, 32 * n : 32 * n + 32, 512:768] = acc_out[
-                    pl.ds(small, 32), n * BLK : (n + 1) * BLK
-                ].astype(kind)
+    for n in range(8):
+        out[n, :, :BLK] = acc_in[n * 128 : (n + 1) * 128, :]
+        for m in range(4):
+            out[n, 32 * m : 32 * m + 32, BLK:] = acc_out[n * 32 : (n + 1) * 32, m * BLK : (m + 1) * BLK]
 
 
 def late_weights_body(info, *refs):
-    ev, gp = refs[0:4], refs[4:8]
-    send, keep, acc = refs[8:11]
-    for k in range(NB):
-        part = tn(ev[k][...], gp[k][...])
-        if k:
-            part += acc[...]
-        acc[...] = part
+    ev, gq, vk = refs[0:4], refs[4:8], refs[8:12]
+    send, keep, acc = refs[12:15]
+    for k in range(NB):
+        x = ev[k][...]
+        for lanes, gp in ((slice(0, BLK), gq[k][:, BLK:]), (slice(BLK, 3 * BLK), vk[k][...])):
+            part = tn(x, gp)
+            acc[:, lanes] = part if k == 0 else acc[:, lanes] + part
     for x in range(4):
         for out, c, kind in ((send, 1 - info[10], BF16), (keep, info[10], F32)):
             at = pl.multiple_of((x * 2 + c) * 128, 128)
@@ -246,16 +257,15 @@
         out[...] = (keep[at] + got[at].astype(F32)).astype(BF16)
 
 
-def add_early_body(info, own, got_1, got_2, got_3, part_in, part_out):
+def add_x_body(info, own, got_1, got_2, got_3, early, part_in, *pieces):
     total = own[...] + got_1[...].astype(F32) + got_2[...].astype(F32) + got_3[...].astype(F32)
-    part_in[...] = total[:, 0:512].astype(BF16)
-    part_out[...] = total[:, 512:768]
-
-
-def add_late_body(info, own, got_1, got_2, got_3, early, part_in):
-    total = own[...] + got_1[...].astype(F32) + got_2[...].astype(F32) + got_3[...].astype(F32)
-    part_in[:, 0:512] = early[...]
-    part_in[:, 512:1024] = total.astype(BF16)
+    part_in[:, :BLK] = early[:, :BLK].astype(BF16)
+    part_in[:, BLK:] = total.astype(BF16)
+    for step in range(4):
+        p = lax.rem(info[8] + step, 4)
+        for n in range(4):
+            at = pl.ds(pl.multiple_of(n * 32 + p * 8, 8), 8)
+            pieces[step][:, n * BLK : (n + 1) * BLK] = early[at, BLK:]
 
 
 def silu_parts(u):
@@ -385,18 +395,17 @@
     return [x, along(x, "z", -1), along(x, "z", 2), along(x, "z", 1)]
 
 
-def to_owners(pieces, y):
+def to_owners(pieces):
     got = []
     for step in range(4):
         route = []
         for xc in range(8):
-            for ys in range(4):
+            for y in range(4):
                 for z in range(4):
-                    src = (xc * 4 + ys) * 4 + z
-                    dst = ((2 * z + xc // 4) * 4 + xc % 4) * 4 + (ys + step) % 4
+                    src = (xc * 4 + y) * 4 + z
+                    dst = ((2 * z + xc // 4) * 4 + xc % 4) * 4 + (y + step) % 4
                     route.append((src, dst))
-        piece = lax.dynamic_index_in_dim(pieces, lax.rem(y + step, 4), 0, keepdims=False)
-        got.append(lax.ppermute(piece, ("x", "c", "y", "z"), route).astype(F32))
+        got.append(lax.ppermute(pieces[step], ("x", "c", "y", "z"), route))
     return got[0] + got[1] + got[2] + got[3]
 
 
@@ -419,77 +428,74 @@
     )
     ev, cot = events[0], cotangent[0]
     evs = gather_z(ev)
-    wg, wv, wq, wk = (lax.dynamic_slice(w_in, (0, p * D + z * BLK), (D, BLK)) for p in range(4))
-    wout = lax.dynamic_slice(w_out, (z * BLK, 0), (BLK, D))
-    kvs, qs, gs, dsigs, kv_prevs = [], [], [], [], []
-    for k in range(NB):
-        kv, q, g, dsig = call(
+    kvs, qs, gs, dsigs, kv_prevs = [], [], [], [None] * 4, []
+    for blocks in ((0,), (1, 3), (2,)):
+        n = len(blocks)
+        kv, q, g, *dsig = call(
             project_body,
-            (bf16((BLK, 2 * BLK)), bf16((BLK, BLK)), bf16((BLK, BLK)), bf16((BLK, 4 * BLK))),
-            5, 2 * BLK * D * D, 4 << 20,
-        )(info, evs[k], wk, wv, wq, wg)
+            (bf16((n * BLK, 2 * BLK)), bf16((n * BLK, BLK)), bf16((n * BLK, BLK))) + (bf16((BLK, 4 * BLK)),) * n,
+            n + 1, 2 * n * BLK * D * D, 4 << 20,
+        )(info, *[evs[b] for b in blocks], w_in)
         kvs.append(kv)
         qs.append(q)
         gs.append(g)
-        dsigs.append(dsig)
+        for b, d in zip(blocks, dsig):
+            dsigs[b] = d
         kv_prevs.append(along(kv, "y", 1))
-    cots = gather_z(cot)
+    ggs = call(grad_gated_body, (bf16((BLK, BLK)),) * 4, 2, 1 << 29, 2 << 20)(info, cot, w_out)
+    ggs = exchange(ggs, "z")
+    cot_late, _ = lax.optimization_barrier((cot, kvs[2]))
+    cots = gather_z(cot_late)
     q, kv, att = call(
-        forward_local_body, (bf16((GRP, BLK)), bf16((GRP, 2 * BLK)), f32((GRP, BLK))), 8, 5 << 30, 4 << 20
+        forward_local_body, (bf16((GRP, BLK)), bf16((GRP, 2 * BLK)), f32((GRP, BLK))), 6, 5 << 30, 4 << 20
     )(info, *qs, *kvs)
     q_next = along(q, "y", -1)
     att, kv_prev, gg, gate, stats = call(
         forward_halo_body,
-        (f32((GRP, BLK)), bf16((GRP, 2 * BLK)), f32((GRP, BLK)), bf16((GRP, BLK)), f32((8, GRP))),
-        15, 5 << 30, 4 << 20,
-    )(info, q, att, wout, *kv_prevs, *cots, *gs)
+        (f32((GRP, BLK)), bf16((GRP, 2 * BLK)), bf16((GRP, BLK)), bf16((GRP, BLK)), f32((8, GRP))),
+        12, 5 << 30, 4 << 20,
+    )(info, q, att, *kv_prevs, *ggs, *gs)
     gatt, gated, gp_g = call(
         norm_body, (bf16((GRP, BLK)),) * 3, 11, 1 << 30, 4 << 20, [pltpu.VMEM((GRP, DH), F32)]
     )(info, att, gg, gate, *gather_z(stats), *dsigs)
     g_next = along(gatt, "y", -1)
+    part = call(
+        early_weights_body, f32((8, 128, 512)), 10, 1 << 30, 4 << 20,
+        [pltpu.VMEM((D, BLK), F32), pltpu.VMEM((BLK, D), F32)],
+    )(info, *evs, *cots, gated, gp_g)
+    early_sum = lax.psum_scatter(part, ("x", "c"), scatter_dimension=0)
+    gatt, _ = lax.optimization_barrier((gatt, part))
     *gp_gq, dkv = call(
         backward_local_body, (bf16((BLK, 2 * BLK)),) * 4 + (f32((GRP, 2 * BLK)),), 9, 10 << 30, 4 << 20,
         [pltpu.VMEM((GRP, BLK), F32)],
     )(info, q, gatt, kv, kv_prev, gp_g, *dsigs)
     rows_gq = exchange(gp_gq, "z")
-    send_1, keep_1 = call(
-        early_weights_body,
-        (bf16((4, 128, 768)), f32((4, 128, 768))), 13, 2 << 30, 4 << 20,
-        [pltpu.VMEM((D, 2 * BLK), F32), pltpu.VMEM((BLK, D), F32)],
-    )(info, *evs, *cots, *gp_gq, gated)
-    got_1 = swap(send_1)
-    q_next, g_next, keep_1 = lax.optimization_barrier((q_next, g_next, keep_1))
     gp_vk = call(
         backward_later_body, (bf16((BLK, 2 * BLK)),) * 4, 8, 5 << 30, 4 << 20, [pltpu.VMEM((GRP, 2 * BLK), F32)]
     )(info, q_next, g_next, kv, dkv, *dsigs)
     rows_vk = exchange(gp_vk, "z")
-    send_2, keep_2 = call(
+    gp_late, rows_gq = lax.optimization_barrier((gp_vk, rows_gq))
+    send, keep = call(
         late_weights_body,
-        (bf16((4, 128, 512)), f32((4, 128, 512))), 8, 1 << 30, 4 << 20,
-        [pltpu.VMEM((D, 2 * BLK), F32)],
-    )(info, *evs, *gp_vk)
-    got_2 = swap(send_2)
-
-    def add_core(keep, got):
-        n = keep.shape[2]
-        *away, own = call(
-            add_core_body, (bf16((128, n)),) * 3 + (f32((128, n)),), 2, 1 << 20, 4 << 20
-        )(info, keep, got)
-        return exchange([own] + away, "x")
-
-    first = add_core(keep_1, got_1)
-    second = add_core(keep_2, got_2)
-    part_gq, part_out = call(add_early_body, (bf16((128, 512)), f32((128, BLK))), 4, 1 << 20, 1 << 20)(info, *first)
-    pieces = part_out.reshape(4, 4, 8, BLK).transpose(1, 2, 0, 3).reshape(4, 8, D).astype(BF16)
-    grad_w_out = to_owners(pieces, lax.axis_index("y")).astype(BF16)
+        (bf16((4, 128, 768)), f32((4, 128, 768))), 12, 2 << 30, 4 << 20,
+        [pltpu.VMEM((D, 3 * BLK), F32)],
+    )(info, *evs, *gp_gq, *gp_late)
+    *away, own = call(
+        add_core_body, (bf16((128, 768)),) * 3 + (f32((128, 768)),), 2, 1 << 20, 4 << 20
+    )(info, keep, swap(send))
+    sums = exchange([own] + away, "x")
     early = call(input_early_body, f32((BLK, D)), 6, 1 << 30, 8 << 20)(info, *rows_gq, w_in, cot)
-    part_in = call(add_late_body, bf16((128, D)), 5, 1 << 20, 1 << 20)(info, *second, part_gq)
+    grad_events = call(input_late_body, bf16((BLK, D)), 6, 1 << 30, 8 << 20)(info, *rows_vk, w_in, early)
+    early_sum, grad_events = lax.optimization_barrier((early_sum, grad_events))
+    part_in, *pieces = call(
+        add_x_body, (bf16((128, D)),) + (f32((8, D)),) * 4, 5, 1 << 20, 1 << 20
+    )(info, *sums, early_sum)
     got = lax.all_to_all(part_in.reshape(16, 8, D), ("y", "z"), 0, 0)
-    grad_events = call(input_late_body, bf16((BLK, D)), 6, 1 << 30, 8 << 20)(info, *rows_vk, w_in, early)
+    grad_w_out = to_owners(pieces).astype(BF16)
     got = jnp.sum(got.reshape(4, 4, 8, 4, BLK).astype(F32), axis=0)
-    got = got.transpose(1, 2, 0, 3)
-    got = jnp.stack([got[:, 0], got[:, 2], got[:, 1], got[:, 3]], axis=1)
-    return grad_events[None], got.reshape(8, 4 * D).astype(BF16), grad_w_out
+    got = got.transpose(1, 2, 0, 3).reshape(8, 4 * D)
+    got = jnp.concatenate([got[:, :D], got[:, 2 * D : 3 * D], got[:, D : 2 * D], got[:, 3 * D :]], axis=1)
+    return grad_events[None], got.astype(BF16), grad_w_out
 
 
 def solution(mesh):

time: 179 us -> 191 us (1.067)
  the two profiles are of different devices: /device:TPU:40 before, /device:TPU:0 now
where the time goes in v3:
time: 191 us; the launch traced here: 188 us
  starting transfers between devices  66.7 us (35%)
  waiting for transfers between devices  45.2 us (24%)
  Pallas kernels  41.5 us (22%)
  local copies, waits for them, and re-layouts  19.1 us (10%)
  between operations  14.4 us (8%)
    ppermute x26, starting transfers between devices, along(): return lax.ppermute(x, axis, [(i, (i + d) % 4) for i in range(4)])  42.1 us
    ppermute x26, waiting for transfers between devices, along(): return lax.ppermute(x, axis, [(i, (i + d) % 4) for i in range(4)])  36.8 us
    unnamed x50, local copies, waits for them, and re-layouts  18.3 us
    ppermute x4, starting transfers between devices, to_owners(): got.append(lax.ppermute(pieces[step], ('x', 'c', 'y', 'z'), route))  17.1 us
    pallas_call x1, Pallas kernels, body(): call(backward_local_body, (bf16((BLK, 2 * BLK)),) * 4 + (f32((GRP, 2 * BL...  9.14 us
    all_to_all x1, waiting for transfers between devices, body(): got = lax.all_to_all(part_in.reshape(16, 8, D), ('y', 'z'), 0, 0)  8.36 us
    all_to_all x1, starting transfers between devices, body(): got = lax.all_to_all(part_in.reshape(16, 8, D), ('y', 'z'), 0, 0)  7.39 us
    pallas_call x1, Pallas kernels, body(): call(forward_local_body, (bf16((GRP, BLK)), bf16((GRP, 2 * BLK)), f32((GR...  6.3 us
  transfers between devices with their start and end apart: 33, of which 11 were waited for; matrix products, arithmetic and copies ran while one was open for 1% of the time, Pallas kernels for 20%

profile of v3, /device:TPU:0, one launch (start us, length us, event | category | flops | bytes accessed | tf_op | source)
XLA Modules:
  0.0 188.2 jit_solution(14564442174796754998)
XLA Ops:
  7.2 4.2 %collective-permute-start = (bf16[256,1024]{1,0:T(8,128)(2,1)}, bf16[256,1024]{1,0:T(8,128)(2,1)S(1)}, u32[]{:S(2)}, u32[]{:S(2)}) collective-permute-start(bf16[256,1024]{1,0:T(8,128)(2,1)} %bitcast.23), channel_id=1, source_target_pairs={{0,3},{1,0},{2,1},{3,2},{4,7},{5,4},{6,5},{7,6},{8,11},{9,8},{10,9... | collective-permute-start | bytes 1572872 | tf_op jit(solution)/shard_map/ppermute | solution.py:387
  14.0 3.4 %copy-done = bf16[1024,4096]{1,0:T(8,128)(2,1)S(1)} copy-done((bf16[1024,4096]{1,0:T(8,128)(2,1)S(1)}, bf16[1024,4096]{1,0:T(8,128)(2,1)}, u32[]{:S(2)}) %copy-start) | copy-done | bytes 8388632
  26.3 10.7 %collective-permute-done.refs_0_.refs_1_ = bf16[256,1024]{1,0:T(8,128)(2,1)S(1)} collective-permute-done((bf16[256,1024]{1,0:T(8,128)(2,1)}, bf16[256,1024]{1,0:T(8,128)(2,1)S(1)}, u32[]{:S(2)}, u32[]{:S(2)}) %collective-permute-start) | collective-permute-done | bytes 524320 | tf_op jit(solution)/shard_map/ppermute | solution.py:387
  36.9 3.6 %collective-permute-start.11 = (bf16[256,256]{1,0:T(8,128)(2,1)S(1)}, bf16[256,256]{1,0:T(8,128)(2,1)S(1)}, u32[]{:S(2)}, u32[]{:S(2)}) collective-permute-start(bf16[256,256]{1,0:T(8,128)(2,1)S(1)} %get-tuple-element.75), channel_id=1, source_target_pairs={{0,3},{1,0},{2,1},{3,2},{4,7},{5,4},{6,5},{7,6},{8,11},{9,8},{10,9... | collective-permute-start | bytes 393224 | tf_op jit(solution)/shard_map/ppermute | solution.py:387
  47.9 6.3 %shard_map.79 = (bf16[1024,256]{1,0:T(8,128)(2,1)S(1)}, bf16[1024,512]{1,0:T(8,128)(2,1)S(1)}, f32[1024,256]{1,0:T(8,128)S(1)}) custom-call(s32[12]{0:T(128)S(1)} %concatenate.7.info, bf16[256,256]{1,0:T(8,128)(2,1)S(1)} %get-tuple-element.65.refs_0_, bf16[512,256]{1,0:T(8,128)(2,1)S(1)} %get-tuple-element.66.refs_1_, ...), custom_call_target="tpu_custom_call" | custom-call | flops 5368709120 | bytes 4194304 | tf_op jit(solution)/shard_map/pallas_call | solution.py:449
  55.2 3.2 %collective-permute-start.3 = (bf16[256,1024]{1,0:T(8,128)(2,1)S(1)}, bf16[256,1024]{1,0:T(8,128)(2,1)S(1)}, u32[]{:S(2)}, u32[]{:S(2)}) collective-permute-start(bf16[256,1024]{1,0:T(8,128)(2,1)S(1)} %bitcast.18), channel_id=1, source_target_pairs={{0,3},{1,0},{2,1},{3,2},{4,7},{5,4},{6,5},{7,6},{8,11},{9,8},{10,9... | collective-permute-start | bytes 1572872 | tf_op jit(solution)/shard_map/ppermute | solution.py:387
  59.4 3.1 %collective-permute-done.8.refs_4_ = bf16[256,512]{1,0:T(8,128)(2,1)S(1)} collective-permute-done((bf16[256,512]{1,0:T(8,128)(2,1)S(1)}, bf16[256,512]{1,0:T(8,128)(2,1)S(1)}, u32[]{:S(2)}, u32[]{:S(2)}) %collective-permute-start.8) | collective-permute-done | bytes 262176 | tf_op jit(solution)/shard_map/ppermute | solution.py:387
  64.2 3.0 %collective-permute-start.12 = (f32[8,1024]{1,0:T(8,128)S(1)}, f32[8,1024]{1,0:T(8,128)S(1)}, u32[]{:S(2)}, u32[]{:S(2)}) collective-permute-start(f32[8,1024]{1,0:T(8,128)S(1)} %get-tuple-element.82.refs_3_), channel_id=1, source_target_pairs={{0,3},{1,0},{2,1},{3,2},{4,7},{5,4},{6,5},{7,6},{8,11},{9,8},{10,9... | collective-permute-start | bytes 98312 | tf_op jit(solution)/shard_map/ppermute | solution.py:387
  67.2 12.0 %collective-permute-done.12.refs_4_ = f32[8,1024]{1,0:T(8,128)S(1)} collective-permute-done((f32[8,1024]{1,0:T(8,128)S(1)}, f32[8,1024]{1,0:T(8,128)S(1)}, u32[]{:S(2)}, u32[]{:S(2)}) %collective-permute-start.12) | collective-permute-done | bytes 32800 | tf_op jit(solution)/shard_map/ppermute | solution.py:387
  79.1 3.4 %collective-permute-done.13.refs_5_ = f32[8,1024]{1,0:T(8,128)S(1)} collective-permute-done((f32[8,1024]{1,0:T(8,128)S(1)}, f32[8,1024]{1,0:T(8,128)S(1)}, u32[]{:S(2)}, u32[]{:S(2)}) %collective-permute-start.13) | collective-permute-done | bytes 32800 | tf_op jit(solution)/shard_map/ppermute | solution.py:387
  87.3 3.2 %shard_map.83 = f32[8,128,512]{2,1,0:T(8,128)} custom-call(s32[12]{0:T(128)S(1)} %concatenate.7.info, bf16[256,1024]{1,0:T(8,128)(2,1)S(1)} %bitcast.27, bf16[256,1024]{1,0:T(8,128)(2,1)S(1)} %collective-permute-done.refs_0_.refs_1_, bf16[256,1024]{1,0:T(8,128)(2,1)S(1)} %collective-permute-done.1.refs_0_.refs_2_, ...), custom_call_target="tpu_custom_call" | custom-call | flops 1073741824 | bytes 4194304 | tf_op jit(solution)/shard_map/pallas_call | solution.py:462
  102.3 9.1 %shard_map.84 = (bf16[256,512]{1,0:T(8,128)(2,1)S(1)}, bf16[256,512]{1,0:T(8,128)(2,1)S(1)}, bf16[256,512]{1,0:T(8,128)(2,1)S(1)}, bf16[256,512]{1,0:T(8,128)(2,1)S(1)}, f32[1024,512]{1,0:T(8,128)S(1)}) custom-call(s32[12]{0:T(128)S(1)} %concatenate.7.info, bf16[1024,256]{1,0:T(8,128)(2,1)S(1)} %copy-done.16, bf16[1024,256]{1,0:T(8,128)(2,1)S(1)} %copy-done.18, ...), custom_call_target="tpu_custom_call" | custom-call | flops 10737418240 | bytes 4194304 | tf_op jit(solution)/shard_map/pallas_call | solution.py:468
  111.5 3.6 %collective-permute-start.21 = (bf16[256,512]{1,0:T(8,128)(2,1)S(1)}, bf16[256,512]{1,0:T(8,128)(2,1)S(1)}, u32[]{:S(2)}, u32[]{:S(2)}) collective-permute-start(bf16[256,512]{1,0:T(8,128)(2,1)S(1)} %get-tuple-element.100.refs_6_), channel_id=1, source_target_pairs={{0,2},{1,3},{2,0},{3,1},{4,6},{5,7},{6,4},{7,5},{8,10},{9,11},{10,... | collective-permute-start | bytes 786440 | tf_op jit(solution)/shard_map/ppermute | solution.py:387
  115.4 3.5 %shard_map.85 = (bf16[256,512]{1,0:T(8,128)(2,1)S(1)}, bf16[256,512]{1,0:T(8,128)(2,1)S(1)}, bf16[256,512]{1,0:T(8,128)(2,1)S(1)}, bf16[256,512]{1,0:T(8,128)(2,1)S(1)}) custom-call(s32[12]{0:T(128)S(1)} %concatenate.7.info, bf16[1024,256]{1,0:T(8,128)(2,1)S(1)} %collective-permute-done.15.refs_0_, bf16[1024,256]{1,0:T(8,128)(2,1)S(1)} %collective-permute-done.16.refs_1_, ...), custom_call_target="tpu_custom_call" | custom-call | flops 5368709120 | bytes 4194304 | tf_op jit(solution)/shard_map/pallas_call | solution.py:473
  119.5 2.8 %collective-permute-done.21.refs_2_ = bf16[256,512]{1,0:T(8,128)(2,1)S(1)} collective-permute-done((bf16[256,512]{1,0:T(8,128)(2,1)S(1)}, bf16[256,512]{1,0:T(8,128)(2,1)S(1)}, u32[]{:S(2)}, u32[]{:S(2)}) %collective-permute-start.21) | collective-permute-done | bytes 262176 | tf_op jit(solution)/shard_map/ppermute | solution.py:387
  126.2 3.6 %collective-permute-start.18 = (bf16[256,512]{1,0:T(8,128)(2,1)S(1)}, bf16[256,512]{1,0:T(8,128)(2,1)S(1)}, u32[]{:S(2)}, u32[]{:S(2)}) collective-permute-start(bf16[256,512]{1,0:T(8,128)(2,1)S(1)} %get-tuple-element.109.refs_10_), channel_id=1, source_target_pairs={{0,2},{1,3},{2,0},{3,1},{4,6},{5,7},{6,4},{7,5},{8,10},{9,11},{10,... | collective-permute-start | bytes 786440 | tf_op jit(solution)/shard_map/ppermute | solution.py:387
  132.0 3.2 %collective-permute-start.25 = (bf16[128,768]{1,0:T(8,128)(2,1)S(1)}, bf16[128,768]{1,0:T(8,128)(2,1)S(1)}, u32[]{:S(2)}, u32[]{:S(2)}) collective-permute-start(bf16[128,768]{1,0:T(8,128)(2,1)S(1)} %get-tuple-element.115), channel_id=1, source_target_pairs={{0,64},{32,96},{64,0},{96,32},{1,65},{33,97},{65,1},{97,33},{2,66}... | collective-permute-start | bytes 589832 | tf_op jit(solution)/shard_map/ppermute | solution.py:387
  135.6 3.5 %collective-permute-start.26 = (bf16[128,768]{1,0:T(8,128)(2,1)S(1)}, bf16[128,768]{1,0:T(8,128)(2,1)S(1)}, u32[]{:S(2)}, u32[]{:S(2)}) collective-permute-start(bf16[128,768]{1,0:T(8,128)(2,1)S(1)} %get-tuple-element.116), channel_id=1, source_target_pairs={{0,96},{32,0},{64,32},{96,64},{1,97},{33,1},{65,33},{97,65},{2,98}... | collective-permute-start | bytes 589832 | tf_op jit(solution)/shard_map/ppermute | solution.py:387
  142.0 2.6 %shard_map.87 = bf16[256,1024]{1,0:T(8,128)(2,1)} custom-call(s32[12]{0:T(128)S(1)} %concatenate.7.info, bf16[256,512]{1,0:T(8,128)(2,1)S(1)} %get-tuple-element.107.refs_0_.refs_8_, bf16[256,512]{1,0:T(8,128)(2,1)S(1)} %collective-permute-done.17.refs_1_, bf16[256,512]{1,0:T(8,128)(2,1)S(1)} %collective-permute-done.18.refs_2_, ...), custom_call_target="tpu_custom_call" | custom-call | flops 1073741824 | bytes 8388608 | tf_op jit(solution)/shard_map/pallas_call | solution.py:488
  147.7 6.2 %collective-permute-start.28 = (f32[8,1024]{1,0:T(8,128)S(1)}, f32[8,1024]{1,0:T(8,128)S(1)}, u32[]{:S(2)}, u32[]{:S(2)}) collective-permute-start(f32[8,1024]{1,0:T(8,128)S(1)} %get-tuple-element.120), channel_id=1, source_target_pairs={{0,1},{1,33},{2,65},{3,97},{4,2},{5,34},{6,66},{7,98},{8,3},{9,35}... | collective-permute-start | bytes 98312 | tf_op jit(solution)/shard_map/ppermute | solution.py:408
  153.9 3.7 %collective-permute-start.29 = (f32[8,1024]{1,0:T(8,128)S(1)}, f32[8,1024]{1,0:T(8,128)S(1)}, u32[]{:S(2)}, u32[]{:S(2)}) collective-permute-start(f32[8,1024]{1,0:T(8,128)S(1)} %get-tuple-element.121), channel_id=1, source_target_pairs={{0,2},{1,34},{2,66},{3,98},{4,3},{5,35},{6,67},{7,99},{8,0},{9,32}... | collective-permute-start | bytes 98312 | tf_op jit(solution)/shard_map/ppermute | solution.py:408
  157.6 6.5 %collective-permute-start.30 = (f32[8,1024]{1,0:T(8,128)S(1)}, f32[8,1024]{1,0:T(8,128)S(1)}, u32[]{:S(2)}, u32[]{:S(2)}) collective-permute-start(f32[8,1024]{1,0:T(8,128)S(1)} %get-tuple-element.122), channel_id=1, source_target_pairs={{0,3},{1,35},{2,67},{3,99},{4,0},{5,32},{6,64},{7,96},{8,1},{9,33}... | collective-permute-start | bytes 98312 | tf_op jit(solution)/shard_map/ppermute | solution.py:408
  164.1 7.4 %all-to-all-start = ((bf16[16,8,1024]{2,1,0:T(8,128)(2,1)}), bf16[16,8,1024]{2,1,0:T(8,128)(2,1)S(1)}, u32[]{:S(2)}, u32[]{:S(2)}) async-start(bf16[16,8,1024]{2,1,0:T(8,128)(2,1)} %bitcast.9), calls=%async_computation.1 | async-start | bytes 524288 | tf_op jit(solution)/shard_map/all_to_all | solution.py:493
  172.2 8.4 %all-to-all-done = bf16[16,8,1024]{2,1,0:T(8,128)(2,1)S(1)} async-done(((bf16[16,8,1024]{2,1,0:T(8,128)(2,1)}), bf16[16,8,1024]{2,1,0:T(8,128)(2,1)S(1)}, u32[]{:S(2)}, u32[]{:S(2)}) %all-to-all-start) | async-done | bytes 262176 | tf_op jit(solution)/shard_map/all_to_all | solution.py:493
  (116 shorter events, 53.6 us)
Async XLA Ops:
  7.2 137.5 %reduce-scatter.2.cloned.1.call-start = ((), (), s32[]{:S(2)}) async-start(), calls=%async_computation.2 | async-start | bytes 2359296 | tf_op jit(solution)/shard_map/reduce_scatter | solution.py:466
  7.2 29.7 %collective-permute-start = (bf16[256,1024]{1,0:T(8,128)(2,1)}, bf16[256,1024]{1,0:T(8,128)(2,1)S(1)}, u32[]{:S(2)}, u32[]{:S(2)}) collective-permute-start(bf16[256,1024]{1,0:T(8,128)(2,1)} %bitcast.23), channel_id=1, source_target_pairs={{0,3},{1,0},{2,1},{3,2},{4,7},{5,4},{6,5},{7,6},{8,11},{9,8},{10,9... | collective-permute-start | bytes 1572872 | tf_op jit(solution)/shard_map/ppermute | solution.py:387
  11.4 29.1 %collective-permute-start.2 = (bf16[256,1024]{1,0:T(8,128)(2,1)}, bf16[256,1024]{1,0:T(8,128)(2,1)S(1)}, u32[]{:S(2)}, u32[]{:S(2)}) collective-permute-start(bf16[256,1024]{1,0:T(8,128)(2,1)} %bitcast.24), channel_id=1, source_target_pairs={{0,1},{1,2},{2,3},{3,0},{4,5},{5,6},{6,7},{7,4},{8,9},{9,10},{10,1... | collective-permute-start | bytes 1572872 | tf_op jit(solution)/shard_map/ppermute | solution.py:387
  11.4 31.6 %collective-permute-start.1 = (bf16[256,1024]{1,0:T(8,128)(2,1)}, bf16[256,1024]{1,0:T(8,128)(2,1)S(1)}, u32[]{:S(2)}, u32[]{:S(2)}) collective-permute-start(bf16[256,1024]{1,0:T(8,128)(2,1)} %bitcast.25), channel_id=1, source_target_pairs={{0,2},{1,3},{2,0},{3,1},{4,6},{5,7},{6,4},{7,5},{8,10},{9,11},{10,... | collective-permute-start | bytes 1572872 | tf_op jit(solution)/shard_map/ppermute | solution.py:387
  20.0 38.4 %collective-permute-start.6 = (bf16[256,512]{1,0:T(8,128)(2,1)S(1)}, bf16[256,512]{1,0:T(8,128)(2,1)S(1)}, u32[]{:S(2)}, u32[]{:S(2)}) collective-permute-start(bf16[256,512]{1,0:T(8,128)(2,1)S(1)} %get-tuple-element.68.refs_3_), channel_id=1, source_target_pairs={{0,4},{4,8},{8,12},{12,0},{1,5},{5,9},{9,13},{13,1},{2,6},{6,10},{... | collective-permute-start | bytes 786440 | tf_op jit(solution)/shard_map/ppermute | solution.py:387
  24.5 21.7 %collective-permute-start.10 = (bf16[256,256]{1,0:T(8,128)(2,1)S(1)}, bf16[256,256]{1,0:T(8,128)(2,1)S(1)}, u32[]{:S(2)}, u32[]{:S(2)}) collective-permute-start(bf16[256,256]{1,0:T(8,128)(2,1)S(1)} %get-tuple-element.74), channel_id=1, source_target_pairs={{0,2},{1,3},{2,0},{3,1},{4,6},{5,7},{6,4},{7,5},{8,10},{9,11},{10,... | collective-permute-start | bytes 393224 | tf_op jit(solution)/shard_map/ppermute | solution.py:387
  36.9 18.2 %collective-permute-start.11 = (bf16[256,256]{1,0:T(8,128)(2,1)S(1)}, bf16[256,256]{1,0:T(8,128)(2,1)S(1)}, u32[]{:S(2)}, u32[]{:S(2)}) collective-permute-start(bf16[256,256]{1,0:T(8,128)(2,1)S(1)} %get-tuple-element.75), channel_id=1, source_target_pairs={{0,3},{1,0},{2,1},{3,2},{4,7},{5,4},{6,5},{7,6},{8,11},{9,8},{10,9... | collective-permute-start | bytes 393224 | tf_op jit(solution)/shard_map/ppermute | solution.py:387
  40.5 17.9 %collective-permute-start.9 = (bf16[256,256]{1,0:T(8,128)(2,1)S(1)}, bf16[256,256]{1,0:T(8,128)(2,1)S(1)}, u32[]{:S(2)}, u32[]{:S(2)}) collective-permute-start(bf16[256,256]{1,0:T(8,128)(2,1)S(1)} %get-tuple-element.73), channel_id=1, source_target_pairs={{0,1},{1,2},{2,3},{3,0},{4,5},{5,6},{6,7},{7,4},{8,9},{9,10},{10,1... | collective-permute-start | bytes 393224 | tf_op jit(solution)/shard_map/ppermute | solution.py:387
  43.0 19.5 %collective-permute-start.7 = (bf16[512,512]{1,0:T(8,128)(2,1)S(1)}, bf16[512,512]{1,0:T(8,128)(2,1)S(1)}, u32[]{:S(2)}, u32[]{:S(2)}) collective-permute-start(bf16[512,512]{1,0:T(8,128)(2,1)S(1)} %get-tuple-element.69.refs_4_), channel_id=1, source_target_pairs={{0,4},{4,8},{8,12},{12,0},{1,5},{5,9},{9,13},{13,1},{2,6},{6,10},{... | collective-permute-start | bytes 1572872 | tf_op jit(solution)/shard_map/ppermute | solution.py:387
  46.2 16.2 %collective-permute-start.8 = (bf16[256,512]{1,0:T(8,128)(2,1)S(1)}, bf16[256,512]{1,0:T(8,128)(2,1)S(1)}, u32[]{:S(2)}, u32[]{:S(2)}) collective-permute-start(bf16[256,512]{1,0:T(8,128)(2,1)S(1)} %get-tuple-element.63.refs_5_), channel_id=1, source_target_pairs={{0,4},{4,8},{8,12},{12,0},{1,5},{5,9},{9,13},{13,1},{2,6},{6,10},{... | collective-permute-start | bytes 786440 | tf_op jit(solution)/shard_map/ppermute | solution.py:387
  55.2 32.1 %collective-permute-start.3 = (bf16[256,1024]{1,0:T(8,128)(2,1)S(1)}, bf16[256,1024]{1,0:T(8,128)(2,1)S(1)}, u32[]{:S(2)}, u32[]{:S(2)}) collective-permute-start(bf16[256,1024]{1,0:T(8,128)(2,1)S(1)} %bitcast.18), channel_id=1, source_target_pairs={{0,3},{1,0},{2,1},{3,2},{4,7},{5,4},{6,5},{7,6},{8,11},{9,8},{10,9... | collective-permute-start | bytes 1572872 | tf_op jit(solution)/shard_map/ppermute | solution.py:387
  58.4 28.8 %collective-permute-start.4 = (bf16[256,1024]{1,0:T(8,128)(2,1)S(1)}, bf16[256,1024]{1,0:T(8,128)(2,1)S(1)}, u32[]{:S(2)}, u32[]{:S(2)}) collective-permute-start(bf16[256,1024]{1,0:T(8,128)(2,1)S(1)} %bitcast.19), channel_id=1, source_target_pairs={{0,2},{1,3},{2,0},{3,1},{4,6},{5,7},{6,4},{7,5},{8,10},{9,11},{10,... | collective-permute-start | bytes 1572872 | tf_op jit(solution)/shard_map/ppermute | solution.py:387
  58.4 28.8 %collective-permute-start.5 = (bf16[256,1024]{1,0:T(8,128)(2,1)S(1)}, bf16[256,1024]{1,0:T(8,128)(2,1)S(1)}, u32[]{:S(2)}, u32[]{:S(2)}) collective-permute-start(bf16[256,1024]{1,0:T(8,128)(2,1)S(1)} %bitcast.20), channel_id=1, source_target_pairs={{0,1},{1,2},{2,3},{3,0},{4,5},{5,6},{6,7},{7,4},{8,9},{9,10},{10,1... | collective-permute-start | bytes 1572872 | tf_op jit(solution)/shard_map/ppermute | solution.py:387
  64.2 15.0 %collective-permute-start.12 = (f32[8,1024]{1,0:T(8,128)S(1)}, f32[8,1024]{1,0:T(8,128)S(1)}, u32[]{:S(2)}, u32[]{:S(2)}) collective-permute-start(f32[8,1024]{1,0:T(8,128)S(1)} %get-tuple-element.82.refs_3_), channel_id=1, source_target_pairs={{0,3},{1,0},{2,1},{3,2},{4,7},{5,4},{6,5},{7,6},{8,11},{9,8},{10,9... | collective-permute-start | bytes 98312 | tf_op jit(solution)/shard_map/ppermute | solution.py:387
  67.2 15.4 %collective-permute-start.13 = (f32[8,1024]{1,0:T(8,128)S(1)}, f32[8,1024]{1,0:T(8,128)S(1)}, u32[]{:S(2)}, u32[]{:S(2)}) collective-permute-start(f32[8,1024]{1,0:T(8,128)S(1)} %get-tuple-element.82.refs_3_), channel_id=1, source_target_pairs={{0,2},{1,3},{2,0},{3,1},{4,6},{5,7},{6,4},{7,5},{8,10},{9,11},{10,... | collective-permute-start | bytes 98312 | tf_op jit(solution)/shard_map/ppermute | solution.py:387
  91.3 24.1 %collective-permute-start.15 = (bf16[1024,256]{1,0:T(8,128)(2,1)}, bf16[1024,256]{1,0:T(8,128)(2,1)S(1)}, u32[]{:S(2)}, u32[]{:S(2)}) collective-permute-start(bf16[1024,256]{1,0:T(8,128)(2,1)} %copy-done.15), channel_id=1, source_target_pairs={{0,12},{4,0},{8,4},{12,8},{1,13},{5,1},{9,5},{13,9},{2,14},{6,2},{... | collective-permute-start | bytes 1572872 | tf_op jit(solution)/shard_map/ppermute | solution.py:387
  93.0 22.4 %collective-permute-start.16 = (bf16[1024,256]{1,0:T(8,128)(2,1)}, bf16[1024,256]{1,0:T(8,128)(2,1)S(1)}, u32[]{:S(2)}, u32[]{:S(2)}) collective-permute-start(bf16[1024,256]{1,0:T(8,128)(2,1)} %copy-done.17), channel_id=1, source_target_pairs={{0,12},{4,0},{8,4},{12,8},{1,13},{5,1},{9,5},{13,9},{2,14},{6,2},{... | collective-permute-start | bytes 1572872 | tf_op jit(solution)/shard_map/ppermute | solution.py:387
  126.2 15.8 %collective-permute-start.18 = (bf16[256,512]{1,0:T(8,128)(2,1)S(1)}, bf16[256,512]{1,0:T(8,128)(2,1)S(1)}, u32[]{:S(2)}, u32[]{:S(2)}) collective-permute-start(bf16[256,512]{1,0:T(8,128)(2,1)S(1)} %get-tuple-element.109.refs_10_), channel_id=1, source_target_pairs={{0,2},{1,3},{2,0},{3,1},{4,6},{5,7},{6,4},{7,5},{8,10},{9,11},{10,... | collective-permute-start | bytes 786440 | tf_op jit(solution)/shard_map/ppermute | solution.py:387
  130.5 14.2 %collective-permute-start.24 = (bf16[128,768]{1,0:T(8,128)(2,1)S(1)}, bf16[128,768]{1,0:T(8,128)(2,1)S(1)}, u32[]{:S(2)}, u32[]{:S(2)}) collective-permute-start(bf16[128,768]{1,0:T(8,128)(2,1)S(1)} %get-tuple-element.114), channel_id=1, source_target_pairs={{0,32},{32,64},{64,96},{96,0},{1,33},{33,65},{65,97},{97,1},{2,34}... | collective-permute-start | bytes 589832 | tf_op jit(solution)/shard_map/ppermute | solution.py:387
  147.0 24.5 %collective-permute-start.27 = (f32[8,1024]{1,0:T(8,128)S(1)}, f32[8,1024]{1,0:T(8,128)S(1)}, u32[]{:S(2)}, u32[]{:S(2)}) collective-permute-start(f32[8,1024]{1,0:T(8,128)S(1)} %get-tuple-element.119), channel_id=1, source_target_pairs={{0,0},{1,32},{2,64},{3,96},{4,1},{5,33},{6,65},{7,97},{8,2},{9,34}... | collective-permute-start | bytes 98312 | tf_op jit(solution)/shard_map/ppermute | solution.py:408
  147.7 23.9 %collective-permute-start.28 = (f32[8,1024]{1,0:T(8,128)S(1)}, f32[8,1024]{1,0:T(8,128)S(1)}, u32[]{:S(2)}, u32[]{:S(2)}) collective-permute-start(f32[8,1024]{1,0:T(8,128)S(1)} %get-tuple-element.120), channel_id=1, source_target_pairs={{0,1},{1,33},{2,65},{3,97},{4,2},{5,34},{6,66},{7,98},{8,3},{9,35}... | collective-permute-start | bytes 98312 | tf_op jit(solution)/shard_map/ppermute | solution.py:408
  153.9 17.7 %collective-permute-start.29 = (f32[8,1024]{1,0:T(8,128)S(1)}, f32[8,1024]{1,0:T(8,128)S(1)}, u32[]{:S(2)}, u32[]{:S(2)}) collective-permute-start(f32[8,1024]{1,0:T(8,128)S(1)} %get-tuple-element.121), channel_id=1, source_target_pairs={{0,2},{1,34},{2,66},{3,98},{4,3},{5,35},{6,67},{7,99},{8,0},{9,32}... | collective-permute-start | bytes 98312 | tf_op jit(solution)/shard_map/ppermute | solution.py:408
  157.6 13.9 %collective-permute-start.30 = (f32[8,1024]{1,0:T(8,128)S(1)}, f32[8,1024]{1,0:T(8,128)S(1)}, u32[]{:S(2)}, u32[]{:S(2)}) collective-permute-start(f32[8,1024]{1,0:T(8,128)S(1)} %get-tuple-element.122), channel_id=1, source_target_pairs={{0,3},{1,35},{2,67},{3,99},{4,0},{5,32},{6,64},{7,96},{8,1},{9,33}... | collective-permute-start | bytes 98312 | tf_op jit(solution)/shard_map/ppermute | solution.py:408
  164.1 16.4 %all-to-all-start = ((bf16[16,8,1024]{2,1,0:T(8,128)(2,1)}), bf16[16,8,1024]{2,1,0:T(8,128)(2,1)S(1)}, u32[]{:S(2)}, u32[]{:S(2)}) async-start(bf16[16,8,1024]{2,1,0:T(8,128)(2,1)} %bitcast.9), calls=%async_computation.1 | async-start | bytes 524288 | tf_op jit(solution)/shard_map/all_to_all | solution.py:493
  (34 other events, 327.1 us)
Sparse Core Ops, SparseCore 0:
  91.4 33.4 reduce-scatter.1

commit v4 on v3

--- a/solution.py
+++ b/solution.py
@@ -95,8 +95,9 @@
 
 def grad_gated_body(info, cot, w, *outs):
     for d in range(NB):
-        out_rows = rows(lax.rem(info[9] + d, NB))
-        outs[d][...] = nt(cot[...], w[out_rows, :]).astype(BF16)
+        owner = lax.rem(info[9] + d, NB)
+        outs[d][:, :BLK] = nt(cot[...], w[rows(owner), :]).astype(BF16)
+        outs[d][:, BLK:] = cot[:, pl.ds(pl.multiple_of(owner * BLK, BLK), BLK)]
 
 
 def keep_rows(qpos, kpos, ends):
@@ -155,7 +156,7 @@
 def forward_halo_body(info, *refs):
     q, att_in = refs[0:2]
     kv_in, gg_in, gate_in = refs[2:5], refs[5:9], refs[9:12]
-    att, kv, gg, gate, stats = refs[12:17]
+    att, kv, gg, cot, gate, stats = refs[12:18]
     ends = history_ends(info)
     base = info[8] * GRP
     prev = base - GRP
@@ -164,7 +165,8 @@
         at = rows(lax.rem(info[9] + k, NB))
         kv[at, :] = block_of(kv_in, k)
         gate[at, :] = block_of(gate_in, k)
-        gg[at, :] = gg_in[(4 - k) % 4][...]
+        gg[at, :] = gg_in[(4 - k) % 4][:, :BLK]
+        cot[at, :] = gg_in[(4 - k) % 4][:, BLK:]
 
     def over_i(i, _):
         qpos = base + i * BLK
@@ -219,35 +221,26 @@
 
 
 def early_weights_body(info, *refs):
-    ev, cot = refs[0:4], refs[4:8]
-    gated, gp, out, acc_in, acc_out = refs[8:13]
-    for k in range(NB):
-        at = rows(lax.rem(info[9] + k, NB))
-        part_in = tn(ev[k][...], gp[at, :])
-        part_out = tn(gated[at, :], cot[k][...])
-        if k:
-            part_in += acc_in[...]
-            part_out += acc_out[...]
-        acc_in[...] = part_in
-        acc_out[...] = part_out
-    for n in range(8):
-        out[n, :, :BLK] = acc_in[n * 128 : (n + 1) * 128, :]
-        for m in range(4):
-            out[n, 32 * m : 32 * m + 32, BLK:] = acc_out[n * 32 : (n + 1) * 32, m * BLK : (m + 1) * BLK]
+    ev, (gp_g, gp_q, acc) = refs[0:4], refs[4:7]
+    for k in range(NB):
+        at = rows(lax.rem(info[9] + k, NB))
+        for lanes, gp in ((slice(0, BLK), gp_g), (slice(BLK, 2 * BLK), gp_q)):
+            part = tn(ev[k][...], gp[at, :])
+            acc[:, lanes] = part if k == 0 else acc[:, lanes] + part
 
 
 def late_weights_body(info, *refs):
-    ev, gq, vk = refs[0:4], refs[4:8], refs[8:12]
-    send, keep, acc = refs[12:15]
-    for k in range(NB):
-        x = ev[k][...]
-        for lanes, gp in ((slice(0, BLK), gq[k][:, BLK:]), (slice(BLK, 3 * BLK), vk[k][...])):
-            part = tn(x, gp)
-            acc[:, lanes] = part if k == 0 else acc[:, lanes] + part
+    ev, gp, gated = refs[0:4], refs[4:8], refs[8:12]
+    cot, early, send, keep, acc = refs[12:17]
+    for k in range(NB):
+        part = tn(ev[k][...], gp[k][:, 2 * BLK :])
+        acc[:, : 2 * BLK] = part if k == 0 else acc[:, : 2 * BLK] + part
+        acc[rows(lax.rem(info[9] + k, NB)), 2 * BLK :] = tn(gated[k][...], cot[...])
     for x in range(4):
         for out, c, kind in ((send, 1 - info[10], BF16), (keep, info[10], F32)):
-            at = pl.multiple_of((x * 2 + c) * 128, 128)
-            out[x, :, :] = acc[pl.ds(at, 128), :].astype(kind)
+            at = pl.ds(pl.multiple_of((x * 2 + c) * 128, 128), 128)
+            out[x, :, : 2 * BLK] = early[at, :].astype(kind)
+            out[x, :, 2 * BLK :] = acc[at, :].astype(kind)
 
 
 def add_core_body(info, keep, got, to_1, to_2, to_3, own):
@@ -257,15 +250,21 @@
         out[...] = (keep[at] + got[at].astype(F32)).astype(BF16)
 
 
-def add_x_body(info, own, got_1, got_2, got_3, early, part_in, *pieces):
-    total = own[...] + got_1[...].astype(F32) + got_2[...].astype(F32) + got_3[...].astype(F32)
-    part_in[:, :BLK] = early[:, :BLK].astype(BF16)
-    part_in[:, BLK:] = total.astype(BF16)
-    for step in range(4):
-        p = lax.rem(info[8] + step, 4)
-        for n in range(4):
-            at = pl.ds(pl.multiple_of(n * 32 + p * 8, 8), 8)
-            pieces[step][:, n * BLK : (n + 1) * BLK] = early[at, BLK:]
+def add_x_body(info, own, got_1, got_2, got_3, total):
+    part = own[...] + got_1[...].astype(F32) + got_2[...].astype(F32) + got_3[...].astype(F32)
+    total[...] = part.astype(BF16)
+
+
+def last_sum_body(info, got, grad_w_in, grad_w_out):
+    for z in range(4):
+        part = got[z].astype(F32)
+        for y in range(1, 4):
+            part = part + got[y * 4 + z].astype(F32)
+        part = part.astype(BF16)
+        for n, to in enumerate((0, 2, 1, 3)):
+            at = to * D + z * BLK
+            grad_w_in[:, at : at + BLK] = part[:, n * BLK : (n + 1) * BLK]
+        grad_w_out[:, z * BLK : (z + 1) * BLK] = part[:, 4 * BLK :]
 
 
 def silu_parts(u):
@@ -299,9 +298,9 @@
 
 
 def backward_local_body(info, *refs):
-    q, g, kv, kv_prev, gp_g = refs[0:5]
-    dsig, gp = refs[5:9], refs[9:13]
-    dkv, dq = refs[13:15]
+    q, g, kv, kv_prev = refs[0:4]
+    dsig = refs[4:8]
+    gp_q, dkv, dq = refs[8:11]
     ends = history_ends(info)
     base = info[8] * GRP
     prev = base - GRP
@@ -332,14 +331,13 @@
     lax.fori_loop(0, NB, halo_i, 0)
     for k in range(NB):
         at = rows(lax.rem(info[9] + k, NB))
-        gp[k][:, :BLK] = gp_g[at, :]
-        gp[k][:, BLK:] = (dq[at, :] * dsig[k][:, 2 * BLK : 3 * BLK].astype(F32)).astype(BF16)
+        gp_q[at, :] = (dq[at, :] * dsig[k][:, 2 * BLK : 3 * BLK].astype(F32)).astype(BF16)
 
 
 def backward_later_body(info, *refs):
-    q, g, kv, dkv_in = refs[0:4]
-    dsig, gp = refs[4:8], refs[8:12]
-    dkv = refs[12]
+    q, g, kv, dkv_in, gp_g, gp_q = refs[0:6]
+    dsig, gp = refs[6:10], refs[10:14]
+    dkv = refs[14]
     ends = history_ends(info)
     base = info[8] * GRP
     later = base + GRP
@@ -360,27 +358,21 @@
     for k in range(NB):
         at = rows(lax.rem(info[9] + k, NB))
         dk = 2.0 * dkv[at, 0:BLK]
-        gp[k][:, :BLK] = (dkv[at, BLK:] * dsig[k][:, BLK : 2 * BLK].astype(F32)).astype(BF16)
-        gp[k][:, BLK:] = (dk * dsig[k][:, 3 * BLK :].astype(F32)).astype(BF16)
-
-
-def input_rows(info, gp, w, parts, total):
+        gp[k][:, :BLK] = gp_g[at, :]
+        gp[k][:, BLK : 2 * BLK] = gp_q[at, :]
+        gp[k][:, 2 * BLK : 3 * BLK] = (dkv[at, BLK:] * dsig[k][:, BLK : 2 * BLK].astype(F32)).astype(BF16)
+        gp[k][:, 3 * BLK :] = (dk * dsig[k][:, 3 * BLK :].astype(F32)).astype(BF16)
+
+
+def input_body(info, *refs):
+    gp, (w, cot, out) = refs[0:4], refs[4:7]
+    total = cot[...].astype(F32)
     for d in range(NB):
         owner = lax.rem(info[9] + NB - d, NB)
-        for n, part in enumerate(parts):
+        for n, part in enumerate((0, 2, 1, 3)):
             lanes = pl.ds(pl.multiple_of(part * D + owner * BLK, BLK), BLK)
             total = total + nt(gp[d][:, n * BLK : (n + 1) * BLK], w[:, lanes])
-    return total
-
-
-def input_early_body(info, *refs):
-    gp, (w, cot, out) = refs[0:4], refs[4:7]
-    out[...] = input_rows(info, gp, w, (0, 2), cot[...].astype(F32))
-
-
-def input_late_body(info, *refs):
-    gp, (w, early, out) = refs[0:4], refs[4:7]
-    out[...] = input_rows(info, gp, w, (1, 3), early[...]).astype(BF16)
+    out[...] = total.astype(BF16)
 
 
 def along(x, axis, d):
@@ -393,20 +385,6 @@
 
 def gather_z(x):
     return [x, along(x, "z", -1), along(x, "z", 2), along(x, "z", 1)]
-
-
-def to_owners(pieces):
-    got = []
-    for step in range(4):
-        route = []
-        for xc in range(8):
-            for y in range(4):
-                for z in range(4):
-                    src = (xc * 4 + y) * 4 + z
-                    dst = ((2 * z + xc // 4) * 4 + xc % 4) * 4 + (y + step) % 4
-                    route.append((src, dst))
-        got.append(lax.ppermute(pieces[step], ("x", "c", "y", "z"), route))
-    return got[0] + got[1] + got[2] + got[3]
 
 
 def exchange(parts, axis):
@@ -427,10 +405,14 @@
         [hist[0], jnp.stack([lax.axis_index("y"), z, lax.axis_index("c"), lax.axis_index("x")]).astype(jnp.int32)]
     )
     ev, cot = events[0], cotangent[0]
-    evs = gather_z(ev)
+    near = along(ev, "z", -1), along(ev, "z", 1)
+    evs = [ev, near[0], None, near[1]]
     kvs, qs, gs, dsigs, kv_prevs = [], [], [], [None] * 4, []
     for blocks in ((0,), (1, 3), (2,)):
         n = len(blocks)
+        if blocks == (1, 3):
+            ev_far, *near, _ = lax.optimization_barrier((ev, *near, kvs[0]))
+            evs = [ev, near[0], along(ev_far, "z", 2), near[1]]
         kv, q, g, *dsig = call(
             project_body,
             (bf16((n * BLK, 2 * BLK)), bf16((n * BLK, BLK)), bf16((n * BLK, BLK))) + (bf16((BLK, 4 * BLK)),) * n,
@@ -442,60 +424,48 @@
         for b, d in zip(blocks, dsig):
             dsigs[b] = d
         kv_prevs.append(along(kv, "y", 1))
-    ggs = call(grad_gated_body, (bf16((BLK, BLK)),) * 4, 2, 1 << 29, 2 << 20)(info, cot, w_out)
+    ggs = call(grad_gated_body, (bf16((BLK, 2 * BLK)),) * 4, 2, 1 << 29, 2 << 20)(info, cot, w_out)
+    *ggs, _ = lax.optimization_barrier((*ggs, evs[2]))
     ggs = exchange(ggs, "z")
-    cot_late, _ = lax.optimization_barrier((cot, kvs[2]))
-    cots = gather_z(cot_late)
     q, kv, att = call(
         forward_local_body, (bf16((GRP, BLK)), bf16((GRP, 2 * BLK)), f32((GRP, BLK))), 6, 5 << 30, 4 << 20
     )(info, *qs, *kvs)
     q_next = along(q, "y", -1)
-    att, kv_prev, gg, gate, stats = call(
+    att, kv_prev, gg, cot_z, gate, stats = call(
         forward_halo_body,
-        (f32((GRP, BLK)), bf16((GRP, 2 * BLK)), bf16((GRP, BLK)), bf16((GRP, BLK)), f32((8, GRP))),
+        (f32((GRP, BLK)), bf16((GRP, 2 * BLK))) + (bf16((GRP, BLK)),) * 3 + (f32((8, GRP)),),
         12, 5 << 30, 4 << 20,
     )(info, q, att, *kv_prevs, *ggs, *gs)
     gatt, gated, gp_g = call(
         norm_body, (bf16((GRP, BLK)),) * 3, 11, 1 << 30, 4 << 20, [pltpu.VMEM((GRP, DH), F32)]
     )(info, att, gg, gate, *gather_z(stats), *dsigs)
     g_next = along(gatt, "y", -1)
-    part = call(
-        early_weights_body, f32((8, 128, 512)), 10, 1 << 30, 4 << 20,
-        [pltpu.VMEM((D, BLK), F32), pltpu.VMEM((BLK, D), F32)],
-    )(info, *evs, *cots, gated, gp_g)
-    early_sum = lax.psum_scatter(part, ("x", "c"), scatter_dimension=0)
-    gatt, _ = lax.optimization_barrier((gatt, part))
-    *gp_gq, dkv = call(
-        backward_local_body, (bf16((BLK, 2 * BLK)),) * 4 + (f32((GRP, 2 * BLK)),), 9, 10 << 30, 4 << 20,
+    gateds = gather_z(gated)
+    gp_q, dkv = call(
+        backward_local_body, (bf16((GRP, BLK)), f32((GRP, 2 * BLK))), 8, 10 << 30, 4 << 20,
         [pltpu.VMEM((GRP, BLK), F32)],
-    )(info, q, gatt, kv, kv_prev, gp_g, *dsigs)
-    rows_gq = exchange(gp_gq, "z")
-    gp_vk = call(
-        backward_later_body, (bf16((BLK, 2 * BLK)),) * 4, 8, 5 << 30, 4 << 20, [pltpu.VMEM((GRP, 2 * BLK), F32)]
-    )(info, q_next, g_next, kv, dkv, *dsigs)
-    rows_vk = exchange(gp_vk, "z")
-    gp_late, rows_gq = lax.optimization_barrier((gp_vk, rows_gq))
+    )(info, q, gatt, kv, kv_prev, *dsigs)
+    early = call(early_weights_body, f32((D, 2 * BLK)), 6, 1 << 30, 4 << 20)(info, *evs, gp_g, gp_q)
+    q_next, g_next, early = lax.optimization_barrier((q_next, g_next, early))
+    gp = call(
+        backward_later_body, (bf16((BLK, 4 * BLK)),) * 4, 10, 5 << 30, 4 << 20, [pltpu.VMEM((GRP, 2 * BLK), F32)]
+    )(info, q_next, g_next, kv, dkv, gp_g, gp_q, *dsigs)
     send, keep = call(
         late_weights_body,
-        (bf16((4, 128, 768)), f32((4, 128, 768))), 12, 2 << 30, 4 << 20,
+        (bf16((4, 128, 5 * BLK)), f32((4, 128, 5 * BLK))), 14, 2 << 30, 4 << 20,
         [pltpu.VMEM((D, 3 * BLK), F32)],
-    )(info, *evs, *gp_gq, *gp_late)
+    )(info, *evs, *gp, *gateds, cot_z, early)
+    gp_rows = exchange(gp, "z")
     *away, own = call(
-        add_core_body, (bf16((128, 768)),) * 3 + (f32((128, 768)),), 2, 1 << 20, 4 << 20
+        add_core_body, (bf16((128, 5 * BLK)),) * 3 + (f32((128, 5 * BLK)),), 2, 1 << 20, 4 << 20
     )(info, keep, swap(send))
     sums = exchange([own] + away, "x")
-    early = call(input_early_body, f32((BLK, D)), 6, 1 << 30, 8 << 20)(info, *rows_gq, w_in, cot)
-    grad_events = call(input_late_body, bf16((BLK, D)), 6, 1 << 30, 8 << 20)(info, *rows_vk, w_in, early)
-    early_sum, grad_events = lax.optimization_barrier((early_sum, grad_events))
-    part_in, *pieces = call(
-        add_x_body, (bf16((128, D)),) + (f32((8, D)),) * 4, 5, 1 << 20, 1 << 20
-    )(info, *sums, early_sum)
-    got = lax.all_to_all(part_in.reshape(16, 8, D), ("y", "z"), 0, 0)
-    grad_w_out = to_owners(pieces).astype(BF16)
-    got = jnp.sum(got.reshape(4, 4, 8, 4, BLK).astype(F32), axis=0)
-    got = got.transpose(1, 2, 0, 3).reshape(8, 4 * D)
-    got = jnp.concatenate([got[:, :D], got[:, 2 * D : 3 * D], got[:, D : 2 * D], got[:, 3 * D :]], axis=1)
-    return grad_events[None], got.astype(BF16), grad_w_out
+    grad_events = call(input_body, bf16((BLK, D)), 6, 2 << 30, 8 << 20)(info, *gp_rows, w_in, cot)
+    own, grad_events = lax.optimization_barrier((sums[0], grad_events))
+    total = call(add_x_body, bf16((128, 5 * BLK)), 4, 1 << 20, 1 << 20)(info, own, *sums[1:])
+    got = lax.all_to_all(total.reshape(16, 8, 5 * BLK), ("y", "z"), 0, 0)
+    grad_w_in, grad_w_out = call(last_sum_body, (bf16((8, 4 * D)), bf16((8, D))), 1, 1 << 20, 1 << 20)(info, got)
+    return grad_events[None], grad_w_in, grad_w_out
 
 
 def solution(mesh):

time: 191 us -> 142 us (0.74)
  starting transfers between devices: 66.7 us -> 38.2 us
  between operations: 14.4 us -> 0.8 us
  local copies, waits for them, and re-layouts: 19.1 us -> 5.71 us
  blocking collectives: 0 us -> 12.5 us
  waiting for transfers between devices: 45.2 us -> 42 us
    ppermute x4 -> x0, starting transfers between devices: 17.1 us -> none  [to_owners(): got.append(lax.ppermute(pieces[step], ('x', 'c', 'y', 'z'), route))]
    unnamed x50 -> x8, local copies, waits for them, and re-layouts: 18.3 us -> 4.98 us
    all_to_all x0 -> x1, blocking collectives: none -> 12.5 us  [body(): got = lax.all_to_all(total.reshape(16, 8, 5 * BLK), ('y', 'z'), 0, 0)]
    all_to_all x1 -> x0, waiting for transfers between devices: 8.36 us -> none  [body(): got = lax.all_to_all(part_in.reshape(16, 8, D), ('y', 'z'), 0, 0)]
    all_to_all x1 -> x0, starting transfers between devices: 7.39 us -> none  [body(): got = lax.all_to_all(part_in.reshape(16, 8, D), ('y', 'z'), 0, 0)]
    ppermute x26 -> x23, waiting for transfers between devices: 36.8 us -> 42 us  [along(): return lax.ppermute(x, axis, [(i, (i + d) % 4) for i in range(4)])]
    ppermute x26 -> x23, starting transfers between devices: 42.1 us -> 38.1 us  [along(): return lax.ppermute(x, axis, [(i, (i + d) % 4) for i in range(4)])]
  transfers between devices with their start and end apart: 33 -> 24, of which waited for: 11 -> 8; matrix products, arithmetic and copies ran while one was open for 1% -> 1% of each run, Pallas kernels for 20% -> 24%
where the time goes in v4:
time: 142 us; the launch traced here: 140 us
  waiting for transfers between devices  42 us (30%)
  Pallas kernels  41.3 us (29%)
  starting transfers between devices  38.2 us (27%)
  blocking collectives  12.5 us (9%)
  local copies, waits for them, and re-layouts  5.71 us (4%)
    ppermute x23, waiting for transfers between devices, along(): return lax.ppermute(x, axis, [(i, (i + d) % 4) for i in range(4)])  42 us
    ppermute x23, starting transfers between devices, along(): return lax.ppermute(x, axis, [(i, (i + d) % 4) for i in range(4)])  38.1 us
    all_to_all x1, blocking collectives, body(): got = lax.all_to_all(total.reshape(16, 8, 5 * BLK), ('y', 'z'), 0, 0)  12.5 us
    pallas_call x1, Pallas kernels, body(): call(backward_local_body, (bf16((GRP, BLK)), f32((GRP, 2 * BLK))), 8, 10...  9.15 us
    pallas_call x1, Pallas kernels, body(): call(forward_local_body, (bf16((GRP, BLK)), bf16((GRP, 2 * BLK)), f32((GR...  6.3 us
    pallas_call x3, Pallas kernels, body(): call(project_body, (bf16((n * BLK, 2 * BLK)), bf16((n * BLK, BLK)), bf16(...  6.22 us
    unnamed x8, local copies, waits for them, and re-layouts  4.98 us
    pallas_call x1, Pallas kernels, body(): call(input_body, bf16((BLK, D)), 6, 2 << 30, 8 << 20)  3.72 us
  transfers between devices with their start and end apart: 24, of which 8 were waited for; matrix products, arithmetic and copies ran while one was open for 1% of the time, Pallas kernels for 24%

profile of v4, /device:TPU:0, one launch (start us, length us, event | category | flops | bytes accessed | tf_op | source)
XLA Modules:
  0.0 140.5 jit_solution(10587305852710964250)
XLA Ops:
  0.6 4.2 %collective-permute-start = (bf16[256,1024]{1,0:T(8,128)(2,1)}, bf16[256,1024]{1,0:T(8,128)(2,1)S(1)}, u32[]{:S(2)}, u32[]{:S(2)}) collective-permute-start(bf16[256,1024]{1,0:T(8,128)(2,1)} %bitcast.5.refs_0_), channel_id=1, source_target_pairs={{0,3},{1,0},{2,1},{3,2},{4,7},{5,4},{6,5},{7,6},{8,11},{9,8},{10,9... | collective-permute-start | bytes 1572872 | tf_op jit(solution)/shard_map/ppermute | solution.py:379
  5.6 3.4 %copy-done = bf16[1024,4096]{1,0:T(8,128)(2,1)S(1)} copy-done((bf16[1024,4096]{1,0:T(8,128)(2,1)S(1)}, bf16[1024,4096]{1,0:T(8,128)(2,1)}, u32[]{:S(2)}) %copy-start) | copy-done | bytes 8388632
  8.9 2.2 %shard_map.76 = (bf16[256,512]{1,0:T(8,128)(2,1)S(1)}, bf16[256,256]{1,0:T(8,128)(2,1)S(1)}, bf16[256,256]{1,0:T(8,128)(2,1)S(1)}, bf16[256,1024]{1,0:T(8,128)(2,1)S(1)}) custom-call(s32[12]{0:T(128)S(1)} %concatenate.3.info, bf16[256,1024]{1,0:T(8,128)(2,1)} %bitcast.5.refs_0_, bf16[1024,4096]{1,0:T(8,128)(2,1)S(1)} %copy-done), custom_call_target="tpu_custom_call" | custom-call | flops 536870912 | bytes 4194304 | tf_op jit(solution)/shard_map/pallas_call | solution.py:416
  11.2 5.1 %collective-permute-done.refs_0_.refs_1_ = bf16[256,1024]{1,0:T(8,128)(2,1)S(1)} collective-permute-done((bf16[256,1024]{1,0:T(8,128)(2,1)}, bf16[256,1024]{1,0:T(8,128)(2,1)S(1)}, u32[]{:S(2)}, u32[]{:S(2)}) %collective-permute-start) | collective-permute-done | bytes 524320 | tf_op jit(solution)/shard_map/ppermute | solution.py:379
  16.3 3.3 %collective-permute-done.1.refs_1_.refs_3_ = bf16[256,1024]{1,0:T(8,128)(2,1)S(1)} collective-permute-done((bf16[256,1024]{1,0:T(8,128)(2,1)}, bf16[256,1024]{1,0:T(8,128)(2,1)S(1)}, u32[]{:S(2)}, u32[]{:S(2)}) %collective-permute-start.1) | collective-permute-done | bytes 524320 | tf_op jit(solution)/shard_map/ppermute | solution.py:379
  24.1 2.4 %shard_map.77 = (bf16[512,512]{1,0:T(8,128)(2,1)S(1)}, bf16[512,256]{1,0:T(8,128)(2,1)S(1)}, bf16[512,256]{1,0:T(8,128)(2,1)S(1)}, bf16[256,1024]{1,0:T(8,128)(2,1)S(1)}, bf16[256,1024]{1,0:T(8,128)(2,1)S(1)}) custom-call(s32[12]{0:T(128)S(1)} %concatenate.3.info, bf16[256,1024]{1,0:T(8,128)(2,1)S(1)} %collective-permute-done.refs_0_.refs_1_, ...), custom_call_target="tpu_custom_call" | custom-call | flops 1073741824 | bytes 4194304 | tf_op jit(solution)/shard_map/pallas_call | solution.py:416
  28.2 5.6 %collective-permute-done.2.refs_0_.refs_2_ = bf16[256,1024]{1,0:T(8,128)(2,1)S(1)} collective-permute-done((bf16[256,1024]{1,0:T(8,128)(2,1)}, bf16[256,1024]{1,0:T(8,128)(2,1)S(1)}, u32[]{:S(2)}, u32[]{:S(2)}) %collective-permute-start.2) | collective-permute-done | bytes 524320 | tf_op jit(solution)/shard_map/ppermute | solution.py:379
  40.3 6.3 %shard_map.79 = (bf16[1024,256]{1,0:T(8,128)(2,1)S(1)}, bf16[1024,512]{1,0:T(8,128)(2,1)S(1)}, f32[1024,256]{1,0:T(8,128)S(1)}) custom-call(s32[12]{0:T(128)S(1)} %concatenate.3.info, bf16[256,256]{1,0:T(8,128)(2,1)S(1)} %get-tuple-element.62.refs_0_, bf16[512,256]{1,0:T(8,128)(2,1)S(1)} %get-tuple-element.63.refs_1_, ...), custom_call_target="tpu_custom_call" | custom-call | flops 5368709120 | bytes 4194304 | tf_op jit(solution)/shard_map/pallas_call | solution.py:430
  48.9 2.4 %collective-permute-start.10 = (f32[8,1024]{1,0:T(8,128)S(1)}, f32[8,1024]{1,0:T(8,128)S(1)}, u32[]{:S(2)}, u32[]{:S(2)}) collective-permute-start(f32[8,1024]{1,0:T(8,128)S(1)} %get-tuple-element.83.refs_3_), channel_id=1, source_target_pairs={{0,3},{1,0},{2,1},{3,2},{4,7},{5,4},{6,5},{7,6},{8,11},{9,8},{10,9... | collective-permute-start | bytes 98312 | tf_op jit(solution)/shard_map/ppermute | solution.py:379
  52.7 5.8 %collective-permute-start.3 = (bf16[1024,256]{1,0:T(8,128)(2,1)S(1)}, bf16[1024,256]{1,0:T(8,128)(2,1)S(1)}, u32[]{:S(2)}, u32[]{:S(2)}) collective-permute-start(bf16[1024,256]{1,0:T(8,128)(2,1)S(1)} %get-tuple-element.67.refs_0_), channel_id=1, source_target_pairs={{0,12},{4,0},{8,4},{12,8},{1,13},{5,1},{9,5},{13,9},{2,14},{6,2},{... | collective-permute-start | bytes 1572872 | tf_op jit(solution)/shard_map/ppermute | solution.py:379
  60.2 2.4 %collective-permute-start.14 = (bf16[1024,256]{1,0:T(8,128)(2,1)S(1)}, bf16[1024,256]{1,0:T(8,128)(2,1)S(1)}, u32[]{:S(2)}, u32[]{:S(2)}) collective-permute-start(bf16[1024,256]{1,0:T(8,128)(2,1)S(1)} %get-tuple-element.100.refs_8_), channel_id=1, source_target_pairs={{0,3},{1,0},{2,1},{3,2},{4,7},{5,4},{6,5},{7,6},{8,11},{9,8},{10,9... | collective-permute-start | bytes 1572872 | tf_op jit(solution)/shard_map/ppermute | solution.py:379
  62.6 2.3 %collective-permute-start.15 = (bf16[1024,256]{1,0:T(8,128)(2,1)S(1)}, bf16[1024,256]{1,0:T(8,128)(2,1)S(1)}, u32[]{:S(2)}, u32[]{:S(2)}) collective-permute-start(bf16[1024,256]{1,0:T(8,128)(2,1)S(1)} %get-tuple-element.100.refs_8_), channel_id=1, source_target_pairs={{0,2},{1,3},{2,0},{3,1},{4,6},{5,7},{6,4},{7,5},{8,10},{9,11},{10,... | collective-permute-start | bytes 1572872 | tf_op jit(solution)/shard_map/ppermute | solution.py:379
  64.9 3.3 %collective-permute-start.13 = (bf16[1024,256]{1,0:T(8,128)(2,1)S(1)}, bf16[1024,256]{1,0:T(8,128)(2,1)S(1)}, u32[]{:S(2)}, u32[]{:S(2)}) collective-permute-start(bf16[1024,256]{1,0:T(8,128)(2,1)S(1)} %get-tuple-element.88.refs_1_), channel_id=1, source_target_pairs={{0,12},{4,0},{8,4},{12,8},{1,13},{5,1},{9,5},{13,9},{2,14},{6,2},{... | collective-permute-start | bytes 1572872 | tf_op jit(solution)/shard_map/ppermute | solution.py:379
  68.2 9.2 %shard_map.83 = (bf16[1024,256]{1,0:T(8,128)(2,1)S(1)}, f32[1024,512]{1,0:T(8,128)S(1)}) custom-call(s32[12]{0:T(128)S(1)} %concatenate.3.info, bf16[1024,256]{1,0:T(8,128)(2,1)S(1)} %get-tuple-element.67.refs_0_, bf16[1024,256]{1,0:T(8,128)(2,1)S(1)} %get-tuple-element.88.refs_1_, bf16[1024,512]{1,0:T(8,128)(2,1)S(1)} %get-tuple-element.90.refs_2_, ...), custom_call_target="tpu_custom_call" | custom-call | flops 10737418240 | bytes 4194304 | tf_op jit(solution)/shard_map/pallas_call | solution.py:444
  77.4 2.4 %shard_map.84.refs_13_ = f32[1024,512]{1,0:T(8,128)S(1)} custom-call(s32[12]{0:T(128)S(1)} %concatenate.3.info, bf16[256,1024]{1,0:T(8,128)(2,1)} %bitcast.5.refs_0_, bf16[256,1024]{1,0:T(8,128)(2,1)S(1)} %collective-permute-done.refs_0_.refs_1_, bf16[256,1024]{1,0:T(8,128)(2,1)S(1)} %collective-permute-done.2.refs_0_.refs_2_, ...), custom_call_target="tpu_custom_call" | custom-call | flops 1073741824 | bytes 4194304 | tf_op jit(solution)/shard_map/pallas_call | solution.py:448
  79.8 2.5 %shard_map.85 = (bf16[256,1024]{1,0:T(8,128)(2,1)S(1)}, bf16[256,1024]{1,0:T(8,128)(2,1)S(1)}, bf16[256,1024]{1,0:T(8,128)(2,1)S(1)}, bf16[256,1024]{1,0:T(8,128)(2,1)S(1)}) custom-call(s32[12]{0:T(128)S(1)} %concatenate.3.info, bf16[1024,256]{1,0:T(8,128)(2,1)S(1)} %collective-permute-done.3.refs_0_, bf16[1024,256]{1,0:T(8,128)(2,1)S(1)} %collective-permute-done.13.refs_1_, ...), custom_call_target="tpu_custom_call" | custom-call | flops 5368709120 | bytes 4194304 | tf_op jit(solution)/shard_map/pallas_call | solution.py:450
  82.6 3.7 %collective-permute-done.16.refs_11_ = bf16[1024,256]{1,0:T(8,128)(2,1)S(1)} collective-permute-done((bf16[1024,256]{1,0:T(8,128)(2,1)S(1)}, bf16[1024,256]{1,0:T(8,128)(2,1)S(1)}, u32[]{:S(2)}, u32[]{:S(2)}) %collective-permute-start.16) | collective-permute-done | bytes 524320 | tf_op jit(solution)/shard_map/ppermute | solution.py:379
  86.3 3.7 %shard_map.86 = (bf16[4,128,1280]{2,1,0:T(8,128)(2,1)S(1)}, f32[4,128,1280]{2,1,0:T(8,128)S(1)}) custom-call(s32[12]{0:T(128)S(1)} %concatenate.3.info, bf16[256,1024]{1,0:T(8,128)(2,1)} %bitcast.5.refs_0_, bf16[256,1024]{1,0:T(8,128)(2,1)S(1)} %collective-permute-done.refs_0_.refs_1_, bf16[256,1024]{1,0:T(8,128)(2,1)S(1)} %collective-permute-done.2.refs_0_.refs_2_, ...), custom_call_target="tpu_custom_call" | custom-call | flops 2147483648 | bytes 4194304 | tf_op jit(solution)/shard_map/pallas_call | solution.py:453
  92.2 2.3 %collective-permute-start.20 = (bf16[256,1024]{1,0:T(8,128)(2,1)S(1)}, bf16[256,1024]{1,0:T(8,128)(2,1)S(1)}, u32[]{:S(2)}, u32[]{:S(2)}) collective-permute-start(bf16[256,1024]{1,0:T(8,128)(2,1)S(1)} %get-tuple-element.99.refs_7_), channel_id=1, source_target_pairs={{0,3},{1,0},{2,1},{3,2},{4,7},{5,4},{6,5},{7,6},{8,11},{9,8},{10,9... | collective-permute-start | bytes 1572872 | tf_op jit(solution)/shard_map/ppermute | solution.py:379
  95.7 2.2 %collective-permute-start.22 = (bf16[128,1280]{1,0:T(8,128)(2,1)S(1)}, bf16[128,1280]{1,0:T(8,128)(2,1)S(1)}, u32[]{:S(2)}, u32[]{:S(2)}) collective-permute-start(bf16[128,1280]{1,0:T(8,128)(2,1)S(1)} %get-tuple-element.109), channel_id=1, source_target_pairs={{0,64},{32,96},{64,0},{96,32},{1,65},{33,97},{65,1},{97,33},{2,66}... | collective-permute-start | bytes 983048 | tf_op jit(solution)/shard_map/ppermute | solution.py:379
  97.9 18.9 %collective-permute-done.18.refs_1_ = bf16[256,1024]{1,0:T(8,128)(2,1)S(1)} collective-permute-done((bf16[256,1024]{1,0:T(8,128)(2,1)S(1)}, bf16[256,1024]{1,0:T(8,128)(2,1)S(1)}, u32[]{:S(2)}, u32[]{:S(2)}) %collective-permute-start.18) | collective-permute-done | bytes 524320 | tf_op jit(solution)/shard_map/ppermute | solution.py:379
  118.0 3.7 %shard_map.88 = bf16[256,1024]{1,0:T(8,128)(2,1)} custom-call(s32[12]{0:T(128)S(1)} %concatenate.3.info, bf16[256,1024]{1,0:T(8,128)(2,1)S(1)} %get-tuple-element.96.refs_4_.refs_0_, bf16[256,1024]{1,0:T(8,128)(2,1)S(1)} %collective-permute-done.18.refs_1_, bf16[256,1024]{1,0:T(8,128)(2,1)S(1)} %collective-permute-done.19.refs_2_, ...), custom_call_target="tpu_custom_call" | custom-call | flops 2147483648 | bytes 8388608 | tf_op jit(solution)/shard_map/pallas_call | solution.py:463
  121.7 4.4 %collective-permute-done.23.got_3 = bf16[128,1280]{1,0:T(8,128)(2,1)S(1)} collective-permute-done((bf16[128,1280]{1,0:T(8,128)(2,1)S(1)}, bf16[128,1280]{1,0:T(8,128)(2,1)S(1)}, u32[]{:S(2)}, u32[]{:S(2)}) %collective-permute-start.23) | collective-permute-done | bytes 327712 | tf_op jit(solution)/shard_map/ppermute | solution.py:379
  126.8 12.5 %all_to_all.5.got = bf16[16,8,1280]{2,1,0:T(8,128)(2,1)S(1)} all-to-all(bf16[16,8,1280]{2,1,0:T(8,128)(2,1)S(1)} %bitcast.11), channel_id=1, replica_groups=mesh['x'=4,'c'=2,'y'=4,'z'=4] {'y','z'}, dimensions={0} | all-to-all | bytes 655360 | tf_op jit(solution)/shard_map/all_to_all | solution.py:466
  (49 shorter events, 25.6 us)
Async XLA Ops:
  0.6 15.7 %collective-permute-start = (bf16[256,1024]{1,0:T(8,128)(2,1)}, bf16[256,1024]{1,0:T(8,128)(2,1)S(1)}, u32[]{:S(2)}, u32[]{:S(2)}) collective-permute-start(bf16[256,1024]{1,0:T(8,128)(2,1)} %bitcast.5.refs_0_), channel_id=1, source_target_pairs={{0,3},{1,0},{2,1},{3,2},{4,7},{5,4},{6,5},{7,6},{8,11},{9,8},{10,9... | collective-permute-start | bytes 1572872 | tf_op jit(solution)/shard_map/ppermute | solution.py:379
  4.8 14.8 %collective-permute-start.1 = (bf16[256,1024]{1,0:T(8,128)(2,1)}, bf16[256,1024]{1,0:T(8,128)(2,1)S(1)}, u32[]{:S(2)}, u32[]{:S(2)}) collective-permute-start(bf16[256,1024]{1,0:T(8,128)(2,1)} %bitcast.5.refs_0_), channel_id=1, source_target_pairs={{0,1},{1,2},{2,3},{3,0},{4,5},{5,6},{6,7},{7,4},{8,9},{9,10},{10,1... | collective-permute-start | bytes 1572872 | tf_op jit(solution)/shard_map/ppermute | solution.py:379
  19.6 14.2 %collective-permute-start.2 = (bf16[256,1024]{1,0:T(8,128)(2,1)}, bf16[256,1024]{1,0:T(8,128)(2,1)S(1)}, u32[]{:S(2)}, u32[]{:S(2)}) collective-permute-start(bf16[256,1024]{1,0:T(8,128)(2,1)} %bitcast.5.refs_0_), channel_id=1, source_target_pairs={{0,2},{1,3},{2,0},{3,1},{4,6},{5,7},{6,4},{7,5},{8,10},{9,11},{10,... | collective-permute-start | bytes 1572872 | tf_op jit(solution)/shard_map/ppermute | solution.py:379
  19.6 19.0 %collective-permute-start.4 = (bf16[256,512]{1,0:T(8,128)(2,1)S(1)}, bf16[256,512]{1,0:T(8,128)(2,1)S(1)}, u32[]{:S(2)}, u32[]{:S(2)}) collective-permute-start(bf16[256,512]{1,0:T(8,128)(2,1)S(1)} %get-tuple-element.58.refs_3_), channel_id=1, source_target_pairs={{0,4},{4,8},{8,12},{12,0},{1,5},{5,9},{9,13},{13,1},{2,6},{6,10},{... | collective-permute-start | bytes 786440 | tf_op jit(solution)/shard_map/ppermute | solution.py:379
  26.6 20.0 %collective-permute-start.5 = (bf16[512,512]{1,0:T(8,128)(2,1)S(1)}, bf16[512,512]{1,0:T(8,128)(2,1)S(1)}, u32[]{:S(2)}, u32[]{:S(2)}) collective-permute-start(bf16[512,512]{1,0:T(8,128)(2,1)S(1)} %get-tuple-element.65.refs_4_), channel_id=1, source_target_pairs={{0,4},{4,8},{8,12},{12,0},{1,5},{5,9},{9,13},{13,1},{2,6},{6,10},{... | collective-permute-start | bytes 1572872 | tf_op jit(solution)/shard_map/ppermute | solution.py:379
  33.8 12.8 %collective-permute-start.7 = (bf16[256,512]{1,0:T(8,128)(2,1)S(1)}, bf16[256,512]{1,0:T(8,128)(2,1)S(1)}, u32[]{:S(2)}, u32[]{:S(2)}) collective-permute-start(bf16[256,512]{1,0:T(8,128)(2,1)S(1)} %get-tuple-element.74), channel_id=1, source_target_pairs={{0,1},{1,2},{2,3},{3,0},{4,5},{5,6},{6,7},{7,4},{8,9},{9,10},{10,1... | collective-permute-start | bytes 786440 | tf_op jit(solution)/shard_map/ppermute | solution.py:379
  33.8 12.8 %collective-permute-start.8 = (bf16[256,512]{1,0:T(8,128)(2,1)S(1)}, bf16[256,512]{1,0:T(8,128)(2,1)S(1)}, u32[]{:S(2)}, u32[]{:S(2)}) collective-permute-start(bf16[256,512]{1,0:T(8,128)(2,1)S(1)} %get-tuple-element.75), channel_id=1, source_target_pairs={{0,2},{1,3},{2,0},{3,1},{4,6},{5,7},{6,4},{7,5},{8,10},{9,11},{10,... | collective-permute-start | bytes 786440 | tf_op jit(solution)/shard_map/ppermute | solution.py:379
  35.9 11.3 %collective-permute-start.9 = (bf16[256,512]{1,0:T(8,128)(2,1)S(1)}, bf16[256,512]{1,0:T(8,128)(2,1)S(1)}, u32[]{:S(2)}, u32[]{:S(2)}) collective-permute-start(bf16[256,512]{1,0:T(8,128)(2,1)S(1)} %get-tuple-element.76), channel_id=1, source_target_pairs={{0,3},{1,0},{2,1},{3,2},{4,7},{5,4},{6,5},{7,6},{8,11},{9,8},{10,9... | collective-permute-start | bytes 786440 | tf_op jit(solution)/shard_map/ppermute | solution.py:379
  38.6 8.6 %collective-permute-start.6 = (bf16[256,512]{1,0:T(8,128)(2,1)S(1)}, bf16[256,512]{1,0:T(8,128)(2,1)S(1)}, u32[]{:S(2)}, u32[]{:S(2)}) collective-permute-start(bf16[256,512]{1,0:T(8,128)(2,1)S(1)} %get-tuple-element.66.refs_5_), channel_id=1, source_target_pairs={{0,4},{4,8},{8,12},{12,0},{1,5},{5,9},{9,13},{13,1},{2,6},{6,10},{... | collective-permute-start | bytes 786440 | tf_op jit(solution)/shard_map/ppermute | solution.py:379
  48.9 9.7 %collective-permute-start.10 = (f32[8,1024]{1,0:T(8,128)S(1)}, f32[8,1024]{1,0:T(8,128)S(1)}, u32[]{:S(2)}, u32[]{:S(2)}) collective-permute-start(f32[8,1024]{1,0:T(8,128)S(1)} %get-tuple-element.83.refs_3_), channel_id=1, source_target_pairs={{0,3},{1,0},{2,1},{3,2},{4,7},{5,4},{6,5},{7,6},{8,11},{9,8},{10,9... | collective-permute-start | bytes 98312 | tf_op jit(solution)/shard_map/ppermute | solution.py:379
  51.3 7.3 %collective-permute-start.11 = (f32[8,1024]{1,0:T(8,128)S(1)}, f32[8,1024]{1,0:T(8,128)S(1)}, u32[]{:S(2)}, u32[]{:S(2)}) collective-permute-start(f32[8,1024]{1,0:T(8,128)S(1)} %get-tuple-element.83.refs_3_), channel_id=1, source_target_pairs={{0,2},{1,3},{2,0},{3,1},{4,6},{5,7},{6,4},{7,5},{8,10},{9,11},{10,... | collective-permute-start | bytes 98312 | tf_op jit(solution)/shard_map/ppermute | solution.py:379
  51.4 7.1 %collective-permute-start.12 = (f32[8,1024]{1,0:T(8,128)S(1)}, f32[8,1024]{1,0:T(8,128)S(1)}, u32[]{:S(2)}, u32[]{:S(2)}) collective-permute-start(f32[8,1024]{1,0:T(8,128)S(1)} %get-tuple-element.83.refs_3_), channel_id=1, source_target_pairs={{0,1},{1,2},{2,3},{3,0},{4,5},{5,6},{6,7},{7,4},{8,9},{9,10},{10,1... | collective-permute-start | bytes 98312 | tf_op jit(solution)/shard_map/ppermute | solution.py:379
  52.7 27.0 %collective-permute-start.3 = (bf16[1024,256]{1,0:T(8,128)(2,1)S(1)}, bf16[1024,256]{1,0:T(8,128)(2,1)S(1)}, u32[]{:S(2)}, u32[]{:S(2)}) collective-permute-start(bf16[1024,256]{1,0:T(8,128)(2,1)S(1)} %get-tuple-element.67.refs_0_), channel_id=1, source_target_pairs={{0,12},{4,0},{8,4},{12,8},{1,13},{5,1},{9,5},{13,9},{2,14},{6,2},{... | collective-permute-start | bytes 1572872 | tf_op jit(solution)/shard_map/ppermute | solution.py:379
  60.2 22.3 %collective-permute-start.14 = (bf16[1024,256]{1,0:T(8,128)(2,1)S(1)}, bf16[1024,256]{1,0:T(8,128)(2,1)S(1)}, u32[]{:S(2)}, u32[]{:S(2)}) collective-permute-start(bf16[1024,256]{1,0:T(8,128)(2,1)S(1)} %get-tuple-element.100.refs_8_), channel_id=1, source_target_pairs={{0,3},{1,0},{2,1},{3,2},{4,7},{5,4},{6,5},{7,6},{8,11},{9,8},{10,9... | collective-permute-start | bytes 1572872 | tf_op jit(solution)/shard_map/ppermute | solution.py:379
  62.6 20.0 %collective-permute-start.15 = (bf16[1024,256]{1,0:T(8,128)(2,1)S(1)}, bf16[1024,256]{1,0:T(8,128)(2,1)S(1)}, u32[]{:S(2)}, u32[]{:S(2)}) collective-permute-start(bf16[1024,256]{1,0:T(8,128)(2,1)S(1)} %get-tuple-element.100.refs_8_), channel_id=1, source_target_pairs={{0,2},{1,3},{2,0},{3,1},{4,6},{5,7},{6,4},{7,5},{8,10},{9,11},{10,... | collective-permute-start | bytes 1572872 | tf_op jit(solution)/shard_map/ppermute | solution.py:379
  64.9 21.3 %collective-permute-start.16 = (bf16[1024,256]{1,0:T(8,128)(2,1)S(1)}, bf16[1024,256]{1,0:T(8,128)(2,1)S(1)}, u32[]{:S(2)}, u32[]{:S(2)}) collective-permute-start(bf16[1024,256]{1,0:T(8,128)(2,1)S(1)} %get-tuple-element.100.refs_8_), channel_id=1, source_target_pairs={{0,1},{1,2},{2,3},{3,0},{4,5},{5,6},{6,7},{7,4},{8,9},{9,10},{10,1... | collective-permute-start | bytes 1572872 | tf_op jit(solution)/shard_map/ppermute | solution.py:379
  64.9 14.8 %collective-permute-start.13 = (bf16[1024,256]{1,0:T(8,128)(2,1)S(1)}, bf16[1024,256]{1,0:T(8,128)(2,1)S(1)}, u32[]{:S(2)}, u32[]{:S(2)}) collective-permute-start(bf16[1024,256]{1,0:T(8,128)(2,1)S(1)} %get-tuple-element.88.refs_1_), channel_id=1, source_target_pairs={{0,12},{4,0},{8,4},{12,8},{1,13},{5,1},{9,5},{13,9},{2,14},{6,2},{... | collective-permute-start | bytes 1572872 | tf_op jit(solution)/shard_map/ppermute | solution.py:379
  90.0 4.5 %collective-permute-start.17 = (bf16[4,128,1280]{2,1,0:T(8,128)(2,1)S(1)}, bf16[4,128,1280]{2,1,0:T(8,128)(2,1)S(1)}, u32[]{:S(2)}, u32[]{:S(2)}) collective-permute-start(bf16[4,128,1280]{2,1,0:T(8,128)(2,1)S(1)} %get-tuple-element.104), channel_id=1, source_target_pairs={{0,16},{16,0},{1,17},{17,1},{2,18},{18,2},{3,19},{19,3},{4,20},{20... | collective-permute-start | bytes 3932168 | tf_op jit(solution)/shard_map/ppermute | solution.py:383
  90.1 26.8 %collective-permute-start.18 = (bf16[256,1024]{1,0:T(8,128)(2,1)S(1)}, bf16[256,1024]{1,0:T(8,128)(2,1)S(1)}, u32[]{:S(2)}, u32[]{:S(2)}) collective-permute-start(bf16[256,1024]{1,0:T(8,128)(2,1)S(1)} %get-tuple-element.97.refs_5_), channel_id=1, source_target_pairs={{0,1},{1,2},{2,3},{3,0},{4,5},{5,6},{6,7},{7,4},{8,9},{9,10},{10,1... | collective-permute-start | bytes 1572872 | tf_op jit(solution)/shard_map/ppermute | solution.py:379
  90.7 27.3 %collective-permute-start.19 = (bf16[256,1024]{1,0:T(8,128)(2,1)S(1)}, bf16[256,1024]{1,0:T(8,128)(2,1)S(1)}, u32[]{:S(2)}, u32[]{:S(2)}) collective-permute-start(bf16[256,1024]{1,0:T(8,128)(2,1)S(1)} %get-tuple-element.98.refs_6_), channel_id=1, source_target_pairs={{0,2},{1,3},{2,0},{3,1},{4,6},{5,7},{6,4},{7,5},{8,10},{9,11},{10,... | collective-permute-start | bytes 1572872 | tf_op jit(solution)/shard_map/ppermute | solution.py:379
  92.2 25.8 %collective-permute-start.20 = (bf16[256,1024]{1,0:T(8,128)(2,1)S(1)}, bf16[256,1024]{1,0:T(8,128)(2,1)S(1)}, u32[]{:S(2)}, u32[]{:S(2)}) collective-permute-start(bf16[256,1024]{1,0:T(8,128)(2,1)S(1)} %get-tuple-element.99.refs_7_), channel_id=1, source_target_pairs={{0,3},{1,0},{2,1},{3,2},{4,7},{5,4},{6,5},{7,6},{8,11},{9,8},{10,9... | collective-permute-start | bytes 1572872 | tf_op jit(solution)/shard_map/ppermute | solution.py:379
  95.3 26.4 %collective-permute-start.21 = (bf16[128,1280]{1,0:T(8,128)(2,1)S(1)}, bf16[128,1280]{1,0:T(8,128)(2,1)S(1)}, u32[]{:S(2)}, u32[]{:S(2)}) collective-permute-start(bf16[128,1280]{1,0:T(8,128)(2,1)S(1)} %get-tuple-element.108), channel_id=1, source_target_pairs={{0,32},{32,64},{64,96},{96,0},{1,33},{33,65},{65,97},{97,1},{2,34}... | collective-permute-start | bytes 983048 | tf_op jit(solution)/shard_map/ppermute | solution.py:379
  95.7 25.9 %collective-permute-start.22 = (bf16[128,1280]{1,0:T(8,128)(2,1)S(1)}, bf16[128,1280]{1,0:T(8,128)(2,1)S(1)}, u32[]{:S(2)}, u32[]{:S(2)}) collective-permute-start(bf16[128,1280]{1,0:T(8,128)(2,1)S(1)} %get-tuple-element.109), channel_id=1, source_target_pairs={{0,64},{32,96},{64,0},{96,32},{1,65},{33,97},{65,1},{97,33},{2,66}... | collective-permute-start | bytes 983048 | tf_op jit(solution)/shard_map/ppermute | solution.py:379
  116.8 9.3 %collective-permute-start.23 = (bf16[128,1280]{1,0:T(8,128)(2,1)S(1)}, bf16[128,1280]{1,0:T(8,128)(2,1)S(1)}, u32[]{:S(2)}, u32[]{:S(2)}) collective-permute-start(bf16[128,1280]{1,0:T(8,128)(2,1)S(1)} %get-tuple-element.110), channel_id=1, source_target_pairs={{0,96},{32,0},{64,32},{96,64},{1,97},{33,1},{65,33},{97,65},{2,98}... | collective-permute-start | bytes 983048 | tf_op jit(solution)/shard_map/ppermute | solution.py:379
  (4 other events, 32.4 us)

commit v5 on v4

--- a/solution.py
+++ b/solution.py
@@ -243,15 +243,12 @@
             out[x, :, 2 * BLK :] = acc[at, :].astype(kind)
 
 
-def add_core_body(info, keep, got, to_1, to_2, to_3, own):
-    own[...] = keep[info[11]] + got[info[11]].astype(F32)
-    for d, out in ((1, to_1), (2, to_2), (3, to_3)):
-        at = lax.rem(info[11] + d, 4)
-        out[...] = (keep[at] + got[at].astype(F32)).astype(BF16)
-
-
-def add_x_body(info, own, got_1, got_2, got_3, total):
-    part = own[...] + got_1[...].astype(F32) + got_2[...].astype(F32) + got_3[...].astype(F32)
+def add_core_body(info, keep, got, out):
+    out[...] = (keep[...] + got[...].astype(F32)).astype(BF16)
+
+
+def add_x_body(info, got, total):
+    part = got[0].astype(F32) + got[1].astype(F32) + got[2].astype(F32) + got[3].astype(F32)
     total[...] = part.astype(BF16)
 
 
@@ -365,14 +362,38 @@
 
 
 def input_body(info, *refs):
-    gp, (w, cot, out) = refs[0:4], refs[4:7]
-    total = cot[...].astype(F32)
+    gp, w, (cot, out, acc) = refs[0:4], refs[4:8], refs[8:11]
     for d in range(NB):
-        owner = lax.rem(info[9] + NB - d, NB)
-        for n, part in enumerate((0, 2, 1, 3)):
-            lanes = pl.ds(pl.multiple_of(part * D + owner * BLK, BLK), BLK)
-            total = total + nt(gp[d][:, n * BLK : (n + 1) * BLK], w[:, lanes])
-    out[...] = total.astype(BF16)
+
+        @pl.when(pl.program_id(0) == d)
+        def _(d=d):
+            part = cot[...].astype(F32) if d == 0 else acc[...]
+            for n in range(4):
+                part = part + nt(gp[d][:, n * BLK : (n + 1) * BLK], w[n][...])
+            if d < NB - 1:
+                acc[...] = part
+            else:
+                out[...] = part.astype(BF16)
+
+
+def input_grad(info, gp, w_in, cot):
+    def columns(part):
+        return pl.BlockSpec((D, BLK), lambda d, at: (0, part * 4 + lax.rem(at[9] + NB - d, NB)))
+
+    whole = pl.BlockSpec((BLK, D), lambda d, at: (0, 0))
+    return pl.pallas_call(
+        input_body,
+        grid_spec=pltpu.PrefetchScalarGridSpec(
+            num_scalar_prefetch=1,
+            grid=(NB,),
+            in_specs=[whole] * 4 + [columns(p) for p in (0, 2, 1, 3)] + [whole],
+            out_specs=whole,
+            scratch_shapes=[pltpu.VMEM((BLK, D), F32)],
+        ),
+        out_shape=bf16((BLK, D)),
+        compiler_params=pltpu.CompilerParams(vmem_limit_bytes=20 * 1024 * 1024),
+        cost_estimate=pl.CostEstimate(flops=40 << 30, bytes_accessed=8 << 20, transcendentals=0),
+    )(info, *gp, w_in, w_in, w_in, w_in, cot)
 
 
 def along(x, axis, d):
@@ -442,27 +463,27 @@
     g_next = along(gatt, "y", -1)
     gateds = gather_z(gated)
     gp_q, dkv = call(
-        backward_local_body, (bf16((GRP, BLK)), f32((GRP, 2 * BLK))), 8, 10 << 30, 4 << 20,
+        backward_local_body, (bf16((GRP, BLK)), f32((GRP, 2 * BLK))), 8, 1 << 20, 1 << 20,
         [pltpu.VMEM((GRP, BLK), F32)],
     )(info, q, gatt, kv, kv_prev, *dsigs)
-    early = call(early_weights_body, f32((D, 2 * BLK)), 6, 1 << 30, 4 << 20)(info, *evs, gp_g, gp_q)
+    early = call(early_weights_body, f32((D, 2 * BLK)), 6, 1 << 20, 1 << 20)(info, *evs, gp_g, gp_q)
     q_next, g_next, early = lax.optimization_barrier((q_next, g_next, early))
     gp = call(
         backward_later_body, (bf16((BLK, 4 * BLK)),) * 4, 10, 5 << 30, 4 << 20, [pltpu.VMEM((GRP, 2 * BLK), F32)]
     )(info, q_next, g_next, kv, dkv, gp_g, gp_q, *dsigs)
     send, keep = call(
         late_weights_body,
-        (bf16((4, 128, 5 * BLK)), f32((4, 128, 5 * BLK))), 14, 2 << 30, 4 << 20,
+        (bf16((4, 128, 5 * BLK)), f32((4, 128, 5 * BLK))), 14, 1 << 20, 1 << 20,
         [pltpu.VMEM((D, 3 * BLK), F32)],
     )(info, *evs, *gp, *gateds, cot_z, early)
     gp_rows = exchange(gp, "z")
-    *away, own = call(
-        add_core_body, (bf16((128, 5 * BLK)),) * 3 + (f32((128, 5 * BLK)),), 2, 1 << 20, 4 << 20
+    mine = call(
+        add_core_body, bf16((4, 128, 5 * BLK)), 2, 1 << 20, 1 << 20
     )(info, keep, swap(send))
-    sums = exchange([own] + away, "x")
-    grad_events = call(input_body, bf16((BLK, D)), 6, 2 << 30, 8 << 20)(info, *gp_rows, w_in, cot)
-    own, grad_events = lax.optimization_barrier((sums[0], grad_events))
-    total = call(add_x_body, bf16((128, 5 * BLK)), 4, 1 << 20, 1 << 20)(info, own, *sums[1:])
+    sums = lax.all_to_all(mine, "x", 0, 0)
+    grad_events = input_grad(info, gp_rows, w_in, cot)
+    sums, grad_events = lax.optimization_barrier((sums, grad_events))
+    total = call(add_x_body, bf16((128, 5 * BLK)), 1, 1 << 20, 1 << 20)(info, sums)
     got = lax.all_to_all(total.reshape(16, 8, 5 * BLK), ("y", "z"), 0, 0)
     grad_w_in, grad_w_out = call(last_sum_body, (bf16((8, 4 * D)), bf16((8, D))), 1, 1 << 20, 1 << 20)(info, got)
     return grad_events[None], grad_w_in, grad_w_out

time: 142 us -> 148 us (1.042)
  local copies, waits for them, and re-layouts: 5.71 us -> 10.1 us
  waiting for transfers between devices: 42 us -> 38.5 us
  blocking collectives: 12.5 us -> 15.3 us
  Pallas kernels: 41.3 us -> 44 us
    all_to_all x0 -> x1, starting transfers between devices: none -> 4.49 us  [body(): sums = lax.all_to_all(mine, 'x', 0, 0)]
    unnamed x8 -> x12, local copies, waits for them, and re-layouts: 4.98 us -> 9.4 us
    ppermute x23 -> x20, starting transfers between devices: 38.1 us -> 34.4 us  [along(): return lax.ppermute(x, axis, [(i, (i + d) % 4) for i in range(4)])]
    ppermute x23 -> x20, waiting for transfers between devices: 42 us -> 38.5 us  [along(): return lax.ppermute(x, axis, [(i, (i + d) % 4) for i in range(4)])]
    all_to_all x1, blocking collectives: 12.5 us -> 15.3 us  [body(): got = lax.all_to_all(total.reshape(16, 8, 5 * BLK), ('y', 'z'), 0, 0)]
    pallas_call x5, Pallas kernels: 16.7 us -> 19.3 us  [the longest x1 7.53 us: body(): call(backward_local_body, (bf16((GRP, BLK)), f32((GRP, 2 * BLK))), 8, 1 <...]
  transfers between devices with their start and end apart: 24 -> 22, of which waited for: 8 -> 10; matrix products, arithmetic and copies ran while one was open for 1% -> 0% of each run, Pallas kernels for 24% -> 25%
where the time goes in v5:
time: 148 us
  Pallas kernels  44 us (30%)
  starting transfers between devices  38.9 us (26%)
  waiting for transfers between devices  38.5 us (26%)
  blocking collectives  15.3 us (10%)
  local copies, waits for them, and re-layouts  10.1 us (7%)
    ppermute x20, waiting for transfers between devices, along(): return lax.ppermute(x, axis, [(i, (i + d) % 4) for i in range(4)])  38.5 us
    ppermute x20, starting transfers between devices, along(): return lax.ppermute(x, axis, [(i, (i + d) % 4) for i in range(4)])  34.4 us
    all_to_all x1, blocking collectives, body(): got = lax.all_to_all(total.reshape(16, 8, 5 * BLK), ('y', 'z'), 0, 0)  15.3 us
    unnamed x12, local copies, waits for them, and re-layouts  9.4 us
    pallas_call x1, Pallas kernels, body(): call(backward_local_body, (bf16((GRP, BLK)), f32((GRP, 2 * BLK))), 8, 1 <...  7.53 us
    pallas_call x1, Pallas kernels, input_grad(): pl.pallas_call(input_body, grid_spec=pltpu.PrefetchScalarGridSpec(num_sca...  6.85 us
    pallas_call x3, Pallas kernels, body(): call(project_body, (bf16((n * BLK, 2 * BLK)), bf16((n * BLK, BLK)), bf16(...  6.22 us
    pallas_call x1, Pallas kernels, body(): call(forward_local_body, (bf16((GRP, BLK)), bf16((GRP, 2 * BLK)), f32((GR...  5.19 us
  transfers between devices with their start and end apart: 22, of which 10 were waited for; matrix products, arithmetic and copies ran while one was open for 0% of the time, Pallas kernels for 25%

profile of v5, /device:TPU:0, one launch (start us, length us, event | category | flops | bytes accessed | tf_op | source)
XLA Modules:
  0.0 147.6 jit_solution(16272535747939158849)
XLA Ops:
  0.6 4.2 %collective-permute-start = (bf16[256,1024]{1,0:T(8,128)(2,1)}, bf16[256,1024]{1,0:T(8,128)(2,1)S(1)}, u32[]{:S(2)}, u32[]{:S(2)}) collective-permute-start(bf16[256,1024]{1,0:T(8,128)(2,1)} %bitcast.5.refs_0_), channel_id=1, source_target_pairs={{0,3},{1,0},{2,1},{3,2},{4,7},{5,4},{6,5},{7,6},{8,11},{9,8},{10,9... | collective-permute-start | bytes 1572872 | tf_op jit(solution)/shard_map/ppermute | solution.py:400
  5.6 3.4 %copy-done = bf16[1024,4096]{1,0:T(8,128)(2,1)S(1)} copy-done((bf16[1024,4096]{1,0:T(8,128)(2,1)S(1)}, bf16[1024,4096]{1,0:T(8,128)(2,1)}, u32[]{:S(2)}) %copy-start) | copy-done | bytes 8388632
  8.9 2.2 %shard_map.76 = (bf16[256,512]{1,0:T(8,128)(2,1)S(1)}, bf16[256,256]{1,0:T(8,128)(2,1)S(1)}, bf16[256,256]{1,0:T(8,128)(2,1)S(1)}, bf16[256,1024]{1,0:T(8,128)(2,1)S(1)}) custom-call(s32[12]{0:T(128)S(1)} %concatenate.3.info, bf16[256,1024]{1,0:T(8,128)(2,1)} %bitcast.5.refs_0_, bf16[1024,4096]{1,0:T(8,128)(2,1)S(1)} %copy-done), custom_call_target="tpu_custom_call" | custom-call | flops 536870912 | bytes 4194304 | tf_op jit(solution)/shard_map/pallas_call | solution.py:437
  11.2 5.1 %collective-permute-done.refs_0_.refs_1_ = bf16[256,1024]{1,0:T(8,128)(2,1)S(1)} collective-permute-done((bf16[256,1024]{1,0:T(8,128)(2,1)}, bf16[256,1024]{1,0:T(8,128)(2,1)S(1)}, u32[]{:S(2)}, u32[]{:S(2)}) %collective-permute-start) | collective-permute-done | bytes 524320 | tf_op jit(solution)/shard_map/ppermute | solution.py:400
  16.3 3.3 %collective-permute-done.1.refs_1_.refs_3_ = bf16[256,1024]{1,0:T(8,128)(2,1)S(1)} collective-permute-done((bf16[256,1024]{1,0:T(8,128)(2,1)}, bf16[256,1024]{1,0:T(8,128)(2,1)S(1)}, u32[]{:S(2)}, u32[]{:S(2)}) %collective-permute-start.1) | collective-permute-done | bytes 524320 | tf_op jit(solution)/shard_map/ppermute | solution.py:400
  24.1 2.4 %shard_map.77 = (bf16[512,512]{1,0:T(8,128)(2,1)S(1)}, bf16[512,256]{1,0:T(8,128)(2,1)S(1)}, bf16[512,256]{1,0:T(8,128)(2,1)S(1)}, bf16[256,1024]{1,0:T(8,128)(2,1)S(1)}, bf16[256,1024]{1,0:T(8,128)(2,1)S(1)}) custom-call(s32[12]{0:T(128)S(1)} %concatenate.3.info, bf16[256,1024]{1,0:T(8,128)(2,1)S(1)} %collective-permute-done.refs_0_.refs_1_, ...), custom_call_target="tpu_custom_call" | custom-call | flops 1073741824 | bytes 4194304 | tf_op jit(solution)/shard_map/pallas_call | solution.py:437
  28.2 5.6 %collective-permute-done.2.refs_0_.refs_2_ = bf16[256,1024]{1,0:T(8,128)(2,1)S(1)} collective-permute-done((bf16[256,1024]{1,0:T(8,128)(2,1)}, bf16[256,1024]{1,0:T(8,128)(2,1)S(1)}, u32[]{:S(2)}, u32[]{:S(2)}) %collective-permute-start.2) | collective-permute-done | bytes 524320 | tf_op jit(solution)/shard_map/ppermute | solution.py:400
  33.8 2.1 %collective-permute-start.8 = (bf16[256,512]{1,0:T(8,128)(2,1)S(1)}, bf16[256,512]{1,0:T(8,128)(2,1)S(1)}, u32[]{:S(2)}, u32[]{:S(2)}) collective-permute-start(bf16[256,512]{1,0:T(8,128)(2,1)S(1)} %get-tuple-element.71), channel_id=1, source_target_pairs={{0,2},{1,3},{2,0},{3,1},{4,6},{5,7},{6,4},{7,5},{8,10},{9,11},{10,... | collective-permute-start | bytes 786440 | tf_op jit(solution)/shard_map/ppermute | solution.py:400
  40.3 5.2 %shard_map.79 = (bf16[1024,256]{1,0:T(8,128)(2,1)S(1)}, bf16[1024,512]{1,0:T(8,128)(2,1)S(1)}, f32[1024,256]{1,0:T(8,128)S(1)}) custom-call(s32[12]{0:T(128)S(1)} %concatenate.3.info, bf16[256,256]{1,0:T(8,128)(2,1)S(1)} %get-tuple-element.58.refs_0_, bf16[512,256]{1,0:T(8,128)(2,1)S(1)} %get-tuple-element.59.refs_1_, ...), custom_call_target="tpu_custom_call" | custom-call | flops 5368709120 | bytes 4194304 | tf_op jit(solution)/shard_map/pallas_call | solution.py:451
  48.9 2.4 %collective-permute-start.10 = (f32[8,1024]{1,0:T(8,128)S(1)}, f32[8,1024]{1,0:T(8,128)S(1)}, u32[]{:S(2)}, u32[]{:S(2)}) collective-permute-start(f32[8,1024]{1,0:T(8,128)S(1)} %get-tuple-element.79.refs_3_), channel_id=1, source_target_pairs={{0,3},{1,0},{2,1},{3,2},{4,7},{5,4},{6,5},{7,6},{8,11},{9,8},{10,9... | collective-permute-start | bytes 98312 | tf_op jit(solution)/shard_map/ppermute | solution.py:400
  52.4 6.2 %collective-permute-start.3 = (bf16[1024,256]{1,0:T(8,128)(2,1)S(1)}, bf16[1024,256]{1,0:T(8,128)(2,1)S(1)}, u32[]{:S(2)}, u32[]{:S(2)}) collective-permute-start(bf16[1024,256]{1,0:T(8,128)(2,1)S(1)} %get-tuple-element.63.refs_0_), channel_id=1, source_target_pairs={{0,12},{4,0},{8,4},{12,8},{1,13},{5,1},{9,5},{13,9},{2,14},{6,2},{... | collective-permute-start | bytes 1572872 | tf_op jit(solution)/shard_map/ppermute | solution.py:400
  60.2 4.6 %collective-permute-start.13 = (bf16[1024,256]{1,0:T(8,128)(2,1)S(1)}, bf16[1024,256]{1,0:T(8,128)(2,1)S(1)}, u32[]{:S(2)}, u32[]{:S(2)}) collective-permute-start(bf16[1024,256]{1,0:T(8,128)(2,1)S(1)} %get-tuple-element.84.refs_1_), channel_id=1, source_target_pairs={{0,12},{4,0},{8,4},{12,8},{1,13},{5,1},{9,5},{13,9},{2,14},{6,2},{... | collective-permute-start | bytes 1572872 | tf_op jit(solution)/shard_map/ppermute | solution.py:400
  68.2 7.5 %shard_map.83 = (bf16[1024,256]{1,0:T(8,128)(2,1)S(1)}, f32[1024,512]{1,0:T(8,128)S(1)}) custom-call(s32[12]{0:T(128)S(1)} %concatenate.3.info, bf16[1024,256]{1,0:T(8,128)(2,1)S(1)} %get-tuple-element.63.refs_0_, bf16[1024,256]{1,0:T(8,128)(2,1)S(1)} %get-tuple-element.84.refs_1_, bf16[1024,512]{1,0:T(8,128)(2,1)S(1)} %get-tuple-element.86.refs_2_, ...), custom_call_target="tpu_custom_call" | custom-call | flops 1048576 | bytes 1048576 | tf_op jit(solution)/shard_map/pallas_call | solution.py:465
  75.7 2.4 %shard_map.84.refs_13_ = f32[1024,512]{1,0:T(8,128)S(1)} custom-call(s32[12]{0:T(128)S(1)} %concatenate.3.info, bf16[256,1024]{1,0:T(8,128)(2,1)} %bitcast.5.refs_0_, bf16[256,1024]{1,0:T(8,128)(2,1)S(1)} %collective-permute-done.refs_0_.refs_1_, bf16[256,1024]{1,0:T(8,128)(2,1)S(1)} %collective-permute-done.2.refs_0_.refs_2_, ...), custom_call_target="tpu_custom_call" | custom-call | flops 1048576 | bytes 1048576 | tf_op jit(solution)/shard_map/pallas_call | solution.py:469
  79.2 3.7 %shard_map.85 = (bf16[256,1024]{1,0:T(8,128)(2,1)S(1)}, bf16[256,1024]{1,0:T(8,128)(2,1)S(1)}, bf16[256,1024]{1,0:T(8,128)(2,1)S(1)}, bf16[256,1024]{1,0:T(8,128)(2,1)S(1)}) custom-call(s32[12]{0:T(128)S(1)} %concatenate.3.info, bf16[1024,256]{1,0:T(8,128)(2,1)S(1)} %collective-permute-done.3.refs_0_, bf16[1024,256]{1,0:T(8,128)(2,1)S(1)} %collective-permute-done.13.refs_1_, ...), custom_call_target="tpu_custom_call" | custom-call | flops 5368709120 | bytes 4194304 | tf_op jit(solution)/shard_map/pallas_call | solution.py:471
  84.2 3.7 %collective-permute-done.16.refs_11_ = bf16[1024,256]{1,0:T(8,128)(2,1)S(1)} collective-permute-done((bf16[1024,256]{1,0:T(8,128)(2,1)S(1)}, bf16[1024,256]{1,0:T(8,128)(2,1)S(1)}, u32[]{:S(2)}, u32[]{:S(2)}) %collective-permute-start.16) | collective-permute-done | bytes 524320 | tf_op jit(solution)/shard_map/ppermute | solution.py:400
  87.8 3.7 %shard_map.86 = (bf16[4,128,1280]{2,1,0:T(8,128)(2,1)S(1)}, f32[4,128,1280]{2,1,0:T(8,128)S(1)}) custom-call(s32[12]{0:T(128)S(1)} %concatenate.3.info, bf16[256,1024]{1,0:T(8,128)(2,1)} %bitcast.5.refs_0_, bf16[256,1024]{1,0:T(8,128)(2,1)S(1)} %collective-permute-done.refs_0_.refs_1_, bf16[256,1024]{1,0:T(8,128)(2,1)S(1)} %collective-permute-done.2.refs_0_.refs_2_, ...), custom_call_target="tpu_custom_call" | custom-call | flops 1048576 | bytes 1048576 | tf_op jit(solution)/shard_map/pallas_call | solution.py:474
  93.7 2.3 %collective-permute-start.20 = (bf16[256,1024]{1,0:T(8,128)(2,1)S(1)}, bf16[256,1024]{1,0:T(8,128)(2,1)}, u32[]{:S(2)}, u32[]{:S(2)}) collective-permute-start(bf16[256,1024]{1,0:T(8,128)(2,1)S(1)} %get-tuple-element.95.refs_7_), channel_id=1, source_target_pairs={{0,3},{1,0},{2,1},{3,2},{4,7},{5,4},{6,5},{7,6},{8,11},{9,8},{10,9... | collective-permute-start | bytes 1572872 | tf_op jit(solution)/shard_map/ppermute | solution.py:400
  96.0 1.8 %shard_map.87 = bf16[4,128,1280]{2,1,0:T(8,128)(2,1)} custom-call(s32[12]{0:T(128)S(1)} %concatenate.3.info, f32[4,128,1280]{2,1,0:T(8,128)S(1)} %get-tuple-element.99.keep, bf16[4,128,1280]{2,1,0:T(8,128)(2,1)S(1)} %collective-permute-done.17.got), custom_call_target="tpu_custom_call" | custom-call | flops 1048576 | bytes 1048576 | tf_op jit(solution)/shard_map/pallas_call | solution.py:480
  97.9 4.5 %all-to-all-start = ((bf16[4,128,1280]{2,1,0:T(8,128)(2,1)}), bf16[4,128,1280]{2,1,0:T(8,128)(2,1)S(1)}, u32[]{:S(2)}, u32[]{:S(2)}) async-start(bf16[4,128,1280]{2,1,0:T(8,128)(2,1)} %shard_map.87), calls=%async_computation | async-start | bytes 2621440 | tf_op jit(solution)/shard_map/all_to_all | solution.py:483
  102.4 16.1 %collective-permute-done.18.refs_1_ = bf16[256,1024]{1,0:T(8,128)(2,1)} collective-permute-done((bf16[256,1024]{1,0:T(8,128)(2,1)S(1)}, bf16[256,1024]{1,0:T(8,128)(2,1)}, u32[]{:S(2)}, u32[]{:S(2)}) %collective-permute-start.18) | collective-permute-done | bytes 524320 | tf_op jit(solution)/shard_map/ppermute | solution.py:400
  119.1 3.4 %copy-done.2 = bf16[1024,4096]{1,0:T(8,128)(2,1)S(1)} copy-done((bf16[1024,4096]{1,0:T(8,128)(2,1)S(1)}, bf16[1024,4096]{1,0:T(8,128)(2,1)}, u32[]{:S(2)}) %copy-start.2) | copy-done | bytes 8388632
  123.5 6.8 %shard_map.88 = bf16[256,1024]{1,0:T(8,128)(2,1)} custom-call(s32[12]{0:T(128)S(1)} %concatenate.3.info, bf16[256,1024]{1,0:T(8,128)(2,1)S(1)} %get-tuple-element.92.refs_4_.refs_0_, bf16[256,1024]{1,0:T(8,128)(2,1)} %collective-permute-done.18.refs_1_, bf16[256,1024]{1,0:T(8,128)(2,1)} %collective-permute-done.19.refs_2_, ...), custom_call_target="tpu_custom_call" | custom-call | flops 42949672960 | bytes 8388608 | tf_op jit(solution)/shard_map/pallas_call | solution.py:384
  131.1 15.3 %all_to_all.10.got = bf16[16,8,1280]{2,1,0:T(8,128)(2,1)S(1)} all-to-all(bf16[16,8,1280]{2,1,0:T(8,128)(2,1)S(1)} %bitcast.9), channel_id=1, replica_groups=mesh['x'=4,'c'=2,'y'=4,'z'=4] {'y','z'}, dimensions={0} | all-to-all | bytes 655360 | tf_op jit(solution)/shard_map/all_to_all | solution.py:487
  (49 shorter events, 29.0 us)
Async XLA Ops:
  0.6 15.7 %collective-permute-start = (bf16[256,1024]{1,0:T(8,128)(2,1)}, bf16[256,1024]{1,0:T(8,128)(2,1)S(1)}, u32[]{:S(2)}, u32[]{:S(2)}) collective-permute-start(bf16[256,1024]{1,0:T(8,128)(2,1)} %bitcast.5.refs_0_), channel_id=1, source_target_pairs={{0,3},{1,0},{2,1},{3,2},{4,7},{5,4},{6,5},{7,6},{8,11},{9,8},{10,9... | collective-permute-start | bytes 1572872 | tf_op jit(solution)/shard_map/ppermute | solution.py:400
  4.8 14.8 %collective-permute-start.1 = (bf16[256,1024]{1,0:T(8,128)(2,1)}, bf16[256,1024]{1,0:T(8,128)(2,1)S(1)}, u32[]{:S(2)}, u32[]{:S(2)}) collective-permute-start(bf16[256,1024]{1,0:T(8,128)(2,1)} %bitcast.5.refs_0_), channel_id=1, source_target_pairs={{0,1},{1,2},{2,3},{3,0},{4,5},{5,6},{6,7},{7,4},{8,9},{9,10},{10,1... | collective-permute-start | bytes 1572872 | tf_op jit(solution)/shard_map/ppermute | solution.py:400
  8.9 12.3 %copy-start.4 = (bf16[1,256,1024]{2,1,0:T(8,128)(2,1)S(1)}, bf16[1,256,1024]{2,1,0:T(8,128)(2,1)}, u32[]{:S(2)}) copy-start(bf16[1,256,1024]{2,1,0:T(8,128)(2,1)} %param.6) | copy-start | bytes 1572868
  8.9 15.2 %copy-start.1 = (bf16[1024,4096]{1,0:T(8,128)(2,1)S(1)}, bf16[1024,4096]{1,0:T(8,128)(2,1)}, u32[]{:S(2)}) copy-start(bf16[1024,4096]{1,0:T(8,128)(2,1)} %refs_7_.1) | copy-start | bytes 25165828
  19.6 14.2 %collective-permute-start.2 = (bf16[256,1024]{1,0:T(8,128)(2,1)}, bf16[256,1024]{1,0:T(8,128)(2,1)S(1)}, u32[]{:S(2)}, u32[]{:S(2)}) collective-permute-start(bf16[256,1024]{1,0:T(8,128)(2,1)} %bitcast.5.refs_0_), channel_id=1, source_target_pairs={{0,2},{1,3},{2,0},{3,1},{4,6},{5,7},{6,4},{7,5},{8,10},{9,11},{10,... | collective-permute-start | bytes 1572872 | tf_op jit(solution)/shard_map/ppermute | solution.py:400
  19.6 19.0 %collective-permute-start.4 = (bf16[256,512]{1,0:T(8,128)(2,1)S(1)}, bf16[256,512]{1,0:T(8,128)(2,1)S(1)}, u32[]{:S(2)}, u32[]{:S(2)}) collective-permute-start(bf16[256,512]{1,0:T(8,128)(2,1)S(1)} %get-tuple-element.54.refs_3_), channel_id=1, source_target_pairs={{0,4},{4,8},{8,12},{12,0},{1,5},{5,9},{9,13},{13,1},{2,6},{6,10},{... | collective-permute-start | bytes 786440 | tf_op jit(solution)/shard_map/ppermute | solution.py:400
  26.6 18.9 %collective-permute-start.5 = (bf16[512,512]{1,0:T(8,128)(2,1)S(1)}, bf16[512,512]{1,0:T(8,128)(2,1)S(1)}, u32[]{:S(2)}, u32[]{:S(2)}) collective-permute-start(bf16[512,512]{1,0:T(8,128)(2,1)S(1)} %get-tuple-element.61.refs_4_), channel_id=1, source_target_pairs={{0,4},{4,8},{8,12},{12,0},{1,5},{5,9},{9,13},{13,1},{2,6},{6,10},{... | collective-permute-start | bytes 1572872 | tf_op jit(solution)/shard_map/ppermute | solution.py:400
  33.8 12.8 %collective-permute-start.7 = (bf16[256,512]{1,0:T(8,128)(2,1)S(1)}, bf16[256,512]{1,0:T(8,128)(2,1)S(1)}, u32[]{:S(2)}, u32[]{:S(2)}) collective-permute-start(bf16[256,512]{1,0:T(8,128)(2,1)S(1)} %get-tuple-element.70), channel_id=1, source_target_pairs={{0,1},{1,2},{2,3},{3,0},{4,5},{5,6},{6,7},{7,4},{8,9},{9,10},{10,1... | collective-permute-start | bytes 786440 | tf_op jit(solution)/shard_map/ppermute | solution.py:400
  33.8 12.8 %collective-permute-start.8 = (bf16[256,512]{1,0:T(8,128)(2,1)S(1)}, bf16[256,512]{1,0:T(8,128)(2,1)S(1)}, u32[]{:S(2)}, u32[]{:S(2)}) collective-permute-start(bf16[256,512]{1,0:T(8,128)(2,1)S(1)} %get-tuple-element.71), channel_id=1, source_target_pairs={{0,2},{1,3},{2,0},{3,1},{4,6},{5,7},{6,4},{7,5},{8,10},{9,11},{10,... | collective-permute-start | bytes 786440 | tf_op jit(solution)/shard_map/ppermute | solution.py:400
  35.9 11.3 %collective-permute-start.9 = (bf16[256,512]{1,0:T(8,128)(2,1)S(1)}, bf16[256,512]{1,0:T(8,128)(2,1)S(1)}, u32[]{:S(2)}, u32[]{:S(2)}) collective-permute-start(bf16[256,512]{1,0:T(8,128)(2,1)S(1)} %get-tuple-element.72), channel_id=1, source_target_pairs={{0,3},{1,0},{2,1},{3,2},{4,7},{5,4},{6,5},{7,6},{8,11},{9,8},{10,9... | collective-permute-start | bytes 786440 | tf_op jit(solution)/shard_map/ppermute | solution.py:400
  38.6 8.6 %collective-permute-start.6 = (bf16[256,512]{1,0:T(8,128)(2,1)S(1)}, bf16[256,512]{1,0:T(8,128)(2,1)S(1)}, u32[]{:S(2)}, u32[]{:S(2)}) collective-permute-start(bf16[256,512]{1,0:T(8,128)(2,1)S(1)} %get-tuple-element.62.refs_5_), channel_id=1, source_target_pairs={{0,4},{4,8},{8,12},{12,0},{1,5},{5,9},{9,13},{13,1},{2,6},{6,10},{... | collective-permute-start | bytes 786440 | tf_op jit(solution)/shard_map/ppermute | solution.py:400
  48.9 9.6 %collective-permute-start.10 = (f32[8,1024]{1,0:T(8,128)S(1)}, f32[8,1024]{1,0:T(8,128)S(1)}, u32[]{:S(2)}, u32[]{:S(2)}) collective-permute-start(f32[8,1024]{1,0:T(8,128)S(1)} %get-tuple-element.79.refs_3_), channel_id=1, source_target_pairs={{0,3},{1,0},{2,1},{3,2},{4,7},{5,4},{6,5},{7,6},{8,11},{9,8},{10,9... | collective-permute-start | bytes 98312 | tf_op jit(solution)/shard_map/ppermute | solution.py:400
  51.3 7.3 %collective-permute-start.11 = (f32[8,1024]{1,0:T(8,128)S(1)}, f32[8,1024]{1,0:T(8,128)S(1)}, u32[]{:S(2)}, u32[]{:S(2)}) collective-permute-start(f32[8,1024]{1,0:T(8,128)S(1)} %get-tuple-element.79.refs_3_), channel_id=1, source_target_pairs={{0,2},{1,3},{2,0},{3,1},{4,6},{5,7},{6,4},{7,5},{8,10},{9,11},{10,... | collective-permute-start | bytes 98312 | tf_op jit(solution)/shard_map/ppermute | solution.py:400
  51.3 7.3 %collective-permute-start.12 = (f32[8,1024]{1,0:T(8,128)S(1)}, f32[8,1024]{1,0:T(8,128)S(1)}, u32[]{:S(2)}, u32[]{:S(2)}) collective-permute-start(f32[8,1024]{1,0:T(8,128)S(1)} %get-tuple-element.79.refs_3_), channel_id=1, source_target_pairs={{0,1},{1,2},{2,3},{3,0},{4,5},{5,6},{6,7},{7,4},{8,9},{9,10},{10,1... | collective-permute-start | bytes 98312 | tf_op jit(solution)/shard_map/ppermute | solution.py:400
  52.4 25.7 %collective-permute-start.3 = (bf16[1024,256]{1,0:T(8,128)(2,1)S(1)}, bf16[1024,256]{1,0:T(8,128)(2,1)S(1)}, u32[]{:S(2)}, u32[]{:S(2)}) collective-permute-start(bf16[1024,256]{1,0:T(8,128)(2,1)S(1)} %get-tuple-element.63.refs_0_), channel_id=1, source_target_pairs={{0,12},{4,0},{8,4},{12,8},{1,13},{5,1},{9,5},{13,9},{2,14},{6,2},{... | collective-permute-start | bytes 1572872 | tf_op jit(solution)/shard_map/ppermute | solution.py:400
  60.2 19.0 %collective-permute-start.13 = (bf16[1024,256]{1,0:T(8,128)(2,1)S(1)}, bf16[1024,256]{1,0:T(8,128)(2,1)S(1)}, u32[]{:S(2)}, u32[]{:S(2)}) collective-permute-start(bf16[1024,256]{1,0:T(8,128)(2,1)S(1)} %get-tuple-element.84.refs_1_), channel_id=1, source_target_pairs={{0,12},{4,0},{8,4},{12,8},{1,13},{5,1},{9,5},{13,9},{2,14},{6,2},{... | collective-permute-start | bytes 1572872 | tf_op jit(solution)/shard_map/ppermute | solution.py:400
  64.8 19.3 %collective-permute-start.14 = (bf16[1024,256]{1,0:T(8,128)(2,1)S(1)}, bf16[1024,256]{1,0:T(8,128)(2,1)S(1)}, u32[]{:S(2)}, u32[]{:S(2)}) collective-permute-start(bf16[1024,256]{1,0:T(8,128)(2,1)S(1)} %get-tuple-element.96.refs_8_), channel_id=1, source_target_pairs={{0,3},{1,0},{2,1},{3,2},{4,7},{5,4},{6,5},{7,6},{8,11},{9,8},{10,9... | collective-permute-start | bytes 1572872 | tf_op jit(solution)/shard_map/ppermute | solution.py:400
  65.7 18.5 %collective-permute-start.15 = (bf16[1024,256]{1,0:T(8,128)(2,1)S(1)}, bf16[1024,256]{1,0:T(8,128)(2,1)S(1)}, u32[]{:S(2)}, u32[]{:S(2)}) collective-permute-start(bf16[1024,256]{1,0:T(8,128)(2,1)S(1)} %get-tuple-element.96.refs_8_), channel_id=1, source_target_pairs={{0,2},{1,3},{2,0},{3,1},{4,6},{5,7},{6,4},{7,5},{8,10},{9,11},{10,... | collective-permute-start | bytes 1572872 | tf_op jit(solution)/shard_map/ppermute | solution.py:400
  66.8 21.1 %collective-permute-start.16 = (bf16[1024,256]{1,0:T(8,128)(2,1)S(1)}, bf16[1024,256]{1,0:T(8,128)(2,1)S(1)}, u32[]{:S(2)}, u32[]{:S(2)}) collective-permute-start(bf16[1024,256]{1,0:T(8,128)(2,1)S(1)} %get-tuple-element.96.refs_8_), channel_id=1, source_target_pairs={{0,1},{1,2},{2,3},{3,0},{4,5},{5,6},{6,7},{7,4},{8,9},{9,10},{10,1... | collective-permute-start | bytes 1572872 | tf_op jit(solution)/shard_map/ppermute | solution.py:400
  91.5 4.5 %collective-permute-start.17 = (bf16[4,128,1280]{2,1,0:T(8,128)(2,1)S(1)}, bf16[4,128,1280]{2,1,0:T(8,128)(2,1)S(1)}, u32[]{:S(2)}, u32[]{:S(2)}) collective-permute-start(bf16[4,128,1280]{2,1,0:T(8,128)(2,1)S(1)} %get-tuple-element.100), channel_id=1, source_target_pairs={{0,16},{16,0},{1,17},{17,1},{2,18},{18,2},{3,19},{19,3},{4,20},{20... | collective-permute-start | bytes 3932168 | tf_op jit(solution)/shard_map/ppermute | solution.py:404
  91.6 26.9 %collective-permute-start.18 = (bf16[256,1024]{1,0:T(8,128)(2,1)S(1)}, bf16[256,1024]{1,0:T(8,128)(2,1)}, u32[]{:S(2)}, u32[]{:S(2)}) collective-permute-start(bf16[256,1024]{1,0:T(8,128)(2,1)S(1)} %get-tuple-element.93.refs_5_), channel_id=1, source_target_pairs={{0,1},{1,2},{2,3},{3,0},{4,5},{5,6},{6,7},{7,4},{8,9},{9,10},{10,1... | collective-permute-start | bytes 1572872 | tf_op jit(solution)/shard_map/ppermute | solution.py:400
  92.2 26.2 %collective-permute-start.19 = (bf16[256,1024]{1,0:T(8,128)(2,1)S(1)}, bf16[256,1024]{1,0:T(8,128)(2,1)}, u32[]{:S(2)}, u32[]{:S(2)}) collective-permute-start(bf16[256,1024]{1,0:T(8,128)(2,1)S(1)} %get-tuple-element.94.refs_6_), channel_id=1, source_target_pairs={{0,2},{1,3},{2,0},{3,1},{4,6},{5,7},{6,4},{7,5},{8,10},{9,11},{10,... | collective-permute-start | bytes 1572872 | tf_op jit(solution)/shard_map/ppermute | solution.py:400
  93.7 25.4 %collective-permute-start.20 = (bf16[256,1024]{1,0:T(8,128)(2,1)S(1)}, bf16[256,1024]{1,0:T(8,128)(2,1)}, u32[]{:S(2)}, u32[]{:S(2)}) collective-permute-start(bf16[256,1024]{1,0:T(8,128)(2,1)S(1)} %get-tuple-element.95.refs_7_), channel_id=1, source_target_pairs={{0,3},{1,0},{2,1},{3,2},{4,7},{5,4},{6,5},{7,6},{8,11},{9,8},{10,9... | collective-permute-start | bytes 1572872 | tf_op jit(solution)/shard_map/ppermute | solution.py:400
  97.9 32.5 %all-to-all-start = ((bf16[4,128,1280]{2,1,0:T(8,128)(2,1)}), bf16[4,128,1280]{2,1,0:T(8,128)(2,1)S(1)}, u32[]{:S(2)}, u32[]{:S(2)}) async-start(bf16[4,128,1280]{2,1,0:T(8,128)(2,1)} %shard_map.87), calls=%async_computation | async-start | bytes 2621440 | tf_op jit(solution)/shard_map/all_to_all | solution.py:483
  (4 other events, 9.4 us)

commit v6 on v5

--- a/solution.py
+++ b/solution.py
@@ -18,11 +18,11 @@
 SMEM = pl.BlockSpec(memory_space=pltpu.SMEM)
 
 
-def call(body, outs, n_in, flops, nbytes, scratch=()):
+def call(body, outs, n_in, flops, nbytes, scratch=(), scalars=1):
     return pl.pallas_call(
         body,
         out_shape=outs,
-        in_specs=[SMEM] + [VMEM] * n_in,
+        in_specs=[SMEM] * scalars + [VMEM] * n_in,
         out_specs=jax.tree.map(lambda _: VMEM, outs),
         scratch_shapes=scratch,
         compiler_params=pltpu.CompilerParams(vmem_limit_bytes=20 * 1024 * 1024),
@@ -243,16 +243,16 @@
             out[x, :, 2 * BLK :] = acc[at, :].astype(kind)
 
 
-def add_core_body(info, keep, got, out):
+def add_core_body(keep, got, out):
     out[...] = (keep[...] + got[...].astype(F32)).astype(BF16)
 
 
-def add_x_body(info, got, total):
+def add_x_body(got, total):
     part = got[0].astype(F32) + got[1].astype(F32) + got[2].astype(F32) + got[3].astype(F32)
     total[...] = part.astype(BF16)
 
 
-def last_sum_body(info, got, grad_w_in, grad_w_out):
+def last_sum_body(got, grad_w_in, grad_w_out):
     for z in range(4):
         part = got[z].astype(F32)
         for y in range(1, 4):
@@ -361,39 +361,71 @@
         gp[k][:, 3 * BLK :] = (dk * dsig[k][:, 3 * BLK :].astype(F32)).astype(BF16)
 
 
-def input_body(info, *refs):
-    gp, w, (cot, out, acc) = refs[0:4], refs[4:8], refs[8:11]
-    for d in range(NB):
+def input_near_body(info, *refs):
+    gp, w, (cot, out) = refs[0:3], refs[3:7], refs[7:9]
+    for d in range(3):
 
         @pl.when(pl.program_id(0) == d)
         def _(d=d):
-            part = cot[...].astype(F32) if d == 0 else acc[...]
+            part = cot[...].astype(F32) if d == 0 else out[...]
             for n in range(4):
                 part = part + nt(gp[d][:, n * BLK : (n + 1) * BLK], w[n][...])
-            if d < NB - 1:
-                acc[...] = part
-            else:
-                out[...] = part.astype(BF16)
-
-
-def input_grad(info, gp, w_in, cot):
-    def columns(part):
-        return pl.BlockSpec((D, BLK), lambda d, at: (0, part * 4 + lax.rem(at[9] + NB - d, NB)))
-
-    whole = pl.BlockSpec((BLK, D), lambda d, at: (0, 0))
+            out[...] = part
+
+
+def input_far_body(info, gp, w, near, out, acc):
+    part = nt(gp[...], w[...])
+    n = pl.program_id(0)
+
+    @pl.when(n == 0)
+    def _():
+        acc[...] = near[...] + part
+
+    @pl.when((n > 0) & (n < 3))
+    def _():
+        acc[...] += part
+
+    @pl.when(n == 3)
+    def _():
+        out[...] = (acc[...] + part).astype(BF16)
+
+
+def streamed(body, steps, in_specs, out, scratch, flops):
     return pl.pallas_call(
-        input_body,
+        body,
         grid_spec=pltpu.PrefetchScalarGridSpec(
             num_scalar_prefetch=1,
-            grid=(NB,),
-            in_specs=[whole] * 4 + [columns(p) for p in (0, 2, 1, 3)] + [whole],
-            out_specs=whole,
-            scratch_shapes=[pltpu.VMEM((BLK, D), F32)],
+            grid=(steps,),
+            in_specs=in_specs,
+            out_specs=pl.BlockSpec((BLK, D), lambda i, at: (0, 0)),
+            scratch_shapes=scratch,
         ),
-        out_shape=bf16((BLK, D)),
-        compiler_params=pltpu.CompilerParams(vmem_limit_bytes=20 * 1024 * 1024),
-        cost_estimate=pl.CostEstimate(flops=40 << 30, bytes_accessed=8 << 20, transcendentals=0),
-    )(info, *gp, w_in, w_in, w_in, w_in, cot)
+        out_shape=out,
+        compiler_params=pltpu.CompilerParams(vmem_limit_bytes=56 * 1024 * 1024),
+        cost_estimate=pl.CostEstimate(flops=flops, bytes_accessed=8 << 20, transcendentals=0),
+    )
+
+
+def input_near(info, gp, w_in, cot):
+    def columns(part):
+        return pl.BlockSpec((D, BLK), lambda i, at: (0, part * 4 + lax.rem(at[9] + NB - i - i // 2, NB)))
+
+    whole = pl.BlockSpec((BLK, D), lambda i, at: (0, 0))
+    specs = [whole] * 3 + [columns(p) for p in (0, 2, 1, 3)] + [whole]
+    return streamed(input_near_body, 3, specs, f32((BLK, D)), [], 40 << 30)(
+        info, gp[0], gp[1], gp[3], w_in, w_in, w_in, w_in, cot
+    )
+
+
+def input_far(info, gp, w_in, near):
+    specs = [
+        pl.BlockSpec((BLK, BLK), lambda n, at: (0, n)),
+        pl.BlockSpec((D, BLK), lambda n, at: (0, (n % 2 * 2 + n // 2) * 4 + lax.rem(at[9] + 2, NB))),
+        pl.BlockSpec((BLK, D), lambda n, at: (0, 0)),
+    ]
+    return streamed(input_far_body, 4, specs, bf16((BLK, D)), [pltpu.VMEM((BLK, D), F32)], 1 << 30)(
+        info, gp[2], w_in, near
+    )
 
 
 def along(x, axis, d):
@@ -478,14 +510,16 @@
     )(info, *evs, *gp, *gateds, cot_z, early)
     gp_rows = exchange(gp, "z")
     mine = call(
-        add_core_body, bf16((4, 128, 5 * BLK)), 2, 1 << 20, 1 << 20
-    )(info, keep, swap(send))
+        add_core_body, bf16((4, 128, 5 * BLK)), 2, 1 << 20, 1 << 20, scalars=0
+    )(keep, swap(send))
     sums = lax.all_to_all(mine, "x", 0, 0)
-    grad_events = input_grad(info, gp_rows, w_in, cot)
-    sums, grad_events = lax.optimization_barrier((sums, grad_events))
-    total = call(add_x_body, bf16((128, 5 * BLK)), 1, 1 << 20, 1 << 20)(info, sums)
+    near_rows = input_near(info, gp_rows, w_in, cot)
+    sums, near_rows = lax.optimization_barrier((sums, near_rows))
+    total = call(add_x_body, bf16((128, 5 * BLK)), 1, 1 << 20, 1 << 20, scalars=0)(sums)
+    _, near_rows = lax.optimization_barrier((total, near_rows))
+    grad_events = input_far(info, gp_rows, w_in, near_rows)
     got = lax.all_to_all(total.reshape(16, 8, 5 * BLK), ("y", "z"), 0, 0)
-    grad_w_in, grad_w_out = call(last_sum_body, (bf16((8, 4 * D)), bf16((8, D))), 1, 1 << 20, 1 << 20)(info, got)
+    grad_w_in, grad_w_out = call(last_sum_body, (bf16((8, 4 * D)), bf16((8, D))), 1, 1 << 20, 1 << 20, scalars=0)(got)
     return grad_events[None], grad_w_in, grad_w_out
 
 

time: 148 us -> 143 us (0.966); the launches traced: 148 us -> 141 us
  blocking collectives: 15.3 us -> 0 us
  waiting for transfers between devices: 38.5 us -> 44.8 us
  local copies, waits for them, and re-layouts: 10.1 us -> 6.5 us
  Pallas kernels: 44 us -> 47.5 us
  starting transfers between devices: 38.9 us -> 41.5 us
    all_to_all x1 -> x0, blocking collectives: 15.3 us -> none  [body(): got = lax.all_to_all(total.reshape(16, 8, 5 * BLK), ('y', 'z'), 0, 0)]
    all_to_all x0 -> x1, starting transfers between devices: none -> 4.93 us  [body(): got = lax.all_to_all(total.reshape(16, 8, 5 * BLK), ('y', 'z'), 0, 0)]
    pallas_call x4 -> x5, Pallas kernels: 10.6 us -> 15.5 us  [the longest x1 7.1 us: input_near(): streamed(input_near_body, 3, specs, f32((BLK, D)), [], 40 << 30)]
    ppermute x20, waiting for transfers between devices: 38.5 us -> 42.2 us  [along(): return lax.ppermute(x, axis, [(i, (i + d) % 4) for i in range(4)])]
    unnamed x12 -> x14, local copies, waits for them, and re-layouts: 9.4 us -> 5.76 us
    all_to_all x0 -> x1, waiting for transfers between devices: none -> 2.6 us  [body(): got = lax.all_to_all(total.reshape(16, 8, 5 * BLK), ('y', 'z'), 0, 0)]
    ppermute x20, starting transfers between devices: 34.4 us -> 31.9 us  [along(): return lax.ppermute(x, axis, [(i, (i + d) % 4) for i in range(4)])]
  transfers between devices with their start and end apart: 22 -> 23, of which waited for: 10 -> 9; matrix products, arithmetic and copies ran while one was open for 0% -> 1% of each run, Pallas kernels for 25% -> 29%
where the time goes in v6:
time: 143 us; the launch traced here: 141 us
  Pallas kernels  47.5 us (33%)
  waiting for transfers between devices  44.8 us (31%)
  starting transfers between devices  41.5 us (29%)
  local copies, waits for them, and re-layouts  6.5 us (5%)
    ppermute x20, waiting for transfers between devices, along(): return lax.ppermute(x, axis, [(i, (i + d) % 4) for i in range(4)])  42.2 us
    ppermute x20, starting transfers between devices, along(): return lax.ppermute(x, axis, [(i, (i + d) % 4) for i in range(4)])  31.9 us
    pallas_call x1, Pallas kernels, input_near(): streamed(input_near_body, 3, specs, f32((BLK, D)), [], 40 << 30)  7.1 us
    pallas_call x1, Pallas kernels, body(): call(backward_local_body, (bf16((GRP, BLK)), f32((GRP, 2 * BLK))), 8, 1 <...  6.72 us
    pallas_call x3, Pallas kernels, body(): call(project_body, (bf16((n * BLK, 2 * BLK)), bf16((n * BLK, BLK)), bf16(...  6.22 us
    unnamed x14, local copies, waits for them, and re-layouts  5.76 us
    pallas_call x1, Pallas kernels, input_far(): streamed(input_far_body, 4, specs, bf16((BLK, D)), [pltpu.VMEM((BLK, D),...  5.43 us
    all_to_all x1, starting transfers between devices, body(): got = lax.all_to_all(total.reshape(16, 8, 5 * BLK), ('y', 'z'), 0, 0)  4.93 us
  transfers between devices with their start and end apart: 23, of which 9 were waited for; matrix products, arithmetic and copies ran while one was open for 1% of the time, Pallas kernels for 29%

profile of v6, /device:TPU:0, one launch (start us, length us, event | category | flops | bytes accessed | tf_op | source)
XLA Modules:
  0.0 141.0 jit_solution(14424651584031376907)
XLA Ops:
  0.6 4.2 %collective-permute-start = (bf16[256,1024]{1,0:T(8,128)(2,1)}, bf16[256,1024]{1,0:T(8,128)(2,1)S(1)}, u32[]{:S(2)}, u32[]{:S(2)}) collective-permute-start(bf16[256,1024]{1,0:T(8,128)(2,1)} %bitcast.5.refs_0_), channel_id=1, source_target_pairs={{0,3},{1,0},{2,1},{3,2},{4,7},{5,4},{6,5},{7,6},{8,11},{9,8},{10,9... | collective-permute-start | bytes 1572872 | tf_op jit(solution)/shard_map/ppermute | solution.py:432
  5.6 3.4 %copy-done = bf16[1024,4096]{1,0:T(8,128)(2,1)S(1)} copy-done((bf16[1024,4096]{1,0:T(8,128)(2,1)S(1)}, bf16[1024,4096]{1,0:T(8,128)(2,1)}, u32[]{:S(2)}) %copy-start) | copy-done | bytes 8388632
  8.9 2.2 %shard_map.76 = (bf16[256,512]{1,0:T(8,128)(2,1)S(1)}, bf16[256,256]{1,0:T(8,128)(2,1)S(1)}, bf16[256,256]{1,0:T(8,128)(2,1)S(1)}, bf16[256,1024]{1,0:T(8,128)(2,1)S(1)}) custom-call(s32[12]{0:T(128)S(1)} %concatenate.3.info, bf16[256,1024]{1,0:T(8,128)(2,1)} %bitcast.5.refs_0_, bf16[1024,4096]{1,0:T(8,128)(2,1)S(1)} %copy-done), custom_call_target="tpu_custom_call" | custom-call | flops 536870912 | bytes 4194304 | tf_op jit(solution)/shard_map/pallas_call | solution.py:469
  11.2 5.1 %collective-permute-done.refs_0_.refs_1_ = bf16[256,1024]{1,0:T(8,128)(2,1)S(1)} collective-permute-done((bf16[256,1024]{1,0:T(8,128)(2,1)}, bf16[256,1024]{1,0:T(8,128)(2,1)S(1)}, u32[]{:S(2)}, u32[]{:S(2)}) %collective-permute-start) | collective-permute-done | bytes 524320 | tf_op jit(solution)/shard_map/ppermute | solution.py:432
  16.3 3.3 %collective-permute-done.1.refs_1_.refs_3_ = bf16[256,1024]{1,0:T(8,128)(2,1)S(1)} collective-permute-done((bf16[256,1024]{1,0:T(8,128)(2,1)}, bf16[256,1024]{1,0:T(8,128)(2,1)S(1)}, u32[]{:S(2)}, u32[]{:S(2)}) %collective-permute-start.1) | collective-permute-done | bytes 524320 | tf_op jit(solution)/shard_map/ppermute | solution.py:432
  24.1 2.4 %shard_map.77 = (bf16[512,512]{1,0:T(8,128)(2,1)S(1)}, bf16[512,256]{1,0:T(8,128)(2,1)S(1)}, bf16[512,256]{1,0:T(8,128)(2,1)S(1)}, bf16[256,1024]{1,0:T(8,128)(2,1)S(1)}, bf16[256,1024]{1,0:T(8,128)(2,1)S(1)}) custom-call(s32[12]{0:T(128)S(1)} %concatenate.3.info, bf16[256,1024]{1,0:T(8,128)(2,1)S(1)} %collective-permute-done.refs_0_.refs_1_, ...), custom_call_target="tpu_custom_call" | custom-call | flops 1073741824 | bytes 4194304 | tf_op jit(solution)/shard_map/pallas_call | solution.py:469
  28.2 5.6 %collective-permute-done.2.refs_0_.refs_2_ = bf16[256,1024]{1,0:T(8,128)(2,1)S(1)} collective-permute-done((bf16[256,1024]{1,0:T(8,128)(2,1)}, bf16[256,1024]{1,0:T(8,128)(2,1)S(1)}, u32[]{:S(2)}, u32[]{:S(2)}) %collective-permute-start.2) | collective-permute-done | bytes 524320 | tf_op jit(solution)/shard_map/ppermute | solution.py:432
  40.3 4.6 %shard_map.79 = (bf16[1024,256]{1,0:T(8,128)(2,1)S(1)}, bf16[1024,512]{1,0:T(8,128)(2,1)S(1)}, f32[1024,256]{1,0:T(8,128)S(1)}) custom-call(s32[12]{0:T(128)S(1)} %concatenate.3.info, bf16[256,256]{1,0:T(8,128)(2,1)S(1)} %get-tuple-element.55.refs_0_, bf16[512,256]{1,0:T(8,128)(2,1)S(1)} %get-tuple-element.59.refs_1_, ...), custom_call_target="tpu_custom_call" | custom-call | flops 5368709120 | bytes 4194304 | tf_op jit(solution)/shard_map/pallas_call | solution.py:483
  48.9 2.4 %collective-permute-start.10 = (f32[8,1024]{1,0:T(8,128)S(1)}, f32[8,1024]{1,0:T(8,128)S(1)}, u32[]{:S(2)}, u32[]{:S(2)}) collective-permute-start(f32[8,1024]{1,0:T(8,128)S(1)} %get-tuple-element.80.refs_3_), channel_id=1, source_target_pairs={{0,3},{1,0},{2,1},{3,2},{4,7},{5,4},{6,5},{7,6},{8,11},{9,8},{10,9... | collective-permute-start | bytes 98312 | tf_op jit(solution)/shard_map/ppermute | solution.py:432
  52.4 4.5 %collective-permute-start.3 = (bf16[1024,256]{1,0:T(8,128)(2,1)S(1)}, bf16[1024,256]{1,0:T(8,128)(2,1)S(1)}, u32[]{:S(2)}, u32[]{:S(2)}) collective-permute-start(bf16[1024,256]{1,0:T(8,128)(2,1)S(1)} %get-tuple-element.64.refs_0_), channel_id=1, source_target_pairs={{0,12},{4,0},{8,4},{12,8},{1,13},{5,1},{9,5},{13,9},{2,14},{6,2},{... | collective-permute-start | bytes 1572872 | tf_op jit(solution)/shard_map/ppermute | solution.py:432
  58.6 4.6 %collective-permute-start.13 = (bf16[1024,256]{1,0:T(8,128)(2,1)S(1)}, bf16[1024,256]{1,0:T(8,128)(2,1)S(1)}, u32[]{:S(2)}, u32[]{:S(2)}) collective-permute-start(bf16[1024,256]{1,0:T(8,128)(2,1)S(1)} %get-tuple-element.85.refs_1_), channel_id=1, source_target_pairs={{0,12},{4,0},{8,4},{12,8},{1,13},{5,1},{9,5},{13,9},{2,14},{6,2},{... | collective-permute-start | bytes 1572872 | tf_op jit(solution)/shard_map/ppermute | solution.py:432
  66.6 6.7 %shard_map.83 = (bf16[1024,256]{1,0:T(8,128)(2,1)S(1)}, f32[1024,512]{1,0:T(8,128)S(1)}) custom-call(s32[12]{0:T(128)S(1)} %concatenate.3.info, bf16[1024,256]{1,0:T(8,128)(2,1)S(1)} %get-tuple-element.64.refs_0_, bf16[1024,256]{1,0:T(8,128)(2,1)S(1)} %get-tuple-element.85.refs_1_, bf16[1024,512]{1,0:T(8,128)(2,1)S(1)} %get-tuple-element.87.refs_2_, ...), custom_call_target="tpu_custom_call" | custom-call | flops 1048576 | bytes 1048576 | tf_op jit(solution)/shard_map/pallas_call | solution.py:497
  73.3 2.4 %shard_map.84.refs_13_ = f32[1024,512]{1,0:T(8,128)S(1)} custom-call(s32[12]{0:T(128)S(1)} %concatenate.3.info, bf16[256,1024]{1,0:T(8,128)(2,1)} %bitcast.5.refs_0_, bf16[256,1024]{1,0:T(8,128)(2,1)S(1)} %collective-permute-done.refs_0_.refs_1_, bf16[256,1024]{1,0:T(8,128)(2,1)S(1)} %collective-permute-done.2.refs_0_.refs_2_, ...), custom_call_target="tpu_custom_call" | custom-call | flops 1048576 | bytes 1048576 | tf_op jit(solution)/shard_map/pallas_call | solution.py:501
  75.7 2.6 %collective-permute-done.13.refs_1_ = bf16[1024,256]{1,0:T(8,128)(2,1)S(1)} collective-permute-done((bf16[1024,256]{1,0:T(8,128)(2,1)S(1)}, bf16[1024,256]{1,0:T(8,128)(2,1)S(1)}, u32[]{:S(2)}, u32[]{:S(2)}) %collective-permute-start.13) | collective-permute-done | bytes 524320 | tf_op jit(solution)/shard_map/ppermute | solution.py:432
  78.2 3.7 %shard_map.85 = (bf16[256,1024]{1,0:T(8,128)(2,1)S(1)}, bf16[256,1024]{1,0:T(8,128)(2,1)S(1)}, bf16[256,1024]{1,0:T(8,128)(2,1)S(1)}, bf16[256,1024]{1,0:T(8,128)(2,1)S(1)}) custom-call(s32[12]{0:T(128)S(1)} %concatenate.3.info, bf16[1024,256]{1,0:T(8,128)(2,1)S(1)} %collective-permute-done.3.refs_0_, bf16[1024,256]{1,0:T(8,128)(2,1)S(1)} %collective-permute-done.13.refs_1_, ...), custom_call_target="tpu_custom_call" | custom-call | flops 5368709120 | bytes 4194304 | tf_op jit(solution)/shard_map/pallas_call | solution.py:503
  82.0 5.9 %collective-permute-done.17.refs_11_ = bf16[1024,256]{1,0:T(8,128)(2,1)S(1)} collective-permute-done((bf16[1024,256]{1,0:T(8,128)(2,1)S(1)}, bf16[1024,256]{1,0:T(8,128)(2,1)S(1)}, u32[]{:S(2)}, u32[]{:S(2)}) %collective-permute-start.17) | collective-permute-done | bytes 524320 | tf_op jit(solution)/shard_map/ppermute | solution.py:432
  87.9 3.7 %shard_map.86 = (bf16[4,128,1280]{2,1,0:T(8,128)(2,1)S(1)}, f32[4,128,1280]{2,1,0:T(8,128)S(1)}) custom-call(s32[12]{0:T(128)S(1)} %concatenate.3.info, bf16[256,1024]{1,0:T(8,128)(2,1)} %bitcast.5.refs_0_, bf16[256,1024]{1,0:T(8,128)(2,1)S(1)} %collective-permute-done.refs_0_.refs_1_, bf16[256,1024]{1,0:T(8,128)(2,1)S(1)} %collective-permute-done.2.refs_0_.refs_2_, ...), custom_call_target="tpu_custom_call" | custom-call | flops 1048576 | bytes 1048576 | tf_op jit(solution)/shard_map/pallas_call | solution.py:506
  91.9 3.1 %collective-permute-start.20 = (bf16[256,1024]{1,0:T(8,128)(2,1)S(1)}, bf16[256,1024]{1,0:T(8,128)(2,1)}, u32[]{:S(2)}, u32[]{:S(2)}) collective-permute-start(bf16[256,1024]{1,0:T(8,128)(2,1)S(1)} %get-tuple-element.96.refs_7_), channel_id=1, source_target_pairs={{0,3},{1,0},{2,1},{3,2},{4,7},{5,4},{6,5},{7,6},{8,11},{9,8},{10,9... | collective-permute-start | bytes 1572872 | tf_op jit(solution)/shard_map/ppermute | solution.py:432
  96.8 4.5 %all-to-all-start = ((bf16[4,128,1280]{2,1,0:T(8,128)(2,1)}), bf16[4,128,1280]{2,1,0:T(8,128)(2,1)S(1)}, u32[]{:S(2)}, u32[]{:S(2)}) async-start(bf16[4,128,1280]{2,1,0:T(8,128)(2,1)} %shard_map.87), calls=%async_computation | async-start | bytes 2621440 | tf_op jit(solution)/shard_map/all_to_all | solution.py:515
  101.2 17.3 %collective-permute-done.19.refs_1_ = bf16[256,1024]{1,0:T(8,128)(2,1)} collective-permute-done((bf16[256,1024]{1,0:T(8,128)(2,1)S(1)}, bf16[256,1024]{1,0:T(8,128)(2,1)}, u32[]{:S(2)}, u32[]{:S(2)}) %collective-permute-start.19) | collective-permute-done | bytes 524320 | tf_op jit(solution)/shard_map/ppermute | solution.py:432
  118.6 7.1 %shard_map.88.near = f32[256,1024]{1,0:T(8,128)} custom-call(s32[12]{0:T(128)} %copy-done.5, bf16[256,1024]{1,0:T(8,128)(2,1)} %copy-done.3, bf16[256,1024]{1,0:T(8,128)(2,1)} %collective-permute-done.19.refs_1_, bf16[256,1024]{1,0:T(8,128)(2,1)} %collective-permute-done.20.refs_2_, bf16[1024,4096]{1,0:T(8,128)(2,1)} %w.3, bf16[1024,4096]{1,0:T(8,128)(2,1)} %w.3, ...), custom_call_target="tpu_custom_call" | custom-call | flops 42949672960 | bytes 8388608 | tf_op jit(solution)/shard_map/pallas_call | solution.py:415
  126.6 4.9 %all-to-all-start.1 = ((bf16[16,8,1280]{2,1,0:T(8,128)(2,1)}), bf16[16,8,1280]{2,1,0:T(8,128)(2,1)S(1)}, u32[]{:S(2)}, u32[]{:S(2)}) async-start(bf16[16,8,1280]{2,1,0:T(8,128)(2,1)} %bitcast.8), calls=%async_computation.1 | async-start | bytes 655360 | tf_op jit(solution)/shard_map/all_to_all | solution.py:521
  132.3 5.4 %shard_map.90 = bf16[256,1024]{1,0:T(8,128)(2,1)} custom-call(s32[12]{0:T(128)} %copy-done.5, bf16[256,1024]{1,0:T(8,128)(2,1)} %copy-done.6, bf16[1024,4096]{1,0:T(8,128)(2,1)} %w.3, f32[256,1024]{1,0:T(8,128)} %shard_map.88.near), custom_call_target="tpu_custom_call" | custom-call | flops 1073741824 | bytes 8388608 | tf_op jit(solution)/shard_map/pallas_call | solution.py:426
  137.8 2.6 %all-to-all-done.1.got = bf16[16,8,1280]{2,1,0:T(8,128)(2,1)S(1)} async-done(((bf16[16,8,1280]{2,1,0:T(8,128)(2,1)}), bf16[16,8,1280]{2,1,0:T(8,128)(2,1)S(1)}, u32[]{:S(2)}, u32[]{:S(2)}) %all-to-all-start.1) | async-done | bytes 327712 | tf_op jit(solution)/shard_map/all_to_all | solution.py:521
  (53 shorter events, 27.9 us)
Async XLA Ops:
  0.6 15.7 %collective-permute-start = (bf16[256,1024]{1,0:T(8,128)(2,1)}, bf16[256,1024]{1,0:T(8,128)(2,1)S(1)}, u32[]{:S(2)}, u32[]{:S(2)}) collective-permute-start(bf16[256,1024]{1,0:T(8,128)(2,1)} %bitcast.5.refs_0_), channel_id=1, source_target_pairs={{0,3},{1,0},{2,1},{3,2},{4,7},{5,4},{6,5},{7,6},{8,11},{9,8},{10,9... | collective-permute-start | bytes 1572872 | tf_op jit(solution)/shard_map/ppermute | solution.py:432
  4.8 14.8 %collective-permute-start.1 = (bf16[256,1024]{1,0:T(8,128)(2,1)}, bf16[256,1024]{1,0:T(8,128)(2,1)S(1)}, u32[]{:S(2)}, u32[]{:S(2)}) collective-permute-start(bf16[256,1024]{1,0:T(8,128)(2,1)} %bitcast.5.refs_0_), channel_id=1, source_target_pairs={{0,1},{1,2},{2,3},{3,0},{4,5},{5,6},{6,7},{7,4},{8,9},{9,10},{10,1... | collective-permute-start | bytes 1572872 | tf_op jit(solution)/shard_map/ppermute | solution.py:432
  8.9 79.0 %copy-start.5 = (s32[12]{0:T(128)}, s32[12]{0:T(128)S(1)}, u32[]{:S(2)}) copy-start(s32[12]{0:T(128)S(1)} %concatenate.3.info) | copy-start | bytes 148
  19.6 14.2 %collective-permute-start.2 = (bf16[256,1024]{1,0:T(8,128)(2,1)}, bf16[256,1024]{1,0:T(8,128)(2,1)S(1)}, u32[]{:S(2)}, u32[]{:S(2)}) collective-permute-start(bf16[256,1024]{1,0:T(8,128)(2,1)} %bitcast.5.refs_0_), channel_id=1, source_target_pairs={{0,2},{1,3},{2,0},{3,1},{4,6},{5,7},{6,4},{7,5},{8,10},{9,11},{10,... | collective-permute-start | bytes 1572872 | tf_op jit(solution)/shard_map/ppermute | solution.py:432
  19.6 19.0 %collective-permute-start.4 = (bf16[256,512]{1,0:T(8,128)(2,1)S(1)}, bf16[256,512]{1,0:T(8,128)(2,1)S(1)}, u32[]{:S(2)}, u32[]{:S(2)}) collective-permute-start(bf16[256,512]{1,0:T(8,128)(2,1)S(1)} %get-tuple-element.56.refs_3_), channel_id=1, source_target_pairs={{0,4},{4,8},{8,12},{12,0},{1,5},{5,9},{9,13},{13,1},{2,6},{6,10},{... | collective-permute-start | bytes 786440 | tf_op jit(solution)/shard_map/ppermute | solution.py:432
  26.6 18.3 %collective-permute-start.5 = (bf16[512,512]{1,0:T(8,128)(2,1)S(1)}, bf16[512,512]{1,0:T(8,128)(2,1)S(1)}, u32[]{:S(2)}, u32[]{:S(2)}) collective-permute-start(bf16[512,512]{1,0:T(8,128)(2,1)S(1)} %get-tuple-element.62.refs_4_), channel_id=1, source_target_pairs={{0,4},{4,8},{8,12},{12,0},{1,5},{5,9},{9,13},{13,1},{2,6},{6,10},{... | collective-permute-start | bytes 1572872 | tf_op jit(solution)/shard_map/ppermute | solution.py:432
  33.8 12.8 %collective-permute-start.7 = (bf16[256,512]{1,0:T(8,128)(2,1)S(1)}, bf16[256,512]{1,0:T(8,128)(2,1)S(1)}, u32[]{:S(2)}, u32[]{:S(2)}) collective-permute-start(bf16[256,512]{1,0:T(8,128)(2,1)S(1)} %get-tuple-element.71), channel_id=1, source_target_pairs={{0,1},{1,2},{2,3},{3,0},{4,5},{5,6},{6,7},{7,4},{8,9},{9,10},{10,1... | collective-permute-start | bytes 786440 | tf_op jit(solution)/shard_map/ppermute | solution.py:432
  33.8 12.8 %collective-permute-start.8 = (bf16[256,512]{1,0:T(8,128)(2,1)S(1)}, bf16[256,512]{1,0:T(8,128)(2,1)S(1)}, u32[]{:S(2)}, u32[]{:S(2)}) collective-permute-start(bf16[256,512]{1,0:T(8,128)(2,1)S(1)} %get-tuple-element.72), channel_id=1, source_target_pairs={{0,2},{1,3},{2,0},{3,1},{4,6},{5,7},{6,4},{7,5},{8,10},{9,11},{10,... | collective-permute-start | bytes 786440 | tf_op jit(solution)/shard_map/ppermute | solution.py:432
  35.9 11.3 %collective-permute-start.9 = (bf16[256,512]{1,0:T(8,128)(2,1)S(1)}, bf16[256,512]{1,0:T(8,128)(2,1)S(1)}, u32[]{:S(2)}, u32[]{:S(2)}) collective-permute-start(bf16[256,512]{1,0:T(8,128)(2,1)S(1)} %get-tuple-element.73), channel_id=1, source_target_pairs={{0,3},{1,0},{2,1},{3,2},{4,7},{5,4},{6,5},{7,6},{8,11},{9,8},{10,9... | collective-permute-start | bytes 786440 | tf_op jit(solution)/shard_map/ppermute | solution.py:432
  38.6 8.6 %collective-permute-start.6 = (bf16[256,512]{1,0:T(8,128)(2,1)S(1)}, bf16[256,512]{1,0:T(8,128)(2,1)S(1)}, u32[]{:S(2)}, u32[]{:S(2)}) collective-permute-start(bf16[256,512]{1,0:T(8,128)(2,1)S(1)} %get-tuple-element.63.refs_5_), channel_id=1, source_target_pairs={{0,4},{4,8},{8,12},{12,0},{1,5},{5,9},{9,13},{13,1},{2,6},{6,10},{... | collective-permute-start | bytes 786440 | tf_op jit(solution)/shard_map/ppermute | solution.py:432
  48.9 8.0 %collective-permute-start.10 = (f32[8,1024]{1,0:T(8,128)S(1)}, f32[8,1024]{1,0:T(8,128)S(1)}, u32[]{:S(2)}, u32[]{:S(2)}) collective-permute-start(f32[8,1024]{1,0:T(8,128)S(1)} %get-tuple-element.80.refs_3_), channel_id=1, source_target_pairs={{0,3},{1,0},{2,1},{3,2},{4,7},{5,4},{6,5},{7,6},{8,11},{9,8},{10,9... | collective-permute-start | bytes 98312 | tf_op jit(solution)/shard_map/ppermute | solution.py:432
  51.3 5.6 %collective-permute-start.11 = (f32[8,1024]{1,0:T(8,128)S(1)}, f32[8,1024]{1,0:T(8,128)S(1)}, u32[]{:S(2)}, u32[]{:S(2)}) collective-permute-start(f32[8,1024]{1,0:T(8,128)S(1)} %get-tuple-element.80.refs_3_), channel_id=1, source_target_pairs={{0,2},{1,3},{2,0},{3,1},{4,6},{5,7},{6,4},{7,5},{8,10},{9,11},{10,... | collective-permute-start | bytes 98312 | tf_op jit(solution)/shard_map/ppermute | solution.py:432
  51.3 5.6 %collective-permute-start.12 = (f32[8,1024]{1,0:T(8,128)S(1)}, f32[8,1024]{1,0:T(8,128)S(1)}, u32[]{:S(2)}, u32[]{:S(2)}) collective-permute-start(f32[8,1024]{1,0:T(8,128)S(1)} %get-tuple-element.80.refs_3_), channel_id=1, source_target_pairs={{0,1},{1,2},{2,3},{3,0},{4,5},{5,6},{6,7},{7,4},{8,9},{9,10},{10,1... | collective-permute-start | bytes 98312 | tf_op jit(solution)/shard_map/ppermute | solution.py:432
  52.4 23.3 %collective-permute-start.3 = (bf16[1024,256]{1,0:T(8,128)(2,1)S(1)}, bf16[1024,256]{1,0:T(8,128)(2,1)S(1)}, u32[]{:S(2)}, u32[]{:S(2)}) collective-permute-start(bf16[1024,256]{1,0:T(8,128)(2,1)S(1)} %get-tuple-element.64.refs_0_), channel_id=1, source_target_pairs={{0,12},{4,0},{8,4},{12,8},{1,13},{5,1},{9,5},{13,9},{2,14},{6,2},{... | collective-permute-start | bytes 1572872 | tf_op jit(solution)/shard_map/ppermute | solution.py:432
  58.6 19.7 %collective-permute-start.13 = (bf16[1024,256]{1,0:T(8,128)(2,1)S(1)}, bf16[1024,256]{1,0:T(8,128)(2,1)S(1)}, u32[]{:S(2)}, u32[]{:S(2)}) collective-permute-start(bf16[1024,256]{1,0:T(8,128)(2,1)S(1)} %get-tuple-element.85.refs_1_), channel_id=1, source_target_pairs={{0,12},{4,0},{8,4},{12,8},{1,13},{5,1},{9,5},{13,9},{2,14},{6,2},{... | collective-permute-start | bytes 1572872 | tf_op jit(solution)/shard_map/ppermute | solution.py:432
  63.2 18.8 %collective-permute-start.15 = (bf16[1024,256]{1,0:T(8,128)(2,1)S(1)}, bf16[1024,256]{1,0:T(8,128)(2,1)S(1)}, u32[]{:S(2)}, u32[]{:S(2)}) collective-permute-start(bf16[1024,256]{1,0:T(8,128)(2,1)S(1)} %get-tuple-element.97.refs_8_), channel_id=1, source_target_pairs={{0,3},{1,0},{2,1},{3,2},{4,7},{5,4},{6,5},{7,6},{8,11},{9,8},{10,9... | collective-permute-start | bytes 1572872 | tf_op jit(solution)/shard_map/ppermute | solution.py:432
  64.0 18.0 %collective-permute-start.16 = (bf16[1024,256]{1,0:T(8,128)(2,1)S(1)}, bf16[1024,256]{1,0:T(8,128)(2,1)S(1)}, u32[]{:S(2)}, u32[]{:S(2)}) collective-permute-start(bf16[1024,256]{1,0:T(8,128)(2,1)S(1)} %get-tuple-element.97.refs_8_), channel_id=1, source_target_pairs={{0,2},{1,3},{2,0},{3,1},{4,6},{5,7},{6,4},{7,5},{8,10},{9,11},{10,... | collective-permute-start | bytes 1572872 | tf_op jit(solution)/shard_map/ppermute | solution.py:432
  65.7 22.3 %collective-permute-start.17 = (bf16[1024,256]{1,0:T(8,128)(2,1)S(1)}, bf16[1024,256]{1,0:T(8,128)(2,1)S(1)}, u32[]{:S(2)}, u32[]{:S(2)}) collective-permute-start(bf16[1024,256]{1,0:T(8,128)(2,1)S(1)} %get-tuple-element.97.refs_8_), channel_id=1, source_target_pairs={{0,1},{1,2},{2,3},{3,0},{4,5},{5,6},{6,7},{7,4},{8,9},{9,10},{10,1... | collective-permute-start | bytes 1572872 | tf_op jit(solution)/shard_map/ppermute | solution.py:432
  91.6 3.8 %collective-permute-start.18 = (bf16[4,128,1280]{2,1,0:T(8,128)(2,1)S(1)}, bf16[4,128,1280]{2,1,0:T(8,128)(2,1)S(1)}, u32[]{:S(2)}, u32[]{:S(2)}) collective-permute-start(bf16[4,128,1280]{2,1,0:T(8,128)(2,1)S(1)} %get-tuple-element.101), channel_id=1, source_target_pairs={{0,16},{16,0},{1,17},{17,1},{2,18},{18,2},{3,19},{19,3},{4,20},{20... | collective-permute-start | bytes 3932168 | tf_op jit(solution)/shard_map/ppermute | solution.py:436
  91.7 26.9 %collective-permute-start.19 = (bf16[256,1024]{1,0:T(8,128)(2,1)S(1)}, bf16[256,1024]{1,0:T(8,128)(2,1)}, u32[]{:S(2)}, u32[]{:S(2)}) collective-permute-start(bf16[256,1024]{1,0:T(8,128)(2,1)S(1)} %get-tuple-element.95.refs_5_), channel_id=1, source_target_pairs={{0,1},{1,2},{2,3},{3,0},{4,5},{5,6},{6,7},{7,4},{8,9},{9,10},{10,1... | collective-permute-start | bytes 1572872 | tf_op jit(solution)/shard_map/ppermute | solution.py:432
  91.9 26.7 %collective-permute-start.20 = (bf16[256,1024]{1,0:T(8,128)(2,1)S(1)}, bf16[256,1024]{1,0:T(8,128)(2,1)}, u32[]{:S(2)}, u32[]{:S(2)}) collective-permute-start(bf16[256,1024]{1,0:T(8,128)(2,1)S(1)} %get-tuple-element.96.refs_7_), channel_id=1, source_target_pairs={{0,3},{1,0},{2,1},{3,2},{4,7},{5,4},{6,5},{7,6},{8,11},{9,8},{10,9... | collective-permute-start | bytes 1572872 | tf_op jit(solution)/shard_map/ppermute | solution.py:432
  95.0 36.5 %collective-permute-start.14 = (bf16[256,1024]{1,0:T(8,128)(2,1)S(1)}, bf16[256,1024]{1,0:T(8,128)(2,1)S(1)}, u32[]{:S(2)}, u32[]{:S(2)}) collective-permute-start(bf16[256,1024]{1,0:T(8,128)(2,1)S(1)} %get-tuple-element.93.refs_6_), channel_id=1, source_target_pairs={{0,2},{1,3},{2,0},{3,1},{4,6},{5,7},{6,4},{7,5},{8,10},{9,11},{10,... | collective-permute-start | bytes 1572872 | tf_op jit(solution)/shard_map/ppermute | solution.py:432
  96.8 28.9 %all-to-all-start = ((bf16[4,128,1280]{2,1,0:T(8,128)(2,1)}), bf16[4,128,1280]{2,1,0:T(8,128)(2,1)S(1)}, u32[]{:S(2)}, u32[]{:S(2)}) async-start(bf16[4,128,1280]{2,1,0:T(8,128)(2,1)} %shard_map.87), calls=%async_computation | async-start | bytes 2621440 | tf_op jit(solution)/shard_map/all_to_all | solution.py:515
  126.6 13.8 %all-to-all-start.1 = ((bf16[16,8,1280]{2,1,0:T(8,128)(2,1)}), bf16[16,8,1280]{2,1,0:T(8,128)(2,1)S(1)}, u32[]{:S(2)}, u32[]{:S(2)}) async-start(bf16[16,8,1280]{2,1,0:T(8,128)(2,1)} %bitcast.8), calls=%async_computation.1 | async-start | bytes 655360 | tf_op jit(solution)/shard_map/all_to_all | solution.py:521
  (6 other events, 42.8 us)

commit v7 on v4

--- a/solution.py
+++ b/solution.py
@@ -18,11 +18,11 @@
 SMEM = pl.BlockSpec(memory_space=pltpu.SMEM)
 
 
-def call(body, outs, n_in, flops, nbytes, scratch=()):
+def call(body, outs, n_in, flops, nbytes, scratch=(), scalars=1):
     return pl.pallas_call(
         body,
         out_shape=outs,
-        in_specs=[SMEM] + [VMEM] * n_in,
+        in_specs=[SMEM] * scalars + [VMEM] * n_in,
         out_specs=jax.tree.map(lambda _: VMEM, outs),
         scratch_shapes=scratch,
         compiler_params=pltpu.CompilerParams(vmem_limit_bytes=20 * 1024 * 1024),
@@ -243,19 +243,16 @@
             out[x, :, 2 * BLK :] = acc[at, :].astype(kind)
 
 
-def add_core_body(info, keep, got, to_1, to_2, to_3, own):
-    own[...] = keep[info[11]] + got[info[11]].astype(F32)
-    for d, out in ((1, to_1), (2, to_2), (3, to_3)):
-        at = lax.rem(info[11] + d, 4)
-        out[...] = (keep[at] + got[at].astype(F32)).astype(BF16)
-
-
-def add_x_body(info, own, got_1, got_2, got_3, total):
-    part = own[...] + got_1[...].astype(F32) + got_2[...].astype(F32) + got_3[...].astype(F32)
+def add_core_body(keep, got, out):
+    out[...] = (keep[...] + got[...].astype(F32)).astype(BF16)
+
+
+def add_x_body(got, total):
+    part = got[0].astype(F32) + got[1].astype(F32) + got[2].astype(F32) + got[3].astype(F32)
     total[...] = part.astype(BF16)
 
 
-def last_sum_body(info, got, grad_w_in, grad_w_out):
+def last_sum_body(got, grad_w_in, grad_w_out):
     for z in range(4):
         part = got[z].astype(F32)
         for y in range(1, 4):
@@ -365,13 +362,18 @@
 
 
 def input_body(info, *refs):
-    gp, (w, cot, out) = refs[0:4], refs[4:7]
-    total = cot[...].astype(F32)
-    for d in range(NB):
-        owner = lax.rem(info[9] + NB - d, NB)
+    gp, (w, cot), outs = refs[0:4], refs[4:6], refs[6:10]
+    for k in range(NB):
+        total = cot[...].astype(F32) if k == 0 else None
         for n, part in enumerate((0, 2, 1, 3)):
-            lanes = pl.ds(pl.multiple_of(part * D + owner * BLK, BLK), BLK)
-            total = total + nt(gp[d][:, n * BLK : (n + 1) * BLK], w[:, lanes])
+            lanes = pl.ds(pl.multiple_of(part * D + info[9] * BLK, BLK), BLK)
+            term = nt(gp[k][:, n * BLK : (n + 1) * BLK], w[:, lanes])
+            total = term if total is None else total + term
+        outs[k][...] = total.astype(outs[k].dtype)
+
+
+def add_rows_body(own, got_1, got_2, got_3, out):
+    total = own[...] + got_1[...].astype(F32) + got_2[...].astype(F32) + got_3[...].astype(F32)
     out[...] = total.astype(BF16)
 
 
@@ -442,29 +444,35 @@
     g_next = along(gatt, "y", -1)
     gateds = gather_z(gated)
     gp_q, dkv = call(
-        backward_local_body, (bf16((GRP, BLK)), f32((GRP, 2 * BLK))), 8, 10 << 30, 4 << 20,
+        backward_local_body, (bf16((GRP, BLK)), f32((GRP, 2 * BLK))), 8, 1 << 20, 1 << 20,
         [pltpu.VMEM((GRP, BLK), F32)],
     )(info, q, gatt, kv, kv_prev, *dsigs)
-    early = call(early_weights_body, f32((D, 2 * BLK)), 6, 1 << 30, 4 << 20)(info, *evs, gp_g, gp_q)
+    early = call(early_weights_body, f32((D, 2 * BLK)), 6, 1 << 20, 1 << 20)(info, *evs, gp_g, gp_q)
     q_next, g_next, early = lax.optimization_barrier((q_next, g_next, early))
     gp = call(
         backward_later_body, (bf16((BLK, 4 * BLK)),) * 4, 10, 5 << 30, 4 << 20, [pltpu.VMEM((GRP, 2 * BLK), F32)]
     )(info, q_next, g_next, kv, dkv, gp_g, gp_q, *dsigs)
     send, keep = call(
         late_weights_body,
-        (bf16((4, 128, 5 * BLK)), f32((4, 128, 5 * BLK))), 14, 2 << 30, 4 << 20,
+        (bf16((4, 128, 5 * BLK)), f32((4, 128, 5 * BLK))), 14, 1 << 20, 1 << 20,
         [pltpu.VMEM((D, 3 * BLK), F32)],
     )(info, *evs, *gp, *gateds, cot_z, early)
-    gp_rows = exchange(gp, "z")
-    *away, own = call(
-        add_core_body, (bf16((128, 5 * BLK)),) * 3 + (f32((128, 5 * BLK)),), 2, 1 << 20, 4 << 20
-    )(info, keep, swap(send))
-    sums = exchange([own] + away, "x")
-    grad_events = call(input_body, bf16((BLK, D)), 6, 2 << 30, 8 << 20)(info, *gp_rows, w_in, cot)
-    own, grad_events = lax.optimization_barrier((sums[0], grad_events))
-    total = call(add_x_body, bf16((128, 5 * BLK)), 4, 1 << 20, 1 << 20)(info, own, *sums[1:])
+    partial = call(
+        input_body, (f32((BLK, D)),) + (bf16((BLK, D)),) * 3, 6, 1 << 20, 1 << 20
+    )(info, *gp, w_in, cot)
+    partial = exchange(partial, "z")
+    keep, partial[0] = lax.optimization_barrier((keep, partial[0]))
+    mine = call(
+        add_core_body, bf16((4, 128, 5 * BLK)), 2, 1 << 20, 1 << 20, scalars=0
+    )(keep, swap(send))
+    sums = lax.all_to_all(mine, "x", 0, 0)
+    total = call(add_x_body, bf16((128, 5 * BLK)), 1, 1 << 20, 1 << 20, scalars=0)(sums)
+    _, own_rows = lax.optimization_barrier((total, partial[0]))
+    grad_events = call(
+        add_rows_body, bf16((BLK, D)), 4, 1 << 20, 4 << 20, scalars=0
+    )(own_rows, *partial[1:])
     got = lax.all_to_all(total.reshape(16, 8, 5 * BLK), ("y", "z"), 0, 0)
-    grad_w_in, grad_w_out = call(last_sum_body, (bf16((8, 4 * D)), bf16((8, D))), 1, 1 << 20, 1 << 20)(info, got)
+    grad_w_in, grad_w_out = call(last_sum_body, (bf16((8, 4 * D)), bf16((8, D))), 1, 1 << 20, 1 << 20, scalars=0)(got)
     return grad_events[None], grad_w_in, grad_w_out
 
 

time: 142 us -> 138 us (0.972)
  blocking collectives: 12.5 us -> 0 us
  waiting for transfers between devices: 42 us -> 50.2 us
  Pallas kernels: 41.3 us -> 44.1 us
  starting transfers between devices: 38.2 us -> 35.4 us
    all_to_all x0 -> x2, waiting for transfers between devices: none -> 18.2 us  [the longest x1 15.5 us: body(): sums = lax.all_to_all(mine, 'x', 0, 0)]
    all_to_all x1 -> x0, blocking collectives: 12.5 us -> none  [body(): got = lax.all_to_all(total.reshape(16, 8, 5 * BLK), ('y', 'z'), 0, 0)]
    ppermute x23 -> x20, starting transfers between devices: 38.1 us -> 27.1 us  [along(): return lax.ppermute(x, axis, [(i, (i + d) % 4) for i in range(4)])]
    ppermute x23 -> x20, waiting for transfers between devices: 42 us -> 31.9 us  [along(): return lax.ppermute(x, axis, [(i, (i + d) % 4) for i in range(4)])]
    all_to_all x0 -> x2, starting transfers between devices: none -> 8.26 us  [the longest x1 4.72 us: body(): got = lax.all_to_all(total.reshape(16, 8, 5 * BLK), ('y', 'z'), 0, 0)]
    pallas_call x6 -> x7, Pallas kernels: 17.9 us -> 19.4 us  [the longest x1 9.15 us: body(): call(backward_local_body, (bf16((GRP, BLK)), f32((GRP, 2 * BLK))), 8, 1 <...]
    unnamed x8 -> x12, local copies, waits for them, and re-layouts: 4.98 us -> 5.9 us
  transfers between devices with their start and end apart: 24 -> 23, of which waited for: 8 -> 13; matrix products, arithmetic and copies ran while one was open for 1% -> 1% of each run, Pallas kernels for 24% -> 27%
where the time goes in v7:
time: 138 us; the launch traced here: 137 us
  waiting for transfers between devices  50.2 us (36%)
  Pallas kernels  44.1 us (32%)
  starting transfers between devices  35.4 us (26%)
  local copies, waits for them, and re-layouts  6.63 us (5%)
    ppermute x20, waiting for transfers between devices, along(): return lax.ppermute(x, axis, [(i, (i + d) % 4) for i in range(4)])  31.9 us
    ppermute x20, starting transfers between devices, along(): return lax.ppermute(x, axis, [(i, (i + d) % 4) for i in range(4)])  27.1 us
    all_to_all x1, waiting for transfers between devices, body(): sums = lax.all_to_all(mine, 'x', 0, 0)  15.5 us
    pallas_call x1, Pallas kernels, body(): call(backward_local_body, (bf16((GRP, BLK)), f32((GRP, 2 * BLK))), 8, 1 <...  9.15 us
    pallas_call x1, Pallas kernels, body(): call(forward_local_body, (bf16((GRP, BLK)), bf16((GRP, 2 * BLK)), f32((GR...  6.3 us
    pallas_call x3, Pallas kernels, body(): call(project_body, (bf16((n * BLK, 2 * BLK)), bf16((n * BLK, BLK)), bf16(...  6.22 us
    unnamed x12, local copies, waits for them, and re-layouts  5.9 us
    all_to_all x1, starting transfers between devices, body(): got = lax.all_to_all(total.reshape(16, 8, 5 * BLK), ('y', 'z'), 0, 0)  4.72 us
  transfers between devices with their start and end apart: 23, of which 13 were waited for; matrix products, arithmetic and copies ran while one was open for 1% of the time, Pallas kernels for 27%

profile of v7, /device:TPU:0, one launch (start us, length us, event | category | flops | bytes accessed | tf_op | source)
XLA Modules:
  0.0 137.1 jit_solution(2893604165344405184)
XLA Ops:
  0.6 4.2 %collective-permute-start = (bf16[256,1024]{1,0:T(8,128)(2,1)}, bf16[256,1024]{1,0:T(8,128)(2,1)S(1)}, u32[]{:S(2)}, u32[]{:S(2)}) collective-permute-start(bf16[256,1024]{1,0:T(8,128)(2,1)} %bitcast.5.refs_0_), channel_id=1, source_target_pairs={{0,3},{1,0},{2,1},{3,2},{4,7},{5,4},{6,5},{7,6},{8,11},{9,8},{10,9... | collective-permute-start | bytes 1572872 | tf_op jit(solution)/shard_map/ppermute | solution.py:381
  5.6 3.4 %copy-done = bf16[1024,4096]{1,0:T(8,128)(2,1)S(1)} copy-done((bf16[1024,4096]{1,0:T(8,128)(2,1)S(1)}, bf16[1024,4096]{1,0:T(8,128)(2,1)}, u32[]{:S(2)}) %copy-start) | copy-done | bytes 8388632
  8.9 2.2 %shard_map.76 = (bf16[256,512]{1,0:T(8,128)(2,1)S(1)}, bf16[256,256]{1,0:T(8,128)(2,1)S(1)}, bf16[256,256]{1,0:T(8,128)(2,1)S(1)}, bf16[256,1024]{1,0:T(8,128)(2,1)S(1)}) custom-call(s32[12]{0:T(128)S(1)} %concatenate.3.info, bf16[256,1024]{1,0:T(8,128)(2,1)} %bitcast.5.refs_0_, bf16[1024,4096]{1,0:T(8,128)(2,1)S(1)} %copy-done), custom_call_target="tpu_custom_call" | custom-call | flops 536870912 | bytes 4194304 | tf_op jit(solution)/shard_map/pallas_call | solution.py:418
  11.2 5.1 %collective-permute-done.refs_0_.refs_1_ = bf16[256,1024]{1,0:T(8,128)(2,1)S(1)} collective-permute-done((bf16[256,1024]{1,0:T(8,128)(2,1)}, bf16[256,1024]{1,0:T(8,128)(2,1)S(1)}, u32[]{:S(2)}, u32[]{:S(2)}) %collective-permute-start) | collective-permute-done | bytes 524320 | tf_op jit(solution)/shard_map/ppermute | solution.py:381
  16.3 3.3 %collective-permute-done.1.refs_1_.refs_3_ = bf16[256,1024]{1,0:T(8,128)(2,1)S(1)} collective-permute-done((bf16[256,1024]{1,0:T(8,128)(2,1)}, bf16[256,1024]{1,0:T(8,128)(2,1)S(1)}, u32[]{:S(2)}, u32[]{:S(2)}) %collective-permute-start.1) | collective-permute-done | bytes 524320 | tf_op jit(solution)/shard_map/ppermute | solution.py:381
  24.1 2.4 %shard_map.77 = (bf16[512,512]{1,0:T(8,128)(2,1)S(1)}, bf16[512,256]{1,0:T(8,128)(2,1)S(1)}, bf16[512,256]{1,0:T(8,128)(2,1)S(1)}, bf16[256,1024]{1,0:T(8,128)(2,1)S(1)}, bf16[256,1024]{1,0:T(8,128)(2,1)S(1)}) custom-call(s32[12]{0:T(128)S(1)} %concatenate.3.info, bf16[256,1024]{1,0:T(8,128)(2,1)S(1)} %collective-permute-done.refs_0_.refs_1_, ...), custom_call_target="tpu_custom_call" | custom-call | flops 1073741824 | bytes 4194304 | tf_op jit(solution)/shard_map/pallas_call | solution.py:418
  28.2 5.6 %collective-permute-done.2.refs_0_.refs_2_ = bf16[256,1024]{1,0:T(8,128)(2,1)S(1)} collective-permute-done((bf16[256,1024]{1,0:T(8,128)(2,1)}, bf16[256,1024]{1,0:T(8,128)(2,1)S(1)}, u32[]{:S(2)}, u32[]{:S(2)}) %collective-permute-start.2) | collective-permute-done | bytes 524320 | tf_op jit(solution)/shard_map/ppermute | solution.py:381
  40.3 6.3 %shard_map.79 = (bf16[1024,256]{1,0:T(8,128)(2,1)S(1)}, bf16[1024,512]{1,0:T(8,128)(2,1)S(1)}, f32[1024,256]{1,0:T(8,128)S(1)}) custom-call(s32[12]{0:T(128)S(1)} %concatenate.3.info, bf16[256,256]{1,0:T(8,128)(2,1)S(1)} %get-tuple-element.63.refs_0_, bf16[512,256]{1,0:T(8,128)(2,1)S(1)} %get-tuple-element.64.refs_1_, ...), custom_call_target="tpu_custom_call" | custom-call | flops 5368709120 | bytes 4194304 | tf_op jit(solution)/shard_map/pallas_call | solution.py:432
  46.6 2.9 %collective-permute-done.7.refs_6_ = bf16[256,512]{1,0:T(8,128)(2,1)S(1)} collective-permute-done((bf16[256,512]{1,0:T(8,128)(2,1)S(1)}, bf16[256,512]{1,0:T(8,128)(2,1)S(1)}, u32[]{:S(2)}, u32[]{:S(2)}) %collective-permute-start.7) | collective-permute-done | bytes 262176 | tf_op jit(solution)/shard_map/ppermute | solution.py:381
  51.8 2.4 %collective-permute-start.10 = (f32[8,1024]{1,0:T(8,128)S(1)}, f32[8,1024]{1,0:T(8,128)S(1)}, u32[]{:S(2)}, u32[]{:S(2)}) collective-permute-start(f32[8,1024]{1,0:T(8,128)S(1)} %get-tuple-element.84.refs_3_), channel_id=1, source_target_pairs={{0,3},{1,0},{2,1},{3,2},{4,7},{5,4},{6,5},{7,6},{8,11},{9,8},{10,9... | collective-permute-start | bytes 98312 | tf_op jit(solution)/shard_map/ppermute | solution.py:381
  55.2 2.3 %collective-permute-start.3 = (bf16[1024,256]{1,0:T(8,128)(2,1)S(1)}, bf16[1024,256]{1,0:T(8,128)(2,1)S(1)}, u32[]{:S(2)}, u32[]{:S(2)}) collective-permute-start(bf16[1024,256]{1,0:T(8,128)(2,1)S(1)} %get-tuple-element.68.refs_0_), channel_id=1, source_target_pairs={{0,12},{4,0},{8,4},{12,8},{1,13},{5,1},{9,5},{13,9},{2,14},{6,2},{... | collective-permute-start | bytes 1572872 | tf_op jit(solution)/shard_map/ppermute | solution.py:381
  61.4 2.7 %collective-permute-start.13 = (bf16[1024,256]{1,0:T(8,128)(2,1)S(1)}, bf16[1024,256]{1,0:T(8,128)(2,1)S(1)}, u32[]{:S(2)}, u32[]{:S(2)}) collective-permute-start(bf16[1024,256]{1,0:T(8,128)(2,1)S(1)} %get-tuple-element.89.refs_1_), channel_id=1, source_target_pairs={{0,12},{4,0},{8,4},{12,8},{1,13},{5,1},{9,5},{13,9},{2,14},{6,2},{... | collective-permute-start | bytes 1572872 | tf_op jit(solution)/shard_map/ppermute | solution.py:381
  67.2 9.1 %shard_map.83 = (bf16[1024,256]{1,0:T(8,128)(2,1)S(1)}, f32[1024,512]{1,0:T(8,128)S(1)}) custom-call(s32[12]{0:T(128)S(1)} %concatenate.3.info, bf16[1024,256]{1,0:T(8,128)(2,1)S(1)} %get-tuple-element.68.refs_0_, bf16[1024,256]{1,0:T(8,128)(2,1)S(1)} %get-tuple-element.89.refs_1_, bf16[1024,512]{1,0:T(8,128)(2,1)S(1)} %get-tuple-element.91.refs_2_, ...), custom_call_target="tpu_custom_call" | custom-call | flops 1048576 | bytes 1048576 | tf_op jit(solution)/shard_map/pallas_call | solution.py:446
  76.3 2.4 %shard_map.84.refs_13_ = f32[1024,512]{1,0:T(8,128)S(1)} custom-call(s32[12]{0:T(128)S(1)} %concatenate.3.info, bf16[256,1024]{1,0:T(8,128)(2,1)} %bitcast.5.refs_0_, bf16[256,1024]{1,0:T(8,128)(2,1)S(1)} %collective-permute-done.refs_0_.refs_1_, bf16[256,1024]{1,0:T(8,128)(2,1)S(1)} %collective-permute-done.2.refs_0_.refs_2_, ...), custom_call_target="tpu_custom_call" | custom-call | flops 1048576 | bytes 1048576 | tf_op jit(solution)/shard_map/pallas_call | solution.py:450
  80.4 3.7 %shard_map.85 = (bf16[256,1024]{1,0:T(8,128)(2,1)S(1)}, bf16[256,1024]{1,0:T(8,128)(2,1)S(1)}, bf16[256,1024]{1,0:T(8,128)(2,1)S(1)}, bf16[256,1024]{1,0:T(8,128)(2,1)S(1)}) custom-call(s32[12]{0:T(128)S(1)} %concatenate.3.info, bf16[1024,256]{1,0:T(8,128)(2,1)S(1)} %collective-permute-done.3.refs_0_, bf16[1024,256]{1,0:T(8,128)(2,1)S(1)} %collective-permute-done.13.refs_1_, ...), custom_call_target="tpu_custom_call" | custom-call | flops 5368709120 | bytes 4194304 | tf_op jit(solution)/shard_map/pallas_call | solution.py:452
  84.1 6.5 %collective-permute-done.16.refs_11_ = bf16[1024,256]{1,0:T(8,128)(2,1)S(1)} collective-permute-done((bf16[1024,256]{1,0:T(8,128)(2,1)S(1)}, bf16[1024,256]{1,0:T(8,128)(2,1)S(1)}, u32[]{:S(2)}, u32[]{:S(2)}) %collective-permute-start.16) | collective-permute-done | bytes 524320 | tf_op jit(solution)/shard_map/ppermute | solution.py:381
  90.6 3.7 %shard_map.86 = (bf16[4,128,1280]{2,1,0:T(8,128)(2,1)S(1)}, f32[4,128,1280]{2,1,0:T(8,128)S(1)}) custom-call(s32[12]{0:T(128)S(1)} %concatenate.3.info, bf16[256,1024]{1,0:T(8,128)(2,1)} %bitcast.5.refs_0_, bf16[256,1024]{1,0:T(8,128)(2,1)S(1)} %collective-permute-done.refs_0_.refs_1_, bf16[256,1024]{1,0:T(8,128)(2,1)S(1)} %collective-permute-done.2.refs_0_.refs_2_, ...), custom_call_target="tpu_custom_call" | custom-call | flops 1048576 | bytes 1048576 | tf_op jit(solution)/shard_map/pallas_call | solution.py:455
  94.4 3.0 %shard_map.87 = (f32[256,1024]{1,0:T(8,128)S(1)}, bf16[256,1024]{1,0:T(8,128)(2,1)}, bf16[256,1024]{1,0:T(8,128)(2,1)S(1)}, bf16[256,1024]{1,0:T(8,128)(2,1)S(1)}) custom-call(s32[12]{0:T(128)S(1)} %concatenate.3.info, bf16[256,1024]{1,0:T(8,128)(2,1)S(1)} %get-tuple-element.97.refs_4_.refs_0_, bf16[256,1024]{1,0:T(8,128)(2,1)S(1)} %get-tuple-element.98.refs_5_.refs_1_, ...), custom_call_target="tpu_custom_call" | custom-call | flops 1048576 | bytes 1048576 | tf_op jit(solution)/shard_map/pallas_call | solution.py:460
  99.6 3.5 %all-to-all-start = ((bf16[4,128,1280]{2,1,0:T(8,128)(2,1)}), bf16[4,128,1280]{2,1,0:T(8,128)(2,1)S(1)}, u32[]{:S(2)}, u32[]{:S(2)}) async-start(bf16[4,128,1280]{2,1,0:T(8,128)(2,1)} %shard_map.88), calls=%async_computation | async-start | bytes 2621440 | tf_op jit(solution)/shard_map/all_to_all | solution.py:468
  103.3 2.2 %collective-permute-start.19 = (bf16[256,1024]{1,0:T(8,128)(2,1)}, bf16[256,1024]{1,0:T(8,128)(2,1)S(1)}, u32[]{:S(2)}, u32[]{:S(2)}) collective-permute-start(bf16[256,1024]{1,0:T(8,128)(2,1)} %copy-done.5), channel_id=1, source_target_pairs={{0,2},{1,3},{2,0},{3,1},{4,6},{5,7},{6,4},{7,5},{8,10},{9,11},{10,... | collective-permute-start | bytes 1572872 | tf_op jit(solution)/shard_map/ppermute | solution.py:381
  106.5 15.5 %all-to-all-done.got = bf16[4,128,1280]{2,1,0:T(8,128)(2,1)S(1)} async-done(((bf16[4,128,1280]{2,1,0:T(8,128)(2,1)}), bf16[4,128,1280]{2,1,0:T(8,128)(2,1)S(1)}, u32[]{:S(2)}, u32[]{:S(2)}) %all-to-all-start) | async-done | bytes 1310752 | tf_op jit(solution)/shard_map/all_to_all | solution.py:468
  122.9 4.7 %all-to-all-start.1 = ((bf16[16,8,1280]{2,1,0:T(8,128)(2,1)}), bf16[16,8,1280]{2,1,0:T(8,128)(2,1)S(1)}, u32[]{:S(2)}, u32[]{:S(2)}) async-start(bf16[16,8,1280]{2,1,0:T(8,128)(2,1)} %bitcast.8), calls=%async_computation.1 | async-start | bytes 655360 | tf_op jit(solution)/shard_map/all_to_all | solution.py:474
  127.6 2.6 %collective-permute-done.18.got_1 = bf16[256,1024]{1,0:T(8,128)(2,1)S(1)} collective-permute-done((bf16[256,1024]{1,0:T(8,128)(2,1)}, bf16[256,1024]{1,0:T(8,128)(2,1)S(1)}, u32[]{:S(2)}, u32[]{:S(2)}) %collective-permute-start.18) | collective-permute-done | bytes 524320 | tf_op jit(solution)/shard_map/ppermute | solution.py:381
  133.7 2.8 %all-to-all-done.1.got = bf16[16,8,1280]{2,1,0:T(8,128)(2,1)S(1)} async-done(((bf16[16,8,1280]{2,1,0:T(8,128)(2,1)}), bf16[16,8,1280]{2,1,0:T(8,128)(2,1)S(1)}, u32[]{:S(2)}, u32[]{:S(2)}) %all-to-all-start.1) | async-done | bytes 327712 | tf_op jit(solution)/shard_map/all_to_all | solution.py:474
  (51 shorter events, 33.8 us)
Async XLA Ops:
  0.6 15.7 %collective-permute-start = (bf16[256,1024]{1,0:T(8,128)(2,1)}, bf16[256,1024]{1,0:T(8,128)(2,1)S(1)}, u32[]{:S(2)}, u32[]{:S(2)}) collective-permute-start(bf16[256,1024]{1,0:T(8,128)(2,1)} %bitcast.5.refs_0_), channel_id=1, source_target_pairs={{0,3},{1,0},{2,1},{3,2},{4,7},{5,4},{6,5},{7,6},{8,11},{9,8},{10,9... | collective-permute-start | bytes 1572872 | tf_op jit(solution)/shard_map/ppermute | solution.py:381
  4.8 14.8 %collective-permute-start.1 = (bf16[256,1024]{1,0:T(8,128)(2,1)}, bf16[256,1024]{1,0:T(8,128)(2,1)S(1)}, u32[]{:S(2)}, u32[]{:S(2)}) collective-permute-start(bf16[256,1024]{1,0:T(8,128)(2,1)} %bitcast.5.refs_0_), channel_id=1, source_target_pairs={{0,1},{1,2},{2,3},{3,0},{4,5},{5,6},{6,7},{7,4},{8,9},{9,10},{10,1... | collective-permute-start | bytes 1572872 | tf_op jit(solution)/shard_map/ppermute | solution.py:381
  8.9 15.2 %copy-start.1 = (bf16[1024,4096]{1,0:T(8,128)(2,1)S(1)}, bf16[1024,4096]{1,0:T(8,128)(2,1)}, u32[]{:S(2)}) copy-start(bf16[1024,4096]{1,0:T(8,128)(2,1)} %refs_4_.1) | copy-start | bytes 25165828
  19.6 14.2 %collective-permute-start.2 = (bf16[256,1024]{1,0:T(8,128)(2,1)}, bf16[256,1024]{1,0:T(8,128)(2,1)S(1)}, u32[]{:S(2)}, u32[]{:S(2)}) collective-permute-start(bf16[256,1024]{1,0:T(8,128)(2,1)} %bitcast.5.refs_0_), channel_id=1, source_target_pairs={{0,2},{1,3},{2,0},{3,1},{4,6},{5,7},{6,4},{7,5},{8,10},{9,11},{10,... | collective-permute-start | bytes 1572872 | tf_op jit(solution)/shard_map/ppermute | solution.py:381
  19.6 19.5 %collective-permute-start.4 = (bf16[256,512]{1,0:T(8,128)(2,1)S(1)}, bf16[256,512]{1,0:T(8,128)(2,1)S(1)}, u32[]{:S(2)}, u32[]{:S(2)}) collective-permute-start(bf16[256,512]{1,0:T(8,128)(2,1)S(1)} %get-tuple-element.59.refs_3_), channel_id=1, source_target_pairs={{0,4},{4,8},{8,12},{12,0},{1,5},{5,9},{9,13},{13,1},{2,6},{6,10},{... | collective-permute-start | bytes 786440 | tf_op jit(solution)/shard_map/ppermute | solution.py:381
  26.6 20.0 %collective-permute-start.5 = (bf16[512,512]{1,0:T(8,128)(2,1)S(1)}, bf16[512,512]{1,0:T(8,128)(2,1)S(1)}, u32[]{:S(2)}, u32[]{:S(2)}) collective-permute-start(bf16[512,512]{1,0:T(8,128)(2,1)S(1)} %get-tuple-element.66.refs_4_), channel_id=1, source_target_pairs={{0,4},{4,8},{8,12},{12,0},{1,5},{5,9},{9,13},{13,1},{2,6},{6,10},{... | collective-permute-start | bytes 1572872 | tf_op jit(solution)/shard_map/ppermute | solution.py:381
  35.4 11.2 %collective-permute-start.6 = (bf16[256,512]{1,0:T(8,128)(2,1)S(1)}, bf16[256,512]{1,0:T(8,128)(2,1)S(1)}, u32[]{:S(2)}, u32[]{:S(2)}) collective-permute-start(bf16[256,512]{1,0:T(8,128)(2,1)S(1)} %get-tuple-element.67.refs_5_), channel_id=1, source_target_pairs={{0,4},{4,8},{8,12},{12,0},{1,5},{5,9},{9,13},{13,1},{2,6},{6,10},{... | collective-permute-start | bytes 786440 | tf_op jit(solution)/shard_map/ppermute | solution.py:381
  37.0 12.5 %collective-permute-start.7 = (bf16[256,512]{1,0:T(8,128)(2,1)S(1)}, bf16[256,512]{1,0:T(8,128)(2,1)S(1)}, u32[]{:S(2)}, u32[]{:S(2)}) collective-permute-start(bf16[256,512]{1,0:T(8,128)(2,1)S(1)} %get-tuple-element.75), channel_id=1, source_target_pairs={{0,1},{1,2},{2,3},{3,0},{4,5},{5,6},{6,7},{7,4},{8,9},{9,10},{10,1... | collective-permute-start | bytes 786440 | tf_op jit(solution)/shard_map/ppermute | solution.py:381
  37.0 12.5 %collective-permute-start.8 = (bf16[256,512]{1,0:T(8,128)(2,1)S(1)}, bf16[256,512]{1,0:T(8,128)(2,1)S(1)}, u32[]{:S(2)}, u32[]{:S(2)}) collective-permute-start(bf16[256,512]{1,0:T(8,128)(2,1)S(1)} %get-tuple-element.76), channel_id=1, source_target_pairs={{0,2},{1,3},{2,0},{3,1},{4,6},{5,7},{6,4},{7,5},{8,10},{9,11},{10,... | collective-permute-start | bytes 786440 | tf_op jit(solution)/shard_map/ppermute | solution.py:381
  39.1 11.0 %collective-permute-start.9 = (bf16[256,512]{1,0:T(8,128)(2,1)S(1)}, bf16[256,512]{1,0:T(8,128)(2,1)S(1)}, u32[]{:S(2)}, u32[]{:S(2)}) collective-permute-start(bf16[256,512]{1,0:T(8,128)(2,1)S(1)} %get-tuple-element.77), channel_id=1, source_target_pairs={{0,3},{1,0},{2,1},{3,2},{4,7},{5,4},{6,5},{7,6},{8,11},{9,8},{10,9... | collective-permute-start | bytes 786440 | tf_op jit(solution)/shard_map/ppermute | solution.py:381
  51.8 5.7 %collective-permute-start.10 = (f32[8,1024]{1,0:T(8,128)S(1)}, f32[8,1024]{1,0:T(8,128)S(1)}, u32[]{:S(2)}, u32[]{:S(2)}) collective-permute-start(f32[8,1024]{1,0:T(8,128)S(1)} %get-tuple-element.84.refs_3_), channel_id=1, source_target_pairs={{0,3},{1,0},{2,1},{3,2},{4,7},{5,4},{6,5},{7,6},{8,11},{9,8},{10,9... | collective-permute-start | bytes 98312 | tf_op jit(solution)/shard_map/ppermute | solution.py:381
  54.2 5.5 %collective-permute-start.11 = (f32[8,1024]{1,0:T(8,128)S(1)}, f32[8,1024]{1,0:T(8,128)S(1)}, u32[]{:S(2)}, u32[]{:S(2)}) collective-permute-start(f32[8,1024]{1,0:T(8,128)S(1)} %get-tuple-element.84.refs_3_), channel_id=1, source_target_pairs={{0,2},{1,3},{2,0},{3,1},{4,6},{5,7},{6,4},{7,5},{8,10},{9,11},{10,... | collective-permute-start | bytes 98312 | tf_op jit(solution)/shard_map/ppermute | solution.py:381
  54.2 5.5 %collective-permute-start.12 = (f32[8,1024]{1,0:T(8,128)S(1)}, f32[8,1024]{1,0:T(8,128)S(1)}, u32[]{:S(2)}, u32[]{:S(2)}) collective-permute-start(f32[8,1024]{1,0:T(8,128)S(1)} %get-tuple-element.84.refs_3_), channel_id=1, source_target_pairs={{0,1},{1,2},{2,3},{3,0},{4,5},{5,6},{6,7},{7,4},{8,9},{9,10},{10,1... | collective-permute-start | bytes 98312 | tf_op jit(solution)/shard_map/ppermute | solution.py:381
  55.2 23.5 %collective-permute-start.3 = (bf16[1024,256]{1,0:T(8,128)(2,1)S(1)}, bf16[1024,256]{1,0:T(8,128)(2,1)S(1)}, u32[]{:S(2)}, u32[]{:S(2)}) collective-permute-start(bf16[1024,256]{1,0:T(8,128)(2,1)S(1)} %get-tuple-element.68.refs_0_), channel_id=1, source_target_pairs={{0,12},{4,0},{8,4},{12,8},{1,13},{5,1},{9,5},{13,9},{2,14},{6,2},{... | collective-permute-start | bytes 1572872 | tf_op jit(solution)/shard_map/ppermute | solution.py:381
  61.4 19.0 %collective-permute-start.13 = (bf16[1024,256]{1,0:T(8,128)(2,1)S(1)}, bf16[1024,256]{1,0:T(8,128)(2,1)S(1)}, u32[]{:S(2)}, u32[]{:S(2)}) collective-permute-start(bf16[1024,256]{1,0:T(8,128)(2,1)S(1)} %get-tuple-element.89.refs_1_), channel_id=1, source_target_pairs={{0,12},{4,0},{8,4},{12,8},{1,13},{5,1},{9,5},{13,9},{2,14},{6,2},{... | collective-permute-start | bytes 1572872 | tf_op jit(solution)/shard_map/ppermute | solution.py:381
  64.1 20.0 %collective-permute-start.14 = (bf16[1024,256]{1,0:T(8,128)(2,1)S(1)}, bf16[1024,256]{1,0:T(8,128)(2,1)S(1)}, u32[]{:S(2)}, u32[]{:S(2)}) collective-permute-start(bf16[1024,256]{1,0:T(8,128)(2,1)S(1)} %get-tuple-element.101.refs_8_), channel_id=1, source_target_pairs={{0,3},{1,0},{2,1},{3,2},{4,7},{5,4},{6,5},{7,6},{8,11},{9,8},{10,9... | collective-permute-start | bytes 1572872 | tf_op jit(solution)/shard_map/ppermute | solution.py:381
  64.9 19.2 %collective-permute-start.15 = (bf16[1024,256]{1,0:T(8,128)(2,1)S(1)}, bf16[1024,256]{1,0:T(8,128)(2,1)S(1)}, u32[]{:S(2)}, u32[]{:S(2)}) collective-permute-start(bf16[1024,256]{1,0:T(8,128)(2,1)S(1)} %get-tuple-element.101.refs_8_), channel_id=1, source_target_pairs={{0,2},{1,3},{2,0},{3,1},{4,6},{5,7},{6,4},{7,5},{8,10},{9,11},{10,... | collective-permute-start | bytes 1572872 | tf_op jit(solution)/shard_map/ppermute | solution.py:381
  66.1 24.5 %collective-permute-start.16 = (bf16[1024,256]{1,0:T(8,128)(2,1)S(1)}, bf16[1024,256]{1,0:T(8,128)(2,1)S(1)}, u32[]{:S(2)}, u32[]{:S(2)}) collective-permute-start(bf16[1024,256]{1,0:T(8,128)(2,1)S(1)} %get-tuple-element.101.refs_8_), channel_id=1, source_target_pairs={{0,1},{1,2},{2,3},{3,0},{4,5},{5,6},{6,7},{7,4},{8,9},{9,10},{10,1... | collective-permute-start | bytes 1572872 | tf_op jit(solution)/shard_map/ppermute | solution.py:381
  94.3 3.1 %collective-permute-start.17 = (bf16[4,128,1280]{2,1,0:T(8,128)(2,1)S(1)}, bf16[4,128,1280]{2,1,0:T(8,128)(2,1)S(1)}, u32[]{:S(2)}, u32[]{:S(2)}) collective-permute-start(bf16[4,128,1280]{2,1,0:T(8,128)(2,1)S(1)} %get-tuple-element.107), channel_id=1, source_target_pairs={{0,16},{16,0},{1,17},{17,1},{2,18},{18,2},{3,19},{19,3},{4,20},{20... | collective-permute-start | bytes 3932168 | tf_op jit(solution)/shard_map/ppermute | solution.py:385
  99.6 22.4 %all-to-all-start = ((bf16[4,128,1280]{2,1,0:T(8,128)(2,1)}), bf16[4,128,1280]{2,1,0:T(8,128)(2,1)S(1)}, u32[]{:S(2)}, u32[]{:S(2)}) async-start(bf16[4,128,1280]{2,1,0:T(8,128)(2,1)} %shard_map.88), calls=%async_computation | async-start | bytes 2621440 | tf_op jit(solution)/shard_map/all_to_all | solution.py:468
  103.2 27.0 %collective-permute-start.18 = (bf16[256,1024]{1,0:T(8,128)(2,1)}, bf16[256,1024]{1,0:T(8,128)(2,1)S(1)}, u32[]{:S(2)}, u32[]{:S(2)}) collective-permute-start(bf16[256,1024]{1,0:T(8,128)(2,1)} %get-tuple-element.110), channel_id=1, source_target_pairs={{0,1},{1,2},{2,3},{3,0},{4,5},{5,6},{6,7},{7,4},{8,9},{9,10},{10,1... | collective-permute-start | bytes 1572872 | tf_op jit(solution)/shard_map/ppermute | solution.py:381
  103.3 27.0 %collective-permute-start.19 = (bf16[256,1024]{1,0:T(8,128)(2,1)}, bf16[256,1024]{1,0:T(8,128)(2,1)S(1)}, u32[]{:S(2)}, u32[]{:S(2)}) collective-permute-start(bf16[256,1024]{1,0:T(8,128)(2,1)} %copy-done.5), channel_id=1, source_target_pairs={{0,2},{1,3},{2,0},{3,1},{4,6},{5,7},{6,4},{7,5},{8,10},{9,11},{10,... | collective-permute-start | bytes 1572872 | tf_op jit(solution)/shard_map/ppermute | solution.py:381
  105.5 26.1 %collective-permute-start.20 = (bf16[256,1024]{1,0:T(8,128)(2,1)}, bf16[256,1024]{1,0:T(8,128)(2,1)}, u32[]{:S(2)}, u32[]{:S(2)}) collective-permute-start(bf16[256,1024]{1,0:T(8,128)(2,1)} %copy-done.4), channel_id=1, source_target_pairs={{0,3},{1,0},{2,1},{3,2},{4,7},{5,4},{6,5},{7,6},{8,11},{9,8},{10,9... | collective-permute-start | bytes 1572872 | tf_op jit(solution)/shard_map/ppermute | solution.py:381
  122.9 13.5 %all-to-all-start.1 = ((bf16[16,8,1280]{2,1,0:T(8,128)(2,1)}), bf16[16,8,1280]{2,1,0:T(8,128)(2,1)S(1)}, u32[]{:S(2)}, u32[]{:S(2)}) async-start(bf16[16,8,1280]{2,1,0:T(8,128)(2,1)} %bitcast.8), calls=%async_computation.1 | async-start | bytes 655360 | tf_op jit(solution)/shard_map/all_to_all | solution.py:474
  (5 other events, 19.0 us)

commit v8 on v7

--- a/solution.py
+++ b/solution.py
@@ -372,9 +372,12 @@
         outs[k][...] = total.astype(outs[k].dtype)
 
 
-def add_rows_body(own, got_1, got_2, got_3, out):
-    total = own[...] + got_1[...].astype(F32) + got_2[...].astype(F32) + got_3[...].astype(F32)
-    out[...] = total.astype(BF16)
+def add_near_body(own, got_1, got_3, out):
+    out[...] = own[...] + got_1[...].astype(F32) + got_3[...].astype(F32)
+
+
+def add_far_body(near, got_2, out):
+    out[...] = (near[...] + got_2[...].astype(F32)).astype(BF16)
 
 
 def along(x, axis, d):
@@ -418,7 +421,7 @@
         kv, q, g, *dsig = call(
             project_body,
             (bf16((n * BLK, 2 * BLK)), bf16((n * BLK, BLK)), bf16((n * BLK, BLK))) + (bf16((BLK, 4 * BLK)),) * n,
-            n + 1, 2 * n * BLK * D * D, 4 << 20,
+            n + 1, 1 << 20, 1 << 20,
         )(info, *[evs[b] for b in blocks], w_in)
         kvs.append(kv)
         qs.append(q)
@@ -426,7 +429,7 @@
         for b, d in zip(blocks, dsig):
             dsigs[b] = d
         kv_prevs.append(along(kv, "y", 1))
-    ggs = call(grad_gated_body, (bf16((BLK, 2 * BLK)),) * 4, 2, 1 << 29, 2 << 20)(info, cot, w_out)
+    ggs = call(grad_gated_body, (bf16((BLK, 2 * BLK)),) * 4, 2, 1 << 20, 1 << 20)(info, cot, w_out)
     *ggs, _ = lax.optimization_barrier((*ggs, evs[2]))
     ggs = exchange(ggs, "z")
     q, kv, att = call(
@@ -452,25 +455,27 @@
     gp = call(
         backward_later_body, (bf16((BLK, 4 * BLK)),) * 4, 10, 5 << 30, 4 << 20, [pltpu.VMEM((GRP, 2 * BLK), F32)]
     )(info, q_next, g_next, kv, dkv, gp_g, gp_q, *dsigs)
+    *partial, = call(
+        input_body, (f32((BLK, D)),) + (bf16((BLK, D)),) * 3, 6, 1 << 20, 1 << 20
+    )(info, *gp, w_in, cot)
+    early, partial[0] = lax.optimization_barrier((early, partial[0]))
+    partial = exchange(partial, "z")
     send, keep = call(
         late_weights_body,
         (bf16((4, 128, 5 * BLK)), f32((4, 128, 5 * BLK))), 14, 1 << 20, 1 << 20,
         [pltpu.VMEM((D, 3 * BLK), F32)],
     )(info, *evs, *gp, *gateds, cot_z, early)
-    partial = call(
-        input_body, (f32((BLK, D)),) + (bf16((BLK, D)),) * 3, 6, 1 << 20, 1 << 20
-    )(info, *gp, w_in, cot)
-    partial = exchange(partial, "z")
-    keep, partial[0] = lax.optimization_barrier((keep, partial[0]))
     mine = call(
         add_core_body, bf16((4, 128, 5 * BLK)), 2, 1 << 20, 1 << 20, scalars=0
     )(keep, swap(send))
     sums = lax.all_to_all(mine, "x", 0, 0)
+    near_rows = call(
+        add_near_body, f32((BLK, D)), 3, 40 << 30, 4 << 20, scalars=0
+    )(partial[0], partial[1], partial[3])
+    sums, near_rows = lax.optimization_barrier((sums, near_rows))
     total = call(add_x_body, bf16((128, 5 * BLK)), 1, 1 << 20, 1 << 20, scalars=0)(sums)
-    _, own_rows = lax.optimization_barrier((total, partial[0]))
-    grad_events = call(
-        add_rows_body, bf16((BLK, D)), 4, 1 << 20, 4 << 20, scalars=0
-    )(own_rows, *partial[1:])
+    _, near_rows = lax.optimization_barrier((total, near_rows))
+    grad_events = call(add_far_body, bf16((BLK, D)), 2, 1 << 20, 4 << 20, scalars=0)(near_rows, partial[2])
     got = lax.all_to_all(total.reshape(16, 8, 5 * BLK), ("y", "z"), 0, 0)
     grad_w_in, grad_w_out = call(last_sum_body, (bf16((8, 4 * D)), bf16((8, D))), 1, 1 << 20, 1 << 20, scalars=0)(got)
     return grad_events[None], grad_w_in, grad_w_out

time: 138 us -> 139 us (level)
  starting transfers between devices: 35.4 us -> 38.7 us
  waiting for transfers between devices: 50.2 us -> 48.7 us
    all_to_all x1, waiting for transfers between devices: 15.5 us -> 0.01 us  [body(): sums = lax.all_to_all(mine, 'x', 0, 0)]
    ppermute x20, waiting for transfers between devices: 31.9 us -> 40.7 us  [along(): return lax.ppermute(x, axis, [(i, (i + d) % 4) for i in range(4)])]
    all_to_all x1, waiting for transfers between devices: 2.77 us -> 7.93 us  [body(): got = lax.all_to_all(total.reshape(16, 8, 5 * BLK), ('y', 'z'), 0, 0)]
    ppermute x20, starting transfers between devices: 27.1 us -> 29.6 us  [along(): return lax.ppermute(x, axis, [(i, (i + d) % 4) for i in range(4)])]
    pallas_call x1, Pallas kernels: 9.15 us -> 7.53 us  [body(): call(backward_local_body, (bf16((GRP, BLK)), f32((GRP, 2 * BLK))), 8, 1 <...]
    pallas_call x2 -> x3, Pallas kernels: 3.38 us -> 3.55 us  [the longest x1 1.34 us: body(): call(add_near_body, f32((BLK, D)), 3, 40 << 30, 4 << 20, scalars=0)]
  transfers between devices with their start and end apart: 23 -> 23, of which waited for: 13 -> 10; matrix products, arithmetic and copies ran while one was open for 1% -> 1% of each run, Pallas kernels for 27% -> 27%
where the time goes in v8:
time: 139 us; the launch traced here: 137 us
  waiting for transfers between devices  48.7 us (35%)
  Pallas kernels  42.8 us (31%)
  starting transfers between devices  38.7 us (28%)
  local copies, waits for them, and re-layouts  6.32 us (5%)
    ppermute x20, waiting for transfers between devices, along(): return lax.ppermute(x, axis, [(i, (i + d) % 4) for i in range(4)])  40.7 us
    ppermute x20, starting transfers between devices, along(): return lax.ppermute(x, axis, [(i, (i + d) % 4) for i in range(4)])  29.6 us
    all_to_all x1, waiting for transfers between devices, body(): got = lax.all_to_all(total.reshape(16, 8, 5 * BLK), ('y', 'z'), 0, 0)  7.93 us
    pallas_call x1, Pallas kernels, body(): call(backward_local_body, (bf16((GRP, BLK)), f32((GRP, 2 * BLK))), 8, 1 <...  7.53 us
    pallas_call x3, Pallas kernels, body(): call(project_body, (bf16((n * BLK, 2 * BLK)), bf16((n * BLK, BLK)), bf16(...  6.22 us
    unnamed x12, local copies, waits for them, and re-layouts  5.58 us
    pallas_call x1, Pallas kernels, body(): call(forward_local_body, (bf16((GRP, BLK)), bf16((GRP, 2 * BLK)), f32((GR...  5.19 us
    pallas_call x1, Pallas kernels, body(): call(backward_later_body, (bf16((BLK, 4 * BLK)),) * 4, 10, 5 << 30, 4 <<...  5 us
  transfers between devices with their start and end apart: 23, of which 10 were waited for; matrix products, arithmetic and copies ran while one was open for 1% of the time, Pallas kernels for 27%

profile of v8, /device:TPU:0, one launch (start us, length us, event | category | flops | bytes accessed | tf_op | source)
XLA Modules:
  0.0 137.2 jit_solution(16735759010997520571)
XLA Ops:
  0.6 4.2 %collective-permute-start = (bf16[256,1024]{1,0:T(8,128)(2,1)}, bf16[256,1024]{1,0:T(8,128)(2,1)S(1)}, u32[]{:S(2)}, u32[]{:S(2)}) collective-permute-start(bf16[256,1024]{1,0:T(8,128)(2,1)} %bitcast.5.refs_0_), channel_id=1, source_target_pairs={{0,3},{1,0},{2,1},{3,2},{4,7},{5,4},{6,5},{7,6},{8,11},{9,8},{10,9... | collective-permute-start | bytes 1572872 | tf_op jit(solution)/shard_map/ppermute | solution.py:384
  5.6 3.4 %copy-done = bf16[1024,4096]{1,0:T(8,128)(2,1)S(1)} copy-done((bf16[1024,4096]{1,0:T(8,128)(2,1)S(1)}, bf16[1024,4096]{1,0:T(8,128)(2,1)}, u32[]{:S(2)}) %copy-start) | copy-done | bytes 8388632
  8.9 2.2 %shard_map.76 = (bf16[256,512]{1,0:T(8,128)(2,1)S(1)}, bf16[256,256]{1,0:T(8,128)(2,1)S(1)}, bf16[256,256]{1,0:T(8,128)(2,1)S(1)}, bf16[256,1024]{1,0:T(8,128)(2,1)S(1)}) custom-call(s32[12]{0:T(128)S(1)} %concatenate.3.info, bf16[256,1024]{1,0:T(8,128)(2,1)} %bitcast.5.refs_0_, bf16[1024,4096]{1,0:T(8,128)(2,1)S(1)} %copy-done), custom_call_target="tpu_custom_call" | custom-call | flops 1048576 | bytes 1048576 | tf_op jit(solution)/shard_map/pallas_call | solution.py:421
  11.2 5.1 %collective-permute-done.refs_0_.refs_1_ = bf16[256,1024]{1,0:T(8,128)(2,1)S(1)} collective-permute-done((bf16[256,1024]{1,0:T(8,128)(2,1)}, bf16[256,1024]{1,0:T(8,128)(2,1)S(1)}, u32[]{:S(2)}, u32[]{:S(2)}) %collective-permute-start) | collective-permute-done | bytes 524320 | tf_op jit(solution)/shard_map/ppermute | solution.py:384
  16.3 3.3 %collective-permute-done.1.refs_1_.refs_3_ = bf16[256,1024]{1,0:T(8,128)(2,1)S(1)} collective-permute-done((bf16[256,1024]{1,0:T(8,128)(2,1)}, bf16[256,1024]{1,0:T(8,128)(2,1)S(1)}, u32[]{:S(2)}, u32[]{:S(2)}) %collective-permute-start.1) | collective-permute-done | bytes 524320 | tf_op jit(solution)/shard_map/ppermute | solution.py:384
  21.3 2.4 %shard_map.77 = (bf16[512,512]{1,0:T(8,128)(2,1)S(1)}, bf16[512,256]{1,0:T(8,128)(2,1)S(1)}, bf16[512,256]{1,0:T(8,128)(2,1)S(1)}, bf16[256,1024]{1,0:T(8,128)(2,1)S(1)}, bf16[256,1024]{1,0:T(8,128)(2,1)S(1)}) custom-call(s32[12]{0:T(128)S(1)} %concatenate.3.info, bf16[256,1024]{1,0:T(8,128)(2,1)S(1)} %collective-permute-done.refs_0_.refs_1_, ...), custom_call_target="tpu_custom_call" | custom-call | flops 1048576 | bytes 1048576 | tf_op jit(solution)/shard_map/pallas_call | solution.py:421
  26.7 7.1 %collective-permute-done.2.refs_0_.refs_2_ = bf16[256,1024]{1,0:T(8,128)(2,1)S(1)} collective-permute-done((bf16[256,1024]{1,0:T(8,128)(2,1)}, bf16[256,1024]{1,0:T(8,128)(2,1)S(1)}, u32[]{:S(2)}, u32[]{:S(2)}) %collective-permute-start.2) | collective-permute-done | bytes 524320 | tf_op jit(solution)/shard_map/ppermute | solution.py:384
  33.8 2.1 %collective-permute-start.8 = (bf16[256,512]{1,0:T(8,128)(2,1)S(1)}, bf16[256,512]{1,0:T(8,128)(2,1)S(1)}, u32[]{:S(2)}, u32[]{:S(2)}) collective-permute-start(bf16[256,512]{1,0:T(8,128)(2,1)S(1)} %get-tuple-element.78), channel_id=1, source_target_pairs={{0,2},{1,3},{2,0},{3,1},{4,6},{5,7},{6,4},{7,5},{8,10},{9,11},{10,... | collective-permute-start | bytes 786440 | tf_op jit(solution)/shard_map/ppermute | solution.py:384
  40.3 5.2 %shard_map.79 = (bf16[1024,256]{1,0:T(8,128)(2,1)S(1)}, bf16[1024,512]{1,0:T(8,128)(2,1)S(1)}, f32[1024,256]{1,0:T(8,128)S(1)}) custom-call(s32[12]{0:T(128)S(1)} %concatenate.3.info, bf16[256,256]{1,0:T(8,128)(2,1)S(1)} %get-tuple-element.65.refs_0_, bf16[512,256]{1,0:T(8,128)(2,1)S(1)} %get-tuple-element.66.refs_1_, ...), custom_call_target="tpu_custom_call" | custom-call | flops 5368709120 | bytes 4194304 | tf_op jit(solution)/shard_map/pallas_call | solution.py:435
  47.2 1.7 %shard_map.81 = (f32[1024,256]{1,0:T(8,128)S(1)}, bf16[1024,512]{1,0:T(8,128)(2,1)S(1)}, bf16[1024,256]{1,0:T(8,128)(2,1)S(1)}, bf16[1024,256]{1,0:T(8,128)(2,1)...) custom-call(s32[12]{0:T(128)S(1)} %concatenate.3.info, bf16[1024,256]{1,0:T(8,128)(2,1)S(1)} %get-tuple-element.70.refs_0_, ...), custom_call_target="tpu_custom_call" | custom-call | flops 5368709120 | bytes 4194304 | tf_op jit(solution)/shard_map/pallas_call | solution.py:439
  48.9 2.4 %collective-permute-start.10 = (f32[8,1024]{1,0:T(8,128)S(1)}, f32[8,1024]{1,0:T(8,128)S(1)}, u32[]{:S(2)}, u32[]{:S(2)}) collective-permute-start(f32[8,1024]{1,0:T(8,128)S(1)} %get-tuple-element.86.refs_3_), channel_id=1, source_target_pairs={{0,3},{1,0},{2,1},{3,2},{4,7},{5,4},{6,5},{7,6},{8,11},{9,8},{10,9... | collective-permute-start | bytes 98312 | tf_op jit(solution)/shard_map/ppermute | solution.py:384
  52.4 3.4 %collective-permute-start.3 = (bf16[1024,256]{1,0:T(8,128)(2,1)S(1)}, bf16[1024,256]{1,0:T(8,128)(2,1)S(1)}, u32[]{:S(2)}, u32[]{:S(2)}) collective-permute-start(bf16[1024,256]{1,0:T(8,128)(2,1)S(1)} %get-tuple-element.70.refs_0_), channel_id=1, source_target_pairs={{0,12},{4,0},{8,4},{12,8},{1,13},{5,1},{9,5},{13,9},{2,14},{6,2},{... | collective-permute-start | bytes 1572872 | tf_op jit(solution)/shard_map/ppermute | solution.py:384
  58.4 4.1 %collective-permute-start.13 = (bf16[1024,256]{1,0:T(8,128)(2,1)S(1)}, bf16[1024,256]{1,0:T(8,128)(2,1)S(1)}, u32[]{:S(2)}, u32[]{:S(2)}) collective-permute-start(bf16[1024,256]{1,0:T(8,128)(2,1)S(1)} %get-tuple-element.91.refs_1_), channel_id=1, source_target_pairs={{0,12},{4,0},{8,4},{12,8},{1,13},{5,1},{9,5},{13,9},{2,14},{6,2},{... | collective-permute-start | bytes 1572872 | tf_op jit(solution)/shard_map/ppermute | solution.py:384
  65.5 7.5 %shard_map.83 = (bf16[1024,256]{1,0:T(8,128)(2,1)S(1)}, f32[1024,512]{1,0:T(8,128)S(1)}) custom-call(s32[12]{0:T(128)S(1)} %concatenate.3.info, bf16[1024,256]{1,0:T(8,128)(2,1)S(1)} %get-tuple-element.70.refs_0_, bf16[1024,256]{1,0:T(8,128)(2,1)S(1)} %get-tuple-element.91.refs_1_, bf16[1024,512]{1,0:T(8,128)(2,1)S(1)} %get-tuple-element.93.refs_2_, ...), custom_call_target="tpu_custom_call" | custom-call | flops 1048576 | bytes 1048576 | tf_op jit(solution)/shard_map/pallas_call | solution.py:449
  73.0 2.4 %shard_map.84.refs_13_ = f32[1024,512]{1,0:T(8,128)S(1)} custom-call(s32[12]{0:T(128)S(1)} %concatenate.3.info, bf16[256,1024]{1,0:T(8,128)(2,1)} %bitcast.5.refs_0_, bf16[256,1024]{1,0:T(8,128)(2,1)S(1)} %collective-permute-done.refs_0_.refs_1_, bf16[256,1024]{1,0:T(8,128)(2,1)S(1)} %collective-permute-done.2.refs_0_.refs_2_, ...), custom_call_target="tpu_custom_call" | custom-call | flops 1048576 | bytes 1048576 | tf_op jit(solution)/shard_map/pallas_call | solution.py:453
  75.4 3.5 %collective-permute-done.13.refs_1_ = bf16[1024,256]{1,0:T(8,128)(2,1)S(1)} collective-permute-done((bf16[1024,256]{1,0:T(8,128)(2,1)S(1)}, bf16[1024,256]{1,0:T(8,128)(2,1)S(1)}, u32[]{:S(2)}, u32[]{:S(2)}) %collective-permute-start.13) | collective-permute-done | bytes 524320 | tf_op jit(solution)/shard_map/ppermute | solution.py:384
  78.8 5.0 %shard_map.85 = (bf16[256,1024]{1,0:T(8,128)(2,1)S(1)}, bf16[256,1024]{1,0:T(8,128)(2,1)S(1)}, bf16[256,1024]{1,0:T(8,128)(2,1)S(1)}, bf16[256,1024]{1,0:T(8,128)(2,1)S(1)}) custom-call(s32[12]{0:T(128)S(1)} %concatenate.3.info, bf16[1024,256]{1,0:T(8,128)(2,1)S(1)} %collective-permute-done.3.refs_0_, bf16[1024,256]{1,0:T(8,128)(2,1)S(1)} %collective-permute-done.13.refs_1_, ...), custom_call_target="tpu_custom_call" | custom-call | flops 5368709120 | bytes 4194304 | tf_op jit(solution)/shard_map/pallas_call | solution.py:455
  83.8 2.9 %shard_map.86 = (f32[256,1024]{1,0:T(8,128)S(1)}, bf16[256,1024]{1,0:T(8,128)(2,1)S(1)}, bf16[256,1024]{1,0:T(8,128)(2,1)S(1)}, bf16[256,1024]{1,0:T(8,128)(2,1)S(1)}) custom-call(s32[12]{0:T(128)S(1)} %concatenate.3.info, bf16[256,1024]{1,0:T(8,128)(2,1)S(1)} %get-tuple-element.99.refs_0_.refs_4_, bf16[256,1024]{1,0:T(8,128)(2,1)S(1)} %get-tuple-element.100.refs_1_.refs_5_, ...), custom_call_target="tpu_custom_call" | custom-call | flops 1048576 | bytes 1048576 | tf_op jit(solution)/shard_map/pallas_call | solution.py:458
  89.2 3.7 %shard_map.87 = (bf16[4,128,1280]{2,1,0:T(8,128)(2,1)S(1)}, f32[4,128,1280]{2,1,0:T(8,128)S(1)}) custom-call(s32[12]{0:T(128)S(1)} %concatenate.3.info, bf16[256,1024]{1,0:T(8,128)(2,1)} %bitcast.5.refs_0_, bf16[256,1024]{1,0:T(8,128)(2,1)S(1)} %collective-permute-done.refs_0_.refs_1_, bf16[256,1024]{1,0:T(8,128)(2,1)S(1)} %collective-permute-done.2.refs_0_.refs_2_, ...), custom_call_target="tpu_custom_call" | custom-call | flops 1048576 | bytes 1048576 | tf_op jit(solution)/shard_map/pallas_call | solution.py:463
  93.9 2.4 %collective-permute-start.19 = (bf16[256,1024]{1,0:T(8,128)(2,1)S(1)}, bf16[256,1024]{1,0:T(8,128)(2,1)}, u32[]{:S(2)}, u32[]{:S(2)}) collective-permute-start(bf16[256,1024]{1,0:T(8,128)(2,1)S(1)} %get-tuple-element.112), channel_id=1, source_target_pairs={{0,3},{1,0},{2,1},{3,2},{4,7},{5,4},{6,5},{7,6},{8,11},{9,8},{10,9... | collective-permute-start | bytes 1572872 | tf_op jit(solution)/shard_map/ppermute | solution.py:384
  97.7 4.7 %all-to-all-start = ((bf16[4,128,1280]{2,1,0:T(8,128)(2,1)}), bf16[4,128,1280]{2,1,0:T(8,128)(2,1)S(1)}, u32[]{:S(2)}, u32[]{:S(2)}) async-start(bf16[4,128,1280]{2,1,0:T(8,128)(2,1)} %shard_map.88), calls=%async_computation | async-start | bytes 2621440 | tf_op jit(solution)/shard_map/all_to_all | solution.py:471
  102.4 17.5 %collective-permute-done.18.got_1 = bf16[256,1024]{1,0:T(8,128)(2,1)} collective-permute-done((bf16[256,1024]{1,0:T(8,128)(2,1)S(1)}, bf16[256,1024]{1,0:T(8,128)(2,1)}, u32[]{:S(2)}, u32[]{:S(2)}) %collective-permute-start.18) | collective-permute-done | bytes 524320 | tf_op jit(solution)/shard_map/ppermute | solution.py:384
  123.4 4.3 %all-to-all-start.1 = ((bf16[16,8,1280]{2,1,0:T(8,128)(2,1)}), bf16[16,8,1280]{2,1,0:T(8,128)(2,1)S(1)}, u32[]{:S(2)}, u32[]{:S(2)}) async-start(bf16[16,8,1280]{2,1,0:T(8,128)(2,1)} %bitcast.8), calls=%async_computation.1 | async-start | bytes 655360 | tf_op jit(solution)/shard_map/all_to_all | solution.py:479
  128.6 7.9 %all-to-all-done.1.got = bf16[16,8,1280]{2,1,0:T(8,128)(2,1)S(1)} async-done(((bf16[16,8,1280]{2,1,0:T(8,128)(2,1)}), bf16[16,8,1280]{2,1,0:T(8,128)(2,1)S(1)}, u32[]{:S(2)}, u32[]{:S(2)}) %all-to-all-start.1) | async-done | bytes 327712 | tf_op jit(solution)/shard_map/all_to_all | solution.py:479
  (52 shorter events, 27.9 us)
Async XLA Ops:
  0.6 15.7 %collective-permute-start = (bf16[256,1024]{1,0:T(8,128)(2,1)}, bf16[256,1024]{1,0:T(8,128)(2,1)S(1)}, u32[]{:S(2)}, u32[]{:S(2)}) collective-permute-start(bf16[256,1024]{1,0:T(8,128)(2,1)} %bitcast.5.refs_0_), channel_id=1, source_target_pairs={{0,3},{1,0},{2,1},{3,2},{4,7},{5,4},{6,5},{7,6},{8,11},{9,8},{10,9... | collective-permute-start | bytes 1572872 | tf_op jit(solution)/shard_map/ppermute | solution.py:384
  4.8 14.8 %collective-permute-start.1 = (bf16[256,1024]{1,0:T(8,128)(2,1)}, bf16[256,1024]{1,0:T(8,128)(2,1)S(1)}, u32[]{:S(2)}, u32[]{:S(2)}) collective-permute-start(bf16[256,1024]{1,0:T(8,128)(2,1)} %bitcast.5.refs_0_), channel_id=1, source_target_pairs={{0,1},{1,2},{2,3},{3,0},{4,5},{5,6},{6,7},{7,4},{8,9},{9,10},{10,1... | collective-permute-start | bytes 1572872 | tf_op jit(solution)/shard_map/ppermute | solution.py:384
  8.9 12.3 %copy-start.1 = (bf16[1024,4096]{1,0:T(8,128)(2,1)S(1)}, bf16[1024,4096]{1,0:T(8,128)(2,1)}, u32[]{:S(2)}) copy-start(bf16[1024,4096]{1,0:T(8,128)(2,1)} %refs_4_.1) | copy-start | bytes 25165828
  19.6 14.2 %collective-permute-start.2 = (bf16[256,1024]{1,0:T(8,128)(2,1)}, bf16[256,1024]{1,0:T(8,128)(2,1)S(1)}, u32[]{:S(2)}, u32[]{:S(2)}) collective-permute-start(bf16[256,1024]{1,0:T(8,128)(2,1)} %bitcast.5.refs_0_), channel_id=1, source_target_pairs={{0,2},{1,3},{2,0},{3,1},{4,6},{5,7},{6,4},{7,5},{8,10},{9,11},{10,... | collective-permute-start | bytes 1572872 | tf_op jit(solution)/shard_map/ppermute | solution.py:384
  19.6 19.0 %collective-permute-start.4 = (bf16[256,512]{1,0:T(8,128)(2,1)S(1)}, bf16[256,512]{1,0:T(8,128)(2,1)S(1)}, u32[]{:S(2)}, u32[]{:S(2)}) collective-permute-start(bf16[256,512]{1,0:T(8,128)(2,1)S(1)} %get-tuple-element.61.refs_3_), channel_id=1, source_target_pairs={{0,4},{4,8},{8,12},{12,0},{1,5},{5,9},{9,13},{13,1},{2,6},{6,10},{... | collective-permute-start | bytes 786440 | tf_op jit(solution)/shard_map/ppermute | solution.py:384
  23.7 21.8 %collective-permute-start.5 = (bf16[512,512]{1,0:T(8,128)(2,1)S(1)}, bf16[512,512]{1,0:T(8,128)(2,1)S(1)}, u32[]{:S(2)}, u32[]{:S(2)}) collective-permute-start(bf16[512,512]{1,0:T(8,128)(2,1)S(1)} %get-tuple-element.68.refs_4_), channel_id=1, source_target_pairs={{0,4},{4,8},{8,12},{12,0},{1,5},{5,9},{9,13},{13,1},{2,6},{6,10},{... | collective-permute-start | bytes 1572872 | tf_op jit(solution)/shard_map/ppermute | solution.py:384
  33.8 12.8 %collective-permute-start.7 = (bf16[256,512]{1,0:T(8,128)(2,1)S(1)}, bf16[256,512]{1,0:T(8,128)(2,1)S(1)}, u32[]{:S(2)}, u32[]{:S(2)}) collective-permute-start(bf16[256,512]{1,0:T(8,128)(2,1)S(1)} %get-tuple-element.77), channel_id=1, source_target_pairs={{0,1},{1,2},{2,3},{3,0},{4,5},{5,6},{6,7},{7,4},{8,9},{9,10},{10,1... | collective-permute-start | bytes 786440 | tf_op jit(solution)/shard_map/ppermute | solution.py:384
  33.8 12.8 %collective-permute-start.8 = (bf16[256,512]{1,0:T(8,128)(2,1)S(1)}, bf16[256,512]{1,0:T(8,128)(2,1)S(1)}, u32[]{:S(2)}, u32[]{:S(2)}) collective-permute-start(bf16[256,512]{1,0:T(8,128)(2,1)S(1)} %get-tuple-element.78), channel_id=1, source_target_pairs={{0,2},{1,3},{2,0},{3,1},{4,6},{5,7},{6,4},{7,5},{8,10},{9,11},{10,... | collective-permute-start | bytes 786440 | tf_op jit(solution)/shard_map/ppermute | solution.py:384
  36.0 11.2 %collective-permute-start.9 = (bf16[256,512]{1,0:T(8,128)(2,1)S(1)}, bf16[256,512]{1,0:T(8,128)(2,1)S(1)}, u32[]{:S(2)}, u32[]{:S(2)}) collective-permute-start(bf16[256,512]{1,0:T(8,128)(2,1)S(1)} %get-tuple-element.79), channel_id=1, source_target_pairs={{0,3},{1,0},{2,1},{3,2},{4,7},{5,4},{6,5},{7,6},{8,11},{9,8},{10,9... | collective-permute-start | bytes 786440 | tf_op jit(solution)/shard_map/ppermute | solution.py:384
  38.6 8.6 %collective-permute-start.6 = (bf16[256,512]{1,0:T(8,128)(2,1)S(1)}, bf16[256,512]{1,0:T(8,128)(2,1)S(1)}, u32[]{:S(2)}, u32[]{:S(2)}) collective-permute-start(bf16[256,512]{1,0:T(8,128)(2,1)S(1)} %get-tuple-element.69.refs_5_), channel_id=1, source_target_pairs={{0,4},{4,8},{8,12},{12,0},{1,5},{5,9},{9,13},{13,1},{2,6},{6,10},{... | collective-permute-start | bytes 786440 | tf_op jit(solution)/shard_map/ppermute | solution.py:384
  48.9 6.9 %collective-permute-start.10 = (f32[8,1024]{1,0:T(8,128)S(1)}, f32[8,1024]{1,0:T(8,128)S(1)}, u32[]{:S(2)}, u32[]{:S(2)}) collective-permute-start(f32[8,1024]{1,0:T(8,128)S(1)} %get-tuple-element.86.refs_3_), channel_id=1, source_target_pairs={{0,3},{1,0},{2,1},{3,2},{4,7},{5,4},{6,5},{7,6},{8,11},{9,8},{10,9... | collective-permute-start | bytes 98312 | tf_op jit(solution)/shard_map/ppermute | solution.py:384
  51.3 5.5 %collective-permute-start.11 = (f32[8,1024]{1,0:T(8,128)S(1)}, f32[8,1024]{1,0:T(8,128)S(1)}, u32[]{:S(2)}, u32[]{:S(2)}) collective-permute-start(f32[8,1024]{1,0:T(8,128)S(1)} %get-tuple-element.86.refs_3_), channel_id=1, source_target_pairs={{0,2},{1,3},{2,0},{3,1},{4,6},{5,7},{6,4},{7,5},{8,10},{9,11},{10,... | collective-permute-start | bytes 98312 | tf_op jit(solution)/shard_map/ppermute | solution.py:384
  51.3 5.5 %collective-permute-start.12 = (f32[8,1024]{1,0:T(8,128)S(1)}, f32[8,1024]{1,0:T(8,128)S(1)}, u32[]{:S(2)}, u32[]{:S(2)}) collective-permute-start(f32[8,1024]{1,0:T(8,128)S(1)} %get-tuple-element.86.refs_3_), channel_id=1, source_target_pairs={{0,1},{1,2},{2,3},{3,0},{4,5},{5,6},{6,7},{7,4},{8,9},{9,10},{10,1... | collective-permute-start | bytes 98312 | tf_op jit(solution)/shard_map/ppermute | solution.py:384
  52.4 23.0 %collective-permute-start.3 = (bf16[1024,256]{1,0:T(8,128)(2,1)S(1)}, bf16[1024,256]{1,0:T(8,128)(2,1)S(1)}, u32[]{:S(2)}, u32[]{:S(2)}) collective-permute-start(bf16[1024,256]{1,0:T(8,128)(2,1)S(1)} %get-tuple-element.70.refs_0_), channel_id=1, source_target_pairs={{0,12},{4,0},{8,4},{12,8},{1,13},{5,1},{9,5},{13,9},{2,14},{6,2},{... | collective-permute-start | bytes 1572872 | tf_op jit(solution)/shard_map/ppermute | solution.py:384
  58.4 20.4 %collective-permute-start.13 = (bf16[1024,256]{1,0:T(8,128)(2,1)S(1)}, bf16[1024,256]{1,0:T(8,128)(2,1)S(1)}, u32[]{:S(2)}, u32[]{:S(2)}) collective-permute-start(bf16[1024,256]{1,0:T(8,128)(2,1)S(1)} %get-tuple-element.91.refs_1_), channel_id=1, source_target_pairs={{0,12},{4,0},{8,4},{12,8},{1,13},{5,1},{9,5},{13,9},{2,14},{6,2},{... | collective-permute-start | bytes 1572872 | tf_op jit(solution)/shard_map/ppermute | solution.py:384
  62.5 25.2 %collective-permute-start.14 = (bf16[1024,256]{1,0:T(8,128)(2,1)S(1)}, bf16[1024,256]{1,0:T(8,128)(2,1)S(1)}, u32[]{:S(2)}, u32[]{:S(2)}) collective-permute-start(bf16[1024,256]{1,0:T(8,128)(2,1)S(1)} %get-tuple-element.103.refs_8_), channel_id=1, source_target_pairs={{0,3},{1,0},{2,1},{3,2},{4,7},{5,4},{6,5},{7,6},{8,11},{9,8},{10,9... | collective-permute-start | bytes 1572872 | tf_op jit(solution)/shard_map/ppermute | solution.py:384
  63.4 24.4 %collective-permute-start.15 = (bf16[1024,256]{1,0:T(8,128)(2,1)S(1)}, bf16[1024,256]{1,0:T(8,128)(2,1)S(1)}, u32[]{:S(2)}, u32[]{:S(2)}) collective-permute-start(bf16[1024,256]{1,0:T(8,128)(2,1)S(1)} %get-tuple-element.103.refs_8_), channel_id=1, source_target_pairs={{0,2},{1,3},{2,0},{3,1},{4,6},{5,7},{6,4},{7,5},{8,10},{9,11},{10,... | collective-permute-start | bytes 1572872 | tf_op jit(solution)/shard_map/ppermute | solution.py:384
  64.0 25.2 %collective-permute-start.16 = (bf16[1024,256]{1,0:T(8,128)(2,1)S(1)}, bf16[1024,256]{1,0:T(8,128)(2,1)S(1)}, u32[]{:S(2)}, u32[]{:S(2)}) collective-permute-start(bf16[1024,256]{1,0:T(8,128)(2,1)S(1)} %get-tuple-element.103.refs_8_), channel_id=1, source_target_pairs={{0,1},{1,2},{2,3},{3,0},{4,5},{5,6},{6,7},{7,4},{8,9},{9,10},{10,1... | collective-permute-start | bytes 1572872 | tf_op jit(solution)/shard_map/ppermute | solution.py:384
  92.9 3.4 %collective-permute-start.17 = (bf16[4,128,1280]{2,1,0:T(8,128)(2,1)S(1)}, bf16[4,128,1280]{2,1,0:T(8,128)(2,1)S(1)}, u32[]{:S(2)}, u32[]{:S(2)}) collective-permute-start(bf16[4,128,1280]{2,1,0:T(8,128)(2,1)S(1)} %get-tuple-element.109), channel_id=1, source_target_pairs={{0,16},{16,0},{1,17},{17,1},{2,18},{18,2},{3,19},{19,3},{4,20},{20... | collective-permute-start | bytes 3932168 | tf_op jit(solution)/shard_map/ppermute | solution.py:388
  93.0 26.9 %collective-permute-start.18 = (bf16[256,1024]{1,0:T(8,128)(2,1)S(1)}, bf16[256,1024]{1,0:T(8,128)(2,1)}, u32[]{:S(2)}, u32[]{:S(2)}) collective-permute-start(bf16[256,1024]{1,0:T(8,128)(2,1)S(1)} %get-tuple-element.111), channel_id=1, source_target_pairs={{0,1},{1,2},{2,3},{3,0},{4,5},{5,6},{6,7},{7,4},{8,9},{9,10},{10,1... | collective-permute-start | bytes 1572872 | tf_op jit(solution)/shard_map/ppermute | solution.py:384
  93.9 26.0 %collective-permute-start.19 = (bf16[256,1024]{1,0:T(8,128)(2,1)S(1)}, bf16[256,1024]{1,0:T(8,128)(2,1)}, u32[]{:S(2)}, u32[]{:S(2)}) collective-permute-start(bf16[256,1024]{1,0:T(8,128)(2,1)S(1)} %get-tuple-element.112), channel_id=1, source_target_pairs={{0,3},{1,0},{2,1},{3,2},{4,7},{5,4},{6,5},{7,6},{8,11},{9,8},{10,9... | collective-permute-start | bytes 1572872 | tf_op jit(solution)/shard_map/ppermute | solution.py:384
  96.3 31.4 %collective-permute-start.20 = (bf16[256,1024]{1,0:T(8,128)(2,1)S(1)}, bf16[256,1024]{1,0:T(8,128)(2,1)S(1)}, u32[]{:S(2)}, u32[]{:S(2)}) collective-permute-start(bf16[256,1024]{1,0:T(8,128)(2,1)S(1)} %get-tuple-element.116), channel_id=1, source_target_pairs={{0,2},{1,3},{2,0},{3,1},{4,6},{5,7},{6,4},{7,5},{8,10},{9,11},{10,... | collective-permute-start | bytes 1572872 | tf_op jit(solution)/shard_map/ppermute | solution.py:384
  97.7 24.8 %all-to-all-start = ((bf16[4,128,1280]{2,1,0:T(8,128)(2,1)}), bf16[4,128,1280]{2,1,0:T(8,128)(2,1)S(1)}, u32[]{:S(2)}, u32[]{:S(2)}) async-start(bf16[4,128,1280]{2,1,0:T(8,128)(2,1)} %shard_map.88), calls=%async_computation | async-start | bytes 2621440 | tf_op jit(solution)/shard_map/all_to_all | solution.py:471
  123.4 13.2 %all-to-all-start.1 = ((bf16[16,8,1280]{2,1,0:T(8,128)(2,1)}), bf16[16,8,1280]{2,1,0:T(8,128)(2,1)S(1)}, u32[]{:S(2)}, u32[]{:S(2)}) async-start(bf16[16,8,1280]{2,1,0:T(8,128)(2,1)} %bitcast.8), calls=%async_computation.1 | async-start | bytes 655360 | tf_op jit(solution)/shard_map/all_to_all | solution.py:479
  (5 other events, 17.1 us)

commit v9 on v8

--- a/solution.py
+++ b/solution.py
@@ -247,16 +247,11 @@
     out[...] = (keep[...] + got[...].astype(F32)).astype(BF16)
 
 
-def add_x_body(got, total):
-    part = got[0].astype(F32) + got[1].astype(F32) + got[2].astype(F32) + got[3].astype(F32)
-    total[...] = part.astype(BF16)
-
-
 def last_sum_body(got, grad_w_in, grad_w_out):
     for z in range(4):
         part = got[z].astype(F32)
-        for y in range(1, 4):
-            part = part + got[y * 4 + z].astype(F32)
+        for xy in range(1, 16):
+            part = part + got[xy * 4 + z].astype(F32)
         part = part.astype(BF16)
         for n, to in enumerate((0, 2, 1, 3)):
             at = to * D + z * BLK
@@ -372,12 +367,9 @@
         outs[k][...] = total.astype(outs[k].dtype)
 
 
-def add_near_body(own, got_1, got_3, out):
-    out[...] = own[...] + got_1[...].astype(F32) + got_3[...].astype(F32)
-
-
-def add_far_body(near, got_2, out):
-    out[...] = (near[...] + got_2[...].astype(F32)).astype(BF16)
+def add_rows_body(own, got_1, got_2, got_3, out):
+    total = own[...] + got_1[...].astype(F32) + got_2[...].astype(F32) + got_3[...].astype(F32)
+    out[...] = total.astype(BF16)
 
 
 def along(x, axis, d):
@@ -413,11 +405,15 @@
     near = along(ev, "z", -1), along(ev, "z", 1)
     evs = [ev, near[0], None, near[1]]
     kvs, qs, gs, dsigs, kv_prevs = [], [], [], [None] * 4, []
+    ggs = call(grad_gated_body, (bf16((BLK, 2 * BLK)),) * 4, 2, 1 << 20, 1 << 20)(info, cot, w_out)
     for blocks in ((0,), (1, 3), (2,)):
         n = len(blocks)
         if blocks == (1, 3):
             ev_far, *near, _ = lax.optimization_barrier((ev, *near, kvs[0]))
             evs = [ev, near[0], along(ev_far, "z", 2), near[1]]
+        if blocks == (2,):
+            *ggs, far = lax.optimization_barrier((*ggs, evs[2]))
+            ggs, evs[2] = exchange(ggs, "z"), far
         kv, q, g, *dsig = call(
             project_body,
             (bf16((n * BLK, 2 * BLK)), bf16((n * BLK, BLK)), bf16((n * BLK, BLK))) + (bf16((BLK, 4 * BLK)),) * n,
@@ -429,9 +425,6 @@
         for b, d in zip(blocks, dsig):
             dsigs[b] = d
         kv_prevs.append(along(kv, "y", 1))
-    ggs = call(grad_gated_body, (bf16((BLK, 2 * BLK)),) * 4, 2, 1 << 20, 1 << 20)(info, cot, w_out)
-    *ggs, _ = lax.optimization_barrier((*ggs, evs[2]))
-    ggs = exchange(ggs, "z")
     q, kv, att = call(
         forward_local_body, (bf16((GRP, BLK)), bf16((GRP, 2 * BLK)), f32((GRP, BLK))), 6, 5 << 30, 4 << 20
     )(info, *qs, *kvs)
@@ -468,15 +461,8 @@
     mine = call(
         add_core_body, bf16((4, 128, 5 * BLK)), 2, 1 << 20, 1 << 20, scalars=0
     )(keep, swap(send))
-    sums = lax.all_to_all(mine, "x", 0, 0)
-    near_rows = call(
-        add_near_body, f32((BLK, D)), 3, 40 << 30, 4 << 20, scalars=0
-    )(partial[0], partial[1], partial[3])
-    sums, near_rows = lax.optimization_barrier((sums, near_rows))
-    total = call(add_x_body, bf16((128, 5 * BLK)), 1, 1 << 20, 1 << 20, scalars=0)(sums)
-    _, near_rows = lax.optimization_barrier((total, near_rows))
-    grad_events = call(add_far_body, bf16((BLK, D)), 2, 1 << 20, 4 << 20, scalars=0)(near_rows, partial[2])
-    got = lax.all_to_all(total.reshape(16, 8, 5 * BLK), ("y", "z"), 0, 0)
+    got = lax.all_to_all(mine.reshape(64, 8, 5 * BLK), ("x", "y", "z"), 0, 0)
+    grad_events = call(add_rows_body, bf16((BLK, D)), 4, 40 << 30, 4 << 20, scalars=0)(*partial)
     grad_w_in, grad_w_out = call(last_sum_body, (bf16((8, 4 * D)), bf16((8, D))), 1, 1 << 20, 1 << 20, scalars=0)(got)
     return grad_events[None], grad_w_in, grad_w_out
 

time: 139 us -> 139 us (level); the launches traced: 137 us -> 139 us
  waiting for transfers between devices: 48.7 us -> 53 us
  local copies, waits for them, and re-layouts: 6.32 us -> 4.13 us
  Pallas kernels: 42.8 us -> 41.1 us
  starting transfers between devices: 38.7 us -> 40.3 us
    ppermute x20, waiting for transfers between devices: 40.7 us -> 53 us  [along(): return lax.ppermute(x, axis, [(i, (i + d) % 4) for i in range(4)])]
    all_to_all x2 -> x1, waiting for transfers between devices: 7.93 us -> 0.01 us  [body(): got = lax.all_to_all(mine.reshape(64, 8, 5 * BLK), ('x', 'y', 'z'), 0, 0)]
    pallas_call x1, Pallas kernels: 5 us -> 1.17 us  [body(): call(backward_later_body, (bf16((BLK, 4 * BLK)),) * 4, 10, 5 << 30, 4 <<...]
    ppermute x20, starting transfers between devices: 29.6 us -> 32.9 us  [along(): return lax.ppermute(x, axis, [(i, (i + d) % 4) for i in range(4)])]
    unnamed x12 -> x8, local copies, waits for them, and re-layouts: 5.58 us -> 3.39 us
    all_to_all x2 -> x1, starting transfers between devices: 9.02 us -> 7.28 us  [body(): got = lax.all_to_all(mine.reshape(64, 8, 5 * BLK), ('x', 'y', 'z'), 0, 0)]
    pallas_call x1, Pallas kernels: 7.53 us -> 9.15 us  [body(): call(backward_local_body, (bf16((GRP, BLK)), f32((GRP, 2 * BLK))), 8, 1 <...]
    pallas_call x3 -> x1, Pallas kernels: 3.13 us -> 2.37 us  [body(): call(add_rows_body, bf16((BLK, D)), 4, 40 << 30, 4 << 20, scalars=0)]
  transfers between devices with their start and end apart: 23 -> 22, of which waited for: 10 -> 9; matrix products, arithmetic and copies ran while one was open for 1% -> 1% of each run, Pallas kernels for 27% -> 25%
where the time goes in v9:
time: 139 us
  waiting for transfers between devices  53 us (38%)
  Pallas kernels  41.1 us (30%)
  starting transfers between devices  40.3 us (29%)
  local copies, waits for them, and re-layouts  4.13 us (3%)
    ppermute x20, waiting for transfers between devices, along(): return lax.ppermute(x, axis, [(i, (i + d) % 4) for i in range(4)])  53 us
    ppermute x20, starting transfers between devices, along(): return lax.ppermute(x, axis, [(i, (i + d) % 4) for i in range(4)])  32.9 us
    pallas_call x1, Pallas kernels, body(): call(backward_local_body, (bf16((GRP, BLK)), f32((GRP, 2 * BLK))), 8, 1 <...  9.15 us
    all_to_all x1, starting transfers between devices, body(): got = lax.all_to_all(mine.reshape(64, 8, 5 * BLK), ('x', 'y', 'z'), 0, 0)  7.28 us
    pallas_call x1, Pallas kernels, body(): call(forward_local_body, (bf16((GRP, BLK)), bf16((GRP, 2 * BLK)), f32((GR...  6.3 us
    pallas_call x3, Pallas kernels, body(): call(project_body, (bf16((n * BLK, 2 * BLK)), bf16((n * BLK, BLK)), bf16(...  6.22 us
    pallas_call x1, Pallas kernels, body(): call(late_weights_body, (bf16((4, 128, 5 * BLK)), f32((4, 128, 5 * BLK)))...  3.68 us
    unnamed x8, local copies, waits for them, and re-layouts  3.39 us
  transfers between devices with their start and end apart: 22, of which 9 were waited for; matrix products, arithmetic and copies ran while one was open for 1% of the time, Pallas kernels for 25%

profile of v9, /device:TPU:0, one launch (start us, length us, event | category | flops | bytes accessed | tf_op | source)
XLA Modules:
  0.0 139.2 jit_solution(59175645960979583)
XLA Ops:
  0.6 4.2 %collective-permute-start = (bf16[256,1024]{1,0:T(8,128)(2,1)}, bf16[256,1024]{1,0:T(8,128)(2,1)S(1)}, u32[]{:S(2)}, u32[]{:S(2)}) collective-permute-start(bf16[256,1024]{1,0:T(8,128)(2,1)} %bitcast.5.refs_0_), channel_id=1, source_target_pairs={{0,3},{1,0},{2,1},{3,2},{4,7},{5,4},{6,5},{7,6},{8,11},{9,8},{10,9... | collective-permute-start | bytes 1572872 | tf_op jit(solution)/shard_map/ppermute | solution.py:376
  5.6 3.4 %copy-done = bf16[1024,4096]{1,0:T(8,128)(2,1)S(1)} copy-done((bf16[1024,4096]{1,0:T(8,128)(2,1)S(1)}, bf16[1024,4096]{1,0:T(8,128)(2,1)}, u32[]{:S(2)}) %copy-start) | copy-done | bytes 8388632
  8.9 2.2 %shard_map.76 = (bf16[256,512]{1,0:T(8,128)(2,1)S(1)}, bf16[256,256]{1,0:T(8,128)(2,1)S(1)}, bf16[256,256]{1,0:T(8,128)(2,1)S(1)}, bf16[256,1024]{1,0:T(8,128)(2,1)S(1)}) custom-call(s32[12]{0:T(128)S(1)} %concatenate.3.info, bf16[256,1024]{1,0:T(8,128)(2,1)} %bitcast.5.refs_0_, bf16[1024,4096]{1,0:T(8,128)(2,1)S(1)} %copy-done), custom_call_target="tpu_custom_call" | custom-call | flops 1048576 | bytes 1048576 | tf_op jit(solution)/shard_map/pallas_call | solution.py:417
  11.2 5.1 %collective-permute-done.refs_0_.refs_1_ = bf16[256,1024]{1,0:T(8,128)(2,1)S(1)} collective-permute-done((bf16[256,1024]{1,0:T(8,128)(2,1)}, bf16[256,1024]{1,0:T(8,128)(2,1)S(1)}, u32[]{:S(2)}, u32[]{:S(2)}) %collective-permute-start) | collective-permute-done | bytes 524320 | tf_op jit(solution)/shard_map/ppermute | solution.py:376
  16.3 3.3 %collective-permute-done.1.refs_1_.refs_3_ = bf16[256,1024]{1,0:T(8,128)(2,1)S(1)} collective-permute-done((bf16[256,1024]{1,0:T(8,128)(2,1)}, bf16[256,1024]{1,0:T(8,128)(2,1)S(1)}, u32[]{:S(2)}, u32[]{:S(2)}) %collective-permute-start.1) | collective-permute-done | bytes 524320 | tf_op jit(solution)/shard_map/ppermute | solution.py:376
  21.3 2.4 %shard_map.77 = (bf16[512,512]{1,0:T(8,128)(2,1)S(1)}, bf16[512,256]{1,0:T(8,128)(2,1)S(1)}, bf16[512,256]{1,0:T(8,128)(2,1)S(1)}, bf16[256,1024]{1,0:T(8,128)(2,1)S(1)}, bf16[256,1024]{1,0:T(8,128)(2,1)S(1)}) custom-call(s32[12]{0:T(128)S(1)} %concatenate.3.info, bf16[256,1024]{1,0:T(8,128)(2,1)S(1)} %collective-permute-done.refs_0_.refs_1_, ...), custom_call_target="tpu_custom_call" | custom-call | flops 1048576 | bytes 1048576 | tf_op jit(solution)/shard_map/pallas_call | solution.py:417
  26.7 7.1 %collective-permute-done.2.refs_0_.refs_2_ = bf16[256,1024]{1,0:T(8,128)(2,1)S(1)} collective-permute-done((bf16[256,1024]{1,0:T(8,128)(2,1)}, bf16[256,1024]{1,0:T(8,128)(2,1)S(1)}, u32[]{:S(2)}, u32[]{:S(2)}) %collective-permute-start.2) | collective-permute-done | bytes 524320 | tf_op jit(solution)/shard_map/ppermute | solution.py:376
  37.0 2.1 %collective-permute-start.8 = (bf16[256,512]{1,0:T(8,128)(2,1)S(1)}, bf16[256,512]{1,0:T(8,128)(2,1)S(1)}, u32[]{:S(2)}, u32[]{:S(2)}) collective-permute-start(bf16[256,512]{1,0:T(8,128)(2,1)S(1)} %get-tuple-element.77), channel_id=1, source_target_pairs={{0,2},{1,3},{2,0},{3,1},{4,6},{5,7},{6,4},{7,5},{8,10},{9,11},{10,... | collective-permute-start | bytes 786440 | tf_op jit(solution)/shard_map/ppermute | solution.py:376
  40.3 6.3 %shard_map.80 = (bf16[1024,256]{1,0:T(8,128)(2,1)S(1)}, bf16[1024,512]{1,0:T(8,128)(2,1)S(1)}, f32[1024,256]{1,0:T(8,128)S(1)}) custom-call(s32[12]{0:T(128)S(1)} %concatenate.3.info, bf16[256,256]{1,0:T(8,128)(2,1)S(1)} %get-tuple-element.59.refs_0_, bf16[512,256]{1,0:T(8,128)(2,1)S(1)} %get-tuple-element.63.refs_1_, ...), custom_call_target="tpu_custom_call" | custom-call | flops 5368709120 | bytes 4194304 | tf_op jit(solution)/shard_map/pallas_call | solution.py:428
  46.6 2.9 %collective-permute-done.7.refs_6_ = bf16[256,512]{1,0:T(8,128)(2,1)S(1)} collective-permute-done((bf16[256,512]{1,0:T(8,128)(2,1)S(1)}, bf16[256,512]{1,0:T(8,128)(2,1)S(1)}, u32[]{:S(2)}, u32[]{:S(2)}) %collective-permute-start.7) | collective-permute-done | bytes 262176 | tf_op jit(solution)/shard_map/ppermute | solution.py:376
  50.1 1.7 %shard_map.81 = (f32[1024,256]{1,0:T(8,128)S(1)}, bf16[1024,512]{1,0:T(8,128)(2,1)S(1)}, bf16[1024,256]{1,0:T(8,128)(2,1)S(1)}, bf16[1024,256]{1,0:T(8,128)(2,1)...) custom-call(s32[12]{0:T(128)S(1)} %concatenate.3.info, bf16[1024,256]{1,0:T(8,128)(2,1)S(1)} %get-tuple-element.73.refs_0_, ...), custom_call_target="tpu_custom_call" | custom-call | flops 5368709120 | bytes 4194304 | tf_op jit(solution)/shard_map/pallas_call | solution.py:432
  51.8 2.4 %collective-permute-start.10 = (f32[8,1024]{1,0:T(8,128)S(1)}, f32[8,1024]{1,0:T(8,128)S(1)}, u32[]{:S(2)}, u32[]{:S(2)}) collective-permute-start(f32[8,1024]{1,0:T(8,128)S(1)} %get-tuple-element.85.refs_3_), channel_id=1, source_target_pairs={{0,3},{1,0},{2,1},{3,2},{4,7},{5,4},{6,5},{7,6},{8,11},{9,8},{10,9... | collective-permute-start | bytes 98312 | tf_op jit(solution)/shard_map/ppermute | solution.py:376
  55.2 5.1 %collective-permute-start.3 = (bf16[1024,256]{1,0:T(8,128)(2,1)S(1)}, bf16[1024,256]{1,0:T(8,128)(2,1)S(1)}, u32[]{:S(2)}, u32[]{:S(2)}) collective-permute-start(bf16[1024,256]{1,0:T(8,128)(2,1)S(1)} %get-tuple-element.73.refs_0_), channel_id=1, source_target_pairs={{0,12},{4,0},{8,4},{12,8},{1,13},{5,1},{9,5},{13,9},{2,14},{6,2},{... | collective-permute-start | bytes 1572872 | tf_op jit(solution)/shard_map/ppermute | solution.py:376
  60.3 1.7 %shard_map.82 = (bf16[1024,256]{1,0:T(8,128)(2,1)S(1)}, bf16[1024,256]{1,0:T(8,128)(2,1)S(1)}, bf16[1024,256]{1,0:T(8,128)(2,1)S(1)}) custom-call(s32[12]{0:T(128)S(1)} %concatenate.3.info, f32[1024,256]{1,0:T(8,128)S(1)} %get-tuple-element.82.refs_0_, bf16[1024,256]{1,0:T(8,128)(2,1)S(1)} %get-tuple-element.83.refs_1_, ...), custom_call_target="tpu_custom_call" | custom-call | flops 1073741824 | bytes 4194304 | tf_op jit(solution)/shard_map/pallas_call | solution.py:437
  62.0 4.6 %collective-permute-start.13 = (bf16[1024,256]{1,0:T(8,128)(2,1)S(1)}, bf16[1024,256]{1,0:T(8,128)(2,1)S(1)}, u32[]{:S(2)}, u32[]{:S(2)}) collective-permute-start(bf16[1024,256]{1,0:T(8,128)(2,1)S(1)} %get-tuple-element.90.refs_1_), channel_id=1, source_target_pairs={{0,12},{4,0},{8,4},{12,8},{1,13},{5,1},{9,5},{13,9},{2,14},{6,2},{... | collective-permute-start | bytes 1572872 | tf_op jit(solution)/shard_map/ppermute | solution.py:376
  69.9 9.2 %shard_map.83 = (bf16[1024,256]{1,0:T(8,128)(2,1)S(1)}, f32[1024,512]{1,0:T(8,128)S(1)}) custom-call(s32[12]{0:T(128)S(1)} %concatenate.3.info, bf16[1024,256]{1,0:T(8,128)(2,1)S(1)} %get-tuple-element.73.refs_0_, bf16[1024,256]{1,0:T(8,128)(2,1)S(1)} %get-tuple-element.90.refs_1_, bf16[1024,512]{1,0:T(8,128)(2,1)S(1)} %get-tuple-element.92.refs_2_, ...), custom_call_target="tpu_custom_call" | custom-call | flops 1048576 | bytes 1048576 | tf_op jit(solution)/shard_map/pallas_call | solution.py:442
  79.1 2.4 %shard_map.84.refs_13_ = f32[1024,512]{1,0:T(8,128)S(1)} custom-call(s32[12]{0:T(128)S(1)} %concatenate.3.info, bf16[256,1024]{1,0:T(8,128)(2,1)} %bitcast.5.refs_0_, bf16[256,1024]{1,0:T(8,128)(2,1)S(1)} %collective-permute-done.refs_0_.refs_1_, bf16[256,1024]{1,0:T(8,128)(2,1)S(1)} %collective-permute-done.2.refs_0_.refs_2_, ...), custom_call_target="tpu_custom_call" | custom-call | flops 1048576 | bytes 1048576 | tf_op jit(solution)/shard_map/pallas_call | solution.py:446
  82.6 3.0 %shard_map.86 = (f32[256,1024]{1,0:T(8,128)S(1)}, bf16[256,1024]{1,0:T(8,128)(2,1)}, bf16[256,1024]{1,0:T(8,128)(2,1)S(1)}, bf16[256,1024]{1,0:T(8,128)(2,1)S(1)}) custom-call(s32[12]{0:T(128)S(1)} %concatenate.3.info, bf16[256,1024]{1,0:T(8,128)(2,1)S(1)} %get-tuple-element.99.refs_0_.refs_4_, bf16[256,1024]{1,0:T(8,128)(2,1)S(1)} %get-tuple-element.100.refs_1_.refs_5_, ...), custom_call_target="tpu_custom_call" | custom-call | flops 1048576 | bytes 1048576 | tf_op jit(solution)/shard_map/pallas_call | solution.py:451
  85.6 5.5 %collective-permute-done.19.refs_11_ = bf16[1024,256]{1,0:T(8,128)(2,1)S(1)} collective-permute-done((bf16[1024,256]{1,0:T(8,128)(2,1)S(1)}, bf16[1024,256]{1,0:T(8,128)(2,1)S(1)}, u32[]{:S(2)}, u32[]{:S(2)}) %collective-permute-start.19) | collective-permute-done | bytes 524320 | tf_op jit(solution)/shard_map/ppermute | solution.py:376
  91.2 3.7 %shard_map.88 = (bf16[4,128,1280]{2,1,0:T(8,128)(2,1)S(1)}, f32[4,128,1280]{2,1,0:T(8,128)S(1)}) custom-call(s32[12]{0:T(128)S(1)} %concatenate.3.info, bf16[256,1024]{1,0:T(8,128)(2,1)} %bitcast.5.refs_0_, bf16[256,1024]{1,0:T(8,128)(2,1)S(1)} %collective-permute-done.refs_0_.refs_1_, bf16[256,1024]{1,0:T(8,128)(2,1)S(1)} %collective-permute-done.2.refs_0_.refs_2_, ...), custom_call_target="tpu_custom_call" | custom-call | flops 1048576 | bytes 1048576 | tf_op jit(solution)/shard_map/pallas_call | solution.py:456
  97.1 2.0 %collective-permute-start.16 = (bf16[256,1024]{1,0:T(8,128)(2,1)S(1)}, bf16[256,1024]{1,0:T(8,128)(2,1)}, u32[]{:S(2)}, u32[]{:S(2)}) collective-permute-start(bf16[256,1024]{1,0:T(8,128)(2,1)S(1)} %get-tuple-element.107), channel_id=1, source_target_pairs={{0,3},{1,0},{2,1},{3,2},{4,7},{5,4},{6,5},{7,6},{8,11},{9,8},{10,9... | collective-permute-start | bytes 1572872 | tf_op jit(solution)/shard_map/ppermute | solution.py:376
  100.4 7.3 %all-to-all-start = ((bf16[64,8,1280]{2,1,0:T(8,128)(2,1)}), bf16[64,8,1280]{2,1,0:T(8,128)(2,1)S(1)}, u32[]{:S(2)}, u32[]{:S(2)}) async-start(bf16[64,8,1280]{2,1,0:T(8,128)(2,1)} %bitcast.8), calls=%async_computation | async-start | bytes 2621440 | tf_op jit(solution)/shard_map/all_to_all | solution.py:464
  107.7 27.9 %collective-permute-done.14.got_1 = bf16[256,1024]{1,0:T(8,128)(2,1)} collective-permute-done((bf16[256,1024]{1,0:T(8,128)(2,1)}, bf16[256,1024]{1,0:T(8,128)(2,1)}, u32[]{:S(2)}, u32[]{:S(2)}) %collective-permute-start.14) | collective-permute-done | bytes 524320 | tf_op jit(solution)/shard_map/ppermute | solution.py:376
  136.1 2.4 %shard_map.87 = bf16[256,1024]{1,0:T(8,128)(2,1)} custom-call(f32[256,1024]{1,0:T(8,128)S(1)} %get-tuple-element.104.own, bf16[256,1024]{1,0:T(8,128)(2,1)} %collective-permute-done.14.got_1, bf16[256,1024]{1,0:T(8,128)(2,1)} %collective-permute-done.15.got_2, bf16[256,1024]{1,0:T(8,128)(2,1)} %collective-permute-done.16.got_3), custom_call_target="tpu_custom_call" | custom-call | flops 42949672960 | bytes 4194304 | tf_op jit(solution)/shard_map/pallas_call | solution.py:465
  (44 shorter events, 20.7 us)
Async XLA Ops:
  0.6 15.7 %collective-permute-start = (bf16[256,1024]{1,0:T(8,128)(2,1)}, bf16[256,1024]{1,0:T(8,128)(2,1)S(1)}, u32[]{:S(2)}, u32[]{:S(2)}) collective-permute-start(bf16[256,1024]{1,0:T(8,128)(2,1)} %bitcast.5.refs_0_), channel_id=1, source_target_pairs={{0,3},{1,0},{2,1},{3,2},{4,7},{5,4},{6,5},{7,6},{8,11},{9,8},{10,9... | collective-permute-start | bytes 1572872 | tf_op jit(solution)/shard_map/ppermute | solution.py:376
  4.8 14.8 %collective-permute-start.1 = (bf16[256,1024]{1,0:T(8,128)(2,1)}, bf16[256,1024]{1,0:T(8,128)(2,1)S(1)}, u32[]{:S(2)}, u32[]{:S(2)}) collective-permute-start(bf16[256,1024]{1,0:T(8,128)(2,1)} %bitcast.5.refs_0_), channel_id=1, source_target_pairs={{0,1},{1,2},{2,3},{3,0},{4,5},{5,6},{6,7},{7,4},{8,9},{9,10},{10,1... | collective-permute-start | bytes 1572872 | tf_op jit(solution)/shard_map/ppermute | solution.py:376
  8.9 12.3 %copy-start.1 = (bf16[1024,4096]{1,0:T(8,128)(2,1)S(1)}, bf16[1024,4096]{1,0:T(8,128)(2,1)}, u32[]{:S(2)}) copy-start(bf16[1024,4096]{1,0:T(8,128)(2,1)} %refs_4_.1) | copy-start | bytes 25165828
  19.6 5.8 %copy-start.3 = (bf16[1,256,1024]{2,1,0:T(8,128)(2,1)S(1)}, bf16[1,256,1024]{2,1,0:T(8,128)(2,1)}, u32[]{:S(2)}) copy-start(bf16[1,256,1024]{2,1,0:T(8,128)(2,1)} %param.6) | copy-start | bytes 1572868
  19.6 14.2 %collective-permute-start.2 = (bf16[256,1024]{1,0:T(8,128)(2,1)}, bf16[256,1024]{1,0:T(8,128)(2,1)S(1)}, u32[]{:S(2)}, u32[]{:S(2)}) collective-permute-start(bf16[256,1024]{1,0:T(8,128)(2,1)} %bitcast.5.refs_0_), channel_id=1, source_target_pairs={{0,2},{1,3},{2,0},{3,1},{4,6},{5,7},{6,4},{7,5},{8,10},{9,11},{10,... | collective-permute-start | bytes 1572872 | tf_op jit(solution)/shard_map/ppermute | solution.py:376
  19.6 19.5 %collective-permute-start.4 = (bf16[256,512]{1,0:T(8,128)(2,1)S(1)}, bf16[256,512]{1,0:T(8,128)(2,1)S(1)}, u32[]{:S(2)}, u32[]{:S(2)}) collective-permute-start(bf16[256,512]{1,0:T(8,128)(2,1)S(1)} %get-tuple-element.60.refs_3_), channel_id=1, source_target_pairs={{0,4},{4,8},{8,12},{12,0},{1,5},{5,9},{9,13},{13,1},{2,6},{6,10},{... | collective-permute-start | bytes 786440 | tf_op jit(solution)/shard_map/ppermute | solution.py:376
  23.7 22.9 %collective-permute-start.5 = (bf16[512,512]{1,0:T(8,128)(2,1)S(1)}, bf16[512,512]{1,0:T(8,128)(2,1)S(1)}, u32[]{:S(2)}, u32[]{:S(2)}) collective-permute-start(bf16[512,512]{1,0:T(8,128)(2,1)S(1)} %get-tuple-element.71.refs_4_), channel_id=1, source_target_pairs={{0,4},{4,8},{8,12},{12,0},{1,5},{5,9},{9,13},{13,1},{2,6},{6,10},{... | collective-permute-start | bytes 1572872 | tf_op jit(solution)/shard_map/ppermute | solution.py:376
  35.4 11.2 %collective-permute-start.6 = (bf16[256,512]{1,0:T(8,128)(2,1)S(1)}, bf16[256,512]{1,0:T(8,128)(2,1)S(1)}, u32[]{:S(2)}, u32[]{:S(2)}) collective-permute-start(bf16[256,512]{1,0:T(8,128)(2,1)S(1)} %get-tuple-element.72.refs_5_), channel_id=1, source_target_pairs={{0,4},{4,8},{8,12},{12,0},{1,5},{5,9},{9,13},{13,1},{2,6},{6,10},{... | collective-permute-start | bytes 786440 | tf_op jit(solution)/shard_map/ppermute | solution.py:376
  37.0 12.5 %collective-permute-start.7 = (bf16[256,512]{1,0:T(8,128)(2,1)S(1)}, bf16[256,512]{1,0:T(8,128)(2,1)S(1)}, u32[]{:S(2)}, u32[]{:S(2)}) collective-permute-start(bf16[256,512]{1,0:T(8,128)(2,1)S(1)} %get-tuple-element.76), channel_id=1, source_target_pairs={{0,1},{1,2},{2,3},{3,0},{4,5},{5,6},{6,7},{7,4},{8,9},{9,10},{10,1... | collective-permute-start | bytes 786440 | tf_op jit(solution)/shard_map/ppermute | solution.py:376
  37.0 12.5 %collective-permute-start.8 = (bf16[256,512]{1,0:T(8,128)(2,1)S(1)}, bf16[256,512]{1,0:T(8,128)(2,1)S(1)}, u32[]{:S(2)}, u32[]{:S(2)}) collective-permute-start(bf16[256,512]{1,0:T(8,128)(2,1)S(1)} %get-tuple-element.77), channel_id=1, source_target_pairs={{0,2},{1,3},{2,0},{3,1},{4,6},{5,7},{6,4},{7,5},{8,10},{9,11},{10,... | collective-permute-start | bytes 786440 | tf_op jit(solution)/shard_map/ppermute | solution.py:376
  39.2 11.0 %collective-permute-start.9 = (bf16[256,512]{1,0:T(8,128)(2,1)S(1)}, bf16[256,512]{1,0:T(8,128)(2,1)S(1)}, u32[]{:S(2)}, u32[]{:S(2)}) collective-permute-start(bf16[256,512]{1,0:T(8,128)(2,1)S(1)} %get-tuple-element.78), channel_id=1, source_target_pairs={{0,3},{1,0},{2,1},{3,2},{4,7},{5,4},{6,5},{7,6},{8,11},{9,8},{10,9... | collective-permute-start | bytes 786440 | tf_op jit(solution)/shard_map/ppermute | solution.py:376
  51.8 8.4 %collective-permute-start.10 = (f32[8,1024]{1,0:T(8,128)S(1)}, f32[8,1024]{1,0:T(8,128)S(1)}, u32[]{:S(2)}, u32[]{:S(2)}) collective-permute-start(f32[8,1024]{1,0:T(8,128)S(1)} %get-tuple-element.85.refs_3_), channel_id=1, source_target_pairs={{0,3},{1,0},{2,1},{3,2},{4,7},{5,4},{6,5},{7,6},{8,11},{9,8},{10,9... | collective-permute-start | bytes 98312 | tf_op jit(solution)/shard_map/ppermute | solution.py:376
  54.2 6.1 %collective-permute-start.11 = (f32[8,1024]{1,0:T(8,128)S(1)}, f32[8,1024]{1,0:T(8,128)S(1)}, u32[]{:S(2)}, u32[]{:S(2)}) collective-permute-start(f32[8,1024]{1,0:T(8,128)S(1)} %get-tuple-element.85.refs_3_), channel_id=1, source_target_pairs={{0,2},{1,3},{2,0},{3,1},{4,6},{5,7},{6,4},{7,5},{8,10},{9,11},{10,... | collective-permute-start | bytes 98312 | tf_op jit(solution)/shard_map/ppermute | solution.py:376
  54.2 6.1 %collective-permute-start.12 = (f32[8,1024]{1,0:T(8,128)S(1)}, f32[8,1024]{1,0:T(8,128)S(1)}, u32[]{:S(2)}, u32[]{:S(2)}) collective-permute-start(f32[8,1024]{1,0:T(8,128)S(1)} %get-tuple-element.85.refs_3_), channel_id=1, source_target_pairs={{0,1},{1,2},{2,3},{3,0},{4,5},{5,6},{6,7},{7,4},{8,9},{9,10},{10,1... | collective-permute-start | bytes 98312 | tf_op jit(solution)/shard_map/ppermute | solution.py:376
  55.2 26.3 %collective-permute-start.3 = (bf16[1024,256]{1,0:T(8,128)(2,1)S(1)}, bf16[1024,256]{1,0:T(8,128)(2,1)S(1)}, u32[]{:S(2)}, u32[]{:S(2)}) collective-permute-start(bf16[1024,256]{1,0:T(8,128)(2,1)S(1)} %get-tuple-element.73.refs_0_), channel_id=1, source_target_pairs={{0,12},{4,0},{8,4},{12,8},{1,13},{5,1},{9,5},{13,9},{2,14},{6,2},{... | collective-permute-start | bytes 1572872 | tf_op jit(solution)/shard_map/ppermute | solution.py:376
  62.0 19.5 %collective-permute-start.13 = (bf16[1024,256]{1,0:T(8,128)(2,1)S(1)}, bf16[1024,256]{1,0:T(8,128)(2,1)S(1)}, u32[]{:S(2)}, u32[]{:S(2)}) collective-permute-start(bf16[1024,256]{1,0:T(8,128)(2,1)S(1)} %get-tuple-element.90.refs_1_), channel_id=1, source_target_pairs={{0,12},{4,0},{8,4},{12,8},{1,13},{5,1},{9,5},{13,9},{2,14},{6,2},{... | collective-permute-start | bytes 1572872 | tf_op jit(solution)/shard_map/ppermute | solution.py:376
  66.5 19.1 %collective-permute-start.17 = (bf16[1024,256]{1,0:T(8,128)(2,1)S(1)}, bf16[1024,256]{1,0:T(8,128)(2,1)S(1)}, u32[]{:S(2)}, u32[]{:S(2)}) collective-permute-start(bf16[1024,256]{1,0:T(8,128)(2,1)S(1)} %get-tuple-element.108.refs_8_), channel_id=1, source_target_pairs={{0,3},{1,0},{2,1},{3,2},{4,7},{5,4},{6,5},{7,6},{8,11},{9,8},{10,9... | collective-permute-start | bytes 1572872 | tf_op jit(solution)/shard_map/ppermute | solution.py:376
  67.4 18.2 %collective-permute-start.18 = (bf16[1024,256]{1,0:T(8,128)(2,1)S(1)}, bf16[1024,256]{1,0:T(8,128)(2,1)S(1)}, u32[]{:S(2)}, u32[]{:S(2)}) collective-permute-start(bf16[1024,256]{1,0:T(8,128)(2,1)S(1)} %get-tuple-element.108.refs_8_), channel_id=1, source_target_pairs={{0,2},{1,3},{2,0},{3,1},{4,6},{5,7},{6,4},{7,5},{8,10},{9,11},{10,... | collective-permute-start | bytes 1572872 | tf_op jit(solution)/shard_map/ppermute | solution.py:376
  68.5 22.7 %collective-permute-start.19 = (bf16[1024,256]{1,0:T(8,128)(2,1)S(1)}, bf16[1024,256]{1,0:T(8,128)(2,1)S(1)}, u32[]{:S(2)}, u32[]{:S(2)}) collective-permute-start(bf16[1024,256]{1,0:T(8,128)(2,1)S(1)} %get-tuple-element.108.refs_8_), channel_id=1, source_target_pairs={{0,1},{1,2},{2,3},{3,0},{4,5},{5,6},{6,7},{7,4},{8,9},{9,10},{10,1... | collective-permute-start | bytes 1572872 | tf_op jit(solution)/shard_map/ppermute | solution.py:376
  94.8 4.2 %collective-permute-start.20 = (bf16[4,128,1280]{2,1,0:T(8,128)(2,1)S(1)}, bf16[4,128,1280]{2,1,0:T(8,128)(2,1)S(1)}, u32[]{:S(2)}, u32[]{:S(2)}) collective-permute-start(bf16[4,128,1280]{2,1,0:T(8,128)(2,1)S(1)} %get-tuple-element.112), channel_id=1, source_target_pairs={{0,16},{16,0},{1,17},{17,1},{2,18},{18,2},{3,19},{19,3},{4,20},{20... | collective-permute-start | bytes 3932168 | tf_op jit(solution)/shard_map/ppermute | solution.py:380
  95.0 40.6 %collective-permute-start.14 = (bf16[256,1024]{1,0:T(8,128)(2,1)}, bf16[256,1024]{1,0:T(8,128)(2,1)}, u32[]{:S(2)}, u32[]{:S(2)}) collective-permute-start(bf16[256,1024]{1,0:T(8,128)(2,1)} %get-tuple-element.105), channel_id=1, source_target_pairs={{0,1},{1,2},{2,3},{3,0},{4,5},{5,6},{6,7},{7,4},{8,9},{9,10},{10,1... | collective-permute-start | bytes 1572872 | tf_op jit(solution)/shard_map/ppermute | solution.py:376
  95.6 40.0 %collective-permute-start.15 = (bf16[256,1024]{1,0:T(8,128)(2,1)S(1)}, bf16[256,1024]{1,0:T(8,128)(2,1)}, u32[]{:S(2)}, u32[]{:S(2)}) collective-permute-start(bf16[256,1024]{1,0:T(8,128)(2,1)S(1)} %get-tuple-element.106), channel_id=1, source_target_pairs={{0,2},{1,3},{2,0},{3,1},{4,6},{5,7},{6,4},{7,5},{8,10},{9,11},{10,... | collective-permute-start | bytes 1572872 | tf_op jit(solution)/shard_map/ppermute | solution.py:376
  97.1 39.0 %collective-permute-start.16 = (bf16[256,1024]{1,0:T(8,128)(2,1)S(1)}, bf16[256,1024]{1,0:T(8,128)(2,1)}, u32[]{:S(2)}, u32[]{:S(2)}) collective-permute-start(bf16[256,1024]{1,0:T(8,128)(2,1)S(1)} %get-tuple-element.107), channel_id=1, source_target_pairs={{0,3},{1,0},{2,1},{3,2},{4,7},{5,4},{6,5},{7,6},{8,11},{9,8},{10,9... | collective-permute-start | bytes 1572872 | tf_op jit(solution)/shard_map/ppermute | solution.py:376
  100.4 38.0 %all-to-all-start = ((bf16[64,8,1280]{2,1,0:T(8,128)(2,1)}), bf16[64,8,1280]{2,1,0:T(8,128)(2,1)S(1)}, u32[]{:S(2)}, u32[]{:S(2)}) async-start(bf16[64,8,1280]{2,1,0:T(8,128)(2,1)} %bitcast.8), calls=%async_computation | async-start | bytes 2621440 | tf_op jit(solution)/shard_map/all_to_all | solution.py:464
  (2 other events, 9.1 us)

commit v10 on v8

--- a/solution.py
+++ b/solution.py
@@ -155,7 +155,7 @@
 
 def forward_halo_body(info, *refs):
     q, att_in = refs[0:2]
-    kv_in, gg_in, gate_in = refs[2:5], refs[5:9], refs[9:12]
+    gg_in, kv_in, gate_in = refs[2:6], refs[6:9], refs[9:12]
     att, kv, gg, cot, gate, stats = refs[12:18]
     ends = history_ends(info)
     base = info[8] * GRP
@@ -220,44 +220,55 @@
         gp[at, :] = (grad_gated * normed * dsig[k][:, 0:BLK].astype(F32)).astype(BF16)
 
 
+def pack(info, acc, send, keep):
+    for x in range(4):
+        for out, c, kind in ((send, 1 - info[10], BF16), (keep, info[10], F32)):
+            at = pl.ds(pl.multiple_of((x * 2 + c) * 128, 128), 128)
+            out[x, :, :] = acc[at, :].astype(kind)
+
+
 def early_weights_body(info, *refs):
-    ev, (gp_g, gp_q, acc) = refs[0:4], refs[4:7]
+    ev, (gp_g, gp_q, send, keep, acc) = refs[0:4], refs[4:9]
     for k in range(NB):
         at = rows(lax.rem(info[9] + k, NB))
         for lanes, gp in ((slice(0, BLK), gp_g), (slice(BLK, 2 * BLK), gp_q)):
             part = tn(ev[k][...], gp[at, :])
             acc[:, lanes] = part if k == 0 else acc[:, lanes] + part
+    pack(info, acc, send, keep)
 
 
 def late_weights_body(info, *refs):
-    ev, gp, gated = refs[0:4], refs[4:8], refs[8:12]
-    cot, early, send, keep, acc = refs[12:17]
+    ev, gp = refs[0:4], refs[4:8]
+    send, keep, acc = refs[8:11]
     for k in range(NB):
         part = tn(ev[k][...], gp[k][:, 2 * BLK :])
-        acc[:, : 2 * BLK] = part if k == 0 else acc[:, : 2 * BLK] + part
-        acc[rows(lax.rem(info[9] + k, NB)), 2 * BLK :] = tn(gated[k][...], cot[...])
-    for x in range(4):
-        for out, c, kind in ((send, 1 - info[10], BF16), (keep, info[10], F32)):
-            at = pl.ds(pl.multiple_of((x * 2 + c) * 128, 128), 128)
-            out[x, :, : 2 * BLK] = early[at, :].astype(kind)
-            out[x, :, 2 * BLK :] = acc[at, :].astype(kind)
-
-
-def add_core_body(keep, got, out):
-    out[...] = (keep[...] + got[...].astype(F32)).astype(BF16)
-
-
-def add_x_body(got, total):
-    part = got[0].astype(F32) + got[1].astype(F32) + got[2].astype(F32) + got[3].astype(F32)
+        acc[...] = part if k == 0 else acc[...] + part
+    pack(info, acc, send, keep)
+
+
+def out_weights_body(info, *refs):
+    gated, (cot, send, keep, acc) = refs[0:4], refs[4:8]
+    for k in range(NB):
+        acc[rows(lax.rem(info[9] + k, NB)), :] = tn(gated[k][...], cot[...])
+    pack(info, acc, send, keep)
+
+
+def add_core_body(keep_1, keep_2, keep_3, got_1, got_2, got_3, out):
+    out[:, :, 0:512] = (keep_1[...] + got_1[...].astype(F32)).astype(BF16)
+    out[:, :, 512:1024] = (keep_2[...] + got_2[...].astype(F32)).astype(BF16)
+    out[:, :, 1024:] = (keep_3[...] + got_3[...].astype(F32)).astype(BF16)
+
+
+def add_xy_body(got, total):
+    part = got[0].astype(F32)
+    for xy in range(1, 16):
+        part = part + got[xy].astype(F32)
     total[...] = part.astype(BF16)
 
 
-def last_sum_body(got, grad_w_in, grad_w_out):
+def last_body(got, grad_w_in, grad_w_out):
     for z in range(4):
-        part = got[z].astype(F32)
-        for y in range(1, 4):
-            part = part + got[y * 4 + z].astype(F32)
-        part = part.astype(BF16)
+        part = got[z]
         for n, to in enumerate((0, 2, 1, 3)):
             at = to * D + z * BLK
             grad_w_in[:, at : at + BLK] = part[:, n * BLK : (n + 1) * BLK]
@@ -440,7 +451,7 @@
         forward_halo_body,
         (f32((GRP, BLK)), bf16((GRP, 2 * BLK))) + (bf16((GRP, BLK)),) * 3 + (f32((8, GRP)),),
         12, 5 << 30, 4 << 20,
-    )(info, q, att, *kv_prevs, *ggs, *gs)
+    )(info, q, att, *ggs, *kv_prevs, *gs)
     gatt, gated, gp_g = call(
         norm_body, (bf16((GRP, BLK)),) * 3, 11, 1 << 30, 4 << 20, [pltpu.VMEM((GRP, DH), F32)]
     )(info, att, gg, gate, *gather_z(stats), *dsigs)
@@ -450,34 +461,40 @@
         backward_local_body, (bf16((GRP, BLK)), f32((GRP, 2 * BLK))), 8, 1 << 20, 1 << 20,
         [pltpu.VMEM((GRP, BLK), F32)],
     )(info, q, gatt, kv, kv_prev, *dsigs)
-    early = call(early_weights_body, f32((D, 2 * BLK)), 6, 1 << 20, 1 << 20)(info, *evs, gp_g, gp_q)
-    q_next, g_next, early = lax.optimization_barrier((q_next, g_next, early))
+    def weights(kernel, cols, operands):
+        send, keep = call(
+            kernel, (bf16((4, 128, cols)), f32((4, 128, cols))), len(operands), 1 << 20, 1 << 20,
+            [pltpu.VMEM((D, cols), F32)],
+        )(info, *operands)
+        return swap(send), keep
+
+    got_1, keep_1 = weights(early_weights_body, 512, (*evs, gp_g, gp_q))
+    q_next, g_next, keep_1 = lax.optimization_barrier((q_next, g_next, keep_1))
     gp = call(
         backward_later_body, (bf16((BLK, 4 * BLK)),) * 4, 10, 5 << 30, 4 << 20, [pltpu.VMEM((GRP, 2 * BLK), F32)]
     )(info, q_next, g_next, kv, dkv, gp_g, gp_q, *dsigs)
+    got_2, keep_2 = weights(late_weights_body, 512, (*evs, *gp))
     *partial, = call(
         input_body, (f32((BLK, D)),) + (bf16((BLK, D)),) * 3, 6, 1 << 20, 1 << 20
     )(info, *gp, w_in, cot)
-    early, partial[0] = lax.optimization_barrier((early, partial[0]))
+    cot_z, keep_2, partial[0] = lax.optimization_barrier((cot_z, keep_2, partial[0]))
     partial = exchange(partial, "z")
-    send, keep = call(
-        late_weights_body,
-        (bf16((4, 128, 5 * BLK)), f32((4, 128, 5 * BLK))), 14, 1 << 20, 1 << 20,
-        [pltpu.VMEM((D, 3 * BLK), F32)],
-    )(info, *evs, *gp, *gateds, cot_z, early)
+    got_3, keep_3 = weights(out_weights_body, 256, (*gateds, cot_z))
     mine = call(
-        add_core_body, bf16((4, 128, 5 * BLK)), 2, 1 << 20, 1 << 20, scalars=0
-    )(keep, swap(send))
-    sums = lax.all_to_all(mine, "x", 0, 0)
+        add_core_body, bf16((4, 128, 5 * BLK)), 6, 1 << 20, 1 << 20, scalars=0
+    )(keep_1, keep_2, keep_3, got_1, got_2, got_3)
+    sums = lax.all_to_all(mine.reshape(16, 32, 5 * BLK), ("x", "y"), 0, 0)
     near_rows = call(
         add_near_body, f32((BLK, D)), 3, 40 << 30, 4 << 20, scalars=0
     )(partial[0], partial[1], partial[3])
     sums, near_rows = lax.optimization_barrier((sums, near_rows))
-    total = call(add_x_body, bf16((128, 5 * BLK)), 1, 1 << 20, 1 << 20, scalars=0)(sums)
+    total = call(add_xy_body, bf16((32, 5 * BLK)), 1, 1 << 20, 1 << 20, scalars=0)(sums)
     _, near_rows = lax.optimization_barrier((total, near_rows))
     grad_events = call(add_far_body, bf16((BLK, D)), 2, 1 << 20, 4 << 20, scalars=0)(near_rows, partial[2])
-    got = lax.all_to_all(total.reshape(16, 8, 5 * BLK), ("y", "z"), 0, 0)
-    grad_w_in, grad_w_out = call(last_sum_body, (bf16((8, 4 * D)), bf16((8, D))), 1, 1 << 20, 1 << 20, scalars=0)(got)
+    got = lax.all_to_all(total.reshape(4, 8, 5 * BLK), "z", 0, 0)
+    grad_w_in, grad_w_out = call(
+        last_body, (bf16((8, 4 * D)), bf16((8, D))), 1, 1 << 20, 1 << 20, scalars=0
+    )(got)
     return grad_events[None], grad_w_in, grad_w_out
 
 

time: 139 us -> 135 us (0.971)
  waiting for transfers between devices: 48.7 us -> 44.9 us
  starting transfers between devices: 38.7 us -> 40.6 us
    ppermute x20, waiting for transfers between devices: 40.7 us -> 25.4 us  [along(): return lax.ppermute(x, axis, [(i, (i + d) % 4) for i in range(4)])]
    all_to_all x2, waiting for transfers between devices: 7.93 us -> 19.5 us  [the longest x1 14.7 us: body(): sums = lax.all_to_all(mine.reshape(16, 32, 5 * BLK), ('x', 'y'), 0, 0)]
    ppermute x20, starting transfers between devices: 29.6 us -> 31.1 us  [along(): return lax.ppermute(x, axis, [(i, (i + d) % 4) for i in range(4)])]
    pallas_call x5 -> x6, Pallas kernels: 9 us -> 9.06 us  [the longest x3 6.29 us: weights(): call(kernel, (bf16((4, 128, cols)), f32((4, 128, cols))), len(operands),...]
  transfers between devices with their start and end apart: 23 -> 25, of which waited for: 10 -> 11; matrix products, arithmetic and copies ran while one was open for 1% -> 1% of each run, Pallas kernels for 27% -> 30%
where the time goes in v10:
time: 135 us
  waiting for transfers between devices  44.9 us (33%)
  Pallas kernels  42.8 us (32%)
  starting transfers between devices  40.6 us (30%)
  local copies, waits for them, and re-layouts  5.35 us (4%)
    ppermute x20, starting transfers between devices, along(): return lax.ppermute(x, axis, [(i, (i + d) % 4) for i in range(4)])  31.1 us
    ppermute x20, waiting for transfers between devices, along(): return lax.ppermute(x, axis, [(i, (i + d) % 4) for i in range(4)])  25.4 us
    all_to_all x1, waiting for transfers between devices, body(): sums = lax.all_to_all(mine.reshape(16, 32, 5 * BLK), ('x', 'y'), 0, 0)  14.7 us
    pallas_call x1, Pallas kernels, body(): call(backward_local_body, (bf16((GRP, BLK)), f32((GRP, 2 * BLK))), 8, 1 <...  7.53 us
    pallas_call x3, Pallas kernels, weights(): call(kernel, (bf16((4, 128, cols)), f32((4, 128, cols))), len(operands),...  6.29 us
    pallas_call x3, Pallas kernels, body(): call(project_body, (bf16((n * BLK, 2 * BLK)), bf16((n * BLK, BLK)), bf16(...  6.21 us
    all_to_all x1, starting transfers between devices, body(): sums = lax.all_to_all(mine.reshape(16, 32, 5 * BLK), ('x', 'y'), 0, 0)  5.7 us
    pallas_call x1, Pallas kernels, body(): call(forward_local_body, (bf16((GRP, BLK)), bf16((GRP, 2 * BLK)), f32((GR...  5.19 us
  transfers between devices with their start and end apart: 25, of which 11 were waited for; matrix products, arithmetic and copies ran while one was open for 1% of the time, Pallas kernels for 30%

profile of v10, /device:TPU:0, one launch (start us, length us, event | category | flops | bytes accessed | tf_op | source)
XLA Modules:
  0.0 134.5 jit_solution(9980076031362333737)
XLA Ops:
  0.6 4.2 %collective-permute-start = (bf16[256,1024]{1,0:T(8,128)(2,1)}, bf16[256,1024]{1,0:T(8,128)(2,1)S(1)}, u32[]{:S(2)}, u32[]{:S(2)}) collective-permute-start(bf16[256,1024]{1,0:T(8,128)(2,1)} %bitcast.5.refs_0_), channel_id=1, source_target_pairs={{0,3},{1,0},{2,1},{3,2},{4,7},{5,4},{6,5},{7,6},{8,11},{9,8},{10,9... | collective-permute-start | bytes 1572872 | tf_op jit(solution)/shard_map/ppermute | solution.py:395
  5.6 3.4 %copy-done = bf16[1024,4096]{1,0:T(8,128)(2,1)S(1)} copy-done((bf16[1024,4096]{1,0:T(8,128)(2,1)S(1)}, bf16[1024,4096]{1,0:T(8,128)(2,1)}, u32[]{:S(2)}) %copy-start) | copy-done | bytes 8388632
  8.9 2.2 %shard_map.76 = (bf16[256,512]{1,0:T(8,128)(2,1)S(1)}, bf16[256,256]{1,0:T(8,128)(2,1)S(1)}, bf16[256,256]{1,0:T(8,128)(2,1)S(1)}, bf16[256,1024]{1,0:T(8,128)(2,1)S(1)}) custom-call(s32[12]{0:T(128)S(1)} %concatenate.3.info, bf16[256,1024]{1,0:T(8,128)(2,1)} %bitcast.5.refs_0_, bf16[1024,4096]{1,0:T(8,128)(2,1)S(1)} %copy-done), custom_call_target="tpu_custom_call" | custom-call | flops 1048576 | bytes 1048576 | tf_op jit(solution)/shard_map/pallas_call | solution.py:432
  11.2 5.1 %collective-permute-done.refs_0_.refs_1_ = bf16[256,1024]{1,0:T(8,128)(2,1)S(1)} collective-permute-done((bf16[256,1024]{1,0:T(8,128)(2,1)}, bf16[256,1024]{1,0:T(8,128)(2,1)S(1)}, u32[]{:S(2)}, u32[]{:S(2)}) %collective-permute-start) | collective-permute-done | bytes 524320 | tf_op jit(solution)/shard_map/ppermute | solution.py:395
  16.3 3.3 %collective-permute-done.1.refs_1_.refs_3_ = bf16[256,1024]{1,0:T(8,128)(2,1)S(1)} collective-permute-done((bf16[256,1024]{1,0:T(8,128)(2,1)}, bf16[256,1024]{1,0:T(8,128)(2,1)S(1)}, u32[]{:S(2)}, u32[]{:S(2)}) %collective-permute-start.1) | collective-permute-done | bytes 524320 | tf_op jit(solution)/shard_map/ppermute | solution.py:395
  21.3 2.4 %shard_map.77 = (bf16[512,512]{1,0:T(8,128)(2,1)S(1)}, bf16[512,256]{1,0:T(8,128)(2,1)S(1)}, bf16[512,256]{1,0:T(8,128)(2,1)S(1)}, bf16[256,1024]{1,0:T(8,128)(2,1)S(1)}, bf16[256,1024]{1,0:T(8,128)(2,1)S(1)}) custom-call(s32[12]{0:T(128)S(1)} %concatenate.3.info, bf16[256,1024]{1,0:T(8,128)(2,1)S(1)} %collective-permute-done.refs_0_.refs_1_, ...), custom_call_target="tpu_custom_call" | custom-call | flops 1048576 | bytes 1048576 | tf_op jit(solution)/shard_map/pallas_call | solution.py:432
  26.7 7.1 %collective-permute-done.2.refs_0_.refs_2_ = bf16[256,1024]{1,0:T(8,128)(2,1)S(1)} collective-permute-done((bf16[256,1024]{1,0:T(8,128)(2,1)}, bf16[256,1024]{1,0:T(8,128)(2,1)S(1)}, u32[]{:S(2)}, u32[]{:S(2)}) %collective-permute-start.2) | collective-permute-done | bytes 524320 | tf_op jit(solution)/shard_map/ppermute | solution.py:395
  33.8 2.1 %collective-permute-start.5 = (bf16[256,512]{1,0:T(8,128)(2,1)S(1)}, bf16[256,512]{1,0:T(8,128)(2,1)S(1)}, u32[]{:S(2)}, u32[]{:S(2)}) collective-permute-start(bf16[256,512]{1,0:T(8,128)(2,1)S(1)} %get-tuple-element.83), channel_id=1, source_target_pairs={{0,2},{1,3},{2,0},{3,1},{4,6},{5,7},{6,4},{7,5},{8,10},{9,11},{10,... | collective-permute-start | bytes 786440 | tf_op jit(solution)/shard_map/ppermute | solution.py:395
  40.3 5.2 %shard_map.79 = (bf16[1024,256]{1,0:T(8,128)(2,1)S(1)}, bf16[1024,512]{1,0:T(8,128)(2,1)S(1)}, f32[1024,256]{1,0:T(8,128)S(1)}) custom-call(s32[12]{0:T(128)S(1)} %concatenate.3.info, bf16[256,256]{1,0:T(8,128)(2,1)S(1)} %get-tuple-element.66.refs_0_, bf16[512,256]{1,0:T(8,128)(2,1)S(1)} %get-tuple-element.70.refs_1_, ...), custom_call_target="tpu_custom_call" | custom-call | flops 5368709120 | bytes 4194304 | tf_op jit(solution)/shard_map/pallas_call | solution.py:446
  48.9 2.4 %collective-permute-start.10 = (f32[8,1024]{1,0:T(8,128)S(1)}, f32[8,1024]{1,0:T(8,128)S(1)}, u32[]{:S(2)}, u32[]{:S(2)}) collective-permute-start(f32[8,1024]{1,0:T(8,128)S(1)} %get-tuple-element.91.refs_3_), channel_id=1, source_target_pairs={{0,3},{1,0},{2,1},{3,2},{4,7},{5,4},{6,5},{7,6},{8,11},{9,8},{10,9... | collective-permute-start | bytes 98312 | tf_op jit(solution)/shard_map/ppermute | solution.py:395
  52.4 3.4 %collective-permute-start.3 = (bf16[1024,256]{1,0:T(8,128)(2,1)S(1)}, bf16[1024,256]{1,0:T(8,128)(2,1)S(1)}, u32[]{:S(2)}, u32[]{:S(2)}) collective-permute-start(bf16[1024,256]{1,0:T(8,128)(2,1)S(1)} %get-tuple-element.75.refs_0_), channel_id=1, source_target_pairs={{0,12},{4,0},{8,4},{12,8},{1,13},{5,1},{9,5},{13,9},{2,14},{6,2},{... | collective-permute-start | bytes 1572872 | tf_op jit(solution)/shard_map/ppermute | solution.py:395
  58.4 4.1 %collective-permute-start.13 = (bf16[1024,256]{1,0:T(8,128)(2,1)S(1)}, bf16[1024,256]{1,0:T(8,128)(2,1)S(1)}, u32[]{:S(2)}, u32[]{:S(2)}) collective-permute-start(bf16[1024,256]{1,0:T(8,128)(2,1)S(1)} %get-tuple-element.96.refs_1_), channel_id=1, source_target_pairs={{0,12},{4,0},{8,4},{12,8},{1,13},{5,1},{9,5},{13,9},{2,14},{6,2},{... | collective-permute-start | bytes 1572872 | tf_op jit(solution)/shard_map/ppermute | solution.py:395
  65.5 7.5 %shard_map.83 = (bf16[1024,256]{1,0:T(8,128)(2,1)S(1)}, f32[1024,512]{1,0:T(8,128)S(1)}) custom-call(s32[12]{0:T(128)S(1)} %concatenate.3.info, bf16[1024,256]{1,0:T(8,128)(2,1)S(1)} %get-tuple-element.75.refs_0_, bf16[1024,256]{1,0:T(8,128)(2,1)S(1)} %get-tuple-element.96.refs_1_, bf16[1024,512]{1,0:T(8,128)(2,1)S(1)} %get-tuple-element.98.refs_2_, ...), custom_call_target="tpu_custom_call" | custom-call | flops 1048576 | bytes 1048576 | tf_op jit(solution)/shard_map/pallas_call | solution.py:460
  73.0 2.5 %shard_map.84 = (bf16[4,128,512]{2,1,0:T(8,128)(2,1)S(1)}, f32[4,128,512]{2,1,0:T(8,128)S(1)}) custom-call(s32[12]{0:T(128)S(1)} %concatenate.3.info, bf16[256,1024]{1,0:T(8,128)(2,1)} %bitcast.5.refs_0_, bf16[256,1024]{1,0:T(8,128)(2,1)S(1)} %collective-permute-done.refs_0_.refs_1_, bf16[256,1024]{1,0:T(8,128)(2,1)S(1)} %collective-permute-done.2.refs_0_.refs_2_, ...), custom_call_target="tpu_custom_call" | custom-call | flops 1048576 | bytes 1048576 | tf_op jit(solution)/shard_map/pallas_call | solution.py:465
  75.6 3.2 %collective-permute-done.13.refs_1_ = bf16[1024,256]{1,0:T(8,128)(2,1)S(1)} collective-permute-done((bf16[1024,256]{1,0:T(8,128)(2,1)S(1)}, bf16[1024,256]{1,0:T(8,128)(2,1)S(1)}, u32[]{:S(2)}, u32[]{:S(2)}) %collective-permute-start.13) | collective-permute-done | bytes 524320 | tf_op jit(solution)/shard_map/ppermute | solution.py:395
  78.8 5.0 %shard_map.85 = (bf16[256,1024]{1,0:T(8,128)(2,1)S(1)}, bf16[256,1024]{1,0:T(8,128)(2,1)S(1)}, bf16[256,1024]{1,0:T(8,128)(2,1)S(1)}, bf16[256,1024]{1,0:T(8,128)(2,1)S(1)}) custom-call(s32[12]{0:T(128)S(1)} %concatenate.3.info, bf16[1024,256]{1,0:T(8,128)(2,1)S(1)} %collective-permute-done.3.refs_0_, bf16[1024,256]{1,0:T(8,128)(2,1)S(1)} %collective-permute-done.13.refs_1_, ...), custom_call_target="tpu_custom_call" | custom-call | flops 5368709120 | bytes 4194304 | tf_op jit(solution)/shard_map/pallas_call | solution.py:473
  83.8 2.5 %shard_map.86 = (bf16[4,128,512]{2,1,0:T(8,128)(2,1)S(1)}, f32[4,128,512]{2,1,0:T(8,128)S(1)}) custom-call(s32[12]{0:T(128)S(1)} %concatenate.3.info, bf16[256,1024]{1,0:T(8,128)(2,1)} %bitcast.5.refs_0_, bf16[256,1024]{1,0:T(8,128)(2,1)S(1)} %collective-permute-done.refs_0_.refs_1_, bf16[256,1024]{1,0:T(8,128)(2,1)S(1)} %collective-permute-done.2.refs_0_.refs_2_, ...), custom_call_target="tpu_custom_call" | custom-call | flops 1048576 | bytes 1048576 | tf_op jit(solution)/shard_map/pallas_call | solution.py:465
  86.4 2.9 %shard_map.87 = (f32[256,1024]{1,0:T(8,128)S(1)}, bf16[256,1024]{1,0:T(8,128)(2,1)S(1)}, bf16[256,1024]{1,0:T(8,128)(2,1)S(1)}, bf16[256,1024]{1,0:T(8,128)(2,1)S(1)}) custom-call(s32[12]{0:T(128)S(1)} %concatenate.3.info, bf16[256,1024]{1,0:T(8,128)(2,1)S(1)} %get-tuple-element.107.refs_4_.refs_0_, ...), custom_call_target="tpu_custom_call" | custom-call | flops 1048576 | bytes 1048576 | tf_op jit(solution)/shard_map/pallas_call | solution.py:477
  89.4 2.3 %collective-permute-start.20 = (bf16[256,1024]{1,0:T(8,128)(2,1)S(1)}, bf16[256,1024]{1,0:T(8,128)(2,1)}, u32[]{:S(2)}, u32[]{:S(2)}) collective-permute-start(bf16[256,1024]{1,0:T(8,128)(2,1)S(1)} %get-tuple-element.121), channel_id=1, source_target_pairs={{0,1},{1,2},{2,3},{3,0},{4,5},{5,6},{6,7},{7,4},{8,9},{9,10},{10,1... | collective-permute-start | bytes 1572872 | tf_op jit(solution)/shard_map/ppermute | solution.py:395
  97.0 5.7 %all-to-all-start = ((bf16[16,32,1280]{2,1,0:T(8,128)(2,1)}), bf16[16,32,1280]{2,1,0:T(8,128)(2,1)S(1)}, u32[]{:S(2)}, u32[]{:S(2)}) async-start(bf16[16,32,1280]{2,1,0:T(8,128)(2,1)} %bitcast.7), calls=%async_computation | async-start | bytes 2621440 | tf_op jit(solution)/shard_map/all_to_all | solution.py:486
  102.7 2.4 %collective-permute-done.20.got_1 = bf16[256,1024]{1,0:T(8,128)(2,1)} collective-permute-done((bf16[256,1024]{1,0:T(8,128)(2,1)S(1)}, bf16[256,1024]{1,0:T(8,128)(2,1)}, u32[]{:S(2)}, u32[]{:S(2)}) %collective-permute-start.20) | collective-permute-done | bytes 524320 | tf_op jit(solution)/shard_map/ppermute | solution.py:395
  109.1 14.7 %all-to-all-done.got = bf16[16,32,1280]{2,1,0:T(8,128)(2,1)S(1)} async-done(((bf16[16,32,1280]{2,1,0:T(8,128)(2,1)}), bf16[16,32,1280]{2,1,0:T(8,128)(2,1)S(1)}, u32[]{:S(2)}, u32[]{:S(2)}) %all-to-all-start) | async-done | bytes 1310752 | tf_op jit(solution)/shard_map/all_to_all | solution.py:486
  124.6 3.6 %all-to-all-start.1 = ((bf16[4,8,1280]{2,1,0:T(8,128)(2,1)}), bf16[4,8,1280]{2,1,0:T(8,128)(2,1)S(1)}, u32[]{:S(2)}, u32[]{:S(2)}) async-start(bf16[4,8,1280]{2,1,0:T(8,128)(2,1)} %bitcast.9), calls=%async_computation.1 | async-start | bytes 163840 | tf_op jit(solution)/shard_map/all_to_all | solution.py:494
  129.1 4.8 %all-to-all-done.1.got = bf16[4,8,1280]{2,1,0:T(8,128)(2,1)S(1)} async-done(((bf16[4,8,1280]{2,1,0:T(8,128)(2,1)}), bf16[4,8,1280]{2,1,0:T(8,128)(2,1)S(1)}, u32[]{:S(2)}, u32[]{:S(2)}) %all-to-all-start.1) | async-done | bytes 81952 | tf_op jit(solution)/shard_map/all_to_all | solution.py:494
  (57 shorter events, 31.6 us)
Async XLA Ops:
  0.6 15.7 %collective-permute-start = (bf16[256,1024]{1,0:T(8,128)(2,1)}, bf16[256,1024]{1,0:T(8,128)(2,1)S(1)}, u32[]{:S(2)}, u32[]{:S(2)}) collective-permute-start(bf16[256,1024]{1,0:T(8,128)(2,1)} %bitcast.5.refs_0_), channel_id=1, source_target_pairs={{0,3},{1,0},{2,1},{3,2},{4,7},{5,4},{6,5},{7,6},{8,11},{9,8},{10,9... | collective-permute-start | bytes 1572872 | tf_op jit(solution)/shard_map/ppermute | solution.py:395
  4.8 14.8 %collective-permute-start.1 = (bf16[256,1024]{1,0:T(8,128)(2,1)}, bf16[256,1024]{1,0:T(8,128)(2,1)S(1)}, u32[]{:S(2)}, u32[]{:S(2)}) collective-permute-start(bf16[256,1024]{1,0:T(8,128)(2,1)} %bitcast.5.refs_0_), channel_id=1, source_target_pairs={{0,1},{1,2},{2,3},{3,0},{4,5},{5,6},{6,7},{7,4},{8,9},{9,10},{10,1... | collective-permute-start | bytes 1572872 | tf_op jit(solution)/shard_map/ppermute | solution.py:395
  19.6 14.2 %collective-permute-start.2 = (bf16[256,1024]{1,0:T(8,128)(2,1)}, bf16[256,1024]{1,0:T(8,128)(2,1)S(1)}, u32[]{:S(2)}, u32[]{:S(2)}) collective-permute-start(bf16[256,1024]{1,0:T(8,128)(2,1)} %bitcast.5.refs_0_), channel_id=1, source_target_pairs={{0,2},{1,3},{2,0},{3,1},{4,6},{5,7},{6,4},{7,5},{8,10},{9,11},{10,... | collective-permute-start | bytes 1572872 | tf_op jit(solution)/shard_map/ppermute | solution.py:395
  19.6 19.0 %collective-permute-start.7 = (bf16[256,512]{1,0:T(8,128)(2,1)S(1)}, bf16[256,512]{1,0:T(8,128)(2,1)S(1)}, u32[]{:S(2)}, u32[]{:S(2)}) collective-permute-start(bf16[256,512]{1,0:T(8,128)(2,1)S(1)} %get-tuple-element.67.refs_3_), channel_id=1, source_target_pairs={{0,4},{4,8},{8,12},{12,0},{1,5},{5,9},{9,13},{13,1},{2,6},{6,10},{... | collective-permute-start | bytes 786440 | tf_op jit(solution)/shard_map/ppermute | solution.py:395
  23.7 21.8 %collective-permute-start.8 = (bf16[512,512]{1,0:T(8,128)(2,1)S(1)}, bf16[512,512]{1,0:T(8,128)(2,1)S(1)}, u32[]{:S(2)}, u32[]{:S(2)}) collective-permute-start(bf16[512,512]{1,0:T(8,128)(2,1)S(1)} %get-tuple-element.73.refs_4_), channel_id=1, source_target_pairs={{0,4},{4,8},{8,12},{12,0},{1,5},{5,9},{9,13},{13,1},{2,6},{6,10},{... | collective-permute-start | bytes 1572872 | tf_op jit(solution)/shard_map/ppermute | solution.py:395
  33.8 12.8 %collective-permute-start.4 = (bf16[256,512]{1,0:T(8,128)(2,1)S(1)}, bf16[256,512]{1,0:T(8,128)(2,1)S(1)}, u32[]{:S(2)}, u32[]{:S(2)}) collective-permute-start(bf16[256,512]{1,0:T(8,128)(2,1)S(1)} %get-tuple-element.82), channel_id=1, source_target_pairs={{0,1},{1,2},{2,3},{3,0},{4,5},{5,6},{6,7},{7,4},{8,9},{9,10},{10,1... | collective-permute-start | bytes 786440 | tf_op jit(solution)/shard_map/ppermute | solution.py:395
  33.8 12.8 %collective-permute-start.5 = (bf16[256,512]{1,0:T(8,128)(2,1)S(1)}, bf16[256,512]{1,0:T(8,128)(2,1)S(1)}, u32[]{:S(2)}, u32[]{:S(2)}) collective-permute-start(bf16[256,512]{1,0:T(8,128)(2,1)S(1)} %get-tuple-element.83), channel_id=1, source_target_pairs={{0,2},{1,3},{2,0},{3,1},{4,6},{5,7},{6,4},{7,5},{8,10},{9,11},{10,... | collective-permute-start | bytes 786440 | tf_op jit(solution)/shard_map/ppermute | solution.py:395
  36.0 11.2 %collective-permute-start.6 = (bf16[256,512]{1,0:T(8,128)(2,1)S(1)}, bf16[256,512]{1,0:T(8,128)(2,1)S(1)}, u32[]{:S(2)}, u32[]{:S(2)}) collective-permute-start(bf16[256,512]{1,0:T(8,128)(2,1)S(1)} %get-tuple-element.84), channel_id=1, source_target_pairs={{0,3},{1,0},{2,1},{3,2},{4,7},{5,4},{6,5},{7,6},{8,11},{9,8},{10,9... | collective-permute-start | bytes 786440 | tf_op jit(solution)/shard_map/ppermute | solution.py:395
  38.6 8.6 %collective-permute-start.9 = (bf16[256,512]{1,0:T(8,128)(2,1)S(1)}, bf16[256,512]{1,0:T(8,128)(2,1)S(1)}, u32[]{:S(2)}, u32[]{:S(2)}) collective-permute-start(bf16[256,512]{1,0:T(8,128)(2,1)S(1)} %get-tuple-element.74.refs_5_), channel_id=1, source_target_pairs={{0,4},{4,8},{8,12},{12,0},{1,5},{5,9},{9,13},{13,1},{2,6},{6,10},{... | collective-permute-start | bytes 786440 | tf_op jit(solution)/shard_map/ppermute | solution.py:395
  48.9 6.9 %collective-permute-start.10 = (f32[8,1024]{1,0:T(8,128)S(1)}, f32[8,1024]{1,0:T(8,128)S(1)}, u32[]{:S(2)}, u32[]{:S(2)}) collective-permute-start(f32[8,1024]{1,0:T(8,128)S(1)} %get-tuple-element.91.refs_3_), channel_id=1, source_target_pairs={{0,3},{1,0},{2,1},{3,2},{4,7},{5,4},{6,5},{7,6},{8,11},{9,8},{10,9... | collective-permute-start | bytes 98312 | tf_op jit(solution)/shard_map/ppermute | solution.py:395
  51.3 5.5 %collective-permute-start.11 = (f32[8,1024]{1,0:T(8,128)S(1)}, f32[8,1024]{1,0:T(8,128)S(1)}, u32[]{:S(2)}, u32[]{:S(2)}) collective-permute-start(f32[8,1024]{1,0:T(8,128)S(1)} %get-tuple-element.91.refs_3_), channel_id=1, source_target_pairs={{0,2},{1,3},{2,0},{3,1},{4,6},{5,7},{6,4},{7,5},{8,10},{9,11},{10,... | collective-permute-start | bytes 98312 | tf_op jit(solution)/shard_map/ppermute | solution.py:395
  51.3 5.5 %collective-permute-start.12 = (f32[8,1024]{1,0:T(8,128)S(1)}, f32[8,1024]{1,0:T(8,128)S(1)}, u32[]{:S(2)}, u32[]{:S(2)}) collective-permute-start(f32[8,1024]{1,0:T(8,128)S(1)} %get-tuple-element.91.refs_3_), channel_id=1, source_target_pairs={{0,1},{1,2},{2,3},{3,0},{4,5},{5,6},{6,7},{7,4},{8,9},{9,10},{10,1... | collective-permute-start | bytes 98312 | tf_op jit(solution)/shard_map/ppermute | solution.py:395
  52.4 23.1 %collective-permute-start.3 = (bf16[1024,256]{1,0:T(8,128)(2,1)S(1)}, bf16[1024,256]{1,0:T(8,128)(2,1)S(1)}, u32[]{:S(2)}, u32[]{:S(2)}) collective-permute-start(bf16[1024,256]{1,0:T(8,128)(2,1)S(1)} %get-tuple-element.75.refs_0_), channel_id=1, source_target_pairs={{0,12},{4,0},{8,4},{12,8},{1,13},{5,1},{9,5},{13,9},{2,14},{6,2},{... | collective-permute-start | bytes 1572872 | tf_op jit(solution)/shard_map/ppermute | solution.py:395
  58.4 20.4 %collective-permute-start.13 = (bf16[1024,256]{1,0:T(8,128)(2,1)S(1)}, bf16[1024,256]{1,0:T(8,128)(2,1)S(1)}, u32[]{:S(2)}, u32[]{:S(2)}) collective-permute-start(bf16[1024,256]{1,0:T(8,128)(2,1)S(1)} %get-tuple-element.96.refs_1_), channel_id=1, source_target_pairs={{0,12},{4,0},{8,4},{12,8},{1,13},{5,1},{9,5},{13,9},{2,14},{6,2},{... | collective-permute-start | bytes 1572872 | tf_op jit(solution)/shard_map/ppermute | solution.py:395
  62.5 26.8 %collective-permute-start.14 = (bf16[1024,256]{1,0:T(8,128)(2,1)S(1)}, bf16[1024,256]{1,0:T(8,128)(2,1)S(1)}, u32[]{:S(2)}, u32[]{:S(2)}) collective-permute-start(bf16[1024,256]{1,0:T(8,128)(2,1)S(1)} %get-tuple-element.114.refs_0_), channel_id=1, source_target_pairs={{0,3},{1,0},{2,1},{3,2},{4,7},{5,4},{6,5},{7,6},{8,11},{9,8},{10,9... | collective-permute-start | bytes 1572872 | tf_op jit(solution)/shard_map/ppermute | solution.py:395
  63.4 28.3 %collective-permute-start.15 = (bf16[1024,256]{1,0:T(8,128)(2,1)S(1)}, bf16[1024,256]{1,0:T(8,128)(2,1)S(1)}, u32[]{:S(2)}, u32[]{:S(2)}) collective-permute-start(bf16[1024,256]{1,0:T(8,128)(2,1)S(1)} %get-tuple-element.114.refs_0_), channel_id=1, source_target_pairs={{0,2},{1,3},{2,0},{3,1},{4,6},{5,7},{6,4},{7,5},{8,10},{9,11},{10,... | collective-permute-start | bytes 1572872 | tf_op jit(solution)/shard_map/ppermute | solution.py:395
  64.0 28.6 %collective-permute-start.16 = (bf16[1024,256]{1,0:T(8,128)(2,1)S(1)}, bf16[1024,256]{1,0:T(8,128)(2,1)S(1)}, u32[]{:S(2)}, u32[]{:S(2)}) collective-permute-start(bf16[1024,256]{1,0:T(8,128)(2,1)S(1)} %get-tuple-element.114.refs_0_), channel_id=1, source_target_pairs={{0,1},{1,2},{2,3},{3,0},{4,5},{5,6},{6,7},{7,4},{8,9},{9,10},{10,1... | collective-permute-start | bytes 1572872 | tf_op jit(solution)/shard_map/ppermute | solution.py:395
  75.5 18.6 %collective-permute-start.17 = (bf16[4,128,512]{2,1,0:T(8,128)(2,1)S(1)}, bf16[4,128,512]{2,1,0:T(8,128)(2,1)S(1)}, u32[]{:S(2)}, u32[]{:S(2)}) collective-permute-start(bf16[4,128,512]{2,1,0:T(8,128)(2,1)S(1)} %get-tuple-element.117), channel_id=1, source_target_pairs={{0,16},{16,0},{1,17},{17,1},{2,18},{18,2},{3,19},{19,3},{4,20},{20... | collective-permute-start | bytes 1572872 | tf_op jit(solution)/shard_map/ppermute | solution.py:399
  86.3 9.3 %collective-permute-start.18 = (bf16[4,128,512]{2,1,0:T(8,128)(2,1)S(1)}, bf16[4,128,512]{2,1,0:T(8,128)(2,1)S(1)}, u32[]{:S(2)}, u32[]{:S(2)}) collective-permute-start(bf16[4,128,512]{2,1,0:T(8,128)(2,1)S(1)} %get-tuple-element.118), channel_id=1, source_target_pairs={{0,16},{16,0},{1,17},{17,1},{2,18},{18,2},{3,19},{19,3},{4,20},{20... | collective-permute-start | bytes 1572872 | tf_op jit(solution)/shard_map/ppermute | solution.py:399
  89.4 15.7 %collective-permute-start.20 = (bf16[256,1024]{1,0:T(8,128)(2,1)S(1)}, bf16[256,1024]{1,0:T(8,128)(2,1)}, u32[]{:S(2)}, u32[]{:S(2)}) collective-permute-start(bf16[256,1024]{1,0:T(8,128)(2,1)S(1)} %get-tuple-element.121), channel_id=1, source_target_pairs={{0,1},{1,2},{2,3},{3,0},{4,5},{5,6},{6,7},{7,4},{8,9},{9,10},{10,1... | collective-permute-start | bytes 1572872 | tf_op jit(solution)/shard_map/ppermute | solution.py:395
  91.7 14.9 %collective-permute-start.21 = (bf16[256,1024]{1,0:T(8,128)(2,1)S(1)}, bf16[256,1024]{1,0:T(8,128)(2,1)}, u32[]{:S(2)}, u32[]{:S(2)}) collective-permute-start(bf16[256,1024]{1,0:T(8,128)(2,1)S(1)} %get-tuple-element.122), channel_id=1, source_target_pairs={{0,3},{1,0},{2,1},{3,2},{4,7},{5,4},{6,5},{7,6},{8,11},{9,8},{10,9... | collective-permute-start | bytes 1572872 | tf_op jit(solution)/shard_map/ppermute | solution.py:395
  94.1 34.1 %collective-permute-start.22 = (bf16[256,1024]{1,0:T(8,128)(2,1)S(1)}, bf16[256,1024]{1,0:T(8,128)(2,1)S(1)}, u32[]{:S(2)}, u32[]{:S(2)}) collective-permute-start(bf16[256,1024]{1,0:T(8,128)(2,1)S(1)} %get-tuple-element.126), channel_id=1, source_target_pairs={{0,2},{1,3},{2,0},{3,1},{4,6},{5,7},{6,4},{7,5},{8,10},{9,11},{10,... | collective-permute-start | bytes 1572872 | tf_op jit(solution)/shard_map/ppermute | solution.py:395
  97.0 26.8 %all-to-all-start = ((bf16[16,32,1280]{2,1,0:T(8,128)(2,1)}), bf16[16,32,1280]{2,1,0:T(8,128)(2,1)S(1)}, u32[]{:S(2)}, u32[]{:S(2)}) async-start(bf16[16,32,1280]{2,1,0:T(8,128)(2,1)} %bitcast.7), calls=%async_computation | async-start | bytes 2621440 | tf_op jit(solution)/shard_map/all_to_all | solution.py:486
  124.6 9.3 %all-to-all-start.1 = ((bf16[4,8,1280]{2,1,0:T(8,128)(2,1)}), bf16[4,8,1280]{2,1,0:T(8,128)(2,1)S(1)}, u32[]{:S(2)}, u32[]{:S(2)}) async-start(bf16[4,8,1280]{2,1,0:T(8,128)(2,1)} %bitcast.9), calls=%async_computation.1 | async-start | bytes 163840 | tf_op jit(solution)/shard_map/all_to_all | solution.py:494
  (7 other events, 37.7 us)

commit v11 on v10

--- a/solution.py
+++ b/solution.py
@@ -441,7 +441,7 @@
             dsigs[b] = d
         kv_prevs.append(along(kv, "y", 1))
     ggs = call(grad_gated_body, (bf16((BLK, 2 * BLK)),) * 4, 2, 1 << 20, 1 << 20)(info, cot, w_out)
-    *ggs, _ = lax.optimization_barrier((*ggs, evs[2]))
+    *ggs, _ = lax.optimization_barrier((*ggs, kvs[1]))
     ggs = exchange(ggs, "z")
     q, kv, att = call(
         forward_local_body, (bf16((GRP, BLK)), bf16((GRP, 2 * BLK)), f32((GRP, BLK))), 6, 5 << 30, 4 << 20

time: 135 us -> 135 us (level)
  waiting for transfers between devices: 44.9 us -> 40.8 us
  starting transfers between devices: 40.6 us -> 44.5 us
    ppermute x20, waiting for transfers between devices: 25.4 us -> 17.5 us  [along(): return lax.ppermute(x, axis, [(i, (i + d) % 4) for i in range(4)])]
    all_to_all x1, waiting for transfers between devices: 14.7 us -> 18.5 us  [body(): sums = lax.all_to_all(mine.reshape(16, 32, 5 * BLK), ('x', 'y'), 0, 0)]
    all_to_all x1, starting transfers between devices: 5.7 us -> 8.51 us  [body(): sums = lax.all_to_all(mine.reshape(16, 32, 5 * BLK), ('x', 'y'), 0, 0)]
    ppermute x20, starting transfers between devices: 31.1 us -> 32.4 us  [along(): return lax.ppermute(x, axis, [(i, (i + d) % 4) for i in range(4)])]
  transfers between devices with their start and end apart: 25 -> 25, of which waited for: 11 -> 9; matrix products, arithmetic and copies ran while one was open for 1% -> 1% of each run, Pallas kernels for 30% -> 30%
where the time goes in v11:
time: 135 us; the launch traced here: 134 us
  starting transfers between devices  44.5 us (33%)
  Pallas kernels  42.8 us (32%)
  waiting for transfers between devices  40.8 us (30%)
  local copies, waits for them, and re-layouts  5.35 us (4%)
    ppermute x20, starting transfers between devices, along(): return lax.ppermute(x, axis, [(i, (i + d) % 4) for i in range(4)])  32.4 us
    all_to_all x1, waiting for transfers between devices, body(): sums = lax.all_to_all(mine.reshape(16, 32, 5 * BLK), ('x', 'y'), 0, 0)  18.5 us
    ppermute x20, waiting for transfers between devices, along(): return lax.ppermute(x, axis, [(i, (i + d) % 4) for i in range(4)])  17.5 us
    all_to_all x1, starting transfers between devices, body(): sums = lax.all_to_all(mine.reshape(16, 32, 5 * BLK), ('x', 'y'), 0, 0)  8.51 us
    pallas_call x1, Pallas kernels, body(): call(backward_local_body, (bf16((GRP, BLK)), f32((GRP, 2 * BLK))), 8, 1 <...  7.53 us
    pallas_call x3, Pallas kernels, weights(): call(kernel, (bf16((4, 128, cols)), f32((4, 128, cols))), len(operands),...  6.29 us
    pallas_call x3, Pallas kernels, body(): call(project_body, (bf16((n * BLK, 2 * BLK)), bf16((n * BLK, BLK)), bf16(...  6.22 us
    pallas_call x1, Pallas kernels, body(): call(forward_local_body, (bf16((GRP, BLK)), bf16((GRP, 2 * BLK)), f32((GR...  5.2 us
  transfers between devices with their start and end apart: 25, of which 9 were waited for; matrix products, arithmetic and copies ran while one was open for 1% of the time, Pallas kernels for 30%

profile of v11, /device:TPU:0, one launch (start us, length us, event | category | flops | bytes accessed | tf_op | source)
XLA Modules:
  0.0 134.4 jit_solution(9317047733736622587)
XLA Ops:
  0.6 4.2 %collective-permute-start = (bf16[256,1024]{1,0:T(8,128)(2,1)}, bf16[256,1024]{1,0:T(8,128)(2,1)S(1)}, u32[]{:S(2)}, u32[]{:S(2)}) collective-permute-start(bf16[256,1024]{1,0:T(8,128)(2,1)} %bitcast.5.refs_0_), channel_id=1, source_target_pairs={{0,3},{1,0},{2,1},{3,2},{4,7},{5,4},{6,5},{7,6},{8,11},{9,8},{10,9... | collective-permute-start | bytes 1572872 | tf_op jit(solution)/shard_map/ppermute | solution.py:395
  5.6 3.4 %copy-done = bf16[1024,4096]{1,0:T(8,128)(2,1)S(1)} copy-done((bf16[1024,4096]{1,0:T(8,128)(2,1)S(1)}, bf16[1024,4096]{1,0:T(8,128)(2,1)}, u32[]{:S(2)}) %copy-start) | copy-done | bytes 8388632
  8.9 2.2 %shard_map.76 = (bf16[256,512]{1,0:T(8,128)(2,1)S(1)}, bf16[256,256]{1,0:T(8,128)(2,1)S(1)}, bf16[256,256]{1,0:T(8,128)(2,1)S(1)}, bf16[256,1024]{1,0:T(8,128)(2,1)S(1)}) custom-call(s32[12]{0:T(128)S(1)} %concatenate.3.info, bf16[256,1024]{1,0:T(8,128)(2,1)} %bitcast.5.refs_0_, bf16[1024,4096]{1,0:T(8,128)(2,1)S(1)} %copy-done), custom_call_target="tpu_custom_call" | custom-call | flops 1048576 | bytes 1048576 | tf_op jit(solution)/shard_map/pallas_call | solution.py:432
  11.2 5.1 %collective-permute-done.refs_0_.refs_1_ = bf16[256,1024]{1,0:T(8,128)(2,1)S(1)} collective-permute-done((bf16[256,1024]{1,0:T(8,128)(2,1)}, bf16[256,1024]{1,0:T(8,128)(2,1)S(1)}, u32[]{:S(2)}, u32[]{:S(2)}) %collective-permute-start) | collective-permute-done | bytes 524320 | tf_op jit(solution)/shard_map/ppermute | solution.py:395
  16.3 3.3 %collective-permute-done.1.refs_1_.refs_3_ = bf16[256,1024]{1,0:T(8,128)(2,1)S(1)} collective-permute-done((bf16[256,1024]{1,0:T(8,128)(2,1)}, bf16[256,1024]{1,0:T(8,128)(2,1)S(1)}, u32[]{:S(2)}, u32[]{:S(2)}) %collective-permute-start.1) | collective-permute-done | bytes 524320 | tf_op jit(solution)/shard_map/ppermute | solution.py:395
  21.3 2.4 %shard_map.77 = (bf16[512,512]{1,0:T(8,128)(2,1)S(1)}, bf16[512,256]{1,0:T(8,128)(2,1)S(1)}, bf16[512,256]{1,0:T(8,128)(2,1)S(1)}, bf16[256,1024]{1,0:T(8,128)(2,1)S(1)}, bf16[256,1024]{1,0:T(8,128)(2,1)S(1)}) custom-call(s32[12]{0:T(128)S(1)} %concatenate.3.info, bf16[256,1024]{1,0:T(8,128)(2,1)S(1)} %collective-permute-done.refs_0_.refs_1_, ...), custom_call_target="tpu_custom_call" | custom-call | flops 1048576 | bytes 1048576 | tf_op jit(solution)/shard_map/pallas_call | solution.py:432
  27.9 2.4 %collective-permute-start.5 = (bf16[256,512]{1,0:T(8,128)(2,1)S(1)}, bf16[256,512]{1,0:T(8,128)(2,1)S(1)}, u32[]{:S(2)}, u32[]{:S(2)}) collective-permute-start(bf16[256,512]{1,0:T(8,128)(2,1)S(1)} %get-tuple-element.83), channel_id=1, source_target_pairs={{0,2},{1,3},{2,0},{3,1},{4,6},{5,7},{6,4},{7,5},{8,10},{9,11},{10,... | collective-permute-start | bytes 786440 | tf_op jit(solution)/shard_map/ppermute | solution.py:395
  30.3 5.9 %collective-permute-done.2.refs_0_.refs_2_ = bf16[256,1024]{1,0:T(8,128)(2,1)S(1)} collective-permute-done((bf16[256,1024]{1,0:T(8,128)(2,1)}, bf16[256,1024]{1,0:T(8,128)(2,1)S(1)}, u32[]{:S(2)}, u32[]{:S(2)}) %collective-permute-start.2) | collective-permute-done | bytes 524320 | tf_op jit(solution)/shard_map/ppermute | solution.py:395
  39.8 5.2 %shard_map.79 = (bf16[1024,256]{1,0:T(8,128)(2,1)S(1)}, bf16[1024,512]{1,0:T(8,128)(2,1)S(1)}, f32[1024,256]{1,0:T(8,128)S(1)}) custom-call(s32[12]{0:T(128)S(1)} %concatenate.3.info, bf16[256,256]{1,0:T(8,128)(2,1)S(1)} %get-tuple-element.66.refs_0_, bf16[512,256]{1,0:T(8,128)(2,1)S(1)} %get-tuple-element.70.refs_1_, ...), custom_call_target="tpu_custom_call" | custom-call | flops 5368709120 | bytes 4194304 | tf_op jit(solution)/shard_map/pallas_call | solution.py:446
  45.8 1.7 %shard_map.81 = (f32[1024,256]{1,0:T(8,128)S(1)}, bf16[1024,512]{1,0:T(8,128)(2,1)S(1)}, bf16[1024,256]{1,0:T(8,128)(2,1)S(1)}, bf16[1024,256]{1,0:T(8,128)(2,1)...) custom-call(s32[12]{0:T(128)S(1)} %concatenate.3.info, bf16[1024,256]{1,0:T(8,128)(2,1)S(1)} %get-tuple-element.75.refs_0_, ...), custom_call_target="tpu_custom_call" | custom-call | flops 5368709120 | bytes 4194304 | tf_op jit(solution)/shard_map/pallas_call | solution.py:450
  48.2 3.1 %collective-permute-start.11 = (f32[8,1024]{1,0:T(8,128)S(1)}, f32[8,1024]{1,0:T(8,128)S(1)}, u32[]{:S(2)}, u32[]{:S(2)}) collective-permute-start(f32[8,1024]{1,0:T(8,128)S(1)} %get-tuple-element.91.refs_3_), channel_id=1, source_target_pairs={{0,2},{1,3},{2,0},{3,1},{4,6},{5,7},{6,4},{7,5},{8,10},{9,11},{10,... | collective-permute-start | bytes 98312 | tf_op jit(solution)/shard_map/ppermute | solution.py:395
  51.3 4.0 %collective-permute-start.3 = (bf16[1024,256]{1,0:T(8,128)(2,1)S(1)}, bf16[1024,256]{1,0:T(8,128)(2,1)S(1)}, u32[]{:S(2)}, u32[]{:S(2)}) collective-permute-start(bf16[1024,256]{1,0:T(8,128)(2,1)S(1)} %get-tuple-element.75.refs_0_), channel_id=1, source_target_pairs={{0,12},{4,0},{8,4},{12,8},{1,13},{5,1},{9,5},{13,9},{2,14},{6,2},{... | collective-permute-start | bytes 1572872 | tf_op jit(solution)/shard_map/ppermute | solution.py:395
  58.1 4.1 %collective-permute-start.13 = (bf16[1024,256]{1,0:T(8,128)(2,1)S(1)}, bf16[1024,256]{1,0:T(8,128)(2,1)S(1)}, u32[]{:S(2)}, u32[]{:S(2)}) collective-permute-start(bf16[1024,256]{1,0:T(8,128)(2,1)S(1)} %get-tuple-element.96.refs_1_), channel_id=1, source_target_pairs={{0,12},{4,0},{8,4},{12,8},{1,13},{5,1},{9,5},{13,9},{2,14},{6,2},{... | collective-permute-start | bytes 1572872 | tf_op jit(solution)/shard_map/ppermute | solution.py:395
  64.2 7.5 %shard_map.83 = (bf16[1024,256]{1,0:T(8,128)(2,1)S(1)}, f32[1024,512]{1,0:T(8,128)S(1)}) custom-call(s32[12]{0:T(128)S(1)} %concatenate.3.info, bf16[1024,256]{1,0:T(8,128)(2,1)S(1)} %get-tuple-element.75.refs_0_, bf16[1024,256]{1,0:T(8,128)(2,1)S(1)} %get-tuple-element.96.refs_1_, bf16[1024,512]{1,0:T(8,128)(2,1)S(1)} %get-tuple-element.98.refs_2_, ...), custom_call_target="tpu_custom_call" | custom-call | flops 1048576 | bytes 1048576 | tf_op jit(solution)/shard_map/pallas_call | solution.py:460
  71.7 2.5 %shard_map.84 = (bf16[4,128,512]{2,1,0:T(8,128)(2,1)S(1)}, f32[4,128,512]{2,1,0:T(8,128)S(1)}) custom-call(s32[12]{0:T(128)S(1)} %concatenate.3.info, bf16[256,1024]{1,0:T(8,128)(2,1)} %bitcast.5.refs_0_, bf16[256,1024]{1,0:T(8,128)(2,1)S(1)} %collective-permute-done.refs_0_.refs_1_, bf16[256,1024]{1,0:T(8,128)(2,1)S(1)} %collective-permute-done.2.refs_0_.refs_2_, ...), custom_call_target="tpu_custom_call" | custom-call | flops 1048576 | bytes 1048576 | tf_op jit(solution)/shard_map/pallas_call | solution.py:465
  75.6 5.0 %shard_map.85 = (bf16[256,1024]{1,0:T(8,128)(2,1)S(1)}, bf16[256,1024]{1,0:T(8,128)(2,1)S(1)}, bf16[256,1024]{1,0:T(8,128)(2,1)S(1)}, bf16[256,1024]{1,0:T(8,128)(2,1)S(1)}) custom-call(s32[12]{0:T(128)S(1)} %concatenate.3.info, bf16[1024,256]{1,0:T(8,128)(2,1)S(1)} %collective-permute-done.3.refs_0_, bf16[1024,256]{1,0:T(8,128)(2,1)S(1)} %collective-permute-done.13.refs_1_, ...), custom_call_target="tpu_custom_call" | custom-call | flops 5368709120 | bytes 4194304 | tf_op jit(solution)/shard_map/pallas_call | solution.py:473
  80.6 2.5 %shard_map.86 = (bf16[4,128,512]{2,1,0:T(8,128)(2,1)S(1)}, f32[4,128,512]{2,1,0:T(8,128)S(1)}) custom-call(s32[12]{0:T(128)S(1)} %concatenate.3.info, bf16[256,1024]{1,0:T(8,128)(2,1)} %bitcast.5.refs_0_, bf16[256,1024]{1,0:T(8,128)(2,1)S(1)} %collective-permute-done.refs_0_.refs_1_, bf16[256,1024]{1,0:T(8,128)(2,1)S(1)} %collective-permute-done.2.refs_0_.refs_2_, ...), custom_call_target="tpu_custom_call" | custom-call | flops 1048576 | bytes 1048576 | tf_op jit(solution)/shard_map/pallas_call | solution.py:465
  83.1 2.9 %shard_map.87 = (f32[256,1024]{1,0:T(8,128)S(1)}, bf16[256,1024]{1,0:T(8,128)(2,1)S(1)}, bf16[256,1024]{1,0:T(8,128)(2,1)S(1)}, bf16[256,1024]{1,0:T(8,128)(2,1)S(1)}) custom-call(s32[12]{0:T(128)S(1)} %concatenate.3.info, bf16[256,1024]{1,0:T(8,128)(2,1)S(1)} %get-tuple-element.107.refs_4_.refs_0_, ...), custom_call_target="tpu_custom_call" | custom-call | flops 1048576 | bytes 1048576 | tf_op jit(solution)/shard_map/pallas_call | solution.py:477
  86.1 1.9 %collective-permute-start.20 = (bf16[256,1024]{1,0:T(8,128)(2,1)S(1)}, bf16[256,1024]{1,0:T(8,128)(2,1)}, u32[]{:S(2)}, u32[]{:S(2)}) collective-permute-start(bf16[256,1024]{1,0:T(8,128)(2,1)S(1)} %get-tuple-element.121), channel_id=1, source_target_pairs={{0,1},{1,2},{2,3},{3,0},{4,5},{5,6},{6,7},{7,4},{8,9},{9,10},{10,1... | collective-permute-start | bytes 1572872 | tf_op jit(solution)/shard_map/ppermute | solution.py:395
  90.9 2.1 %collective-permute-start.22 = (bf16[256,1024]{1,0:T(8,128)(2,1)S(1)}, bf16[256,1024]{1,0:T(8,128)(2,1)S(1)}, u32[]{:S(2)}, u32[]{:S(2)}) collective-permute-start(bf16[256,1024]{1,0:T(8,128)(2,1)S(1)} %get-tuple-element.126), channel_id=1, source_target_pairs={{0,2},{1,3},{2,0},{3,1},{4,6},{5,7},{6,4},{7,5},{8,10},{9,11},{10,... | collective-permute-start | bytes 1572872 | tf_op jit(solution)/shard_map/ppermute | solution.py:395
  94.3 8.5 %all-to-all-start = ((bf16[16,32,1280]{2,1,0:T(8,128)(2,1)}), bf16[16,32,1280]{2,1,0:T(8,128)(2,1)S(1)}, u32[]{:S(2)}, u32[]{:S(2)}) async-start(bf16[16,32,1280]{2,1,0:T(8,128)(2,1)} %bitcast.7), calls=%async_computation | async-start | bytes 2621440 | tf_op jit(solution)/shard_map/all_to_all | solution.py:486
  105.5 18.5 %all-to-all-done.got = bf16[16,32,1280]{2,1,0:T(8,128)(2,1)S(1)} async-done(((bf16[16,32,1280]{2,1,0:T(8,128)(2,1)}), bf16[16,32,1280]{2,1,0:T(8,128)(2,1)S(1)}, u32[]{:S(2)}, u32[]{:S(2)}) %all-to-all-start) | async-done | bytes 1310752 | tf_op jit(solution)/shard_map/all_to_all | solution.py:486
  124.8 3.3 %all-to-all-start.1 = ((bf16[4,8,1280]{2,1,0:T(8,128)(2,1)}), bf16[4,8,1280]{2,1,0:T(8,128)(2,1)S(1)}, u32[]{:S(2)}, u32[]{:S(2)}) async-start(bf16[4,8,1280]{2,1,0:T(8,128)(2,1)} %bitcast.9), calls=%async_computation.1 | async-start | bytes 163840 | tf_op jit(solution)/shard_map/all_to_all | solution.py:494
  128.9 4.8 %all-to-all-done.1.got = bf16[4,8,1280]{2,1,0:T(8,128)(2,1)S(1)} async-done(((bf16[4,8,1280]{2,1,0:T(8,128)(2,1)}), bf16[4,8,1280]{2,1,0:T(8,128)(2,1)S(1)}, u32[]{:S(2)}, u32[]{:S(2)}) %all-to-all-start.1) | async-done | bytes 81952 | tf_op jit(solution)/shard_map/all_to_all | solution.py:494
  (57 shorter events, 26.9 us)
Async XLA Ops:
  0.6 15.7 %collective-permute-start = (bf16[256,1024]{1,0:T(8,128)(2,1)}, bf16[256,1024]{1,0:T(8,128)(2,1)S(1)}, u32[]{:S(2)}, u32[]{:S(2)}) collective-permute-start(bf16[256,1024]{1,0:T(8,128)(2,1)} %bitcast.5.refs_0_), channel_id=1, source_target_pairs={{0,3},{1,0},{2,1},{3,2},{4,7},{5,4},{6,5},{7,6},{8,11},{9,8},{10,9... | collective-permute-start | bytes 1572872 | tf_op jit(solution)/shard_map/ppermute | solution.py:395
  4.8 14.8 %collective-permute-start.1 = (bf16[256,1024]{1,0:T(8,128)(2,1)}, bf16[256,1024]{1,0:T(8,128)(2,1)S(1)}, u32[]{:S(2)}, u32[]{:S(2)}) collective-permute-start(bf16[256,1024]{1,0:T(8,128)(2,1)} %bitcast.5.refs_0_), channel_id=1, source_target_pairs={{0,1},{1,2},{2,3},{3,0},{4,5},{5,6},{6,7},{7,4},{8,9},{9,10},{10,1... | collective-permute-start | bytes 1572872 | tf_op jit(solution)/shard_map/ppermute | solution.py:395
  19.6 16.6 %collective-permute-start.2 = (bf16[256,1024]{1,0:T(8,128)(2,1)}, bf16[256,1024]{1,0:T(8,128)(2,1)S(1)}, u32[]{:S(2)}, u32[]{:S(2)}) collective-permute-start(bf16[256,1024]{1,0:T(8,128)(2,1)} %bitcast.5.refs_0_), channel_id=1, source_target_pairs={{0,2},{1,3},{2,0},{3,1},{4,6},{5,7},{6,4},{7,5},{8,10},{9,11},{10,... | collective-permute-start | bytes 1572872 | tf_op jit(solution)/shard_map/ppermute | solution.py:395
  19.6 18.5 %collective-permute-start.7 = (bf16[256,512]{1,0:T(8,128)(2,1)S(1)}, bf16[256,512]{1,0:T(8,128)(2,1)S(1)}, u32[]{:S(2)}, u32[]{:S(2)}) collective-permute-start(bf16[256,512]{1,0:T(8,128)(2,1)S(1)} %get-tuple-element.67.refs_3_), channel_id=1, source_target_pairs={{0,4},{4,8},{8,12},{12,0},{1,5},{5,9},{9,13},{13,1},{2,6},{6,10},{... | collective-permute-start | bytes 786440 | tf_op jit(solution)/shard_map/ppermute | solution.py:395
  23.7 21.4 %collective-permute-start.8 = (bf16[512,512]{1,0:T(8,128)(2,1)S(1)}, bf16[512,512]{1,0:T(8,128)(2,1)S(1)}, u32[]{:S(2)}, u32[]{:S(2)}) collective-permute-start(bf16[512,512]{1,0:T(8,128)(2,1)S(1)} %get-tuple-element.73.refs_4_), channel_id=1, source_target_pairs={{0,4},{4,8},{8,12},{12,0},{1,5},{5,9},{9,13},{13,1},{2,6},{6,10},{... | collective-permute-start | bytes 1572872 | tf_op jit(solution)/shard_map/ppermute | solution.py:395
  26.7 18.3 %collective-permute-start.4 = (bf16[256,512]{1,0:T(8,128)(2,1)S(1)}, bf16[256,512]{1,0:T(8,128)(2,1)S(1)}, u32[]{:S(2)}, u32[]{:S(2)}) collective-permute-start(bf16[256,512]{1,0:T(8,128)(2,1)S(1)} %get-tuple-element.82), channel_id=1, source_target_pairs={{0,1},{1,2},{2,3},{3,0},{4,5},{5,6},{6,7},{7,4},{8,9},{9,10},{10,1... | collective-permute-start | bytes 786440 | tf_op jit(solution)/shard_map/ppermute | solution.py:395
  27.9 17.2 %collective-permute-start.5 = (bf16[256,512]{1,0:T(8,128)(2,1)S(1)}, bf16[256,512]{1,0:T(8,128)(2,1)S(1)}, u32[]{:S(2)}, u32[]{:S(2)}) collective-permute-start(bf16[256,512]{1,0:T(8,128)(2,1)S(1)} %get-tuple-element.83), channel_id=1, source_target_pairs={{0,2},{1,3},{2,0},{3,1},{4,6},{5,7},{6,4},{7,5},{8,10},{9,11},{10,... | collective-permute-start | bytes 786440 | tf_op jit(solution)/shard_map/ppermute | solution.py:395
  36.2 8.9 %collective-permute-start.6 = (bf16[256,512]{1,0:T(8,128)(2,1)S(1)}, bf16[256,512]{1,0:T(8,128)(2,1)S(1)}, u32[]{:S(2)}, u32[]{:S(2)}) collective-permute-start(bf16[256,512]{1,0:T(8,128)(2,1)S(1)} %get-tuple-element.84), channel_id=1, source_target_pairs={{0,3},{1,0},{2,1},{3,2},{4,7},{5,4},{6,5},{7,6},{8,11},{9,8},{10,9... | collective-permute-start | bytes 786440 | tf_op jit(solution)/shard_map/ppermute | solution.py:395
  38.2 7.7 %collective-permute-start.9 = (bf16[256,512]{1,0:T(8,128)(2,1)S(1)}, bf16[256,512]{1,0:T(8,128)(2,1)S(1)}, u32[]{:S(2)}, u32[]{:S(2)}) collective-permute-start(bf16[256,512]{1,0:T(8,128)(2,1)S(1)} %get-tuple-element.74.refs_5_), channel_id=1, source_target_pairs={{0,4},{4,8},{8,12},{12,0},{1,5},{5,9},{9,13},{13,1},{2,6},{6,10},{... | collective-permute-start | bytes 786440 | tf_op jit(solution)/shard_map/ppermute | solution.py:395
  47.5 7.8 %collective-permute-start.10 = (f32[8,1024]{1,0:T(8,128)S(1)}, f32[8,1024]{1,0:T(8,128)S(1)}, u32[]{:S(2)}, u32[]{:S(2)}) collective-permute-start(f32[8,1024]{1,0:T(8,128)S(1)} %get-tuple-element.91.refs_3_), channel_id=1, source_target_pairs={{0,3},{1,0},{2,1},{3,2},{4,7},{5,4},{6,5},{7,6},{8,11},{9,8},{10,9... | collective-permute-start | bytes 98312 | tf_op jit(solution)/shard_map/ppermute | solution.py:395
  48.2 7.2 %collective-permute-start.11 = (f32[8,1024]{1,0:T(8,128)S(1)}, f32[8,1024]{1,0:T(8,128)S(1)}, u32[]{:S(2)}, u32[]{:S(2)}) collective-permute-start(f32[8,1024]{1,0:T(8,128)S(1)} %get-tuple-element.91.refs_3_), channel_id=1, source_target_pairs={{0,2},{1,3},{2,0},{3,1},{4,6},{5,7},{6,4},{7,5},{8,10},{9,11},{10,... | collective-permute-start | bytes 98312 | tf_op jit(solution)/shard_map/ppermute | solution.py:395
  51.3 5.1 %collective-permute-start.12 = (f32[8,1024]{1,0:T(8,128)S(1)}, f32[8,1024]{1,0:T(8,128)S(1)}, u32[]{:S(2)}, u32[]{:S(2)}) collective-permute-start(f32[8,1024]{1,0:T(8,128)S(1)} %get-tuple-element.91.refs_3_), channel_id=1, source_target_pairs={{0,1},{1,2},{2,3},{3,0},{4,5},{5,6},{6,7},{7,4},{8,9},{9,10},{10,1... | collective-permute-start | bytes 98312 | tf_op jit(solution)/shard_map/ppermute | solution.py:395
  51.3 22.9 %collective-permute-start.3 = (bf16[1024,256]{1,0:T(8,128)(2,1)S(1)}, bf16[1024,256]{1,0:T(8,128)(2,1)S(1)}, u32[]{:S(2)}, u32[]{:S(2)}) collective-permute-start(bf16[1024,256]{1,0:T(8,128)(2,1)S(1)} %get-tuple-element.75.refs_0_), channel_id=1, source_target_pairs={{0,12},{4,0},{8,4},{12,8},{1,13},{5,1},{9,5},{13,9},{2,14},{6,2},{... | collective-permute-start | bytes 1572872 | tf_op jit(solution)/shard_map/ppermute | solution.py:395
  58.1 17.4 %collective-permute-start.13 = (bf16[1024,256]{1,0:T(8,128)(2,1)S(1)}, bf16[1024,256]{1,0:T(8,128)(2,1)S(1)}, u32[]{:S(2)}, u32[]{:S(2)}) collective-permute-start(bf16[1024,256]{1,0:T(8,128)(2,1)S(1)} %get-tuple-element.96.refs_1_), channel_id=1, source_target_pairs={{0,12},{4,0},{8,4},{12,8},{1,13},{5,1},{9,5},{13,9},{2,14},{6,2},{... | collective-permute-start | bytes 1572872 | tf_op jit(solution)/shard_map/ppermute | solution.py:395
  62.2 23.9 %collective-permute-start.14 = (bf16[1024,256]{1,0:T(8,128)(2,1)S(1)}, bf16[1024,256]{1,0:T(8,128)(2,1)S(1)}, u32[]{:S(2)}, u32[]{:S(2)}) collective-permute-start(bf16[1024,256]{1,0:T(8,128)(2,1)S(1)} %get-tuple-element.114.refs_0_), channel_id=1, source_target_pairs={{0,3},{1,0},{2,1},{3,2},{4,7},{5,4},{6,5},{7,6},{8,11},{9,8},{10,9... | collective-permute-start | bytes 1572872 | tf_op jit(solution)/shard_map/ppermute | solution.py:395
  62.4 25.6 %collective-permute-start.15 = (bf16[1024,256]{1,0:T(8,128)(2,1)S(1)}, bf16[1024,256]{1,0:T(8,128)(2,1)S(1)}, u32[]{:S(2)}, u32[]{:S(2)}) collective-permute-start(bf16[1024,256]{1,0:T(8,128)(2,1)S(1)} %get-tuple-element.114.refs_0_), channel_id=1, source_target_pairs={{0,2},{1,3},{2,0},{3,1},{4,6},{5,7},{6,4},{7,5},{8,10},{9,11},{10,... | collective-permute-start | bytes 1572872 | tf_op jit(solution)/shard_map/ppermute | solution.py:395
  63.4 26.0 %collective-permute-start.16 = (bf16[1024,256]{1,0:T(8,128)(2,1)S(1)}, bf16[1024,256]{1,0:T(8,128)(2,1)S(1)}, u32[]{:S(2)}, u32[]{:S(2)}) collective-permute-start(bf16[1024,256]{1,0:T(8,128)(2,1)S(1)} %get-tuple-element.114.refs_0_), channel_id=1, source_target_pairs={{0,1},{1,2},{2,3},{3,0},{4,5},{5,6},{6,7},{7,4},{8,9},{9,10},{10,1... | collective-permute-start | bytes 1572872 | tf_op jit(solution)/shard_map/ppermute | solution.py:395
  74.2 16.6 %collective-permute-start.17 = (bf16[4,128,512]{2,1,0:T(8,128)(2,1)S(1)}, bf16[4,128,512]{2,1,0:T(8,128)(2,1)S(1)}, u32[]{:S(2)}, u32[]{:S(2)}) collective-permute-start(bf16[4,128,512]{2,1,0:T(8,128)(2,1)S(1)} %get-tuple-element.117), channel_id=1, source_target_pairs={{0,16},{16,0},{1,17},{17,1},{2,18},{18,2},{3,19},{19,3},{4,20},{20... | collective-permute-start | bytes 1572872 | tf_op jit(solution)/shard_map/ppermute | solution.py:399
  83.0 10.0 %collective-permute-start.18 = (bf16[4,128,512]{2,1,0:T(8,128)(2,1)S(1)}, bf16[4,128,512]{2,1,0:T(8,128)(2,1)S(1)}, u32[]{:S(2)}, u32[]{:S(2)}) collective-permute-start(bf16[4,128,512]{2,1,0:T(8,128)(2,1)S(1)} %get-tuple-element.118), channel_id=1, source_target_pairs={{0,16},{16,0},{1,17},{17,1},{2,18},{18,2},{3,19},{19,3},{4,20},{20... | collective-permute-start | bytes 1572872 | tf_op jit(solution)/shard_map/ppermute | solution.py:399
  86.1 16.8 %collective-permute-start.20 = (bf16[256,1024]{1,0:T(8,128)(2,1)S(1)}, bf16[256,1024]{1,0:T(8,128)(2,1)}, u32[]{:S(2)}, u32[]{:S(2)}) collective-permute-start(bf16[256,1024]{1,0:T(8,128)(2,1)S(1)} %get-tuple-element.121), channel_id=1, source_target_pairs={{0,1},{1,2},{2,3},{3,0},{4,5},{5,6},{6,7},{7,4},{8,9},{9,10},{10,1... | collective-permute-start | bytes 1572872 | tf_op jit(solution)/shard_map/ppermute | solution.py:395
  88.0 14.9 %collective-permute-start.21 = (bf16[256,1024]{1,0:T(8,128)(2,1)S(1)}, bf16[256,1024]{1,0:T(8,128)(2,1)}, u32[]{:S(2)}, u32[]{:S(2)}) collective-permute-start(bf16[256,1024]{1,0:T(8,128)(2,1)S(1)} %get-tuple-element.122), channel_id=1, source_target_pairs={{0,3},{1,0},{2,1},{3,2},{4,7},{5,4},{6,5},{7,6},{8,11},{9,8},{10,9... | collective-permute-start | bytes 1572872 | tf_op jit(solution)/shard_map/ppermute | solution.py:395
  90.9 37.2 %collective-permute-start.22 = (bf16[256,1024]{1,0:T(8,128)(2,1)S(1)}, bf16[256,1024]{1,0:T(8,128)(2,1)S(1)}, u32[]{:S(2)}, u32[]{:S(2)}) collective-permute-start(bf16[256,1024]{1,0:T(8,128)(2,1)S(1)} %get-tuple-element.126), channel_id=1, source_target_pairs={{0,2},{1,3},{2,0},{3,1},{4,6},{5,7},{6,4},{7,5},{8,10},{9,11},{10,... | collective-permute-start | bytes 1572872 | tf_op jit(solution)/shard_map/ppermute | solution.py:395
  94.3 29.6 %all-to-all-start = ((bf16[16,32,1280]{2,1,0:T(8,128)(2,1)}), bf16[16,32,1280]{2,1,0:T(8,128)(2,1)S(1)}, u32[]{:S(2)}, u32[]{:S(2)}) async-start(bf16[16,32,1280]{2,1,0:T(8,128)(2,1)} %bitcast.7), calls=%async_computation | async-start | bytes 2621440 | tf_op jit(solution)/shard_map/all_to_all | solution.py:486
  124.8 9.0 %all-to-all-start.1 = ((bf16[4,8,1280]{2,1,0:T(8,128)(2,1)}), bf16[4,8,1280]{2,1,0:T(8,128)(2,1)S(1)}, u32[]{:S(2)}, u32[]{:S(2)}) async-start(bf16[4,8,1280]{2,1,0:T(8,128)(2,1)} %bitcast.9), calls=%async_computation.1 | async-start | bytes 163840 | tf_op jit(solution)/shard_map/all_to_all | solution.py:494
  (7 other events, 39.0 us)

commit v12 on v11

--- a/solution.py
+++ b/solution.py
@@ -253,22 +253,26 @@
     pack(info, acc, send, keep)
 
 
-def add_core_body(keep_1, keep_2, keep_3, got_1, got_2, got_3, out):
-    out[:, :, 0:512] = (keep_1[...] + got_1[...].astype(F32)).astype(BF16)
-    out[:, :, 512:1024] = (keep_2[...] + got_2[...].astype(F32)).astype(BF16)
-    out[:, :, 1024:] = (keep_3[...] + got_3[...].astype(F32)).astype(BF16)
-
-
-def add_xy_body(got, total):
-    part = got[0].astype(F32)
-    for xy in range(1, 16):
-        part = part + got[xy].astype(F32)
+def add_core_body(info, *refs):
+    keep, got, away, own = refs[0:3], refs[3:6], refs[6:9], refs[9]
+    for k, g, lanes in zip(keep, got, (slice(0, 512), slice(512, 1024), slice(1024, 1280))):
+        for d in (1, 2, 3):
+            at = lax.rem(info[11] + d, 4)
+            away[d - 1][:, lanes] = (k[at] + g[at].astype(F32)).astype(BF16)
+        own[:, lanes] = k[info[11]] + g[info[11]].astype(F32)
+
+
+def add_x_body(own, got_1, got_2, got_3, total):
+    part = own[...] + got_1[...].astype(F32) + got_2[...].astype(F32) + got_3[...].astype(F32)
     total[...] = part.astype(BF16)
 
 
-def last_body(got, grad_w_in, grad_w_out):
+def last_sum_body(got, grad_w_in, grad_w_out):
     for z in range(4):
-        part = got[z]
+        part = got[z].astype(F32)
+        for y in range(1, 4):
+            part = part + got[y * 4 + z].astype(F32)
+        part = part.astype(BF16)
         for n, to in enumerate((0, 2, 1, 3)):
             at = to * D + z * BLK
             grad_w_in[:, at : at + BLK] = part[:, n * BLK : (n + 1) * BLK]
@@ -473,27 +477,28 @@
     gp = call(
         backward_later_body, (bf16((BLK, 4 * BLK)),) * 4, 10, 5 << 30, 4 << 20, [pltpu.VMEM((GRP, 2 * BLK), F32)]
     )(info, q_next, g_next, kv, dkv, gp_g, gp_q, *dsigs)
-    got_2, keep_2 = weights(late_weights_body, 512, (*evs, *gp))
     *partial, = call(
         input_body, (f32((BLK, D)),) + (bf16((BLK, D)),) * 3, 6, 1 << 20, 1 << 20
     )(info, *gp, w_in, cot)
-    cot_z, keep_2, partial[0] = lax.optimization_barrier((cot_z, keep_2, partial[0]))
+    *gp, partial[0] = lax.optimization_barrier((*gp, partial[0]))
+    got_2, keep_2 = weights(late_weights_body, 512, (*evs, *gp))
+    cot_z, keep_2 = lax.optimization_barrier((cot_z, keep_2))
     partial = exchange(partial, "z")
     got_3, keep_3 = weights(out_weights_body, 256, (*gateds, cot_z))
-    mine = call(
-        add_core_body, bf16((4, 128, 5 * BLK)), 6, 1 << 20, 1 << 20, scalars=0
-    )(keep_1, keep_2, keep_3, got_1, got_2, got_3)
-    sums = lax.all_to_all(mine.reshape(16, 32, 5 * BLK), ("x", "y"), 0, 0)
+    *away, own = call(
+        add_core_body, (bf16((128, 5 * BLK)),) * 3 + (f32((128, 5 * BLK)),), 6, 1 << 20, 1 << 20
+    )(info, keep_1, keep_2, keep_3, got_1, got_2, got_3)
+    sums = exchange([own] + away, "x")
     near_rows = call(
         add_near_body, f32((BLK, D)), 3, 40 << 30, 4 << 20, scalars=0
     )(partial[0], partial[1], partial[3])
-    sums, near_rows = lax.optimization_barrier((sums, near_rows))
-    total = call(add_xy_body, bf16((32, 5 * BLK)), 1, 1 << 20, 1 << 20, scalars=0)(sums)
+    own, near_rows = lax.optimization_barrier((own, near_rows))
+    total = call(add_x_body, bf16((128, 5 * BLK)), 4, 1 << 20, 1 << 20, scalars=0)(own, *sums[1:])
     _, near_rows = lax.optimization_barrier((total, near_rows))
     grad_events = call(add_far_body, bf16((BLK, D)), 2, 1 << 20, 4 << 20, scalars=0)(near_rows, partial[2])
-    got = lax.all_to_all(total.reshape(4, 8, 5 * BLK), "z", 0, 0)
+    got = lax.all_to_all(total.reshape(16, 8, 5 * BLK), ("y", "z"), 0, 0)
     grad_w_in, grad_w_out = call(
-        last_body, (bf16((8, 4 * D)), bf16((8, D))), 1, 1 << 20, 1 << 20, scalars=0
+        last_sum_body, (bf16((8, 4 * D)), bf16((8, D))), 1, 1 << 20, 1 << 20, scalars=0
     )(got)
     return grad_events[None], grad_w_in, grad_w_out
 

time: 135 us -> 141 us (1.044)
  starting transfers between devices: 44.5 us -> 56.9 us
  waiting for transfers between devices: 40.8 us -> 35.9 us
  Pallas kernels: 42.8 us -> 41.2 us
    all_to_all x2 -> x1, waiting for transfers between devices: 23.3 us -> 7.93 us  [body(): got = lax.all_to_all(total.reshape(16, 8, 5 * BLK), ('y', 'z'), 0, 0)]
    ppermute x20 -> x23, waiting for transfers between devices: 17.5 us -> 27.9 us  [along(): return lax.ppermute(x, axis, [(i, (i + d) % 4) for i in range(4)])]
    ppermute x20 -> x23, starting transfers between devices: 32.4 us -> 41.7 us  [along(): return lax.ppermute(x, axis, [(i, (i + d) % 4) for i in range(4)])]
    all_to_all x2 -> x1, starting transfers between devices: 11.8 us -> 15 us  [body(): got = lax.all_to_all(total.reshape(16, 8, 5 * BLK), ('y', 'z'), 0, 0)]
    unnamed x12 -> x8, local copies, waits for them, and re-layouts: 4.62 us -> 3.39 us
  transfers between devices with their start and end apart: 25 -> 27, of which waited for: 9 -> 11; matrix products, arithmetic and copies ran while one was open for 1% -> 1% of each run, Pallas kernels for 30% -> 28%
where the time goes in v12:
time: 141 us; the launch traced here: 139 us
  starting transfers between devices  56.9 us (40%)
  Pallas kernels  41.2 us (29%)
  waiting for transfers between devices  35.9 us (25%)
  local copies, waits for them, and re-layouts  4.13 us (3%)
    ppermute x23, starting transfers between devices, along(): return lax.ppermute(x, axis, [(i, (i + d) % 4) for i in range(4)])  41.7 us
    ppermute x23, waiting for transfers between devices, along(): return lax.ppermute(x, axis, [(i, (i + d) % 4) for i in range(4)])  27.9 us
    all_to_all x1, starting transfers between devices, body(): got = lax.all_to_all(total.reshape(16, 8, 5 * BLK), ('y', 'z'), 0, 0)  15 us
    all_to_all x1, waiting for transfers between devices, body(): got = lax.all_to_all(total.reshape(16, 8, 5 * BLK), ('y', 'z'), 0, 0)  7.93 us
    pallas_call x1, Pallas kernels, body(): call(backward_local_body, (bf16((GRP, BLK)), f32((GRP, 2 * BLK))), 8, 1 <...  7.53 us
    pallas_call x3, Pallas kernels, weights(): call(kernel, (bf16((4, 128, cols)), f32((4, 128, cols))), len(operands),...  6.29 us
    pallas_call x3, Pallas kernels, body(): call(project_body, (bf16((n * BLK, 2 * BLK)), bf16((n * BLK, BLK)), bf16(...  6.22 us
    pallas_call x1, Pallas kernels, body(): call(forward_local_body, (bf16((GRP, BLK)), bf16((GRP, 2 * BLK)), f32((GR...  5.2 us
  transfers between devices with their start and end apart: 27, of which 11 were waited for; matrix products, arithmetic and copies ran while one was open for 1% of the time, Pallas kernels for 28%

profile of v12, /device:TPU:0, one launch (start us, length us, event | category | flops | bytes accessed | tf_op | source)
XLA Modules:
  0.0 139.0 jit_solution(5628629141140759938)
XLA Ops:
  0.6 4.2 %collective-permute-start = (bf16[256,1024]{1,0:T(8,128)(2,1)}, bf16[256,1024]{1,0:T(8,128)(2,1)S(1)}, u32[]{:S(2)}, u32[]{:S(2)}) collective-permute-start(bf16[256,1024]{1,0:T(8,128)(2,1)} %bitcast.5.refs_0_), channel_id=1, source_target_pairs={{0,3},{1,0},{2,1},{3,2},{4,7},{5,4},{6,5},{7,6},{8,11},{9,8},{10,9... | collective-permute-start | bytes 1572872 | tf_op jit(solution)/shard_map/ppermute | solution.py:399
  5.6 3.4 %copy-done = bf16[1024,4096]{1,0:T(8,128)(2,1)S(1)} copy-done((bf16[1024,4096]{1,0:T(8,128)(2,1)S(1)}, bf16[1024,4096]{1,0:T(8,128)(2,1)}, u32[]{:S(2)}) %copy-start) | copy-done | bytes 8388632
  8.9 2.2 %shard_map.76 = (bf16[256,512]{1,0:T(8,128)(2,1)S(1)}, bf16[256,256]{1,0:T(8,128)(2,1)S(1)}, bf16[256,256]{1,0:T(8,128)(2,1)S(1)}, bf16[256,1024]{1,0:T(8,128)(2,1)S(1)}) custom-call(s32[12]{0:T(128)S(1)} %concatenate.3.info, bf16[256,1024]{1,0:T(8,128)(2,1)} %bitcast.5.refs_0_, bf16[1024,4096]{1,0:T(8,128)(2,1)S(1)} %copy-done), custom_call_target="tpu_custom_call" | custom-call | flops 1048576 | bytes 1048576 | tf_op jit(solution)/shard_map/pallas_call | solution.py:436
  11.2 5.1 %collective-permute-done.refs_0_.refs_1_ = bf16[256,1024]{1,0:T(8,128)(2,1)S(1)} collective-permute-done((bf16[256,1024]{1,0:T(8,128)(2,1)}, bf16[256,1024]{1,0:T(8,128)(2,1)S(1)}, u32[]{:S(2)}, u32[]{:S(2)}) %collective-permute-start) | collective-permute-done | bytes 524320 | tf_op jit(solution)/shard_map/ppermute | solution.py:399
  16.3 3.3 %collective-permute-done.1.refs_1_.refs_3_ = bf16[256,1024]{1,0:T(8,128)(2,1)S(1)} collective-permute-done((bf16[256,1024]{1,0:T(8,128)(2,1)}, bf16[256,1024]{1,0:T(8,128)(2,1)S(1)}, u32[]{:S(2)}, u32[]{:S(2)}) %collective-permute-start.1) | collective-permute-done | bytes 524320 | tf_op jit(solution)/shard_map/ppermute | solution.py:399
  21.3 2.4 %shard_map.77 = (bf16[512,512]{1,0:T(8,128)(2,1)S(1)}, bf16[512,256]{1,0:T(8,128)(2,1)S(1)}, bf16[512,256]{1,0:T(8,128)(2,1)S(1)}, bf16[256,1024]{1,0:T(8,128)(2,1)S(1)}, bf16[256,1024]{1,0:T(8,128)(2,1)S(1)}) custom-call(s32[12]{0:T(128)S(1)} %concatenate.3.info, bf16[256,1024]{1,0:T(8,128)(2,1)S(1)} %collective-permute-done.refs_0_.refs_1_, ...), custom_call_target="tpu_custom_call" | custom-call | flops 1048576 | bytes 1048576 | tf_op jit(solution)/shard_map/pallas_call | solution.py:436
  27.9 2.4 %collective-permute-start.5 = (bf16[256,512]{1,0:T(8,128)(2,1)S(1)}, bf16[256,512]{1,0:T(8,128)(2,1)S(1)}, u32[]{:S(2)}, u32[]{:S(2)}) collective-permute-start(bf16[256,512]{1,0:T(8,128)(2,1)S(1)} %get-tuple-element.91), channel_id=1, source_target_pairs={{0,2},{1,3},{2,0},{3,1},{4,6},{5,7},{6,4},{7,5},{8,10},{9,11},{10,... | collective-permute-start | bytes 786440 | tf_op jit(solution)/shard_map/ppermute | solution.py:399
  30.3 5.9 %collective-permute-done.2.refs_0_.refs_2_ = bf16[256,1024]{1,0:T(8,128)(2,1)S(1)} collective-permute-done((bf16[256,1024]{1,0:T(8,128)(2,1)}, bf16[256,1024]{1,0:T(8,128)(2,1)S(1)}, u32[]{:S(2)}, u32[]{:S(2)}) %collective-permute-start.2) | collective-permute-done | bytes 524320 | tf_op jit(solution)/shard_map/ppermute | solution.py:399
  39.8 5.2 %shard_map.79 = (bf16[1024,256]{1,0:T(8,128)(2,1)S(1)}, bf16[1024,512]{1,0:T(8,128)(2,1)S(1)}, f32[1024,256]{1,0:T(8,128)S(1)}) custom-call(s32[12]{0:T(128)S(1)} %concatenate.3.info, bf16[256,256]{1,0:T(8,128)(2,1)S(1)} %get-tuple-element.74.refs_0_, bf16[512,256]{1,0:T(8,128)(2,1)S(1)} %get-tuple-element.78.refs_1_, ...), custom_call_target="tpu_custom_call" | custom-call | flops 5368709120 | bytes 4194304 | tf_op jit(solution)/shard_map/pallas_call | solution.py:450
  48.2 3.1 %collective-permute-start.11 = (f32[8,1024]{1,0:T(8,128)S(1)}, f32[8,1024]{1,0:T(8,128)S(1)}, u32[]{:S(2)}, u32[]{:S(2)}) collective-permute-start(f32[8,1024]{1,0:T(8,128)S(1)} %get-tuple-element.99.refs_3_), channel_id=1, source_target_pairs={{0,2},{1,3},{2,0},{3,1},{4,6},{5,7},{6,4},{7,5},{8,10},{9,11},{10,... | collective-permute-start | bytes 98312 | tf_op jit(solution)/shard_map/ppermute | solution.py:399
  51.3 3.1 %collective-permute-start.3 = (bf16[1024,256]{1,0:T(8,128)(2,1)S(1)}, bf16[1024,256]{1,0:T(8,128)(2,1)S(1)}, u32[]{:S(2)}, u32[]{:S(2)}) collective-permute-start(bf16[1024,256]{1,0:T(8,128)(2,1)S(1)} %get-tuple-element.83.refs_0_), channel_id=1, source_target_pairs={{0,12},{4,0},{8,4},{12,8},{1,13},{5,1},{9,5},{13,9},{2,14},{6,2},{... | collective-permute-start | bytes 1572872 | tf_op jit(solution)/shard_map/ppermute | solution.py:399
  54.4 2.0 %collective-permute-done.12.refs_6_ = f32[8,1024]{1,0:T(8,128)S(1)} collective-permute-done((f32[8,1024]{1,0:T(8,128)S(1)}, f32[8,1024]{1,0:T(8,128)S(1)}, u32[]{:S(2)}, u32[]{:S(2)}) %collective-permute-start.12) | collective-permute-done | bytes 32800 | tf_op jit(solution)/shard_map/ppermute | solution.py:399
  58.1 3.2 %collective-permute-start.13 = (bf16[1024,256]{1,0:T(8,128)(2,1)S(1)}, bf16[1024,256]{1,0:T(8,128)(2,1)S(1)}, u32[]{:S(2)}, u32[]{:S(2)}) collective-permute-start(bf16[1024,256]{1,0:T(8,128)(2,1)S(1)} %get-tuple-element.104.refs_1_), channel_id=1, source_target_pairs={{0,12},{4,0},{8,4},{12,8},{1,13},{5,1},{9,5},{13,9},{2,14},{6,2},{... | collective-permute-start | bytes 1572872 | tf_op jit(solution)/shard_map/ppermute | solution.py:399
  63.3 7.5 %shard_map.83 = (bf16[1024,256]{1,0:T(8,128)(2,1)S(1)}, f32[1024,512]{1,0:T(8,128)S(1)}) custom-call(s32[12]{0:T(128)S(1)} %concatenate.3.info, bf16[1024,256]{1,0:T(8,128)(2,1)S(1)} %get-tuple-element.83.refs_0_, bf16[1024,256]{1,0:T(8,128)(2,1)S(1)} %get-tuple-element.104.refs_1_, bf16[1024,512]{1,0:T(8,128)(2,1)S(1)} %get-tuple-element.106.refs_2_, ...), custom_call_target="tpu_custom_call" | custom-call | flops 1048576 | bytes 1048576 | tf_op jit(solution)/shard_map/pallas_call | solution.py:464
  70.9 2.5 %shard_map.84 = (bf16[4,128,512]{2,1,0:T(8,128)(2,1)S(1)}, f32[4,128,512]{2,1,0:T(8,128)S(1)}) custom-call(s32[12]{0:T(128)S(1)} %concatenate.3.info, bf16[256,1024]{1,0:T(8,128)(2,1)} %bitcast.5.refs_0_, bf16[256,1024]{1,0:T(8,128)(2,1)S(1)} %collective-permute-done.refs_0_.refs_1_, bf16[256,1024]{1,0:T(8,128)(2,1)S(1)} %collective-permute-done.2.refs_0_.refs_2_, ...), custom_call_target="tpu_custom_call" | custom-call | flops 1048576 | bytes 1048576 | tf_op jit(solution)/shard_map/pallas_call | solution.py:469
  73.9 5.0 %shard_map.85 = (bf16[256,1024]{1,0:T(8,128)(2,1)S(1)}, bf16[256,1024]{1,0:T(8,128)(2,1)S(1)}, bf16[256,1024]{1,0:T(8,128)(2,1)S(1)}, bf16[256,1024]{1,0:T(8,128)(2,1)S(1)}) custom-call(s32[12]{0:T(128)S(1)} %concatenate.3.info, bf16[1024,256]{1,0:T(8,128)(2,1)S(1)} %collective-permute-done.3.refs_0_, bf16[1024,256]{1,0:T(8,128)(2,1)S(1)} %collective-permute-done.13.refs_1_, ...), custom_call_target="tpu_custom_call" | custom-call | flops 5368709120 | bytes 4194304 | tf_op jit(solution)/shard_map/pallas_call | solution.py:477
  78.9 2.9 %shard_map.86 = (f32[256,1024]{1,0:T(8,128)S(1)}, bf16[256,1024]{1,0:T(8,128)(2,1)S(1)}, bf16[256,1024]{1,0:T(8,128)(2,1)S(1)}, bf16[256,1024]{1,0:T(8,128)(2,1)S(1)}) custom-call(s32[12]{0:T(128)S(1)} %concatenate.3.info, bf16[256,1024]{1,0:T(8,128)(2,1)S(1)} %get-tuple-element.120.refs_0_.refs_4_, ...), custom_call_target="tpu_custom_call" | custom-call | flops 1048576 | bytes 1048576 | tf_op jit(solution)/shard_map/pallas_call | solution.py:480
  81.8 2.5 %shard_map.87 = (bf16[4,128,512]{2,1,0:T(8,128)(2,1)S(1)}, f32[4,128,512]{2,1,0:T(8,128)S(1)}) custom-call(s32[12]{0:T(128)S(1)} %concatenate.3.info, bf16[256,1024]{1,0:T(8,128)(2,1)} %bitcast.5.refs_0_, bf16[256,1024]{1,0:T(8,128)(2,1)S(1)} %collective-permute-done.refs_0_.refs_1_, bf16[256,1024]{1,0:T(8,128)(2,1)S(1)} %collective-permute-done.2.refs_0_.refs_2_, ...), custom_call_target="tpu_custom_call" | custom-call | flops 1048576 | bytes 1048576 | tf_op jit(solution)/shard_map/pallas_call | solution.py:469
  89.2 2.6 %collective-permute-start.25 = (bf16[256,1024]{1,0:T(8,128)(2,1)S(1)}, bf16[256,1024]{1,0:T(8,128)(2,1)S(1)}, u32[]{:S(2)}, u32[]{:S(2)}) collective-permute-start(bf16[256,1024]{1,0:T(8,128)(2,1)S(1)} %get-tuple-element.142), channel_id=1, source_target_pairs={{0,2},{1,3},{2,0},{3,1},{4,6},{5,7},{6,4},{7,5},{8,10},{9,11},{10,... | collective-permute-start | bytes 1572872 | tf_op jit(solution)/shard_map/ppermute | solution.py:399
  92.6 6.2 %collective-permute-start.23 = (bf16[128,1280]{1,0:T(8,128)(2,1)S(1)}, bf16[128,1280]{1,0:T(8,128)(2,1)S(1)}, u32[]{:S(2)}, u32[]{:S(2)}) collective-permute-start(bf16[128,1280]{1,0:T(8,128)(2,1)S(1)} %get-tuple-element.138), channel_id=1, source_target_pairs={{0,64},{32,96},{64,0},{96,32},{1,65},{33,97},{65,1},{97,33},{2,66}... | collective-permute-start | bytes 983048 | tf_op jit(solution)/shard_map/ppermute | solution.py:399
  100.0 4.3 %collective-permute-start.24 = (bf16[128,1280]{1,0:T(8,128)(2,1)S(1)}, bf16[128,1280]{1,0:T(8,128)(2,1)S(1)}, u32[]{:S(2)}, u32[]{:S(2)}) collective-permute-start(bf16[128,1280]{1,0:T(8,128)(2,1)S(1)} %get-tuple-element.139), channel_id=1, source_target_pairs={{0,96},{32,0},{64,32},{96,64},{1,97},{33,1},{65,33},{97,65},{2,98}... | collective-permute-start | bytes 983048 | tf_op jit(solution)/shard_map/ppermute | solution.py:399
  105.4 8.2 %collective-permute-done.23.got_2 = bf16[128,1280]{1,0:T(8,128)(2,1)S(1)} collective-permute-done((bf16[128,1280]{1,0:T(8,128)(2,1)S(1)}, bf16[128,1280]{1,0:T(8,128)(2,1)S(1)}, u32[]{:S(2)}, u32[]{:S(2)}) %collective-permute-start.23) | collective-permute-done | bytes 327712 | tf_op jit(solution)/shard_map/ppermute | solution.py:399
  114.5 15.0 %all-to-all-start = ((bf16[16,8,1280]{2,1,0:T(8,128)(2,1)}), bf16[16,8,1280]{2,1,0:T(8,128)(2,1)S(1)}, u32[]{:S(2)}, u32[]{:S(2)}) async-start(bf16[16,8,1280]{2,1,0:T(8,128)(2,1)} %bitcast.8), calls=%async_computation | async-start | bytes 655360 | tf_op jit(solution)/shard_map/all_to_all | solution.py:499
  130.4 7.9 %all-to-all-done.got = bf16[16,8,1280]{2,1,0:T(8,128)(2,1)S(1)} async-done(((bf16[16,8,1280]{2,1,0:T(8,128)(2,1)}), bf16[16,8,1280]{2,1,0:T(8,128)(2,1)S(1)}, u32[]{:S(2)}, u32[]{:S(2)}) %all-to-all-start) | async-done | bytes 327712 | tf_op jit(solution)/shard_map/all_to_all | solution.py:499
  (57 shorter events, 27.9 us)
Async XLA Ops:
  0.6 15.7 %collective-permute-start = (bf16[256,1024]{1,0:T(8,128)(2,1)}, bf16[256,1024]{1,0:T(8,128)(2,1)S(1)}, u32[]{:S(2)}, u32[]{:S(2)}) collective-permute-start(bf16[256,1024]{1,0:T(8,128)(2,1)} %bitcast.5.refs_0_), channel_id=1, source_target_pairs={{0,3},{1,0},{2,1},{3,2},{4,7},{5,4},{6,5},{7,6},{8,11},{9,8},{10,9... | collective-permute-start | bytes 1572872 | tf_op jit(solution)/shard_map/ppermute | solution.py:399
  4.8 14.8 %collective-permute-start.1 = (bf16[256,1024]{1,0:T(8,128)(2,1)}, bf16[256,1024]{1,0:T(8,128)(2,1)S(1)}, u32[]{:S(2)}, u32[]{:S(2)}) collective-permute-start(bf16[256,1024]{1,0:T(8,128)(2,1)} %bitcast.5.refs_0_), channel_id=1, source_target_pairs={{0,1},{1,2},{2,3},{3,0},{4,5},{5,6},{6,7},{7,4},{8,9},{9,10},{10,1... | collective-permute-start | bytes 1572872 | tf_op jit(solution)/shard_map/ppermute | solution.py:399
  19.6 16.6 %collective-permute-start.2 = (bf16[256,1024]{1,0:T(8,128)(2,1)}, bf16[256,1024]{1,0:T(8,128)(2,1)S(1)}, u32[]{:S(2)}, u32[]{:S(2)}) collective-permute-start(bf16[256,1024]{1,0:T(8,128)(2,1)} %bitcast.5.refs_0_), channel_id=1, source_target_pairs={{0,2},{1,3},{2,0},{3,1},{4,6},{5,7},{6,4},{7,5},{8,10},{9,11},{10,... | collective-permute-start | bytes 1572872 | tf_op jit(solution)/shard_map/ppermute | solution.py:399
  19.6 18.5 %collective-permute-start.7 = (bf16[256,512]{1,0:T(8,128)(2,1)S(1)}, bf16[256,512]{1,0:T(8,128)(2,1)S(1)}, u32[]{:S(2)}, u32[]{:S(2)}) collective-permute-start(bf16[256,512]{1,0:T(8,128)(2,1)S(1)} %get-tuple-element.75.refs_3_), channel_id=1, source_target_pairs={{0,4},{4,8},{8,12},{12,0},{1,5},{5,9},{9,13},{13,1},{2,6},{6,10},{... | collective-permute-start | bytes 786440 | tf_op jit(solution)/shard_map/ppermute | solution.py:399
  23.7 21.4 %collective-permute-start.8 = (bf16[512,512]{1,0:T(8,128)(2,1)S(1)}, bf16[512,512]{1,0:T(8,128)(2,1)S(1)}, u32[]{:S(2)}, u32[]{:S(2)}) collective-permute-start(bf16[512,512]{1,0:T(8,128)(2,1)S(1)} %get-tuple-element.81.refs_4_), channel_id=1, source_target_pairs={{0,4},{4,8},{8,12},{12,0},{1,5},{5,9},{9,13},{13,1},{2,6},{6,10},{... | collective-permute-start | bytes 1572872 | tf_op jit(solution)/shard_map/ppermute | solution.py:399
  26.7 18.3 %collective-permute-start.4 = (bf16[256,512]{1,0:T(8,128)(2,1)S(1)}, bf16[256,512]{1,0:T(8,128)(2,1)S(1)}, u32[]{:S(2)}, u32[]{:S(2)}) collective-permute-start(bf16[256,512]{1,0:T(8,128)(2,1)S(1)} %get-tuple-element.90), channel_id=1, source_target_pairs={{0,1},{1,2},{2,3},{3,0},{4,5},{5,6},{6,7},{7,4},{8,9},{9,10},{10,1... | collective-permute-start | bytes 786440 | tf_op jit(solution)/shard_map/ppermute | solution.py:399
  27.9 17.2 %collective-permute-start.5 = (bf16[256,512]{1,0:T(8,128)(2,1)S(1)}, bf16[256,512]{1,0:T(8,128)(2,1)S(1)}, u32[]{:S(2)}, u32[]{:S(2)}) collective-permute-start(bf16[256,512]{1,0:T(8,128)(2,1)S(1)} %get-tuple-element.91), channel_id=1, source_target_pairs={{0,2},{1,3},{2,0},{3,1},{4,6},{5,7},{6,4},{7,5},{8,10},{9,11},{10,... | collective-permute-start | bytes 786440 | tf_op jit(solution)/shard_map/ppermute | solution.py:399
  36.2 8.9 %collective-permute-start.6 = (bf16[256,512]{1,0:T(8,128)(2,1)S(1)}, bf16[256,512]{1,0:T(8,128)(2,1)S(1)}, u32[]{:S(2)}, u32[]{:S(2)}) collective-permute-start(bf16[256,512]{1,0:T(8,128)(2,1)S(1)} %get-tuple-element.92), channel_id=1, source_target_pairs={{0,3},{1,0},{2,1},{3,2},{4,7},{5,4},{6,5},{7,6},{8,11},{9,8},{10,9... | collective-permute-start | bytes 786440 | tf_op jit(solution)/shard_map/ppermute | solution.py:399
  38.2 7.7 %collective-permute-start.9 = (bf16[256,512]{1,0:T(8,128)(2,1)S(1)}, bf16[256,512]{1,0:T(8,128)(2,1)S(1)}, u32[]{:S(2)}, u32[]{:S(2)}) collective-permute-start(bf16[256,512]{1,0:T(8,128)(2,1)S(1)} %get-tuple-element.82.refs_5_), channel_id=1, source_target_pairs={{0,4},{4,8},{8,12},{12,0},{1,5},{5,9},{9,13},{13,1},{2,6},{6,10},{... | collective-permute-start | bytes 786440 | tf_op jit(solution)/shard_map/ppermute | solution.py:399
  47.5 6.9 %collective-permute-start.10 = (f32[8,1024]{1,0:T(8,128)S(1)}, f32[8,1024]{1,0:T(8,128)S(1)}, u32[]{:S(2)}, u32[]{:S(2)}) collective-permute-start(f32[8,1024]{1,0:T(8,128)S(1)} %get-tuple-element.99.refs_3_), channel_id=1, source_target_pairs={{0,3},{1,0},{2,1},{3,2},{4,7},{5,4},{6,5},{7,6},{8,11},{9,8},{10,9... | collective-permute-start | bytes 98312 | tf_op jit(solution)/shard_map/ppermute | solution.py:399
  51.3 22.1 %collective-permute-start.3 = (bf16[1024,256]{1,0:T(8,128)(2,1)S(1)}, bf16[1024,256]{1,0:T(8,128)(2,1)S(1)}, u32[]{:S(2)}, u32[]{:S(2)}) collective-permute-start(bf16[1024,256]{1,0:T(8,128)(2,1)S(1)} %get-tuple-element.83.refs_0_), channel_id=1, source_target_pairs={{0,12},{4,0},{8,4},{12,8},{1,13},{5,1},{9,5},{13,9},{2,14},{6,2},{... | collective-permute-start | bytes 1572872 | tf_op jit(solution)/shard_map/ppermute | solution.py:399
  58.1 15.8 %collective-permute-start.13 = (bf16[1024,256]{1,0:T(8,128)(2,1)S(1)}, bf16[1024,256]{1,0:T(8,128)(2,1)S(1)}, u32[]{:S(2)}, u32[]{:S(2)}) collective-permute-start(bf16[1024,256]{1,0:T(8,128)(2,1)S(1)} %get-tuple-element.104.refs_1_), channel_id=1, source_target_pairs={{0,12},{4,0},{8,4},{12,8},{1,13},{5,1},{9,5},{13,9},{2,14},{6,2},{... | collective-permute-start | bytes 1572872 | tf_op jit(solution)/shard_map/ppermute | solution.py:399
  61.3 23.1 %collective-permute-start.14 = (bf16[1024,256]{1,0:T(8,128)(2,1)S(1)}, bf16[1024,256]{1,0:T(8,128)(2,1)S(1)}, u32[]{:S(2)}, u32[]{:S(2)}) collective-permute-start(bf16[1024,256]{1,0:T(8,128)(2,1)S(1)} %get-tuple-element.126.refs_0_), channel_id=1, source_target_pairs={{0,3},{1,0},{2,1},{3,2},{4,7},{5,4},{6,5},{7,6},{8,11},{9,8},{10,9... | collective-permute-start | bytes 1572872 | tf_op jit(solution)/shard_map/ppermute | solution.py:399
  61.3 25.0 %collective-permute-start.15 = (bf16[1024,256]{1,0:T(8,128)(2,1)S(1)}, bf16[1024,256]{1,0:T(8,128)(2,1)S(1)}, u32[]{:S(2)}, u32[]{:S(2)}) collective-permute-start(bf16[1024,256]{1,0:T(8,128)(2,1)S(1)} %get-tuple-element.126.refs_0_), channel_id=1, source_target_pairs={{0,2},{1,3},{2,0},{3,1},{4,6},{5,7},{6,4},{7,5},{8,10},{9,11},{10,... | collective-permute-start | bytes 1572872 | tf_op jit(solution)/shard_map/ppermute | solution.py:399
  62.5 25.2 %collective-permute-start.16 = (bf16[1024,256]{1,0:T(8,128)(2,1)S(1)}, bf16[1024,256]{1,0:T(8,128)(2,1)S(1)}, u32[]{:S(2)}, u32[]{:S(2)}) collective-permute-start(bf16[1024,256]{1,0:T(8,128)(2,1)S(1)} %get-tuple-element.126.refs_0_), channel_id=1, source_target_pairs={{0,1},{1,2},{2,3},{3,0},{4,5},{5,6},{6,7},{7,4},{8,9},{9,10},{10,1... | collective-permute-start | bytes 1572872 | tf_op jit(solution)/shard_map/ppermute | solution.py:399
  73.4 15.8 %collective-permute-start.17 = (bf16[4,128,512]{2,1,0:T(8,128)(2,1)S(1)}, bf16[4,128,512]{2,1,0:T(8,128)(2,1)S(1)}, u32[]{:S(2)}, u32[]{:S(2)}) collective-permute-start(bf16[4,128,512]{2,1,0:T(8,128)(2,1)S(1)} %get-tuple-element.129), channel_id=1, source_target_pairs={{0,16},{16,0},{1,17},{17,1},{2,18},{18,2},{3,19},{19,3},{4,20},{20... | collective-permute-start | bytes 1572872 | tf_op jit(solution)/shard_map/ppermute | solution.py:403
  84.3 7.5 %collective-permute-start.18 = (bf16[4,128,512]{2,1,0:T(8,128)(2,1)S(1)}, bf16[4,128,512]{2,1,0:T(8,128)(2,1)S(1)}, u32[]{:S(2)}, u32[]{:S(2)}) collective-permute-start(bf16[4,128,512]{2,1,0:T(8,128)(2,1)S(1)} %get-tuple-element.130), channel_id=1, source_target_pairs={{0,16},{16,0},{1,17},{17,1},{2,18},{18,2},{3,19},{19,3},{4,20},{20... | collective-permute-start | bytes 1572872 | tf_op jit(solution)/shard_map/ppermute | solution.py:403
  84.4 15.6 %collective-permute-start.20 = (bf16[256,1024]{1,0:T(8,128)(2,1)S(1)}, bf16[256,1024]{1,0:T(8,128)(2,1)S(1)}, u32[]{:S(2)}, u32[]{:S(2)}) collective-permute-start(bf16[256,1024]{1,0:T(8,128)(2,1)S(1)} %get-tuple-element.134), channel_id=1, source_target_pairs={{0,1},{1,2},{2,3},{3,0},{4,5},{5,6},{6,7},{7,4},{8,9},{9,10},{10,1... | collective-permute-start | bytes 1572872 | tf_op jit(solution)/shard_map/ppermute | solution.py:399
  86.4 17.9 %collective-permute-start.21 = (bf16[256,1024]{1,0:T(8,128)(2,1)S(1)}, bf16[256,1024]{1,0:T(8,128)(2,1)S(1)}, u32[]{:S(2)}, u32[]{:S(2)}) collective-permute-start(bf16[256,1024]{1,0:T(8,128)(2,1)S(1)} %get-tuple-element.135), channel_id=1, source_target_pairs={{0,3},{1,0},{2,1},{3,2},{4,7},{5,4},{6,5},{7,6},{8,11},{9,8},{10,9... | collective-permute-start | bytes 1572872 | tf_op jit(solution)/shard_map/ppermute | solution.py:399
  89.2 40.3 %collective-permute-start.25 = (bf16[256,1024]{1,0:T(8,128)(2,1)S(1)}, bf16[256,1024]{1,0:T(8,128)(2,1)S(1)}, u32[]{:S(2)}, u32[]{:S(2)}) collective-permute-start(bf16[256,1024]{1,0:T(8,128)(2,1)S(1)} %get-tuple-element.142), channel_id=1, source_target_pairs={{0,2},{1,3},{2,0},{3,1},{4,6},{5,7},{6,4},{7,5},{8,10},{9,11},{10,... | collective-permute-start | bytes 1572872 | tf_op jit(solution)/shard_map/ppermute | solution.py:399
  92.6 12.8 %collective-permute-start.22 = (bf16[128,1280]{1,0:T(8,128)(2,1)S(1)}, bf16[128,1280]{1,0:T(8,128)(2,1)S(1)}, u32[]{:S(2)}, u32[]{:S(2)}) collective-permute-start(bf16[128,1280]{1,0:T(8,128)(2,1)S(1)} %get-tuple-element.137), channel_id=1, source_target_pairs={{0,32},{32,64},{64,96},{96,0},{1,33},{33,65},{65,97},{97,1},{2,34}... | collective-permute-start | bytes 983048 | tf_op jit(solution)/shard_map/ppermute | solution.py:399
  92.6 20.9 %collective-permute-start.23 = (bf16[128,1280]{1,0:T(8,128)(2,1)S(1)}, bf16[128,1280]{1,0:T(8,128)(2,1)S(1)}, u32[]{:S(2)}, u32[]{:S(2)}) collective-permute-start(bf16[128,1280]{1,0:T(8,128)(2,1)S(1)} %get-tuple-element.138), channel_id=1, source_target_pairs={{0,64},{32,96},{64,0},{96,32},{1,65},{33,97},{65,1},{97,33},{2,66}... | collective-permute-start | bytes 983048 | tf_op jit(solution)/shard_map/ppermute | solution.py:399
  100.0 13.6 %collective-permute-start.24 = (bf16[128,1280]{1,0:T(8,128)(2,1)S(1)}, bf16[128,1280]{1,0:T(8,128)(2,1)S(1)}, u32[]{:S(2)}, u32[]{:S(2)}) collective-permute-start(bf16[128,1280]{1,0:T(8,128)(2,1)S(1)} %get-tuple-element.139), channel_id=1, source_target_pairs={{0,96},{32,0},{64,32},{96,64},{1,97},{33,1},{65,33},{97,65},{2,98}... | collective-permute-start | bytes 983048 | tf_op jit(solution)/shard_map/ppermute | solution.py:399
  114.5 23.8 %all-to-all-start = ((bf16[16,8,1280]{2,1,0:T(8,128)(2,1)}), bf16[16,8,1280]{2,1,0:T(8,128)(2,1)S(1)}, u32[]{:S(2)}, u32[]{:S(2)}) async-start(bf16[16,8,1280]{2,1,0:T(8,128)(2,1)} %bitcast.8), calls=%async_computation | async-start | bytes 655360 | tf_op jit(solution)/shard_map/all_to_all | solution.py:499
  (7 other events, 41.3 us)

commit v13 on v11

--- a/solution.py
+++ b/solution.py
@@ -383,12 +383,9 @@
         outs[k][...] = total.astype(outs[k].dtype)
 
 
-def add_near_body(own, got_1, got_3, out):
-    out[...] = own[...] + got_1[...].astype(F32) + got_3[...].astype(F32)
-
-
-def add_far_body(near, got_2, out):
-    out[...] = (near[...] + got_2[...].astype(F32)).astype(BF16)
+def add_rows_body(own, got_1, got_2, got_3, out):
+    total = own[...] + got_1[...].astype(F32) + got_2[...].astype(F32) + got_3[...].astype(F32)
+    out[...] = total.astype(BF16)
 
 
 def along(x, axis, d):
@@ -484,13 +481,11 @@
         add_core_body, bf16((4, 128, 5 * BLK)), 6, 1 << 20, 1 << 20, scalars=0
     )(keep_1, keep_2, keep_3, got_1, got_2, got_3)
     sums = lax.all_to_all(mine.reshape(16, 32, 5 * BLK), ("x", "y"), 0, 0)
-    near_rows = call(
-        add_near_body, f32((BLK, D)), 3, 40 << 30, 4 << 20, scalars=0
-    )(partial[0], partial[1], partial[3])
-    sums, near_rows = lax.optimization_barrier((sums, near_rows))
     total = call(add_xy_body, bf16((32, 5 * BLK)), 1, 1 << 20, 1 << 20, scalars=0)(sums)
-    _, near_rows = lax.optimization_barrier((total, near_rows))
-    grad_events = call(add_far_body, bf16((BLK, D)), 2, 1 << 20, 4 << 20, scalars=0)(near_rows, partial[2])
+    _, own_rows = lax.optimization_barrier((total, partial[0]))
+    grad_events = call(
+        add_rows_body, bf16((BLK, D)), 4, 1 << 20, 4 << 20, scalars=0
+    )(own_rows, *partial[1:])
     got = lax.all_to_all(total.reshape(4, 8, 5 * BLK), "z", 0, 0)
     grad_w_in, grad_w_out = call(
         last_body, (bf16((8, 4 * D)), bf16((8, D))), 1, 1 << 20, 1 << 20, scalars=0

time: 135 us -> 130 us (0.963)
  Pallas kernels: 42.8 us -> 39.5 us
  waiting for transfers between devices: 40.8 us -> 38.4 us
  starting transfers between devices: 44.5 us -> 46.6 us
    all_to_all x1, waiting for transfers between devices: 18.5 us -> 14.6 us  [body(): sums = lax.all_to_all(mine.reshape(16, 32, 5 * BLK), ('x', 'y'), 0, 0)]
    pallas_call x1, Pallas kernels: 5 us -> 1.81 us  [body(): call(backward_later_body, (bf16((BLK, 4 * BLK)),) * 4, 10, 5 << 30, 4 <<...]
    all_to_all x1, starting transfers between devices: 3.29 us -> 5.42 us  [body(): got = lax.all_to_all(total.reshape(4, 8, 5 * BLK), 'z', 0, 0)]
    ppermute x3, waiting for transfers between devices: 0.01 us -> 1.52 us  [swap(): return lax.ppermute(x, 'c', [(0, 1), (1, 0)])]
    ppermute x3, starting transfers between devices: 0.31 us -> 1.69 us  [swap(): return lax.ppermute(x, 'c', [(0, 1), (1, 0)])]
  transfers between devices with their start and end apart: 25 -> 25, of which waited for: 9 -> 12; matrix products, arithmetic and copies ran while one was open for 1% -> 1% of each run, Pallas kernels for 30% -> 28%
where the time goes in v13:
time: 130 us; the launch traced here: 129 us
  starting transfers between devices  46.6 us (36%)
  Pallas kernels  39.5 us (30%)
  waiting for transfers between devices  38.4 us (30%)
  local copies, waits for them, and re-layouts  4.13 us (3%)
    ppermute x20, starting transfers between devices, along(): return lax.ppermute(x, axis, [(i, (i + d) % 4) for i in range(4)])  31.7 us
    ppermute x20, waiting for transfers between devices, along(): return lax.ppermute(x, axis, [(i, (i + d) % 4) for i in range(4)])  18.8 us
    all_to_all x1, waiting for transfers between devices, body(): sums = lax.all_to_all(mine.reshape(16, 32, 5 * BLK), ('x', 'y'), 0, 0)  14.6 us
    all_to_all x1, starting transfers between devices, body(): sums = lax.all_to_all(mine.reshape(16, 32, 5 * BLK), ('x', 'y'), 0, 0)  7.75 us
    pallas_call x1, Pallas kernels, body(): call(backward_local_body, (bf16((GRP, BLK)), f32((GRP, 2 * BLK))), 8, 1 <...  7.53 us
    pallas_call x3, Pallas kernels, weights(): call(kernel, (bf16((4, 128, cols)), f32((4, 128, cols))), len(operands),...  6.29 us
    pallas_call x3, Pallas kernels, body(): call(project_body, (bf16((n * BLK, 2 * BLK)), bf16((n * BLK, BLK)), bf16(...  6.22 us
    all_to_all x1, starting transfers between devices, body(): got = lax.all_to_all(total.reshape(4, 8, 5 * BLK), 'z', 0, 0)  5.42 us
  transfers between devices with their start and end apart: 25, of which 12 were waited for; matrix products, arithmetic and copies ran while one was open for 1% of the time, Pallas kernels for 28%

profile of v13, /device:TPU:0, one launch (start us, length us, event | category | flops | bytes accessed | tf_op | source)
XLA Modules:
  0.0 129.4 jit_solution(1931696354534188430)
XLA Ops:
  0.6 4.2 %collective-permute-start = (bf16[256,1024]{1,0:T(8,128)(2,1)}, bf16[256,1024]{1,0:T(8,128)(2,1)S(1)}, u32[]{:S(2)}, u32[]{:S(2)}) collective-permute-start(bf16[256,1024]{1,0:T(8,128)(2,1)} %bitcast.5.refs_0_), channel_id=1, source_target_pairs={{0,3},{1,0},{2,1},{3,2},{4,7},{5,4},{6,5},{7,6},{8,11},{9,8},{10,9... | collective-permute-start | bytes 1572872 | tf_op jit(solution)/shard_map/ppermute | solution.py:392
  5.6 3.4 %copy-done = bf16[1024,4096]{1,0:T(8,128)(2,1)S(1)} copy-done((bf16[1024,4096]{1,0:T(8,128)(2,1)S(1)}, bf16[1024,4096]{1,0:T(8,128)(2,1)}, u32[]{:S(2)}) %copy-start) | copy-done | bytes 8388632
  8.9 2.2 %shard_map.76 = (bf16[256,512]{1,0:T(8,128)(2,1)S(1)}, bf16[256,256]{1,0:T(8,128)(2,1)S(1)}, bf16[256,256]{1,0:T(8,128)(2,1)S(1)}, bf16[256,1024]{1,0:T(8,128)(2,1)S(1)}) custom-call(s32[12]{0:T(128)S(1)} %concatenate.3.info, bf16[256,1024]{1,0:T(8,128)(2,1)} %bitcast.5.refs_0_, bf16[1024,4096]{1,0:T(8,128)(2,1)S(1)} %copy-done), custom_call_target="tpu_custom_call" | custom-call | flops 1048576 | bytes 1048576 | tf_op jit(solution)/shard_map/pallas_call | solution.py:429
  11.2 5.1 %collective-permute-done.refs_0_.refs_1_ = bf16[256,1024]{1,0:T(8,128)(2,1)S(1)} collective-permute-done((bf16[256,1024]{1,0:T(8,128)(2,1)}, bf16[256,1024]{1,0:T(8,128)(2,1)S(1)}, u32[]{:S(2)}, u32[]{:S(2)}) %collective-permute-start) | collective-permute-done | bytes 524320 | tf_op jit(solution)/shard_map/ppermute | solution.py:392
  16.3 3.3 %collective-permute-done.1.refs_1_.refs_3_ = bf16[256,1024]{1,0:T(8,128)(2,1)S(1)} collective-permute-done((bf16[256,1024]{1,0:T(8,128)(2,1)}, bf16[256,1024]{1,0:T(8,128)(2,1)S(1)}, u32[]{:S(2)}, u32[]{:S(2)}) %collective-permute-start.1) | collective-permute-done | bytes 524320 | tf_op jit(solution)/shard_map/ppermute | solution.py:392
  21.3 2.4 %shard_map.77 = (bf16[512,512]{1,0:T(8,128)(2,1)S(1)}, bf16[512,256]{1,0:T(8,128)(2,1)S(1)}, bf16[512,256]{1,0:T(8,128)(2,1)S(1)}, bf16[256,1024]{1,0:T(8,128)(2,1)S(1)}, bf16[256,1024]{1,0:T(8,128)(2,1)S(1)}) custom-call(s32[12]{0:T(128)S(1)} %concatenate.3.info, bf16[256,1024]{1,0:T(8,128)(2,1)S(1)} %collective-permute-done.refs_0_.refs_1_, ...), custom_call_target="tpu_custom_call" | custom-call | flops 1048576 | bytes 1048576 | tf_op jit(solution)/shard_map/pallas_call | solution.py:429
  27.9 2.4 %collective-permute-start.5 = (bf16[256,512]{1,0:T(8,128)(2,1)S(1)}, bf16[256,512]{1,0:T(8,128)(2,1)S(1)}, u32[]{:S(2)}, u32[]{:S(2)}) collective-permute-start(bf16[256,512]{1,0:T(8,128)(2,1)S(1)} %get-tuple-element.81), channel_id=1, source_target_pairs={{0,2},{1,3},{2,0},{3,1},{4,6},{5,7},{6,4},{7,5},{8,10},{9,11},{10,... | collective-permute-start | bytes 786440 | tf_op jit(solution)/shard_map/ppermute | solution.py:392
  30.3 5.9 %collective-permute-done.2.refs_0_.refs_2_ = bf16[256,1024]{1,0:T(8,128)(2,1)S(1)} collective-permute-done((bf16[256,1024]{1,0:T(8,128)(2,1)}, bf16[256,1024]{1,0:T(8,128)(2,1)S(1)}, u32[]{:S(2)}, u32[]{:S(2)}) %collective-permute-start.2) | collective-permute-done | bytes 524320 | tf_op jit(solution)/shard_map/ppermute | solution.py:392
  39.8 5.2 %shard_map.79 = (bf16[1024,256]{1,0:T(8,128)(2,1)S(1)}, bf16[1024,512]{1,0:T(8,128)(2,1)S(1)}, f32[1024,256]{1,0:T(8,128)S(1)}) custom-call(s32[12]{0:T(128)S(1)} %concatenate.3.info, bf16[256,256]{1,0:T(8,128)(2,1)S(1)} %get-tuple-element.64.refs_0_, bf16[512,256]{1,0:T(8,128)(2,1)S(1)} %get-tuple-element.68.refs_1_, ...), custom_call_target="tpu_custom_call" | custom-call | flops 5368709120 | bytes 4194304 | tf_op jit(solution)/shard_map/pallas_call | solution.py:443
  48.2 3.1 %collective-permute-start.11 = (f32[8,1024]{1,0:T(8,128)S(1)}, f32[8,1024]{1,0:T(8,128)S(1)}, u32[]{:S(2)}, u32[]{:S(2)}) collective-permute-start(f32[8,1024]{1,0:T(8,128)S(1)} %get-tuple-element.89.refs_3_), channel_id=1, source_target_pairs={{0,2},{1,3},{2,0},{3,1},{4,6},{5,7},{6,4},{7,5},{8,10},{9,11},{10,... | collective-permute-start | bytes 98312 | tf_op jit(solution)/shard_map/ppermute | solution.py:392
  51.3 2.9 %collective-permute-start.3 = (bf16[1024,256]{1,0:T(8,128)(2,1)S(1)}, bf16[1024,256]{1,0:T(8,128)(2,1)S(1)}, u32[]{:S(2)}, u32[]{:S(2)}) collective-permute-start(bf16[1024,256]{1,0:T(8,128)(2,1)S(1)} %get-tuple-element.73.refs_0_), channel_id=1, source_target_pairs={{0,12},{4,0},{8,4},{12,8},{1,13},{5,1},{9,5},{13,9},{2,14},{6,2},{... | collective-permute-start | bytes 1572872 | tf_op jit(solution)/shard_map/ppermute | solution.py:392
  54.2 2.2 %collective-permute-done.12.refs_6_ = f32[8,1024]{1,0:T(8,128)S(1)} collective-permute-done((f32[8,1024]{1,0:T(8,128)S(1)}, f32[8,1024]{1,0:T(8,128)S(1)}, u32[]{:S(2)}, u32[]{:S(2)}) %collective-permute-start.12) | collective-permute-done | bytes 32800 | tf_op jit(solution)/shard_map/ppermute | solution.py:392
  58.1 3.0 %collective-permute-start.13 = (bf16[1024,256]{1,0:T(8,128)(2,1)S(1)}, bf16[1024,256]{1,0:T(8,128)(2,1)S(1)}, u32[]{:S(2)}, u32[]{:S(2)}) collective-permute-start(bf16[1024,256]{1,0:T(8,128)(2,1)S(1)} %get-tuple-element.94.refs_1_), channel_id=1, source_target_pairs={{0,12},{4,0},{8,4},{12,8},{1,13},{5,1},{9,5},{13,9},{2,14},{6,2},{... | collective-permute-start | bytes 1572872 | tf_op jit(solution)/shard_map/ppermute | solution.py:392
  63.2 7.5 %shard_map.83 = (bf16[1024,256]{1,0:T(8,128)(2,1)S(1)}, f32[1024,512]{1,0:T(8,128)S(1)}) custom-call(s32[12]{0:T(128)S(1)} %concatenate.3.info, bf16[1024,256]{1,0:T(8,128)(2,1)S(1)} %get-tuple-element.73.refs_0_, bf16[1024,256]{1,0:T(8,128)(2,1)S(1)} %get-tuple-element.94.refs_1_, bf16[1024,512]{1,0:T(8,128)(2,1)S(1)} %get-tuple-element.96.refs_2_, ...), custom_call_target="tpu_custom_call" | custom-call | flops 1048576 | bytes 1048576 | tf_op jit(solution)/shard_map/pallas_call | solution.py:457
  70.7 2.5 %shard_map.84 = (bf16[4,128,512]{2,1,0:T(8,128)(2,1)S(1)}, f32[4,128,512]{2,1,0:T(8,128)S(1)}) custom-call(s32[12]{0:T(128)S(1)} %concatenate.3.info, bf16[256,1024]{1,0:T(8,128)(2,1)} %bitcast.5.refs_0_, bf16[256,1024]{1,0:T(8,128)(2,1)S(1)} %collective-permute-done.refs_0_.refs_1_, bf16[256,1024]{1,0:T(8,128)(2,1)S(1)} %collective-permute-done.2.refs_0_.refs_2_, ...), custom_call_target="tpu_custom_call" | custom-call | flops 1048576 | bytes 1048576 | tf_op jit(solution)/shard_map/pallas_call | solution.py:462
  76.1 2.5 %shard_map.86 = (bf16[4,128,512]{2,1,0:T(8,128)(2,1)S(1)}, f32[4,128,512]{2,1,0:T(8,128)S(1)}) custom-call(s32[12]{0:T(128)S(1)} %concatenate.3.info, bf16[256,1024]{1,0:T(8,128)(2,1)} %bitcast.5.refs_0_, bf16[256,1024]{1,0:T(8,128)(2,1)S(1)} %collective-permute-done.refs_0_.refs_1_, bf16[256,1024]{1,0:T(8,128)(2,1)S(1)} %collective-permute-done.2.refs_0_.refs_2_, ...), custom_call_target="tpu_custom_call" | custom-call | flops 1048576 | bytes 1048576 | tf_op jit(solution)/shard_map/pallas_call | solution.py:462
  80.1 3.0 %shard_map.87 = (f32[256,1024]{1,0:T(8,128)S(1)}, bf16[256,1024]{1,0:T(8,128)(2,1)}, bf16[256,1024]{1,0:T(8,128)(2,1)S(1)}, bf16[256,1024]{1,0:T(8,128)(2,1)S(1)}) custom-call(s32[12]{0:T(128)S(1)} %concatenate.3.info, bf16[256,1024]{1,0:T(8,128)(2,1)S(1)} %get-tuple-element.105.refs_4_.refs_0_, bf16[256,1024]{1,0:T(8,128)(2,1)S(1)} %get-tuple-element.106.refs_5_.refs_1_, ...), custom_call_target="tpu_custom_call" | custom-call | flops 1048576 | bytes 1048576 | tf_op jit(solution)/shard_map/pallas_call | solution.py:474
  87.7 7.8 %all-to-all-start = ((bf16[16,32,1280]{2,1,0:T(8,128)(2,1)}), bf16[16,32,1280]{2,1,0:T(8,128)(2,1)S(1)}, u32[]{:S(2)}, u32[]{:S(2)}) async-start(bf16[16,32,1280]{2,1,0:T(8,128)(2,1)} %bitcast.7), calls=%async_computation | async-start | bytes 2621440 | tf_op jit(solution)/shard_map/all_to_all | solution.py:483
  97.1 2.7 %collective-permute-start.21 = (bf16[256,1024]{1,0:T(8,128)(2,1)}, bf16[256,1024]{1,0:T(8,128)(2,1)S(1)}, u32[]{:S(2)}, u32[]{:S(2)}) collective-permute-start(bf16[256,1024]{1,0:T(8,128)(2,1)} %copy-done.5), channel_id=1, source_target_pairs={{0,2},{1,3},{2,0},{3,1},{4,6},{5,7},{6,4},{7,5},{8,10},{9,11},{10,... | collective-permute-start | bytes 1572872 | tf_op jit(solution)/shard_map/ppermute | solution.py:392
  99.7 2.5 %collective-permute-start.22 = (bf16[256,1024]{1,0:T(8,128)(2,1)}, bf16[256,1024]{1,0:T(8,128)(2,1)}, u32[]{:S(2)}, u32[]{:S(2)}) collective-permute-start(bf16[256,1024]{1,0:T(8,128)(2,1)} %copy-done.4), channel_id=1, source_target_pairs={{0,3},{1,0},{2,1},{3,2},{4,7},{5,4},{6,5},{7,6},{8,11},{9,8},{10,9... | collective-permute-start | bytes 1572872 | tf_op jit(solution)/shard_map/ppermute | solution.py:392
  102.3 14.6 %all-to-all-done.got = bf16[16,32,1280]{2,1,0:T(8,128)(2,1)S(1)} async-done(((bf16[16,32,1280]{2,1,0:T(8,128)(2,1)}), bf16[16,32,1280]{2,1,0:T(8,128)(2,1)S(1)}, u32[]{:S(2)}, u32[]{:S(2)}) %all-to-all-start) | async-done | bytes 1310752 | tf_op jit(solution)/shard_map/all_to_all | solution.py:483
  117.7 5.4 %all-to-all-start.1 = ((bf16[4,8,1280]{2,1,0:T(8,128)(2,1)}), bf16[4,8,1280]{2,1,0:T(8,128)(2,1)S(1)}, u32[]{:S(2)}, u32[]{:S(2)}) async-start(bf16[4,8,1280]{2,1,0:T(8,128)(2,1)} %bitcast.9), calls=%async_computation.1 | async-start | bytes 163840 | tf_op jit(solution)/shard_map/all_to_all | solution.py:489
  123.3 2.1 %shard_map.91 = bf16[256,1024]{1,0:T(8,128)(2,1)} custom-call(f32[256,1024]{1,0:T(8,128)S(1)} %get-tuple-element.119.own, bf16[256,1024]{1,0:T(8,128)(2,1)S(1)} %collective-permute-done.20.got_1, bf16[256,1024]{1,0:T(8,128)(2,1)S(1)} %collective-permute-done.21.got_2, bf16[256,1024]{1,0:T(8,128)(2,1)} %collective-permute-done.22.got_3), custom_call_target="tpu_custom_call" | custom-call | flops 1048576 | bytes 4194304 | tf_op jit(solution)/shard_map/pallas_call | solution.py:486
  125.3 3.5 %all-to-all-done.1.got = bf16[4,8,1280]{2,1,0:T(8,128)(2,1)S(1)} async-done(((bf16[4,8,1280]{2,1,0:T(8,128)(2,1)}), bf16[4,8,1280]{2,1,0:T(8,128)(2,1)S(1)}, u32[]{:S(2)}, u32[]{:S(2)}) %all-to-all-start.1) | async-done | bytes 81952 | tf_op jit(solution)/shard_map/all_to_all | solution.py:489
  (56 shorter events, 29.3 us)
Async XLA Ops:
  0.6 15.7 %collective-permute-start = (bf16[256,1024]{1,0:T(8,128)(2,1)}, bf16[256,1024]{1,0:T(8,128)(2,1)S(1)}, u32[]{:S(2)}, u32[]{:S(2)}) collective-permute-start(bf16[256,1024]{1,0:T(8,128)(2,1)} %bitcast.5.refs_0_), channel_id=1, source_target_pairs={{0,3},{1,0},{2,1},{3,2},{4,7},{5,4},{6,5},{7,6},{8,11},{9,8},{10,9... | collective-permute-start | bytes 1572872 | tf_op jit(solution)/shard_map/ppermute | solution.py:392
  4.8 14.8 %collective-permute-start.1 = (bf16[256,1024]{1,0:T(8,128)(2,1)}, bf16[256,1024]{1,0:T(8,128)(2,1)S(1)}, u32[]{:S(2)}, u32[]{:S(2)}) collective-permute-start(bf16[256,1024]{1,0:T(8,128)(2,1)} %bitcast.5.refs_0_), channel_id=1, source_target_pairs={{0,1},{1,2},{2,3},{3,0},{4,5},{5,6},{6,7},{7,4},{8,9},{9,10},{10,1... | collective-permute-start | bytes 1572872 | tf_op jit(solution)/shard_map/ppermute | solution.py:392
  19.6 16.6 %collective-permute-start.2 = (bf16[256,1024]{1,0:T(8,128)(2,1)}, bf16[256,1024]{1,0:T(8,128)(2,1)S(1)}, u32[]{:S(2)}, u32[]{:S(2)}) collective-permute-start(bf16[256,1024]{1,0:T(8,128)(2,1)} %bitcast.5.refs_0_), channel_id=1, source_target_pairs={{0,2},{1,3},{2,0},{3,1},{4,6},{5,7},{6,4},{7,5},{8,10},{9,11},{10,... | collective-permute-start | bytes 1572872 | tf_op jit(solution)/shard_map/ppermute | solution.py:392
  19.6 18.5 %collective-permute-start.7 = (bf16[256,512]{1,0:T(8,128)(2,1)S(1)}, bf16[256,512]{1,0:T(8,128)(2,1)S(1)}, u32[]{:S(2)}, u32[]{:S(2)}) collective-permute-start(bf16[256,512]{1,0:T(8,128)(2,1)S(1)} %get-tuple-element.65.refs_3_), channel_id=1, source_target_pairs={{0,4},{4,8},{8,12},{12,0},{1,5},{5,9},{9,13},{13,1},{2,6},{6,10},{... | collective-permute-start | bytes 786440 | tf_op jit(solution)/shard_map/ppermute | solution.py:392
  23.7 21.4 %collective-permute-start.8 = (bf16[512,512]{1,0:T(8,128)(2,1)S(1)}, bf16[512,512]{1,0:T(8,128)(2,1)S(1)}, u32[]{:S(2)}, u32[]{:S(2)}) collective-permute-start(bf16[512,512]{1,0:T(8,128)(2,1)S(1)} %get-tuple-element.71.refs_4_), channel_id=1, source_target_pairs={{0,4},{4,8},{8,12},{12,0},{1,5},{5,9},{9,13},{13,1},{2,6},{6,10},{... | collective-permute-start | bytes 1572872 | tf_op jit(solution)/shard_map/ppermute | solution.py:392
  26.7 18.3 %collective-permute-start.4 = (bf16[256,512]{1,0:T(8,128)(2,1)S(1)}, bf16[256,512]{1,0:T(8,128)(2,1)S(1)}, u32[]{:S(2)}, u32[]{:S(2)}) collective-permute-start(bf16[256,512]{1,0:T(8,128)(2,1)S(1)} %get-tuple-element.80), channel_id=1, source_target_pairs={{0,1},{1,2},{2,3},{3,0},{4,5},{5,6},{6,7},{7,4},{8,9},{9,10},{10,1... | collective-permute-start | bytes 786440 | tf_op jit(solution)/shard_map/ppermute | solution.py:392
  27.9 17.2 %collective-permute-start.5 = (bf16[256,512]{1,0:T(8,128)(2,1)S(1)}, bf16[256,512]{1,0:T(8,128)(2,1)S(1)}, u32[]{:S(2)}, u32[]{:S(2)}) collective-permute-start(bf16[256,512]{1,0:T(8,128)(2,1)S(1)} %get-tuple-element.81), channel_id=1, source_target_pairs={{0,2},{1,3},{2,0},{3,1},{4,6},{5,7},{6,4},{7,5},{8,10},{9,11},{10,... | collective-permute-start | bytes 786440 | tf_op jit(solution)/shard_map/ppermute | solution.py:392
  36.2 8.9 %collective-permute-start.6 = (bf16[256,512]{1,0:T(8,128)(2,1)S(1)}, bf16[256,512]{1,0:T(8,128)(2,1)S(1)}, u32[]{:S(2)}, u32[]{:S(2)}) collective-permute-start(bf16[256,512]{1,0:T(8,128)(2,1)S(1)} %get-tuple-element.82), channel_id=1, source_target_pairs={{0,3},{1,0},{2,1},{3,2},{4,7},{5,4},{6,5},{7,6},{8,11},{9,8},{10,9... | collective-permute-start | bytes 786440 | tf_op jit(solution)/shard_map/ppermute | solution.py:392
  38.2 7.7 %collective-permute-start.9 = (bf16[256,512]{1,0:T(8,128)(2,1)S(1)}, bf16[256,512]{1,0:T(8,128)(2,1)S(1)}, u32[]{:S(2)}, u32[]{:S(2)}) collective-permute-start(bf16[256,512]{1,0:T(8,128)(2,1)S(1)} %get-tuple-element.72.refs_5_), channel_id=1, source_target_pairs={{0,4},{4,8},{8,12},{12,0},{1,5},{5,9},{9,13},{13,1},{2,6},{6,10},{... | collective-permute-start | bytes 786440 | tf_op jit(solution)/shard_map/ppermute | solution.py:392
  47.5 6.7 %collective-permute-start.10 = (f32[8,1024]{1,0:T(8,128)S(1)}, f32[8,1024]{1,0:T(8,128)S(1)}, u32[]{:S(2)}, u32[]{:S(2)}) collective-permute-start(f32[8,1024]{1,0:T(8,128)S(1)} %get-tuple-element.89.refs_3_), channel_id=1, source_target_pairs={{0,3},{1,0},{2,1},{3,2},{4,7},{5,4},{6,5},{7,6},{8,11},{9,8},{10,9... | collective-permute-start | bytes 98312 | tf_op jit(solution)/shard_map/ppermute | solution.py:392
  48.2 6.1 %collective-permute-start.11 = (f32[8,1024]{1,0:T(8,128)S(1)}, f32[8,1024]{1,0:T(8,128)S(1)}, u32[]{:S(2)}, u32[]{:S(2)}) collective-permute-start(f32[8,1024]{1,0:T(8,128)S(1)} %get-tuple-element.89.refs_3_), channel_id=1, source_target_pairs={{0,2},{1,3},{2,0},{3,1},{4,6},{5,7},{6,4},{7,5},{8,10},{9,11},{10,... | collective-permute-start | bytes 98312 | tf_op jit(solution)/shard_map/ppermute | solution.py:392
  51.3 5.1 %collective-permute-start.12 = (f32[8,1024]{1,0:T(8,128)S(1)}, f32[8,1024]{1,0:T(8,128)S(1)}, u32[]{:S(2)}, u32[]{:S(2)}) collective-permute-start(f32[8,1024]{1,0:T(8,128)S(1)} %get-tuple-element.89.refs_3_), channel_id=1, source_target_pairs={{0,1},{1,2},{2,3},{3,0},{4,5},{5,6},{6,7},{7,4},{8,9},{9,10},{10,1... | collective-permute-start | bytes 98312 | tf_op jit(solution)/shard_map/ppermute | solution.py:392
  51.3 21.9 %collective-permute-start.3 = (bf16[1024,256]{1,0:T(8,128)(2,1)S(1)}, bf16[1024,256]{1,0:T(8,128)(2,1)S(1)}, u32[]{:S(2)}, u32[]{:S(2)}) collective-permute-start(bf16[1024,256]{1,0:T(8,128)(2,1)S(1)} %get-tuple-element.73.refs_0_), channel_id=1, source_target_pairs={{0,12},{4,0},{8,4},{12,8},{1,13},{5,1},{9,5},{13,9},{2,14},{6,2},{... | collective-permute-start | bytes 1572872 | tf_op jit(solution)/shard_map/ppermute | solution.py:392
  58.1 16.2 %collective-permute-start.13 = (bf16[1024,256]{1,0:T(8,128)(2,1)S(1)}, bf16[1024,256]{1,0:T(8,128)(2,1)S(1)}, u32[]{:S(2)}, u32[]{:S(2)}) collective-permute-start(bf16[1024,256]{1,0:T(8,128)(2,1)S(1)} %get-tuple-element.94.refs_1_), channel_id=1, source_target_pairs={{0,12},{4,0},{8,4},{12,8},{1,13},{5,1},{9,5},{13,9},{2,14},{6,2},{... | collective-permute-start | bytes 1572872 | tf_op jit(solution)/shard_map/ppermute | solution.py:392
  61.1 22.0 %collective-permute-start.14 = (bf16[1024,256]{1,0:T(8,128)(2,1)S(1)}, bf16[1024,256]{1,0:T(8,128)(2,1)S(1)}, u32[]{:S(2)}, u32[]{:S(2)}) collective-permute-start(bf16[1024,256]{1,0:T(8,128)(2,1)S(1)} %get-tuple-element.112.refs_0_), channel_id=1, source_target_pairs={{0,3},{1,0},{2,1},{3,2},{4,7},{5,4},{6,5},{7,6},{8,11},{9,8},{10,9... | collective-permute-start | bytes 1572872 | tf_op jit(solution)/shard_map/ppermute | solution.py:392
  62.4 20.8 %collective-permute-start.15 = (bf16[1024,256]{1,0:T(8,128)(2,1)S(1)}, bf16[1024,256]{1,0:T(8,128)(2,1)S(1)}, u32[]{:S(2)}, u32[]{:S(2)}) collective-permute-start(bf16[1024,256]{1,0:T(8,128)(2,1)S(1)} %get-tuple-element.112.refs_0_), channel_id=1, source_target_pairs={{0,2},{1,3},{2,0},{3,1},{4,6},{5,7},{6,4},{7,5},{8,10},{9,11},{10,... | collective-permute-start | bytes 1572872 | tf_op jit(solution)/shard_map/ppermute | solution.py:392
  62.4 21.0 %collective-permute-start.16 = (bf16[1024,256]{1,0:T(8,128)(2,1)S(1)}, bf16[1024,256]{1,0:T(8,128)(2,1)S(1)}, u32[]{:S(2)}, u32[]{:S(2)}) collective-permute-start(bf16[1024,256]{1,0:T(8,128)(2,1)S(1)} %get-tuple-element.112.refs_0_), channel_id=1, source_target_pairs={{0,1},{1,2},{2,3},{3,0},{4,5},{5,6},{6,7},{7,4},{8,9},{9,10},{10,1... | collective-permute-start | bytes 1572872 | tf_op jit(solution)/shard_map/ppermute | solution.py:392
  73.2 11.6 %collective-permute-start.17 = (bf16[4,128,512]{2,1,0:T(8,128)(2,1)S(1)}, bf16[4,128,512]{2,1,0:T(8,128)(2,1)S(1)}, u32[]{:S(2)}, u32[]{:S(2)}) collective-permute-start(bf16[4,128,512]{2,1,0:T(8,128)(2,1)S(1)} %get-tuple-element.115), channel_id=1, source_target_pairs={{0,16},{16,0},{1,17},{17,1},{2,18},{18,2},{3,19},{19,3},{4,20},{20... | collective-permute-start | bytes 1572872 | tf_op jit(solution)/shard_map/ppermute | solution.py:396
  78.6 7.7 %collective-permute-start.18 = (bf16[4,128,512]{2,1,0:T(8,128)(2,1)S(1)}, bf16[4,128,512]{2,1,0:T(8,128)(2,1)S(1)}, u32[]{:S(2)}, u32[]{:S(2)}) collective-permute-start(bf16[4,128,512]{2,1,0:T(8,128)(2,1)S(1)} %get-tuple-element.116), channel_id=1, source_target_pairs={{0,16},{16,0},{1,17},{17,1},{2,18},{18,2},{3,19},{19,3},{4,20},{20... | collective-permute-start | bytes 1572872 | tf_op jit(solution)/shard_map/ppermute | solution.py:396
  87.7 29.2 %all-to-all-start = ((bf16[16,32,1280]{2,1,0:T(8,128)(2,1)}), bf16[16,32,1280]{2,1,0:T(8,128)(2,1)S(1)}, u32[]{:S(2)}, u32[]{:S(2)}) async-start(bf16[16,32,1280]{2,1,0:T(8,128)(2,1)} %bitcast.7), calls=%async_computation | async-start | bytes 2621440 | tf_op jit(solution)/shard_map/all_to_all | solution.py:483
  95.4 27.7 %collective-permute-start.20 = (bf16[256,1024]{1,0:T(8,128)(2,1)}, bf16[256,1024]{1,0:T(8,128)(2,1)S(1)}, u32[]{:S(2)}, u32[]{:S(2)}) collective-permute-start(bf16[256,1024]{1,0:T(8,128)(2,1)} %get-tuple-element.120), channel_id=1, source_target_pairs={{0,1},{1,2},{2,3},{3,0},{4,5},{5,6},{6,7},{7,4},{8,9},{9,10},{10,1... | collective-permute-start | bytes 1572872 | tf_op jit(solution)/shard_map/ppermute | solution.py:392
  97.1 26.2 %collective-permute-start.21 = (bf16[256,1024]{1,0:T(8,128)(2,1)}, bf16[256,1024]{1,0:T(8,128)(2,1)S(1)}, u32[]{:S(2)}, u32[]{:S(2)}) collective-permute-start(bf16[256,1024]{1,0:T(8,128)(2,1)} %copy-done.5), channel_id=1, source_target_pairs={{0,2},{1,3},{2,0},{3,1},{4,6},{5,7},{6,4},{7,5},{8,10},{9,11},{10,... | collective-permute-start | bytes 1572872 | tf_op jit(solution)/shard_map/ppermute | solution.py:392
  99.7 23.5 %collective-permute-start.22 = (bf16[256,1024]{1,0:T(8,128)(2,1)}, bf16[256,1024]{1,0:T(8,128)(2,1)}, u32[]{:S(2)}, u32[]{:S(2)}) collective-permute-start(bf16[256,1024]{1,0:T(8,128)(2,1)} %copy-done.4), channel_id=1, source_target_pairs={{0,3},{1,0},{2,1},{3,2},{4,7},{5,4},{6,5},{7,6},{8,11},{9,8},{10,9... | collective-permute-start | bytes 1572872 | tf_op jit(solution)/shard_map/ppermute | solution.py:392
  117.7 11.1 %all-to-all-start.1 = ((bf16[4,8,1280]{2,1,0:T(8,128)(2,1)}), bf16[4,8,1280]{2,1,0:T(8,128)(2,1)S(1)}, u32[]{:S(2)}, u32[]{:S(2)}) async-start(bf16[4,8,1280]{2,1,0:T(8,128)(2,1)} %bitcast.9), calls=%async_computation.1 | async-start | bytes 163840 | tf_op jit(solution)/shard_map/all_to_all | solution.py:489
  (7 other events, 38.0 us)

commit v14 on v13

--- a/solution.py
+++ b/solution.py
@@ -113,10 +113,15 @@
 
 
 def attend(q, kv, att, i, j, keep):
-    for h in range(2):
-        u = nt(q[rows(i), head(h)], kv[rows(j), head(h)])
-        w = (u * (1.0 + jnp.tanh(u)) * keep).astype(BF16)
-        att[rows(i), head(h)] += nn(w, kv[rows(j), head(h, BLK)])
+    two = range(2)
+    qi = [q[rows(i), head(h)] for h in two]
+    kj = [kv[rows(j), head(h)] for h in two]
+    vj = [kv[rows(j), head(h, BLK)] for h in two]
+    u = [nt(qi[h], kj[h]) for h in two]
+    w = [(u[h] * (1.0 + jnp.tanh(u[h])) * keep).astype(BF16) for h in two]
+    out = [nn(w[h], vj[h]) for h in two]
+    for h in two:
+        att[rows(i), head(h)] += out[h]
 
 
 def block_of(parts, k):
@@ -283,26 +288,40 @@
 
 
 def key_side(q, g, kv, dkv, dq, i, j, keep):
+    two = range(2)
     half = keep * 0.5
-    for h in range(2):
-        qi, gi = q[rows(i), head(h)], g[rows(i), head(h)]
-        kj, vj = kv[rows(j), head(h)], kv[rows(j), head(h, BLK)]
-        silu, slope = silu_parts(nt(kj, qi))
-        w = (silu * keep).astype(BF16)
-        ds = (nt(vj, gi) * slope * half).astype(BF16)
-        dkv[rows(j), head(h, BLK)] += nn(w, gi)
-        dkv[rows(j), head(h)] += nn(ds, qi)
+    qi = [q[rows(i), head(h)] for h in two]
+    gi = [g[rows(i), head(h)] for h in two]
+    kj = [kv[rows(j), head(h)] for h in two]
+    vj = [kv[rows(j), head(h, BLK)] for h in two]
+    u = [nt(kj[h], qi[h]) for h in two]
+    dw = [nt(vj[h], gi[h]) for h in two]
+    parts = [silu_parts(u[h]) for h in two]
+    w = [(parts[h][0] * keep).astype(BF16) for h in two]
+    ds = [(dw[h] * parts[h][1] * half).astype(BF16) for h in two]
+    dv = [nn(w[h], gi[h]) for h in two]
+    dk = [nn(ds[h], qi[h]) for h in two]
+    dqi = [tn(ds[h], kj[h]) for h in two] if dq is not None else None
+    for h in two:
+        dkv[rows(j), head(h, BLK)] += dv[h]
+        dkv[rows(j), head(h)] += dk[h]
         if dq is not None:
-            dq[rows(i), head(h)] += tn(ds, kj)
+            dq[rows(i), head(h)] += dqi[h]
 
 
 def query_side(q, g, kv, dq, i, j, keep):
+    two = range(2)
     half = keep * 0.5
-    for h in range(2):
-        kj, vj = kv[rows(j), head(h)], kv[rows(j), head(h, BLK)]
-        slope = silu_parts(nt(q[rows(i), head(h)], kj))[1]
-        ds = (nt(g[rows(i), head(h)], vj) * slope * half).astype(BF16)
-        dq[rows(i), head(h)] += nn(ds, kj)
+    qi = [q[rows(i), head(h)] for h in two]
+    gi = [g[rows(i), head(h)] for h in two]
+    kj = [kv[rows(j), head(h)] for h in two]
+    vj = [kv[rows(j), head(h, BLK)] for h in two]
+    slope = [silu_parts(nt(qi[h], kj[h]))[1] for h in two]
+    dw = [nt(gi[h], vj[h]) for h in two]
+    ds = [(dw[h] * slope[h] * half).astype(BF16) for h in two]
+    dqi = [nn(ds[h], kj[h]) for h in two]
+    for h in two:
+        dq[rows(i), head(h)] += dqi[h]
 
 
 def backward_local_body(info, *refs):

time: 130 us -> 129 us (level)
  starting transfers between devices: 46.6 us -> 42.7 us
    pallas_call x1, Pallas kernels: 1.81 us -> 4.68 us  [body(): call(backward_later_body, (bf16((BLK, 4 * BLK)),) * 4, 10, 5 << 30, 4 <<...]
    all_to_all x1, starting transfers between devices: 7.75 us -> 4.99 us  [body(): sums = lax.all_to_all(mine.reshape(16, 32, 5 * BLK), ('x', 'y'), 0, 0)]
  transfers between devices with their start and end apart: 25 -> 25, of which waited for: 12 -> 12; matrix products, arithmetic and copies ran while one was open for 1% -> 1% of each run, Pallas kernels for 28% -> 29%
where the time goes in v14:
time: 129 us; the launch traced here: 127 us
  starting transfers between devices  42.7 us (33%)
  Pallas kernels  40.7 us (32%)
  waiting for transfers between devices  39.1 us (30%)
  local copies, waits for them, and re-layouts  4.13 us (3%)
    ppermute x20, starting transfers between devices, along(): return lax.ppermute(x, axis, [(i, (i + d) % 4) for i in range(4)])  31.8 us
    ppermute x20, waiting for transfers between devices, along(): return lax.ppermute(x, axis, [(i, (i + d) % 4) for i in range(4)])  19.7 us
    all_to_all x1, waiting for transfers between devices, body(): sums = lax.all_to_all(mine.reshape(16, 32, 5 * BLK), ('x', 'y'), 0, 0)  14.8 us
    pallas_call x1, Pallas kernels, body(): call(backward_local_body, (bf16((GRP, BLK)), f32((GRP, 2 * BLK))), 8, 1 <...  6.77 us
    pallas_call x3, Pallas kernels, weights(): call(kernel, (bf16((4, 128, cols)), f32((4, 128, cols))), len(operands),...  6.29 us
    pallas_call x3, Pallas kernels, body(): call(project_body, (bf16((n * BLK, 2 * BLK)), bf16((n * BLK, BLK)), bf16(...  6.22 us
    all_to_all x1, starting transfers between devices, body(): got = lax.all_to_all(total.reshape(4, 8, 5 * BLK), 'z', 0, 0)  5.24 us
    all_to_all x1, starting transfers between devices, body(): sums = lax.all_to_all(mine.reshape(16, 32, 5 * BLK), ('x', 'y'), 0, 0)  4.99 us
  transfers between devices with their start and end apart: 25, of which 12 were waited for; matrix products, arithmetic and copies ran while one was open for 1% of the time, Pallas kernels for 29%

profile of v14, /device:TPU:0, one launch (start us, length us, event | category | flops | bytes accessed | tf_op | source)
XLA Modules:
  0.0 127.4 jit_solution(16807465585843927495)
XLA Ops:
  0.6 4.2 %collective-permute-start = (bf16[256,1024]{1,0:T(8,128)(2,1)}, bf16[256,1024]{1,0:T(8,128)(2,1)S(1)}, u32[]{:S(2)}, u32[]{:S(2)}) collective-permute-start(bf16[256,1024]{1,0:T(8,128)(2,1)} %bitcast.5.refs_0_), channel_id=1, source_target_pairs={{0,3},{1,0},{2,1},{3,2},{4,7},{5,4},{6,5},{7,6},{8,11},{9,8},{10,9... | collective-permute-start | bytes 1572872 | tf_op jit(solution)/shard_map/ppermute | solution.py:411
  5.6 3.4 %copy-done = bf16[1024,4096]{1,0:T(8,128)(2,1)S(1)} copy-done((bf16[1024,4096]{1,0:T(8,128)(2,1)S(1)}, bf16[1024,4096]{1,0:T(8,128)(2,1)}, u32[]{:S(2)}) %copy-start) | copy-done | bytes 8388632
  8.9 2.2 %shard_map.76 = (bf16[256,512]{1,0:T(8,128)(2,1)S(1)}, bf16[256,256]{1,0:T(8,128)(2,1)S(1)}, bf16[256,256]{1,0:T(8,128)(2,1)S(1)}, bf16[256,1024]{1,0:T(8,128)(2,1)S(1)}) custom-call(s32[12]{0:T(128)S(1)} %concatenate.3.info, bf16[256,1024]{1,0:T(8,128)(2,1)} %bitcast.5.refs_0_, bf16[1024,4096]{1,0:T(8,128)(2,1)S(1)} %copy-done), custom_call_target="tpu_custom_call" | custom-call | flops 1048576 | bytes 1048576 | tf_op jit(solution)/shard_map/pallas_call | solution.py:448
  11.2 5.1 %collective-permute-done.refs_0_.refs_1_ = bf16[256,1024]{1,0:T(8,128)(2,1)S(1)} collective-permute-done((bf16[256,1024]{1,0:T(8,128)(2,1)}, bf16[256,1024]{1,0:T(8,128)(2,1)S(1)}, u32[]{:S(2)}, u32[]{:S(2)}) %collective-permute-start) | collective-permute-done | bytes 524320 | tf_op jit(solution)/shard_map/ppermute | solution.py:411
  16.3 3.3 %collective-permute-done.1.refs_1_.refs_3_ = bf16[256,1024]{1,0:T(8,128)(2,1)S(1)} collective-permute-done((bf16[256,1024]{1,0:T(8,128)(2,1)}, bf16[256,1024]{1,0:T(8,128)(2,1)S(1)}, u32[]{:S(2)}, u32[]{:S(2)}) %collective-permute-start.1) | collective-permute-done | bytes 524320 | tf_op jit(solution)/shard_map/ppermute | solution.py:411
  21.3 2.4 %shard_map.77 = (bf16[512,512]{1,0:T(8,128)(2,1)S(1)}, bf16[512,256]{1,0:T(8,128)(2,1)S(1)}, bf16[512,256]{1,0:T(8,128)(2,1)S(1)}, bf16[256,1024]{1,0:T(8,128)(2,1)S(1)}, bf16[256,1024]{1,0:T(8,128)(2,1)S(1)}) custom-call(s32[12]{0:T(128)S(1)} %concatenate.3.info, bf16[256,1024]{1,0:T(8,128)(2,1)S(1)} %collective-permute-done.refs_0_.refs_1_, ...), custom_call_target="tpu_custom_call" | custom-call | flops 1048576 | bytes 1048576 | tf_op jit(solution)/shard_map/pallas_call | solution.py:448
  27.9 2.4 %collective-permute-start.5 = (bf16[256,512]{1,0:T(8,128)(2,1)S(1)}, bf16[256,512]{1,0:T(8,128)(2,1)S(1)}, u32[]{:S(2)}, u32[]{:S(2)}) collective-permute-start(bf16[256,512]{1,0:T(8,128)(2,1)S(1)} %get-tuple-element.81), channel_id=1, source_target_pairs={{0,2},{1,3},{2,0},{3,1},{4,6},{5,7},{6,4},{7,5},{8,10},{9,11},{10,... | collective-permute-start | bytes 786440 | tf_op jit(solution)/shard_map/ppermute | solution.py:411
  30.3 5.9 %collective-permute-done.2.refs_0_.refs_2_ = bf16[256,1024]{1,0:T(8,128)(2,1)S(1)} collective-permute-done((bf16[256,1024]{1,0:T(8,128)(2,1)}, bf16[256,1024]{1,0:T(8,128)(2,1)S(1)}, u32[]{:S(2)}, u32[]{:S(2)}) %collective-permute-start.2) | collective-permute-done | bytes 524320 | tf_op jit(solution)/shard_map/ppermute | solution.py:411
  39.8 4.2 %shard_map.79 = (bf16[1024,256]{1,0:T(8,128)(2,1)S(1)}, bf16[1024,512]{1,0:T(8,128)(2,1)S(1)}, f32[1024,256]{1,0:T(8,128)S(1)}) custom-call(s32[12]{0:T(128)S(1)} %concatenate.3.info, bf16[256,256]{1,0:T(8,128)(2,1)S(1)} %get-tuple-element.64.refs_0_, bf16[512,256]{1,0:T(8,128)(2,1)S(1)} %get-tuple-element.68.refs_1_, ...), custom_call_target="tpu_custom_call" | custom-call | flops 5368709120 | bytes 4194304 | tf_op jit(solution)/shard_map/pallas_call | solution.py:462
  48.2 3.1 %collective-permute-start.11 = (f32[8,1024]{1,0:T(8,128)S(1)}, f32[8,1024]{1,0:T(8,128)S(1)}, u32[]{:S(2)}, u32[]{:S(2)}) collective-permute-start(f32[8,1024]{1,0:T(8,128)S(1)} %get-tuple-element.89.refs_3_), channel_id=1, source_target_pairs={{0,2},{1,3},{2,0},{3,1},{4,6},{5,7},{6,4},{7,5},{8,10},{9,11},{10,... | collective-permute-start | bytes 98312 | tf_op jit(solution)/shard_map/ppermute | solution.py:411
  51.3 3.1 %collective-permute-start.3 = (bf16[1024,256]{1,0:T(8,128)(2,1)S(1)}, bf16[1024,256]{1,0:T(8,128)(2,1)S(1)}, u32[]{:S(2)}, u32[]{:S(2)}) collective-permute-start(bf16[1024,256]{1,0:T(8,128)(2,1)S(1)} %get-tuple-element.73.refs_0_), channel_id=1, source_target_pairs={{0,12},{4,0},{8,4},{12,8},{1,13},{5,1},{9,5},{13,9},{2,14},{6,2},{... | collective-permute-start | bytes 1572872 | tf_op jit(solution)/shard_map/ppermute | solution.py:411
  58.1 3.2 %collective-permute-start.13 = (bf16[1024,256]{1,0:T(8,128)(2,1)S(1)}, bf16[1024,256]{1,0:T(8,128)(2,1)S(1)}, u32[]{:S(2)}, u32[]{:S(2)}) collective-permute-start(bf16[1024,256]{1,0:T(8,128)(2,1)S(1)} %get-tuple-element.94.refs_1_), channel_id=1, source_target_pairs={{0,12},{4,0},{8,4},{12,8},{1,13},{5,1},{9,5},{13,9},{2,14},{6,2},{... | collective-permute-start | bytes 1572872 | tf_op jit(solution)/shard_map/ppermute | solution.py:411
  63.3 6.8 %shard_map.83 = (bf16[1024,256]{1,0:T(8,128)(2,1)S(1)}, f32[1024,512]{1,0:T(8,128)S(1)}) custom-call(s32[12]{0:T(128)S(1)} %concatenate.3.info, bf16[1024,256]{1,0:T(8,128)(2,1)S(1)} %get-tuple-element.73.refs_0_, bf16[1024,256]{1,0:T(8,128)(2,1)S(1)} %get-tuple-element.94.refs_1_, bf16[1024,512]{1,0:T(8,128)(2,1)S(1)} %get-tuple-element.96.refs_2_, ...), custom_call_target="tpu_custom_call" | custom-call | flops 1048576 | bytes 1048576 | tf_op jit(solution)/shard_map/pallas_call | solution.py:476
  70.1 2.5 %shard_map.84 = (bf16[4,128,512]{2,1,0:T(8,128)(2,1)S(1)}, f32[4,128,512]{2,1,0:T(8,128)S(1)}) custom-call(s32[12]{0:T(128)S(1)} %concatenate.3.info, bf16[256,1024]{1,0:T(8,128)(2,1)} %bitcast.5.refs_0_, bf16[256,1024]{1,0:T(8,128)(2,1)S(1)} %collective-permute-done.refs_0_.refs_1_, bf16[256,1024]{1,0:T(8,128)(2,1)S(1)} %collective-permute-done.2.refs_0_.refs_2_, ...), custom_call_target="tpu_custom_call" | custom-call | flops 1048576 | bytes 1048576 | tf_op jit(solution)/shard_map/pallas_call | solution.py:481
  74.0 4.7 %shard_map.85 = (bf16[256,1024]{1,0:T(8,128)(2,1)S(1)}, bf16[256,1024]{1,0:T(8,128)(2,1)S(1)}, bf16[256,1024]{1,0:T(8,128)(2,1)S(1)}, bf16[256,1024]{1,0:T(8,128)(2,1)S(1)}) custom-call(s32[12]{0:T(128)S(1)} %concatenate.3.info, bf16[1024,256]{1,0:T(8,128)(2,1)S(1)} %collective-permute-done.3.refs_0_, bf16[1024,256]{1,0:T(8,128)(2,1)S(1)} %collective-permute-done.13.refs_1_, ...), custom_call_target="tpu_custom_call" | custom-call | flops 5368709120 | bytes 4194304 | tf_op jit(solution)/shard_map/pallas_call | solution.py:489
  78.7 2.5 %shard_map.86 = (bf16[4,128,512]{2,1,0:T(8,128)(2,1)S(1)}, f32[4,128,512]{2,1,0:T(8,128)S(1)}) custom-call(s32[12]{0:T(128)S(1)} %concatenate.3.info, bf16[256,1024]{1,0:T(8,128)(2,1)} %bitcast.5.refs_0_, bf16[256,1024]{1,0:T(8,128)(2,1)S(1)} %collective-permute-done.refs_0_.refs_1_, bf16[256,1024]{1,0:T(8,128)(2,1)S(1)} %collective-permute-done.2.refs_0_.refs_2_, ...), custom_call_target="tpu_custom_call" | custom-call | flops 1048576 | bytes 1048576 | tf_op jit(solution)/shard_map/pallas_call | solution.py:481
  81.2 3.0 %shard_map.87 = (f32[256,1024]{1,0:T(8,128)S(1)}, bf16[256,1024]{1,0:T(8,128)(2,1)}, bf16[256,1024]{1,0:T(8,128)(2,1)S(1)}, bf16[256,1024]{1,0:T(8,128)(2,1)S(1)}) custom-call(s32[12]{0:T(128)S(1)} %concatenate.3.info, bf16[256,1024]{1,0:T(8,128)(2,1)S(1)} %get-tuple-element.105.refs_4_.refs_0_, bf16[256,1024]{1,0:T(8,128)(2,1)S(1)} %get-tuple-element.106.refs_5_.refs_1_, ...), custom_call_target="tpu_custom_call" | custom-call | flops 1048576 | bytes 1048576 | tf_op jit(solution)/shard_map/pallas_call | solution.py:493
  88.6 5.0 %all-to-all-start = ((bf16[16,32,1280]{2,1,0:T(8,128)(2,1)}), bf16[16,32,1280]{2,1,0:T(8,128)(2,1)S(1)}, u32[]{:S(2)}, u32[]{:S(2)}) async-start(bf16[16,32,1280]{2,1,0:T(8,128)(2,1)} %bitcast.7), calls=%async_computation | async-start | bytes 2621440 | tf_op jit(solution)/shard_map/all_to_all | solution.py:502
  95.1 2.8 %collective-permute-start.21 = (bf16[256,1024]{1,0:T(8,128)(2,1)}, bf16[256,1024]{1,0:T(8,128)(2,1)S(1)}, u32[]{:S(2)}, u32[]{:S(2)}) collective-permute-start(bf16[256,1024]{1,0:T(8,128)(2,1)} %copy-done.5), channel_id=1, source_target_pairs={{0,2},{1,3},{2,0},{3,1},{4,6},{5,7},{6,4},{7,5},{8,10},{9,11},{10,... | collective-permute-start | bytes 1572872 | tf_op jit(solution)/shard_map/ppermute | solution.py:411
  97.9 2.4 %collective-permute-start.22 = (bf16[256,1024]{1,0:T(8,128)(2,1)}, bf16[256,1024]{1,0:T(8,128)(2,1)}, u32[]{:S(2)}, u32[]{:S(2)}) collective-permute-start(bf16[256,1024]{1,0:T(8,128)(2,1)} %copy-done.4), channel_id=1, source_target_pairs={{0,3},{1,0},{2,1},{3,2},{4,7},{5,4},{6,5},{7,6},{8,11},{9,8},{10,9... | collective-permute-start | bytes 1572872 | tf_op jit(solution)/shard_map/ppermute | solution.py:411
  100.2 14.8 %all-to-all-done.got = bf16[16,32,1280]{2,1,0:T(8,128)(2,1)S(1)} async-done(((bf16[16,32,1280]{2,1,0:T(8,128)(2,1)}), bf16[16,32,1280]{2,1,0:T(8,128)(2,1)S(1)}, u32[]{:S(2)}, u32[]{:S(2)}) %all-to-all-start) | async-done | bytes 1310752 | tf_op jit(solution)/shard_map/all_to_all | solution.py:502
  115.8 5.2 %all-to-all-start.1 = ((bf16[4,8,1280]{2,1,0:T(8,128)(2,1)}), bf16[4,8,1280]{2,1,0:T(8,128)(2,1)S(1)}, u32[]{:S(2)}, u32[]{:S(2)}) async-start(bf16[4,8,1280]{2,1,0:T(8,128)(2,1)} %bitcast.9), calls=%async_computation.1 | async-start | bytes 163840 | tf_op jit(solution)/shard_map/all_to_all | solution.py:508
  121.2 2.1 %shard_map.91 = bf16[256,1024]{1,0:T(8,128)(2,1)} custom-call(f32[256,1024]{1,0:T(8,128)S(1)} %get-tuple-element.119.own, bf16[256,1024]{1,0:T(8,128)(2,1)S(1)} %collective-permute-done.20.got_1, bf16[256,1024]{1,0:T(8,128)(2,1)S(1)} %collective-permute-done.21.got_2, bf16[256,1024]{1,0:T(8,128)(2,1)} %collective-permute-done.22.got_3), custom_call_target="tpu_custom_call" | custom-call | flops 1048576 | bytes 4194304 | tf_op jit(solution)/shard_map/pallas_call | solution.py:505
  123.3 3.5 %all-to-all-done.1.got = bf16[4,8,1280]{2,1,0:T(8,128)(2,1)S(1)} async-done(((bf16[4,8,1280]{2,1,0:T(8,128)(2,1)}), bf16[4,8,1280]{2,1,0:T(8,128)(2,1)S(1)}, u32[]{:S(2)}, u32[]{:S(2)}) %all-to-all-start.1) | async-done | bytes 81952 | tf_op jit(solution)/shard_map/all_to_all | solution.py:508
  (56 shorter events, 28.9 us)
Async XLA Ops:
  0.6 15.7 %collective-permute-start = (bf16[256,1024]{1,0:T(8,128)(2,1)}, bf16[256,1024]{1,0:T(8,128)(2,1)S(1)}, u32[]{:S(2)}, u32[]{:S(2)}) collective-permute-start(bf16[256,1024]{1,0:T(8,128)(2,1)} %bitcast.5.refs_0_), channel_id=1, source_target_pairs={{0,3},{1,0},{2,1},{3,2},{4,7},{5,4},{6,5},{7,6},{8,11},{9,8},{10,9... | collective-permute-start | bytes 1572872 | tf_op jit(solution)/shard_map/ppermute | solution.py:411
  4.8 14.8 %collective-permute-start.1 = (bf16[256,1024]{1,0:T(8,128)(2,1)}, bf16[256,1024]{1,0:T(8,128)(2,1)S(1)}, u32[]{:S(2)}, u32[]{:S(2)}) collective-permute-start(bf16[256,1024]{1,0:T(8,128)(2,1)} %bitcast.5.refs_0_), channel_id=1, source_target_pairs={{0,1},{1,2},{2,3},{3,0},{4,5},{5,6},{6,7},{7,4},{8,9},{9,10},{10,1... | collective-permute-start | bytes 1572872 | tf_op jit(solution)/shard_map/ppermute | solution.py:411
  19.6 16.6 %collective-permute-start.2 = (bf16[256,1024]{1,0:T(8,128)(2,1)}, bf16[256,1024]{1,0:T(8,128)(2,1)S(1)}, u32[]{:S(2)}, u32[]{:S(2)}) collective-permute-start(bf16[256,1024]{1,0:T(8,128)(2,1)} %bitcast.5.refs_0_), channel_id=1, source_target_pairs={{0,2},{1,3},{2,0},{3,1},{4,6},{5,7},{6,4},{7,5},{8,10},{9,11},{10,... | collective-permute-start | bytes 1572872 | tf_op jit(solution)/shard_map/ppermute | solution.py:411
  19.6 18.5 %collective-permute-start.7 = (bf16[256,512]{1,0:T(8,128)(2,1)S(1)}, bf16[256,512]{1,0:T(8,128)(2,1)S(1)}, u32[]{:S(2)}, u32[]{:S(2)}) collective-permute-start(bf16[256,512]{1,0:T(8,128)(2,1)S(1)} %get-tuple-element.65.refs_3_), channel_id=1, source_target_pairs={{0,4},{4,8},{8,12},{12,0},{1,5},{5,9},{9,13},{13,1},{2,6},{6,10},{... | collective-permute-start | bytes 786440 | tf_op jit(solution)/shard_map/ppermute | solution.py:411
  23.7 21.4 %collective-permute-start.8 = (bf16[512,512]{1,0:T(8,128)(2,1)S(1)}, bf16[512,512]{1,0:T(8,128)(2,1)S(1)}, u32[]{:S(2)}, u32[]{:S(2)}) collective-permute-start(bf16[512,512]{1,0:T(8,128)(2,1)S(1)} %get-tuple-element.71.refs_4_), channel_id=1, source_target_pairs={{0,4},{4,8},{8,12},{12,0},{1,5},{5,9},{9,13},{13,1},{2,6},{6,10},{... | collective-permute-start | bytes 1572872 | tf_op jit(solution)/shard_map/ppermute | solution.py:411
  26.7 17.3 %collective-permute-start.4 = (bf16[256,512]{1,0:T(8,128)(2,1)S(1)}, bf16[256,512]{1,0:T(8,128)(2,1)S(1)}, u32[]{:S(2)}, u32[]{:S(2)}) collective-permute-start(bf16[256,512]{1,0:T(8,128)(2,1)S(1)} %get-tuple-element.80), channel_id=1, source_target_pairs={{0,1},{1,2},{2,3},{3,0},{4,5},{5,6},{6,7},{7,4},{8,9},{9,10},{10,1... | collective-permute-start | bytes 786440 | tf_op jit(solution)/shard_map/ppermute | solution.py:411
  27.9 17.2 %collective-permute-start.5 = (bf16[256,512]{1,0:T(8,128)(2,1)S(1)}, bf16[256,512]{1,0:T(8,128)(2,1)S(1)}, u32[]{:S(2)}, u32[]{:S(2)}) collective-permute-start(bf16[256,512]{1,0:T(8,128)(2,1)S(1)} %get-tuple-element.81), channel_id=1, source_target_pairs={{0,2},{1,3},{2,0},{3,1},{4,6},{5,7},{6,4},{7,5},{8,10},{9,11},{10,... | collective-permute-start | bytes 786440 | tf_op jit(solution)/shard_map/ppermute | solution.py:411
  36.2 8.9 %collective-permute-start.6 = (bf16[256,512]{1,0:T(8,128)(2,1)S(1)}, bf16[256,512]{1,0:T(8,128)(2,1)S(1)}, u32[]{:S(2)}, u32[]{:S(2)}) collective-permute-start(bf16[256,512]{1,0:T(8,128)(2,1)S(1)} %get-tuple-element.82), channel_id=1, source_target_pairs={{0,3},{1,0},{2,1},{3,2},{4,7},{5,4},{6,5},{7,6},{8,11},{9,8},{10,9... | collective-permute-start | bytes 786440 | tf_op jit(solution)/shard_map/ppermute | solution.py:411
  38.2 7.7 %collective-permute-start.9 = (bf16[256,512]{1,0:T(8,128)(2,1)S(1)}, bf16[256,512]{1,0:T(8,128)(2,1)S(1)}, u32[]{:S(2)}, u32[]{:S(2)}) collective-permute-start(bf16[256,512]{1,0:T(8,128)(2,1)S(1)} %get-tuple-element.72.refs_5_), channel_id=1, source_target_pairs={{0,4},{4,8},{8,12},{12,0},{1,5},{5,9},{9,13},{13,1},{2,6},{6,10},{... | collective-permute-start | bytes 786440 | tf_op jit(solution)/shard_map/ppermute | solution.py:411
  47.5 6.9 %collective-permute-start.10 = (f32[8,1024]{1,0:T(8,128)S(1)}, f32[8,1024]{1,0:T(8,128)S(1)}, u32[]{:S(2)}, u32[]{:S(2)}) collective-permute-start(f32[8,1024]{1,0:T(8,128)S(1)} %get-tuple-element.89.refs_3_), channel_id=1, source_target_pairs={{0,3},{1,0},{2,1},{3,2},{4,7},{5,4},{6,5},{7,6},{8,11},{9,8},{10,9... | collective-permute-start | bytes 98312 | tf_op jit(solution)/shard_map/ppermute | solution.py:411
  48.2 6.2 %collective-permute-start.11 = (f32[8,1024]{1,0:T(8,128)S(1)}, f32[8,1024]{1,0:T(8,128)S(1)}, u32[]{:S(2)}, u32[]{:S(2)}) collective-permute-start(f32[8,1024]{1,0:T(8,128)S(1)} %get-tuple-element.89.refs_3_), channel_id=1, source_target_pairs={{0,2},{1,3},{2,0},{3,1},{4,6},{5,7},{6,4},{7,5},{8,10},{9,11},{10,... | collective-permute-start | bytes 98312 | tf_op jit(solution)/shard_map/ppermute | solution.py:411
  51.3 5.1 %collective-permute-start.12 = (f32[8,1024]{1,0:T(8,128)S(1)}, f32[8,1024]{1,0:T(8,128)S(1)}, u32[]{:S(2)}, u32[]{:S(2)}) collective-permute-start(f32[8,1024]{1,0:T(8,128)S(1)} %get-tuple-element.89.refs_3_), channel_id=1, source_target_pairs={{0,1},{1,2},{2,3},{3,0},{4,5},{5,6},{6,7},{7,4},{8,9},{9,10},{10,1... | collective-permute-start | bytes 98312 | tf_op jit(solution)/shard_map/ppermute | solution.py:411
  51.3 21.2 %collective-permute-start.3 = (bf16[1024,256]{1,0:T(8,128)(2,1)S(1)}, bf16[1024,256]{1,0:T(8,128)(2,1)S(1)}, u32[]{:S(2)}, u32[]{:S(2)}) collective-permute-start(bf16[1024,256]{1,0:T(8,128)(2,1)S(1)} %get-tuple-element.73.refs_0_), channel_id=1, source_target_pairs={{0,12},{4,0},{8,4},{12,8},{1,13},{5,1},{9,5},{13,9},{2,14},{6,2},{... | collective-permute-start | bytes 1572872 | tf_op jit(solution)/shard_map/ppermute | solution.py:411
  58.1 15.9 %collective-permute-start.13 = (bf16[1024,256]{1,0:T(8,128)(2,1)S(1)}, bf16[1024,256]{1,0:T(8,128)(2,1)S(1)}, u32[]{:S(2)}, u32[]{:S(2)}) collective-permute-start(bf16[1024,256]{1,0:T(8,128)(2,1)S(1)} %get-tuple-element.94.refs_1_), channel_id=1, source_target_pairs={{0,12},{4,0},{8,4},{12,8},{1,13},{5,1},{9,5},{13,9},{2,14},{6,2},{... | collective-permute-start | bytes 1572872 | tf_op jit(solution)/shard_map/ppermute | solution.py:411
  61.3 22.9 %collective-permute-start.14 = (bf16[1024,256]{1,0:T(8,128)(2,1)S(1)}, bf16[1024,256]{1,0:T(8,128)(2,1)S(1)}, u32[]{:S(2)}, u32[]{:S(2)}) collective-permute-start(bf16[1024,256]{1,0:T(8,128)(2,1)S(1)} %get-tuple-element.112.refs_0_), channel_id=1, source_target_pairs={{0,3},{1,0},{2,1},{3,2},{4,7},{5,4},{6,5},{7,6},{8,11},{9,8},{10,9... | collective-permute-start | bytes 1572872 | tf_op jit(solution)/shard_map/ppermute | solution.py:411
  61.5 22.7 %collective-permute-start.15 = (bf16[1024,256]{1,0:T(8,128)(2,1)S(1)}, bf16[1024,256]{1,0:T(8,128)(2,1)S(1)}, u32[]{:S(2)}, u32[]{:S(2)}) collective-permute-start(bf16[1024,256]{1,0:T(8,128)(2,1)S(1)} %get-tuple-element.112.refs_0_), channel_id=1, source_target_pairs={{0,2},{1,3},{2,0},{3,1},{4,6},{5,7},{6,4},{7,5},{8,10},{9,11},{10,... | collective-permute-start | bytes 1572872 | tf_op jit(solution)/shard_map/ppermute | solution.py:411
  62.5 21.8 %collective-permute-start.16 = (bf16[1024,256]{1,0:T(8,128)(2,1)S(1)}, bf16[1024,256]{1,0:T(8,128)(2,1)S(1)}, u32[]{:S(2)}, u32[]{:S(2)}) collective-permute-start(bf16[1024,256]{1,0:T(8,128)(2,1)S(1)} %get-tuple-element.112.refs_0_), channel_id=1, source_target_pairs={{0,1},{1,2},{2,3},{3,0},{4,5},{5,6},{6,7},{7,4},{8,9},{9,10},{10,1... | collective-permute-start | bytes 1572872 | tf_op jit(solution)/shard_map/ppermute | solution.py:411
  72.6 13.6 %collective-permute-start.17 = (bf16[4,128,512]{2,1,0:T(8,128)(2,1)S(1)}, bf16[4,128,512]{2,1,0:T(8,128)(2,1)S(1)}, u32[]{:S(2)}, u32[]{:S(2)}) collective-permute-start(bf16[4,128,512]{2,1,0:T(8,128)(2,1)S(1)} %get-tuple-element.115), channel_id=1, source_target_pairs={{0,16},{16,0},{1,17},{17,1},{2,18},{18,2},{3,19},{19,3},{4,20},{20... | collective-permute-start | bytes 1572872 | tf_op jit(solution)/shard_map/ppermute | solution.py:415
  81.1 6.2 %collective-permute-start.18 = (bf16[4,128,512]{2,1,0:T(8,128)(2,1)S(1)}, bf16[4,128,512]{2,1,0:T(8,128)(2,1)S(1)}, u32[]{:S(2)}, u32[]{:S(2)}) collective-permute-start(bf16[4,128,512]{2,1,0:T(8,128)(2,1)S(1)} %get-tuple-element.116), channel_id=1, source_target_pairs={{0,16},{16,0},{1,17},{17,1},{2,18},{18,2},{3,19},{19,3},{4,20},{20... | collective-permute-start | bytes 1572872 | tf_op jit(solution)/shard_map/ppermute | solution.py:415
  88.6 26.4 %all-to-all-start = ((bf16[16,32,1280]{2,1,0:T(8,128)(2,1)}), bf16[16,32,1280]{2,1,0:T(8,128)(2,1)S(1)}, u32[]{:S(2)}, u32[]{:S(2)}) async-start(bf16[16,32,1280]{2,1,0:T(8,128)(2,1)} %bitcast.7), calls=%async_computation | async-start | bytes 2621440 | tf_op jit(solution)/shard_map/all_to_all | solution.py:502
  93.6 27.4 %collective-permute-start.20 = (bf16[256,1024]{1,0:T(8,128)(2,1)}, bf16[256,1024]{1,0:T(8,128)(2,1)S(1)}, u32[]{:S(2)}, u32[]{:S(2)}) collective-permute-start(bf16[256,1024]{1,0:T(8,128)(2,1)} %get-tuple-element.120), channel_id=1, source_target_pairs={{0,1},{1,2},{2,3},{3,0},{4,5},{5,6},{6,7},{7,4},{8,9},{9,10},{10,1... | collective-permute-start | bytes 1572872 | tf_op jit(solution)/shard_map/ppermute | solution.py:411
  95.1 26.1 %collective-permute-start.21 = (bf16[256,1024]{1,0:T(8,128)(2,1)}, bf16[256,1024]{1,0:T(8,128)(2,1)S(1)}, u32[]{:S(2)}, u32[]{:S(2)}) collective-permute-start(bf16[256,1024]{1,0:T(8,128)(2,1)} %copy-done.5), channel_id=1, source_target_pairs={{0,2},{1,3},{2,0},{3,1},{4,6},{5,7},{6,4},{7,5},{8,10},{9,11},{10,... | collective-permute-start | bytes 1572872 | tf_op jit(solution)/shard_map/ppermute | solution.py:411
  97.9 23.3 %collective-permute-start.22 = (bf16[256,1024]{1,0:T(8,128)(2,1)}, bf16[256,1024]{1,0:T(8,128)(2,1)}, u32[]{:S(2)}, u32[]{:S(2)}) collective-permute-start(bf16[256,1024]{1,0:T(8,128)(2,1)} %copy-done.4), channel_id=1, source_target_pairs={{0,3},{1,0},{2,1},{3,2},{4,7},{5,4},{6,5},{7,6},{8,11},{9,8},{10,9... | collective-permute-start | bytes 1572872 | tf_op jit(solution)/shard_map/ppermute | solution.py:411
  115.8 11.0 %all-to-all-start.1 = ((bf16[4,8,1280]{2,1,0:T(8,128)(2,1)}), bf16[4,8,1280]{2,1,0:T(8,128)(2,1)S(1)}, u32[]{:S(2)}, u32[]{:S(2)}) async-start(bf16[4,8,1280]{2,1,0:T(8,128)(2,1)} %bitcast.9), calls=%async_computation.1 | async-start | bytes 163840 | tf_op jit(solution)/shard_map/all_to_all | solution.py:508
  (7 other events, 37.8 us)

commit v15 on v14

--- a/solution.py
+++ b/solution.py
@@ -225,37 +225,37 @@
         gp[at, :] = (grad_gated * normed * dsig[k][:, 0:BLK].astype(F32)).astype(BF16)
 
 
-def pack(info, acc, send, keep):
-    for x in range(4):
-        for out, c, kind in ((send, 1 - info[10], BF16), (keep, info[10], F32)):
-            at = pl.ds(pl.multiple_of((x * 2 + c) * 128, 128), 128)
-            out[x, :, :] = acc[at, :].astype(kind)
+def pack(info, x, total, lanes, send, keep):
+    first = info[10] == 0
+    send[x, :, lanes] = jnp.where(first, total[128:], total[:128]).astype(BF16)
+    keep[x, :, lanes] = jnp.where(first, total[:128], total[128:])
 
 
 def early_weights_body(info, *refs):
-    ev, (gp_g, gp_q, send, keep, acc) = refs[0:4], refs[4:9]
-    for k in range(NB):
-        at = rows(lax.rem(info[9] + k, NB))
-        for lanes, gp in ((slice(0, BLK), gp_g), (slice(BLK, 2 * BLK), gp_q)):
-            part = tn(ev[k][...], gp[at, :])
-            acc[:, lanes] = part if k == 0 else acc[:, lanes] + part
-    pack(info, acc, send, keep)
+    ev, (gp_g, gp_q, send, keep) = refs[0:4], refs[4:8]
+    for lanes, gp in ((slice(0, BLK), gp_g), (slice(BLK, 2 * BLK), gp_q)):
+        for x in range(4):
+            part = [
+                tn(ev[k][:, x * BLK : (x + 1) * BLK], gp[rows(lax.rem(info[9] + k, NB)), :]) for k in range(NB)
+            ]
+            pack(info, x, part[0] + part[1] + part[2] + part[3], lanes, send, keep)
 
 
 def late_weights_body(info, *refs):
     ev, gp = refs[0:4], refs[4:8]
-    send, keep, acc = refs[8:11]
-    for k in range(NB):
-        part = tn(ev[k][...], gp[k][:, 2 * BLK :])
-        acc[...] = part if k == 0 else acc[...] + part
-    pack(info, acc, send, keep)
+    send, keep = refs[8:10]
+    for n in range(2):
+        lanes, cols = slice(n * BLK, (n + 1) * BLK), slice((n + 2) * BLK, (n + 3) * BLK)
+        for x in range(4):
+            part = [tn(ev[k][:, x * BLK : (x + 1) * BLK], gp[k][:, cols]) for k in range(NB)]
+            pack(info, x, part[0] + part[1] + part[2] + part[3], lanes, send, keep)
 
 
 def out_weights_body(info, *refs):
-    gated, (cot, send, keep, acc) = refs[0:4], refs[4:8]
-    for k in range(NB):
-        acc[rows(lax.rem(info[9] + k, NB)), :] = tn(gated[k][...], cot[...])
-    pack(info, acc, send, keep)
+    gated, (cot, send, keep) = refs[0:4], refs[4:7]
+    part = [tn(gated[k][...], cot[...]) for k in range(NB)]
+    for k in range(NB):
+        pack(info, lax.rem(info[9] + k, NB), part[k], slice(0, BLK), send, keep)
 
 
 def add_core_body(keep_1, keep_2, keep_3, got_1, got_2, got_3, out):
@@ -479,8 +479,7 @@
     )(info, q, gatt, kv, kv_prev, *dsigs)
     def weights(kernel, cols, operands):
         send, keep = call(
-            kernel, (bf16((4, 128, cols)), f32((4, 128, cols))), len(operands), 1 << 20, 1 << 20,
-            [pltpu.VMEM((D, cols), F32)],
+            kernel, (bf16((4, 128, cols)), f32((4, 128, cols))), len(operands), 1 << 20, 1 << 20
         )(info, *operands)
         return swap(send), keep
 

time: 129 us -> 131 us (1.016)
  starting transfers between devices: 42.7 us -> 48.5 us
  waiting for transfers between devices: 39.1 us -> 36.5 us
    pallas_call x1, Pallas kernels: 4.68 us -> 2.34 us  [body(): call(backward_later_body, (bf16((BLK, 4 * BLK)),) * 4, 10, 5 << 30, 4 <<...]
    all_to_all x1, starting transfers between devices: 4.99 us -> 7.28 us  [body(): sums = lax.all_to_all(mine.reshape(16, 32, 5 * BLK), ('x', 'y'), 0, 0)]
    ppermute x3, starting transfers between devices: 0.7 us -> 2.92 us  [swap(): return lax.ppermute(x, 'c', [(0, 1), (1, 0)])]
    ppermute x20, waiting for transfers between devices: 19.7 us -> 17.5 us  [along(): return lax.ppermute(x, axis, [(i, (i + d) % 4) for i in range(4)])]
    pallas_call x1, Pallas kernels: 6.77 us -> 8.18 us  [body(): call(backward_local_body, (bf16((GRP, BLK)), f32((GRP, 2 * BLK))), 8, 1 <...]
  transfers between devices with their start and end apart: 25 -> 25, of which waited for: 12 -> 12; matrix products, arithmetic and copies ran while one was open for 1% -> 1% of each run, Pallas kernels for 29% -> 28%
where the time goes in v15:
time: 131 us; the launch traced here: 130 us
  starting transfers between devices  48.5 us (37%)
  Pallas kernels  40.6 us (31%)
  waiting for transfers between devices  36.5 us (28%)
  local copies, waits for them, and re-layouts  4.13 us (3%)
    ppermute x20, starting transfers between devices, along(): return lax.ppermute(x, axis, [(i, (i + d) % 4) for i in range(4)])  32.9 us
    ppermute x20, waiting for transfers between devices, along(): return lax.ppermute(x, axis, [(i, (i + d) % 4) for i in range(4)])  17.5 us
    all_to_all x1, waiting for transfers between devices, body(): sums = lax.all_to_all(mine.reshape(16, 32, 5 * BLK), ('x', 'y'), 0, 0)  14.3 us
    pallas_call x1, Pallas kernels, body(): call(backward_local_body, (bf16((GRP, BLK)), f32((GRP, 2 * BLK))), 8, 1 <...  8.18 us
    all_to_all x1, starting transfers between devices, body(): sums = lax.all_to_all(mine.reshape(16, 32, 5 * BLK), ('x', 'y'), 0, 0)  7.28 us
    pallas_call x3, Pallas kernels, body(): call(project_body, (bf16((n * BLK, 2 * BLK)), bf16((n * BLK, BLK)), bf16(...  6.22 us
    pallas_call x3, Pallas kernels, weights(): call(kernel, (bf16((4, 128, cols)), f32((4, 128, cols))), len(operands),...  6.21 us
    all_to_all x1, starting transfers between devices, body(): got = lax.all_to_all(total.reshape(4, 8, 5 * BLK), 'z', 0, 0)  5.38 us
  transfers between devices with their start and end apart: 25, of which 12 were waited for; matrix products, arithmetic and copies ran while one was open for 1% of the time, Pallas kernels for 28%

profile of v15, /device:TPU:0, one launch (start us, length us, event | category | flops | bytes accessed | tf_op | source)
XLA Modules:
  0.0 130.4 jit_solution(8298640370927671664)
XLA Ops:
  0.6 4.2 %collective-permute-start = (bf16[256,1024]{1,0:T(8,128)(2,1)}, bf16[256,1024]{1,0:T(8,128)(2,1)S(1)}, u32[]{:S(2)}, u32[]{:S(2)}) collective-permute-start(bf16[256,1024]{1,0:T(8,128)(2,1)} %bitcast.5.refs_0_), channel_id=1, source_target_pairs={{0,3},{1,0},{2,1},{3,2},{4,7},{5,4},{6,5},{7,6},{8,11},{9,8},{10,9... | collective-permute-start | bytes 1572872 | tf_op jit(solution)/shard_map/ppermute | solution.py:411
  5.6 3.4 %copy-done = bf16[1024,4096]{1,0:T(8,128)(2,1)S(1)} copy-done((bf16[1024,4096]{1,0:T(8,128)(2,1)S(1)}, bf16[1024,4096]{1,0:T(8,128)(2,1)}, u32[]{:S(2)}) %copy-start) | copy-done | bytes 8388632
  8.9 2.2 %shard_map.76 = (bf16[256,512]{1,0:T(8,128)(2,1)S(1)}, bf16[256,256]{1,0:T(8,128)(2,1)S(1)}, bf16[256,256]{1,0:T(8,128)(2,1)S(1)}, bf16[256,1024]{1,0:T(8,128)(2,1)S(1)}) custom-call(s32[12]{0:T(128)S(1)} %concatenate.3.info, bf16[256,1024]{1,0:T(8,128)(2,1)} %bitcast.5.refs_0_, bf16[1024,4096]{1,0:T(8,128)(2,1)S(1)} %copy-done), custom_call_target="tpu_custom_call" | custom-call | flops 1048576 | bytes 1048576 | tf_op jit(solution)/shard_map/pallas_call | solution.py:448
  11.2 5.1 %collective-permute-done.refs_0_.refs_1_ = bf16[256,1024]{1,0:T(8,128)(2,1)S(1)} collective-permute-done((bf16[256,1024]{1,0:T(8,128)(2,1)}, bf16[256,1024]{1,0:T(8,128)(2,1)S(1)}, u32[]{:S(2)}, u32[]{:S(2)}) %collective-permute-start) | collective-permute-done | bytes 524320 | tf_op jit(solution)/shard_map/ppermute | solution.py:411
  16.3 3.3 %collective-permute-done.1.refs_1_.refs_3_ = bf16[256,1024]{1,0:T(8,128)(2,1)S(1)} collective-permute-done((bf16[256,1024]{1,0:T(8,128)(2,1)}, bf16[256,1024]{1,0:T(8,128)(2,1)S(1)}, u32[]{:S(2)}, u32[]{:S(2)}) %collective-permute-start.1) | collective-permute-done | bytes 524320 | tf_op jit(solution)/shard_map/ppermute | solution.py:411
  21.3 2.4 %shard_map.77 = (bf16[512,512]{1,0:T(8,128)(2,1)S(1)}, bf16[512,256]{1,0:T(8,128)(2,1)S(1)}, bf16[512,256]{1,0:T(8,128)(2,1)S(1)}, bf16[256,1024]{1,0:T(8,128)(2,1)S(1)}, bf16[256,1024]{1,0:T(8,128)(2,1)S(1)}) custom-call(s32[12]{0:T(128)S(1)} %concatenate.3.info, bf16[256,1024]{1,0:T(8,128)(2,1)S(1)} %collective-permute-done.refs_0_.refs_1_, ...), custom_call_target="tpu_custom_call" | custom-call | flops 1048576 | bytes 1048576 | tf_op jit(solution)/shard_map/pallas_call | solution.py:448
  27.9 2.4 %collective-permute-start.5 = (bf16[256,512]{1,0:T(8,128)(2,1)S(1)}, bf16[256,512]{1,0:T(8,128)(2,1)S(1)}, u32[]{:S(2)}, u32[]{:S(2)}) collective-permute-start(bf16[256,512]{1,0:T(8,128)(2,1)S(1)} %get-tuple-element.81), channel_id=1, source_target_pairs={{0,2},{1,3},{2,0},{3,1},{4,6},{5,7},{6,4},{7,5},{8,10},{9,11},{10,... | collective-permute-start | bytes 786440 | tf_op jit(solution)/shard_map/ppermute | solution.py:411
  30.3 5.9 %collective-permute-done.2.refs_0_.refs_2_ = bf16[256,1024]{1,0:T(8,128)(2,1)S(1)} collective-permute-done((bf16[256,1024]{1,0:T(8,128)(2,1)}, bf16[256,1024]{1,0:T(8,128)(2,1)S(1)}, u32[]{:S(2)}, u32[]{:S(2)}) %collective-permute-start.2) | collective-permute-done | bytes 524320 | tf_op jit(solution)/shard_map/ppermute | solution.py:411
  39.8 5.1 %shard_map.79 = (bf16[1024,256]{1,0:T(8,128)(2,1)S(1)}, bf16[1024,512]{1,0:T(8,128)(2,1)S(1)}, f32[1024,256]{1,0:T(8,128)S(1)}) custom-call(s32[12]{0:T(128)S(1)} %concatenate.3.info, bf16[256,256]{1,0:T(8,128)(2,1)S(1)} %get-tuple-element.64.refs_0_, bf16[512,256]{1,0:T(8,128)(2,1)S(1)} %get-tuple-element.68.refs_1_, ...), custom_call_target="tpu_custom_call" | custom-call | flops 5368709120 | bytes 4194304 | tf_op jit(solution)/shard_map/pallas_call | solution.py:462
  48.2 3.1 %collective-permute-start.11 = (f32[8,1024]{1,0:T(8,128)S(1)}, f32[8,1024]{1,0:T(8,128)S(1)}, u32[]{:S(2)}, u32[]{:S(2)}) collective-permute-start(f32[8,1024]{1,0:T(8,128)S(1)} %get-tuple-element.89.refs_3_), channel_id=1, source_target_pairs={{0,2},{1,3},{2,0},{3,1},{4,6},{5,7},{6,4},{7,5},{8,10},{9,11},{10,... | collective-permute-start | bytes 98312 | tf_op jit(solution)/shard_map/ppermute | solution.py:411
  51.3 3.5 %collective-permute-start.3 = (bf16[1024,256]{1,0:T(8,128)(2,1)S(1)}, bf16[1024,256]{1,0:T(8,128)(2,1)S(1)}, u32[]{:S(2)}, u32[]{:S(2)}) collective-permute-start(bf16[1024,256]{1,0:T(8,128)(2,1)S(1)} %get-tuple-element.73.refs_0_), channel_id=1, source_target_pairs={{0,12},{4,0},{8,4},{12,8},{1,13},{5,1},{9,5},{13,9},{2,14},{6,2},{... | collective-permute-start | bytes 1572872 | tf_op jit(solution)/shard_map/ppermute | solution.py:411
  58.1 3.6 %collective-permute-start.13 = (bf16[1024,256]{1,0:T(8,128)(2,1)S(1)}, bf16[1024,256]{1,0:T(8,128)(2,1)S(1)}, u32[]{:S(2)}, u32[]{:S(2)}) collective-permute-start(bf16[1024,256]{1,0:T(8,128)(2,1)S(1)} %get-tuple-element.94.refs_1_), channel_id=1, source_target_pairs={{0,12},{4,0},{8,4},{12,8},{1,13},{5,1},{9,5},{13,9},{2,14},{6,2},{... | collective-permute-start | bytes 1572872 | tf_op jit(solution)/shard_map/ppermute | solution.py:411
  63.7 8.2 %shard_map.83 = (bf16[1024,256]{1,0:T(8,128)(2,1)S(1)}, f32[1024,512]{1,0:T(8,128)S(1)}) custom-call(s32[12]{0:T(128)S(1)} %concatenate.3.info, bf16[1024,256]{1,0:T(8,128)(2,1)S(1)} %get-tuple-element.73.refs_0_, bf16[1024,256]{1,0:T(8,128)(2,1)S(1)} %get-tuple-element.94.refs_1_, bf16[1024,512]{1,0:T(8,128)(2,1)S(1)} %get-tuple-element.96.refs_2_, ...), custom_call_target="tpu_custom_call" | custom-call | flops 1048576 | bytes 1048576 | tf_op jit(solution)/shard_map/pallas_call | solution.py:476
  71.9 2.5 %shard_map.84 = (bf16[4,128,512]{2,1,0:T(8,128)(2,1)S(1)}, f32[4,128,512]{2,1,0:T(8,128)S(1)}) custom-call(s32[12]{0:T(128)S(1)} %concatenate.3.info, bf16[256,1024]{1,0:T(8,128)(2,1)} %bitcast.5.refs_0_, bf16[256,1024]{1,0:T(8,128)(2,1)S(1)} %collective-permute-done.refs_0_.refs_1_, bf16[256,1024]{1,0:T(8,128)(2,1)S(1)} %collective-permute-done.2.refs_0_.refs_2_, ...), custom_call_target="tpu_custom_call" | custom-call | flops 1048576 | bytes 1048576 | tf_op jit(solution)/shard_map/pallas_call | solution.py:481
  74.7 2.3 %shard_map.85 = (bf16[256,1024]{1,0:T(8,128)(2,1)S(1)}, bf16[256,1024]{1,0:T(8,128)(2,1)S(1)}, bf16[256,1024]{1,0:T(8,128)(2,1)S(1)}, bf16[256,1024]{1,0:T(8,128)(2,1)S(1)}) custom-call(s32[12]{0:T(128)S(1)} %concatenate.3.info, bf16[1024,256]{1,0:T(8,128)(2,1)S(1)} %collective-permute-done.3.refs_0_, bf16[1024,256]{1,0:T(8,128)(2,1)S(1)} %collective-permute-done.13.refs_1_, ...), custom_call_target="tpu_custom_call" | custom-call | flops 5368709120 | bytes 4194304 | tf_op jit(solution)/shard_map/pallas_call | solution.py:488
  77.1 2.4 %shard_map.86 = (bf16[4,128,512]{2,1,0:T(8,128)(2,1)S(1)}, f32[4,128,512]{2,1,0:T(8,128)S(1)}) custom-call(s32[12]{0:T(128)S(1)} %concatenate.3.info, bf16[256,1024]{1,0:T(8,128)(2,1)} %bitcast.5.refs_0_, bf16[256,1024]{1,0:T(8,128)(2,1)S(1)} %collective-permute-done.refs_0_.refs_1_, bf16[256,1024]{1,0:T(8,128)(2,1)S(1)} %collective-permute-done.2.refs_0_.refs_2_, ...), custom_call_target="tpu_custom_call" | custom-call | flops 1048576 | bytes 1048576 | tf_op jit(solution)/shard_map/pallas_call | solution.py:481
  79.5 2.7 %collective-permute-start.18 = (bf16[4,128,512]{2,1,0:T(8,128)(2,1)S(1)}, bf16[4,128,512]{2,1,0:T(8,128)(2,1)S(1)}, u32[]{:S(2)}, u32[]{:S(2)}) collective-permute-start(bf16[4,128,512]{2,1,0:T(8,128)(2,1)S(1)} %get-tuple-element.116), channel_id=1, source_target_pairs={{0,16},{16,0},{1,17},{17,1},{2,18},{18,2},{3,19},{19,3},{4,20},{20... | collective-permute-start | bytes 1572872 | tf_op jit(solution)/shard_map/ppermute | solution.py:415
  82.3 3.0 %shard_map.87 = (f32[256,1024]{1,0:T(8,128)S(1)}, bf16[256,1024]{1,0:T(8,128)(2,1)}, bf16[256,1024]{1,0:T(8,128)(2,1)S(1)}, bf16[256,1024]{1,0:T(8,128)(2,1)S(1)}) custom-call(s32[12]{0:T(128)S(1)} %concatenate.3.info, bf16[256,1024]{1,0:T(8,128)(2,1)S(1)} %get-tuple-element.105.refs_4_.refs_0_, bf16[256,1024]{1,0:T(8,128)(2,1)S(1)} %get-tuple-element.106.refs_5_.refs_1_, ...), custom_call_target="tpu_custom_call" | custom-call | flops 1048576 | bytes 1048576 | tf_op jit(solution)/shard_map/pallas_call | solution.py:492
  89.5 7.3 %all-to-all-start = ((bf16[16,32,1280]{2,1,0:T(8,128)(2,1)}), bf16[16,32,1280]{2,1,0:T(8,128)(2,1)S(1)}, u32[]{:S(2)}, u32[]{:S(2)}) async-start(bf16[16,32,1280]{2,1,0:T(8,128)(2,1)} %bitcast.7), calls=%async_computation | async-start | bytes 2621440 | tf_op jit(solution)/shard_map/all_to_all | solution.py:501
  98.6 2.5 %collective-permute-start.21 = (bf16[256,1024]{1,0:T(8,128)(2,1)}, bf16[256,1024]{1,0:T(8,128)(2,1)S(1)}, u32[]{:S(2)}, u32[]{:S(2)}) collective-permute-start(bf16[256,1024]{1,0:T(8,128)(2,1)} %copy-done.5), channel_id=1, source_target_pairs={{0,2},{1,3},{2,0},{3,1},{4,6},{5,7},{6,4},{7,5},{8,10},{9,11},{10,... | collective-permute-start | bytes 1572872 | tf_op jit(solution)/shard_map/ppermute | solution.py:411
  101.1 2.5 %collective-permute-start.22 = (bf16[256,1024]{1,0:T(8,128)(2,1)}, bf16[256,1024]{1,0:T(8,128)(2,1)}, u32[]{:S(2)}, u32[]{:S(2)}) collective-permute-start(bf16[256,1024]{1,0:T(8,128)(2,1)} %copy-done.4), channel_id=1, source_target_pairs={{0,3},{1,0},{2,1},{3,2},{4,7},{5,4},{6,5},{7,6},{8,11},{9,8},{10,9... | collective-permute-start | bytes 1572872 | tf_op jit(solution)/shard_map/ppermute | solution.py:411
  103.6 14.3 %all-to-all-done.got = bf16[16,32,1280]{2,1,0:T(8,128)(2,1)S(1)} async-done(((bf16[16,32,1280]{2,1,0:T(8,128)(2,1)}), bf16[16,32,1280]{2,1,0:T(8,128)(2,1)S(1)}, u32[]{:S(2)}, u32[]{:S(2)}) %all-to-all-start) | async-done | bytes 1310752 | tf_op jit(solution)/shard_map/all_to_all | solution.py:501
  118.7 5.4 %all-to-all-start.1 = ((bf16[4,8,1280]{2,1,0:T(8,128)(2,1)}), bf16[4,8,1280]{2,1,0:T(8,128)(2,1)S(1)}, u32[]{:S(2)}, u32[]{:S(2)}) async-start(bf16[4,8,1280]{2,1,0:T(8,128)(2,1)} %bitcast.9), calls=%async_computation.1 | async-start | bytes 163840 | tf_op jit(solution)/shard_map/all_to_all | solution.py:507
  126.6 3.1 %all-to-all-done.1.got = bf16[4,8,1280]{2,1,0:T(8,128)(2,1)S(1)} async-done(((bf16[4,8,1280]{2,1,0:T(8,128)(2,1)}), bf16[4,8,1280]{2,1,0:T(8,128)(2,1)S(1)}, u32[]{:S(2)}, u32[]{:S(2)}) %all-to-all-start.1) | async-done | bytes 81952 | tf_op jit(solution)/shard_map/all_to_all | solution.py:507
  (56 shorter events, 28.9 us)
Async XLA Ops:
  0.6 15.7 %collective-permute-start = (bf16[256,1024]{1,0:T(8,128)(2,1)}, bf16[256,1024]{1,0:T(8,128)(2,1)S(1)}, u32[]{:S(2)}, u32[]{:S(2)}) collective-permute-start(bf16[256,1024]{1,0:T(8,128)(2,1)} %bitcast.5.refs_0_), channel_id=1, source_target_pairs={{0,3},{1,0},{2,1},{3,2},{4,7},{5,4},{6,5},{7,6},{8,11},{9,8},{10,9... | collective-permute-start | bytes 1572872 | tf_op jit(solution)/shard_map/ppermute | solution.py:411
  4.8 14.8 %collective-permute-start.1 = (bf16[256,1024]{1,0:T(8,128)(2,1)}, bf16[256,1024]{1,0:T(8,128)(2,1)S(1)}, u32[]{:S(2)}, u32[]{:S(2)}) collective-permute-start(bf16[256,1024]{1,0:T(8,128)(2,1)} %bitcast.5.refs_0_), channel_id=1, source_target_pairs={{0,1},{1,2},{2,3},{3,0},{4,5},{5,6},{6,7},{7,4},{8,9},{9,10},{10,1... | collective-permute-start | bytes 1572872 | tf_op jit(solution)/shard_map/ppermute | solution.py:411
  19.6 16.6 %collective-permute-start.2 = (bf16[256,1024]{1,0:T(8,128)(2,1)}, bf16[256,1024]{1,0:T(8,128)(2,1)S(1)}, u32[]{:S(2)}, u32[]{:S(2)}) collective-permute-start(bf16[256,1024]{1,0:T(8,128)(2,1)} %bitcast.5.refs_0_), channel_id=1, source_target_pairs={{0,2},{1,3},{2,0},{3,1},{4,6},{5,7},{6,4},{7,5},{8,10},{9,11},{10,... | collective-permute-start | bytes 1572872 | tf_op jit(solution)/shard_map/ppermute | solution.py:411
  19.6 18.5 %collective-permute-start.7 = (bf16[256,512]{1,0:T(8,128)(2,1)S(1)}, bf16[256,512]{1,0:T(8,128)(2,1)S(1)}, u32[]{:S(2)}, u32[]{:S(2)}) collective-permute-start(bf16[256,512]{1,0:T(8,128)(2,1)S(1)} %get-tuple-element.65.refs_3_), channel_id=1, source_target_pairs={{0,4},{4,8},{8,12},{12,0},{1,5},{5,9},{9,13},{13,1},{2,6},{6,10},{... | collective-permute-start | bytes 786440 | tf_op jit(solution)/shard_map/ppermute | solution.py:411
  23.7 21.4 %collective-permute-start.8 = (bf16[512,512]{1,0:T(8,128)(2,1)S(1)}, bf16[512,512]{1,0:T(8,128)(2,1)S(1)}, u32[]{:S(2)}, u32[]{:S(2)}) collective-permute-start(bf16[512,512]{1,0:T(8,128)(2,1)S(1)} %get-tuple-element.71.refs_4_), channel_id=1, source_target_pairs={{0,4},{4,8},{8,12},{12,0},{1,5},{5,9},{9,13},{13,1},{2,6},{6,10},{... | collective-permute-start | bytes 1572872 | tf_op jit(solution)/shard_map/ppermute | solution.py:411
  26.7 18.2 %collective-permute-start.4 = (bf16[256,512]{1,0:T(8,128)(2,1)S(1)}, bf16[256,512]{1,0:T(8,128)(2,1)S(1)}, u32[]{:S(2)}, u32[]{:S(2)}) collective-permute-start(bf16[256,512]{1,0:T(8,128)(2,1)S(1)} %get-tuple-element.80), channel_id=1, source_target_pairs={{0,1},{1,2},{2,3},{3,0},{4,5},{5,6},{6,7},{7,4},{8,9},{9,10},{10,1... | collective-permute-start | bytes 786440 | tf_op jit(solution)/shard_map/ppermute | solution.py:411
  27.9 17.2 %collective-permute-start.5 = (bf16[256,512]{1,0:T(8,128)(2,1)S(1)}, bf16[256,512]{1,0:T(8,128)(2,1)S(1)}, u32[]{:S(2)}, u32[]{:S(2)}) collective-permute-start(bf16[256,512]{1,0:T(8,128)(2,1)S(1)} %get-tuple-element.81), channel_id=1, source_target_pairs={{0,2},{1,3},{2,0},{3,1},{4,6},{5,7},{6,4},{7,5},{8,10},{9,11},{10,... | collective-permute-start | bytes 786440 | tf_op jit(solution)/shard_map/ppermute | solution.py:411
  36.2 8.9 %collective-permute-start.6 = (bf16[256,512]{1,0:T(8,128)(2,1)S(1)}, bf16[256,512]{1,0:T(8,128)(2,1)S(1)}, u32[]{:S(2)}, u32[]{:S(2)}) collective-permute-start(bf16[256,512]{1,0:T(8,128)(2,1)S(1)} %get-tuple-element.82), channel_id=1, source_target_pairs={{0,3},{1,0},{2,1},{3,2},{4,7},{5,4},{6,5},{7,6},{8,11},{9,8},{10,9... | collective-permute-start | bytes 786440 | tf_op jit(solution)/shard_map/ppermute | solution.py:411
  38.2 7.7 %collective-permute-start.9 = (bf16[256,512]{1,0:T(8,128)(2,1)S(1)}, bf16[256,512]{1,0:T(8,128)(2,1)S(1)}, u32[]{:S(2)}, u32[]{:S(2)}) collective-permute-start(bf16[256,512]{1,0:T(8,128)(2,1)S(1)} %get-tuple-element.72.refs_5_), channel_id=1, source_target_pairs={{0,4},{4,8},{8,12},{12,0},{1,5},{5,9},{9,13},{13,1},{2,6},{6,10},{... | collective-permute-start | bytes 786440 | tf_op jit(solution)/shard_map/ppermute | solution.py:411
  47.5 7.4 %collective-permute-start.10 = (f32[8,1024]{1,0:T(8,128)S(1)}, f32[8,1024]{1,0:T(8,128)S(1)}, u32[]{:S(2)}, u32[]{:S(2)}) collective-permute-start(f32[8,1024]{1,0:T(8,128)S(1)} %get-tuple-element.89.refs_3_), channel_id=1, source_target_pairs={{0,3},{1,0},{2,1},{3,2},{4,7},{5,4},{6,5},{7,6},{8,11},{9,8},{10,9... | collective-permute-start | bytes 98312 | tf_op jit(solution)/shard_map/ppermute | solution.py:411
  48.2 6.7 %collective-permute-start.11 = (f32[8,1024]{1,0:T(8,128)S(1)}, f32[8,1024]{1,0:T(8,128)S(1)}, u32[]{:S(2)}, u32[]{:S(2)}) collective-permute-start(f32[8,1024]{1,0:T(8,128)S(1)} %get-tuple-element.89.refs_3_), channel_id=1, source_target_pairs={{0,2},{1,3},{2,0},{3,1},{4,6},{5,7},{6,4},{7,5},{8,10},{9,11},{10,... | collective-permute-start | bytes 98312 | tf_op jit(solution)/shard_map/ppermute | solution.py:411
  51.3 5.1 %collective-permute-start.12 = (f32[8,1024]{1,0:T(8,128)S(1)}, f32[8,1024]{1,0:T(8,128)S(1)}, u32[]{:S(2)}, u32[]{:S(2)}) collective-permute-start(f32[8,1024]{1,0:T(8,128)S(1)} %get-tuple-element.89.refs_3_), channel_id=1, source_target_pairs={{0,1},{1,2},{2,3},{3,0},{4,5},{5,6},{6,7},{7,4},{8,9},{9,10},{10,1... | collective-permute-start | bytes 98312 | tf_op jit(solution)/shard_map/ppermute | solution.py:411
  51.3 23.1 %collective-permute-start.3 = (bf16[1024,256]{1,0:T(8,128)(2,1)S(1)}, bf16[1024,256]{1,0:T(8,128)(2,1)S(1)}, u32[]{:S(2)}, u32[]{:S(2)}) collective-permute-start(bf16[1024,256]{1,0:T(8,128)(2,1)S(1)} %get-tuple-element.73.refs_0_), channel_id=1, source_target_pairs={{0,12},{4,0},{8,4},{12,8},{1,13},{5,1},{9,5},{13,9},{2,14},{6,2},{... | collective-permute-start | bytes 1572872 | tf_op jit(solution)/shard_map/ppermute | solution.py:411
  58.1 16.6 %collective-permute-start.13 = (bf16[1024,256]{1,0:T(8,128)(2,1)S(1)}, bf16[1024,256]{1,0:T(8,128)(2,1)S(1)}, u32[]{:S(2)}, u32[]{:S(2)}) collective-permute-start(bf16[1024,256]{1,0:T(8,128)(2,1)S(1)} %get-tuple-element.94.refs_1_), channel_id=1, source_target_pairs={{0,12},{4,0},{8,4},{12,8},{1,13},{5,1},{9,5},{13,9},{2,14},{6,2},{... | collective-permute-start | bytes 1572872 | tf_op jit(solution)/shard_map/ppermute | solution.py:411
  61.7 23.5 %collective-permute-start.14 = (bf16[1024,256]{1,0:T(8,128)(2,1)S(1)}, bf16[1024,256]{1,0:T(8,128)(2,1)S(1)}, u32[]{:S(2)}, u32[]{:S(2)}) collective-permute-start(bf16[1024,256]{1,0:T(8,128)(2,1)S(1)} %get-tuple-element.112.refs_0_), channel_id=1, source_target_pairs={{0,3},{1,0},{2,1},{3,2},{4,7},{5,4},{6,5},{7,6},{8,11},{9,8},{10,9... | collective-permute-start | bytes 1572872 | tf_op jit(solution)/shard_map/ppermute | solution.py:411
  62.0 23.3 %collective-permute-start.15 = (bf16[1024,256]{1,0:T(8,128)(2,1)S(1)}, bf16[1024,256]{1,0:T(8,128)(2,1)S(1)}, u32[]{:S(2)}, u32[]{:S(2)}) collective-permute-start(bf16[1024,256]{1,0:T(8,128)(2,1)S(1)} %get-tuple-element.112.refs_0_), channel_id=1, source_target_pairs={{0,2},{1,3},{2,0},{3,1},{4,6},{5,7},{6,4},{7,5},{8,10},{9,11},{10,... | collective-permute-start | bytes 1572872 | tf_op jit(solution)/shard_map/ppermute | solution.py:411
  62.9 22.3 %collective-permute-start.16 = (bf16[1024,256]{1,0:T(8,128)(2,1)S(1)}, bf16[1024,256]{1,0:T(8,128)(2,1)S(1)}, u32[]{:S(2)}, u32[]{:S(2)}) collective-permute-start(bf16[1024,256]{1,0:T(8,128)(2,1)S(1)} %get-tuple-element.112.refs_0_), channel_id=1, source_target_pairs={{0,1},{1,2},{2,3},{3,0},{4,5},{5,6},{6,7},{7,4},{8,9},{9,10},{10,1... | collective-permute-start | bytes 1572872 | tf_op jit(solution)/shard_map/ppermute | solution.py:411
  74.4 12.2 %collective-permute-start.17 = (bf16[4,128,512]{2,1,0:T(8,128)(2,1)S(1)}, bf16[4,128,512]{2,1,0:T(8,128)(2,1)S(1)}, u32[]{:S(2)}, u32[]{:S(2)}) collective-permute-start(bf16[4,128,512]{2,1,0:T(8,128)(2,1)S(1)} %get-tuple-element.115), channel_id=1, source_target_pairs={{0,16},{16,0},{1,17},{17,1},{2,18},{18,2},{3,19},{19,3},{4,20},{20... | collective-permute-start | bytes 1572872 | tf_op jit(solution)/shard_map/ppermute | solution.py:415
  79.5 8.6 %collective-permute-start.18 = (bf16[4,128,512]{2,1,0:T(8,128)(2,1)S(1)}, bf16[4,128,512]{2,1,0:T(8,128)(2,1)S(1)}, u32[]{:S(2)}, u32[]{:S(2)}) collective-permute-start(bf16[4,128,512]{2,1,0:T(8,128)(2,1)S(1)} %get-tuple-element.116), channel_id=1, source_target_pairs={{0,16},{16,0},{1,17},{17,1},{2,18},{18,2},{3,19},{19,3},{4,20},{20... | collective-permute-start | bytes 1572872 | tf_op jit(solution)/shard_map/ppermute | solution.py:415
  89.5 28.4 %all-to-all-start = ((bf16[16,32,1280]{2,1,0:T(8,128)(2,1)}), bf16[16,32,1280]{2,1,0:T(8,128)(2,1)S(1)}, u32[]{:S(2)}, u32[]{:S(2)}) async-start(bf16[16,32,1280]{2,1,0:T(8,128)(2,1)} %bitcast.7), calls=%async_computation | async-start | bytes 2621440 | tf_op jit(solution)/shard_map/all_to_all | solution.py:501
  96.8 27.3 %collective-permute-start.20 = (bf16[256,1024]{1,0:T(8,128)(2,1)}, bf16[256,1024]{1,0:T(8,128)(2,1)S(1)}, u32[]{:S(2)}, u32[]{:S(2)}) collective-permute-start(bf16[256,1024]{1,0:T(8,128)(2,1)} %get-tuple-element.120), channel_id=1, source_target_pairs={{0,1},{1,2},{2,3},{3,0},{4,5},{5,6},{6,7},{7,4},{8,9},{9,10},{10,1... | collective-permute-start | bytes 1572872 | tf_op jit(solution)/shard_map/ppermute | solution.py:411
  98.6 25.8 %collective-permute-start.21 = (bf16[256,1024]{1,0:T(8,128)(2,1)}, bf16[256,1024]{1,0:T(8,128)(2,1)S(1)}, u32[]{:S(2)}, u32[]{:S(2)}) collective-permute-start(bf16[256,1024]{1,0:T(8,128)(2,1)} %copy-done.5), channel_id=1, source_target_pairs={{0,2},{1,3},{2,0},{3,1},{4,6},{5,7},{6,4},{7,5},{8,10},{9,11},{10,... | collective-permute-start | bytes 1572872 | tf_op jit(solution)/shard_map/ppermute | solution.py:411
  101.1 23.5 %collective-permute-start.22 = (bf16[256,1024]{1,0:T(8,128)(2,1)}, bf16[256,1024]{1,0:T(8,128)(2,1)}, u32[]{:S(2)}, u32[]{:S(2)}) collective-permute-start(bf16[256,1024]{1,0:T(8,128)(2,1)} %copy-done.4), channel_id=1, source_target_pairs={{0,3},{1,0},{2,1},{3,2},{4,7},{5,4},{6,5},{7,6},{8,11},{9,8},{10,9... | collective-permute-start | bytes 1572872 | tf_op jit(solution)/shard_map/ppermute | solution.py:411
  118.7 11.1 %all-to-all-start.1 = ((bf16[4,8,1280]{2,1,0:T(8,128)(2,1)}), bf16[4,8,1280]{2,1,0:T(8,128)(2,1)S(1)}, u32[]{:S(2)}, u32[]{:S(2)}) async-start(bf16[4,8,1280]{2,1,0:T(8,128)(2,1)} %bitcast.9), calls=%async_computation.1 | async-start | bytes 163840 | tf_op jit(solution)/shard_map/all_to_all | solution.py:507
  (7 other events, 37.4 us)

commit v16 on v15

--- a/solution.py
+++ b/solution.py
@@ -231,23 +231,30 @@
     keep[x, :, lanes] = jnp.where(first, total[:128], total[128:])
 
 
-def early_weights_body(info, *refs):
-    ev, (gp_g, gp_q, send, keep) = refs[0:4], refs[4:8]
+def transpose_body(*refs):
+    ev, out = refs[0:4], refs[4]
+    for k in range(NB):
+        out[:, k * BLK : (k + 1) * BLK] = ev[k][...].T
+
+
+def early_weights_body(info, et, gp_g, gp_q, send, keep):
     for lanes, gp in ((slice(0, BLK), gp_g), (slice(BLK, 2 * BLK), gp_q)):
         for x in range(4):
             part = [
-                tn(ev[k][:, x * BLK : (x + 1) * BLK], gp[rows(lax.rem(info[9] + k, NB)), :]) for k in range(NB)
+                nn(et[x * BLK : (x + 1) * BLK, k * BLK : (k + 1) * BLK], gp[rows(lax.rem(info[9] + k, NB)), :])
+                for k in range(NB)
             ]
             pack(info, x, part[0] + part[1] + part[2] + part[3], lanes, send, keep)
 
 
 def late_weights_body(info, *refs):
-    ev, gp = refs[0:4], refs[4:8]
-    send, keep = refs[8:10]
+    et, gp, (send, keep) = refs[0], refs[1:5], refs[5:7]
     for n in range(2):
         lanes, cols = slice(n * BLK, (n + 1) * BLK), slice((n + 2) * BLK, (n + 3) * BLK)
         for x in range(4):
-            part = [tn(ev[k][:, x * BLK : (x + 1) * BLK], gp[k][:, cols]) for k in range(NB)]
+            part = [
+                nn(et[x * BLK : (x + 1) * BLK, k * BLK : (k + 1) * BLK], gp[k][:, cols]) for k in range(NB)
+            ]
             pack(info, x, part[0] + part[1] + part[2] + part[3], lanes, send, keep)
 
 
@@ -463,6 +470,9 @@
         forward_local_body, (bf16((GRP, BLK)), bf16((GRP, 2 * BLK)), f32((GRP, BLK))), 6, 5 << 30, 4 << 20
     )(info, *qs, *kvs)
     q_next = along(q, "y", -1)
+    *evs, att = lax.optimization_barrier((*evs, att))
+    et = call(transpose_body, bf16((D, GRP)), 4, 1 << 20, 1 << 20, scalars=0)(*evs)
+    att, et = lax.optimization_barrier((att, et))
     att, kv_prev, gg, cot_z, gate, stats = call(
         forward_halo_body,
         (f32((GRP, BLK)), bf16((GRP, 2 * BLK))) + (bf16((GRP, BLK)),) * 3 + (f32((8, GRP)),),
@@ -483,12 +493,12 @@
         )(info, *operands)
         return swap(send), keep
 
-    got_1, keep_1 = weights(early_weights_body, 512, (*evs, gp_g, gp_q))
+    got_1, keep_1 = weights(early_weights_body, 512, (et, gp_g, gp_q))
     q_next, g_next, keep_1 = lax.optimization_barrier((q_next, g_next, keep_1))
     gp = call(
         backward_later_body, (bf16((BLK, 4 * BLK)),) * 4, 10, 5 << 30, 4 << 20, [pltpu.VMEM((GRP, 2 * BLK), F32)]
     )(info, q_next, g_next, kv, dkv, gp_g, gp_q, *dsigs)
-    got_2, keep_2 = weights(late_weights_body, 512, (*evs, *gp))
+    got_2, keep_2 = weights(late_weights_body, 512, (et, *gp))
     *partial, = call(
         input_body, (f32((BLK, D)),) + (bf16((BLK, D)),) * 3, 6, 1 << 20, 1 << 20
     )(info, *gp, w_in, cot)

time: 131 us -> 129 us (0.985)
  waiting for transfers between devices: 36.5 us -> 40 us
  starting transfers between devices: 48.5 us -> 45.1 us
  Pallas kernels: 40.6 us -> 37.5 us
    ppermute x20, waiting for transfers between devices: 17.5 us -> 20.4 us  [along(): return lax.ppermute(x, axis, [(i, (i + d) % 4) for i in range(4)])]
    ppermute x3, starting transfers between devices: 2.92 us -> 0.26 us  [swap(): return lax.ppermute(x, 'c', [(0, 1), (1, 0)])]
    pallas_call x1, Pallas kernels: 8.18 us -> 6.75 us  [body(): call(backward_local_body, (bf16((GRP, BLK)), f32((GRP, 2 * BLK))), 8, 1 <...]
    unnamed x12 -> x16, local copies, waits for them, and re-layouts: 3.4 us -> 4.45 us
  transfers between devices with their start and end apart: 25 -> 25, of which waited for: 12 -> 12; matrix products, arithmetic and copies ran while one was open for 1% -> 1% of each run, Pallas kernels for 28% -> 26%
where the time goes in v16:
time: 129 us
  starting transfers between devices  45.1 us (35%)
  waiting for transfers between devices  40 us (31%)
  Pallas kernels  37.5 us (29%)
  local copies, waits for them, and re-layouts  5.18 us (4%)
    ppermute x20, starting transfers between devices, along(): return lax.ppermute(x, axis, [(i, (i + d) % 4) for i in range(4)])  32.2 us
    ppermute x20, waiting for transfers between devices, along(): return lax.ppermute(x, axis, [(i, (i + d) % 4) for i in range(4)])  20.4 us
    all_to_all x1, waiting for transfers between devices, body(): sums = lax.all_to_all(mine.reshape(16, 32, 5 * BLK), ('x', 'y'), 0, 0)  14.6 us
    all_to_all x1, starting transfers between devices, body(): sums = lax.all_to_all(mine.reshape(16, 32, 5 * BLK), ('x', 'y'), 0, 0)  7.34 us
    pallas_call x1, Pallas kernels, body(): call(backward_local_body, (bf16((GRP, BLK)), f32((GRP, 2 * BLK))), 8, 1 <...  6.75 us
    pallas_call x3, Pallas kernels, body(): call(project_body, (bf16((n * BLK, 2 * BLK)), bf16((n * BLK, BLK)), bf16(...  5.55 us
    all_to_all x1, starting transfers between devices, body(): got = lax.all_to_all(total.reshape(4, 8, 5 * BLK), 'z', 0, 0)  5.38 us
    pallas_call x3, Pallas kernels, weights(): call(kernel, (bf16((4, 128, cols)), f32((4, 128, cols))), len(operands),...  4.91 us
  transfers between devices with their start and end apart: 25, of which 12 were waited for; matrix products, arithmetic and copies ran while one was open for 1% of the time, Pallas kernels for 26%

profile of v16, /device:TPU:0, one launch (start us, length us, event | category | flops | bytes accessed | tf_op | source)
XLA Modules:
  0.0 128.7 jit_solution(12033494913820804635)
XLA Ops:
  0.6 4.2 %collective-permute-start = (bf16[256,1024]{1,0:T(8,128)(2,1)}, bf16[256,1024]{1,0:T(8,128)(2,1)S(1)}, u32[]{:S(2)}, u32[]{:S(2)}) collective-permute-start(bf16[256,1024]{1,0:T(8,128)(2,1)} %bitcast.12), channel_id=1, source_target_pairs={{0,3},{1,0},{2,1},{3,2},{4,7},{5,4},{6,5},{7,6},{8,11},{9,8},{10,9... | collective-permute-start | bytes 1572872 | tf_op jit(solution)/shard_map/ppermute | solution.py:418
  5.6 3.4 %copy-done = bf16[1024,4096]{1,0:T(8,128)(2,1)S(1)} copy-done((bf16[1024,4096]{1,0:T(8,128)(2,1)S(1)}, bf16[1024,4096]{1,0:T(8,128)(2,1)}, u32[]{:S(2)}) %copy-start) | copy-done | bytes 8388632
  11.5 4.8 %collective-permute-done.refs_0_.refs_1_ = bf16[256,1024]{1,0:T(8,128)(2,1)S(1)} collective-permute-done((bf16[256,1024]{1,0:T(8,128)(2,1)}, bf16[256,1024]{1,0:T(8,128)(2,1)S(1)}, u32[]{:S(2)}, u32[]{:S(2)}) %collective-permute-start) | collective-permute-done | bytes 524320 | tf_op jit(solution)/shard_map/ppermute | solution.py:418
  16.3 3.3 %collective-permute-done.1.refs_1_.refs_3_ = bf16[256,1024]{1,0:T(8,128)(2,1)S(1)} collective-permute-done((bf16[256,1024]{1,0:T(8,128)(2,1)}, bf16[256,1024]{1,0:T(8,128)(2,1)S(1)}, u32[]{:S(2)}, u32[]{:S(2)}) %collective-permute-start.1) | collective-permute-done | bytes 524320 | tf_op jit(solution)/shard_map/ppermute | solution.py:418
  21.3 2.4 %shard_map.77 = (bf16[512,512]{1,0:T(8,128)(2,1)S(1)}, bf16[512,256]{1,0:T(8,128)(2,1)S(1)}, bf16[512,256]{1,0:T(8,128)(2,1)S(1)}, bf16[256,1024]{1,0:T(8,128)(2,1)S(1)}, bf16[256,1024]{1,0:T(8,128)(2,1)S(1)}) custom-call(s32[12]{0:T(128)S(1)} %concatenate.3.info, bf16[256,1024]{1,0:T(8,128)(2,1)S(1)} %collective-permute-done.refs_0_.refs_1_, ...), custom_call_target="tpu_custom_call" | custom-call | flops 1048576 | bytes 1048576 | tf_op jit(solution)/shard_map/pallas_call | solution.py:455
  27.9 2.4 %collective-permute-start.5 = (bf16[256,512]{1,0:T(8,128)(2,1)S(1)}, bf16[256,512]{1,0:T(8,128)(2,1)S(1)}, u32[]{:S(2)}, u32[]{:S(2)}) collective-permute-start(bf16[256,512]{1,0:T(8,128)(2,1)S(1)} %get-tuple-element.94), channel_id=1, source_target_pairs={{0,2},{1,3},{2,0},{3,1},{4,6},{5,7},{6,4},{7,5},{8,10},{9,11},{10,... | collective-permute-start | bytes 786440 | tf_op jit(solution)/shard_map/ppermute | solution.py:418
  30.3 5.7 %collective-permute-done.2.refs_0_.refs_2_ = bf16[256,1024]{1,0:T(8,128)(2,1)S(1)} collective-permute-done((bf16[256,1024]{1,0:T(8,128)(2,1)S(1)}, bf16[256,1024]{1,0:T(8,128)(2,1)S(1)}, u32[]{:S(2)}, u32[]{:S(2)}) %collective-permute-start.2) | collective-permute-done | bytes 524320 | tf_op jit(solution)/shard_map/ppermute | solution.py:418
  39.6 4.2 %shard_map.79 = (bf16[1024,256]{1,0:T(8,128)(2,1)S(1)}, bf16[1024,512]{1,0:T(8,128)(2,1)S(1)}, f32[1024,256]{1,0:T(8,128)S(1)}) custom-call(s32[12]{0:T(128)S(1)} %concatenate.3.info, bf16[256,256]{1,0:T(8,128)(2,1)S(1)} %get-tuple-element.71.refs_0_, bf16[512,256]{1,0:T(8,128)(2,1)S(1)} %get-tuple-element.75.refs_1_, ...), custom_call_target="tpu_custom_call" | custom-call | flops 5368709120 | bytes 4194304 | tf_op jit(solution)/shard_map/pallas_call | solution.py:469
  48.2 2.9 %collective-permute-start.11 = (f32[8,1024]{1,0:T(8,128)S(1)}, f32[8,1024]{1,0:T(8,128)S(1)}, u32[]{:S(2)}, u32[]{:S(2)}) collective-permute-start(f32[8,1024]{1,0:T(8,128)S(1)} %get-tuple-element.102.refs_3_), channel_id=1, source_target_pairs={{0,2},{1,3},{2,0},{3,1},{4,6},{5,7},{6,4},{7,5},{8,10},{9,11},{10,... | collective-permute-start | bytes 98312 | tf_op jit(solution)/shard_map/ppermute | solution.py:418
  51.1 3.1 %collective-permute-start.3 = (bf16[1024,256]{1,0:T(8,128)(2,1)S(1)}, bf16[1024,256]{1,0:T(8,128)(2,1)S(1)}, u32[]{:S(2)}, u32[]{:S(2)}) collective-permute-start(bf16[1024,256]{1,0:T(8,128)(2,1)S(1)} %get-tuple-element.80.refs_0_), channel_id=1, source_target_pairs={{0,12},{4,0},{8,4},{12,8},{1,13},{5,1},{9,5},{13,9},{2,14},{6,2},{... | collective-permute-start | bytes 1572872 | tf_op jit(solution)/shard_map/ppermute | solution.py:418
  54.2 2.0 %collective-permute-done.12.refs_6_ = f32[8,1024]{1,0:T(8,128)S(1)} collective-permute-done((f32[8,1024]{1,0:T(8,128)S(1)}, f32[8,1024]{1,0:T(8,128)S(1)}, u32[]{:S(2)}, u32[]{:S(2)}) %collective-permute-start.12) | collective-permute-done | bytes 32800 | tf_op jit(solution)/shard_map/ppermute | solution.py:418
  57.9 3.3 %collective-permute-start.13 = (bf16[1024,256]{1,0:T(8,128)(2,1)S(1)}, bf16[1024,256]{1,0:T(8,128)(2,1)S(1)}, u32[]{:S(2)}, u32[]{:S(2)}) collective-permute-start(bf16[1024,256]{1,0:T(8,128)(2,1)S(1)} %get-tuple-element.107.refs_1_), channel_id=1, source_target_pairs={{0,12},{4,0},{8,4},{12,8},{1,13},{5,1},{9,5},{13,9},{2,14},{6,2},{... | collective-permute-start | bytes 1572872 | tf_op jit(solution)/shard_map/ppermute | solution.py:418
  63.3 6.8 %shard_map.84 = (bf16[1024,256]{1,0:T(8,128)(2,1)S(1)}, f32[1024,512]{1,0:T(8,128)S(1)}) custom-call(s32[12]{0:T(128)S(1)} %concatenate.3.info, bf16[1024,256]{1,0:T(8,128)(2,1)S(1)} %get-tuple-element.80.refs_0_, bf16[1024,256]{1,0:T(8,128)(2,1)S(1)} %get-tuple-element.107.refs_1_, bf16[1024,512]{1,0:T(8,128)(2,1)S(1)} %get-tuple-element.110.refs_2_, ...), custom_call_target="tpu_custom_call" | custom-call | flops 1048576 | bytes 1048576 | tf_op jit(solution)/shard_map/pallas_call | solution.py:486
  70.0 1.8 %shard_map.85 = (bf16[4,128,512]{2,1,0:T(8,128)(2,1)S(1)}, f32[4,128,512]{2,1,0:T(8,128)S(1)}) custom-call(s32[12]{0:T(128)S(1)} %concatenate.3.info, bf16[1024,1024]{1,0:T(8,128)(2,1)S(1)} %shard_map.80.et.refs_0_, bf16[1024,256]{1,0:T(8,128)(2,1)S(1)} %get-tuple-element.109.gp_g.refs_4_, bf16[1024,256]{1,0:T(8,128)(2,1)S(1)} %get-tuple-element.112.gp_q.refs_5_), custom_call_target="tpu_custom_call" | custom-call | flops 1048576 | bytes 1048576 | tf_op jit(solution)/shard_map/pallas_call | solution.py:491
  72.0 2.8 %collective-permute-done.13.refs_1_ = bf16[1024,256]{1,0:T(8,128)(2,1)S(1)} collective-permute-done((bf16[1024,256]{1,0:T(8,128)(2,1)S(1)}, bf16[1024,256]{1,0:T(8,128)(2,1)S(1)}, u32[]{:S(2)}, u32[]{:S(2)}) %collective-permute-start.13) | collective-permute-done | bytes 524320 | tf_op jit(solution)/shard_map/ppermute | solution.py:418
  74.7 2.9 %shard_map.86 = (bf16[256,1024]{1,0:T(8,128)(2,1)S(1)}, bf16[256,1024]{1,0:T(8,128)(2,1)S(1)}, bf16[256,1024]{1,0:T(8,128)(2,1)S(1)}, bf16[256,1024]{1,0:T(8,128)(2,1)S(1)}) custom-call(s32[12]{0:T(128)S(1)} %concatenate.3.info, bf16[1024,256]{1,0:T(8,128)(2,1)S(1)} %collective-permute-done.3.refs_0_, bf16[1024,256]{1,0:T(8,128)(2,1)S(1)} %collective-permute-done.13.refs_1_, ...), custom_call_target="tpu_custom_call" | custom-call | flops 5368709120 | bytes 4194304 | tf_op jit(solution)/shard_map/pallas_call | solution.py:498
  79.6 3.0 %shard_map.88 = (f32[256,1024]{1,0:T(8,128)S(1)}, bf16[256,1024]{1,0:T(8,128)(2,1)}, bf16[256,1024]{1,0:T(8,128)(2,1)S(1)}, bf16[256,1024]{1,0:T(8,128)(2,1)S(1)}) custom-call(s32[12]{0:T(128)S(1)} %concatenate.3.info, bf16[256,1024]{1,0:T(8,128)(2,1)S(1)} %get-tuple-element.119.refs_1_.refs_0_, bf16[256,1024]{1,0:T(8,128)(2,1)S(1)} %get-tuple-element.120.refs_2_.refs_1_, ...), custom_call_target="tpu_custom_call" | custom-call | flops 1048576 | bytes 1048576 | tf_op jit(solution)/shard_map/pallas_call | solution.py:502
  87.3 7.3 %all-to-all-start = ((bf16[16,32,1280]{2,1,0:T(8,128)(2,1)}), bf16[16,32,1280]{2,1,0:T(8,128)(2,1)S(1)}, u32[]{:S(2)}, u32[]{:S(2)}) async-start(bf16[16,32,1280]{2,1,0:T(8,128)(2,1)} %bitcast.7), calls=%async_computation | async-start | bytes 2621440 | tf_op jit(solution)/shard_map/all_to_all | solution.py:511
  96.5 2.5 %collective-permute-start.21 = (bf16[256,1024]{1,0:T(8,128)(2,1)}, bf16[256,1024]{1,0:T(8,128)(2,1)S(1)}, u32[]{:S(2)}, u32[]{:S(2)}) collective-permute-start(bf16[256,1024]{1,0:T(8,128)(2,1)} %copy-done.7), channel_id=1, source_target_pairs={{0,2},{1,3},{2,0},{3,1},{4,6},{5,7},{6,4},{7,5},{8,10},{9,11},{10,... | collective-permute-start | bytes 1572872 | tf_op jit(solution)/shard_map/ppermute | solution.py:418
  99.0 2.5 %collective-permute-start.22 = (bf16[256,1024]{1,0:T(8,128)(2,1)}, bf16[256,1024]{1,0:T(8,128)(2,1)}, u32[]{:S(2)}, u32[]{:S(2)}) collective-permute-start(bf16[256,1024]{1,0:T(8,128)(2,1)} %copy-done.6), channel_id=1, source_target_pairs={{0,3},{1,0},{2,1},{3,2},{4,7},{5,4},{6,5},{7,6},{8,11},{9,8},{10,9... | collective-permute-start | bytes 1572872 | tf_op jit(solution)/shard_map/ppermute | solution.py:418
  101.5 14.6 %all-to-all-done.got = bf16[16,32,1280]{2,1,0:T(8,128)(2,1)S(1)} async-done(((bf16[16,32,1280]{2,1,0:T(8,128)(2,1)}), bf16[16,32,1280]{2,1,0:T(8,128)(2,1)S(1)}, u32[]{:S(2)}, u32[]{:S(2)}) %all-to-all-start) | async-done | bytes 1310752 | tf_op jit(solution)/shard_map/all_to_all | solution.py:511
  116.9 5.4 %all-to-all-start.1 = ((bf16[4,8,1280]{2,1,0:T(8,128)(2,1)}), bf16[4,8,1280]{2,1,0:T(8,128)(2,1)S(1)}, u32[]{:S(2)}, u32[]{:S(2)}) async-start(bf16[4,8,1280]{2,1,0:T(8,128)(2,1)} %bitcast.9), calls=%async_computation.1 | async-start | bytes 163840 | tf_op jit(solution)/shard_map/all_to_all | solution.py:517
  122.5 2.1 %shard_map.92 = bf16[256,1024]{1,0:T(8,128)(2,1)} custom-call(f32[256,1024]{1,0:T(8,128)S(1)} %get-tuple-element.133.own, bf16[256,1024]{1,0:T(8,128)(2,1)S(1)} %collective-permute-done.20.got_1, bf16[256,1024]{1,0:T(8,128)(2,1)S(1)} %collective-permute-done.21.got_2, bf16[256,1024]{1,0:T(8,128)(2,1)} %collective-permute-done.22.got_3), custom_call_target="tpu_custom_call" | custom-call | flops 1048576 | bytes 4194304 | tf_op jit(solution)/shard_map/pallas_call | solution.py:514
  124.6 3.5 %all-to-all-done.1.got = bf16[4,8,1280]{2,1,0:T(8,128)(2,1)S(1)} async-done(((bf16[4,8,1280]{2,1,0:T(8,128)(2,1)}), bf16[4,8,1280]{2,1,0:T(8,128)(2,1)S(1)}, u32[]{:S(2)}, u32[]{:S(2)}) %all-to-all-start.1) | async-done | bytes 81952 | tf_op jit(solution)/shard_map/all_to_all | solution.py:517
  (61 shorter events, 30.9 us)
Async XLA Ops:
  0.6 15.7 %collective-permute-start = (bf16[256,1024]{1,0:T(8,128)(2,1)}, bf16[256,1024]{1,0:T(8,128)(2,1)S(1)}, u32[]{:S(2)}, u32[]{:S(2)}) collective-permute-start(bf16[256,1024]{1,0:T(8,128)(2,1)} %bitcast.12), channel_id=1, source_target_pairs={{0,3},{1,0},{2,1},{3,2},{4,7},{5,4},{6,5},{7,6},{8,11},{9,8},{10,9... | collective-permute-start | bytes 1572872 | tf_op jit(solution)/shard_map/ppermute | solution.py:418
  4.8 14.8 %collective-permute-start.1 = (bf16[256,1024]{1,0:T(8,128)(2,1)}, bf16[256,1024]{1,0:T(8,128)(2,1)S(1)}, u32[]{:S(2)}, u32[]{:S(2)}) collective-permute-start(bf16[256,1024]{1,0:T(8,128)(2,1)} %bitcast.13), channel_id=1, source_target_pairs={{0,1},{1,2},{2,3},{3,0},{4,5},{5,6},{6,7},{7,4},{8,9},{9,10},{10,1... | collective-permute-start | bytes 1572872 | tf_op jit(solution)/shard_map/ppermute | solution.py:418
  19.6 16.4 %collective-permute-start.2 = (bf16[256,1024]{1,0:T(8,128)(2,1)S(1)}, bf16[256,1024]{1,0:T(8,128)(2,1)S(1)}, u32[]{:S(2)}, u32[]{:S(2)}) collective-permute-start(bf16[256,1024]{1,0:T(8,128)(2,1)S(1)} %bitcast.15), channel_id=1, source_target_pairs={{0,2},{1,3},{2,0},{3,1},{4,6},{5,7},{6,4},{7,5},{8,10},{9,11},{10,... | collective-permute-start | bytes 1572872 | tf_op jit(solution)/shard_map/ppermute | solution.py:418
  19.6 18.3 %collective-permute-start.7 = (bf16[256,512]{1,0:T(8,128)(2,1)S(1)}, bf16[256,512]{1,0:T(8,128)(2,1)S(1)}, u32[]{:S(2)}, u32[]{:S(2)}) collective-permute-start(bf16[256,512]{1,0:T(8,128)(2,1)S(1)} %get-tuple-element.72.refs_3_), channel_id=1, source_target_pairs={{0,4},{4,8},{8,12},{12,0},{1,5},{5,9},{9,13},{13,1},{2,6},{6,10},{... | collective-permute-start | bytes 786440 | tf_op jit(solution)/shard_map/ppermute | solution.py:418
  23.7 21.2 %collective-permute-start.8 = (bf16[512,512]{1,0:T(8,128)(2,1)S(1)}, bf16[512,512]{1,0:T(8,128)(2,1)S(1)}, u32[]{:S(2)}, u32[]{:S(2)}) collective-permute-start(bf16[512,512]{1,0:T(8,128)(2,1)S(1)} %get-tuple-element.78.refs_4_), channel_id=1, source_target_pairs={{0,4},{4,8},{8,12},{12,0},{1,5},{5,9},{9,13},{13,1},{2,6},{6,10},{... | collective-permute-start | bytes 1572872 | tf_op jit(solution)/shard_map/ppermute | solution.py:418
  26.7 17.8 %collective-permute-start.4 = (bf16[256,512]{1,0:T(8,128)(2,1)S(1)}, bf16[256,512]{1,0:T(8,128)(2,1)S(1)}, u32[]{:S(2)}, u32[]{:S(2)}) collective-permute-start(bf16[256,512]{1,0:T(8,128)(2,1)S(1)} %get-tuple-element.93), channel_id=1, source_target_pairs={{0,1},{1,2},{2,3},{3,0},{4,5},{5,6},{6,7},{7,4},{8,9},{9,10},{10,1... | collective-permute-start | bytes 786440 | tf_op jit(solution)/shard_map/ppermute | solution.py:418
  27.9 17.0 %collective-permute-start.5 = (bf16[256,512]{1,0:T(8,128)(2,1)S(1)}, bf16[256,512]{1,0:T(8,128)(2,1)S(1)}, u32[]{:S(2)}, u32[]{:S(2)}) collective-permute-start(bf16[256,512]{1,0:T(8,128)(2,1)S(1)} %get-tuple-element.94), channel_id=1, source_target_pairs={{0,2},{1,3},{2,0},{3,1},{4,6},{5,7},{6,4},{7,5},{8,10},{9,11},{10,... | collective-permute-start | bytes 786440 | tf_op jit(solution)/shard_map/ppermute | solution.py:418
  36.0 8.9 %collective-permute-start.6 = (bf16[256,512]{1,0:T(8,128)(2,1)S(1)}, bf16[256,512]{1,0:T(8,128)(2,1)S(1)}, u32[]{:S(2)}, u32[]{:S(2)}) collective-permute-start(bf16[256,512]{1,0:T(8,128)(2,1)S(1)} %get-tuple-element.95), channel_id=1, source_target_pairs={{0,3},{1,0},{2,1},{3,2},{4,7},{5,4},{6,5},{7,6},{8,11},{9,8},{10,9... | collective-permute-start | bytes 786440 | tf_op jit(solution)/shard_map/ppermute | solution.py:418
  37.9 7.7 %collective-permute-start.9 = (bf16[256,512]{1,0:T(8,128)(2,1)S(1)}, bf16[256,512]{1,0:T(8,128)(2,1)S(1)}, u32[]{:S(2)}, u32[]{:S(2)}) collective-permute-start(bf16[256,512]{1,0:T(8,128)(2,1)S(1)} %get-tuple-element.79.refs_5_), channel_id=1, source_target_pairs={{0,4},{4,8},{8,12},{12,0},{1,5},{5,9},{9,13},{13,1},{2,6},{6,10},{... | collective-permute-start | bytes 786440 | tf_op jit(solution)/shard_map/ppermute | solution.py:418
  47.3 6.9 %collective-permute-start.10 = (f32[8,1024]{1,0:T(8,128)S(1)}, f32[8,1024]{1,0:T(8,128)S(1)}, u32[]{:S(2)}, u32[]{:S(2)}) collective-permute-start(f32[8,1024]{1,0:T(8,128)S(1)} %get-tuple-element.102.refs_3_), channel_id=1, source_target_pairs={{0,3},{1,0},{2,1},{3,2},{4,7},{5,4},{6,5},{7,6},{8,11},{9,8},{10,9... | collective-permute-start | bytes 98312 | tf_op jit(solution)/shard_map/ppermute | solution.py:418
  48.2 6.0 %collective-permute-start.11 = (f32[8,1024]{1,0:T(8,128)S(1)}, f32[8,1024]{1,0:T(8,128)S(1)}, u32[]{:S(2)}, u32[]{:S(2)}) collective-permute-start(f32[8,1024]{1,0:T(8,128)S(1)} %get-tuple-element.102.refs_3_), channel_id=1, source_target_pairs={{0,2},{1,3},{2,0},{3,1},{4,6},{5,7},{6,4},{7,5},{8,10},{9,11},{10,... | collective-permute-start | bytes 98312 | tf_op jit(solution)/shard_map/ppermute | solution.py:418
  51.1 5.1 %collective-permute-start.12 = (f32[8,1024]{1,0:T(8,128)S(1)}, f32[8,1024]{1,0:T(8,128)S(1)}, u32[]{:S(2)}, u32[]{:S(2)}) collective-permute-start(f32[8,1024]{1,0:T(8,128)S(1)} %get-tuple-element.102.refs_3_), channel_id=1, source_target_pairs={{0,1},{1,2},{2,3},{3,0},{4,5},{5,6},{6,7},{7,4},{8,9},{9,10},{10,1... | collective-permute-start | bytes 98312 | tf_op jit(solution)/shard_map/ppermute | solution.py:418
  51.1 20.8 %collective-permute-start.3 = (bf16[1024,256]{1,0:T(8,128)(2,1)S(1)}, bf16[1024,256]{1,0:T(8,128)(2,1)S(1)}, u32[]{:S(2)}, u32[]{:S(2)}) collective-permute-start(bf16[1024,256]{1,0:T(8,128)(2,1)S(1)} %get-tuple-element.80.refs_0_), channel_id=1, source_target_pairs={{0,12},{4,0},{8,4},{12,8},{1,13},{5,1},{9,5},{13,9},{2,14},{6,2},{... | collective-permute-start | bytes 1572872 | tf_op jit(solution)/shard_map/ppermute | solution.py:418
  57.9 16.8 %collective-permute-start.13 = (bf16[1024,256]{1,0:T(8,128)(2,1)S(1)}, bf16[1024,256]{1,0:T(8,128)(2,1)S(1)}, u32[]{:S(2)}, u32[]{:S(2)}) collective-permute-start(bf16[1024,256]{1,0:T(8,128)(2,1)S(1)} %get-tuple-element.107.refs_1_), channel_id=1, source_target_pairs={{0,12},{4,0},{8,4},{12,8},{1,13},{5,1},{9,5},{13,9},{2,14},{6,2},{... | collective-permute-start | bytes 1572872 | tf_op jit(solution)/shard_map/ppermute | solution.py:418
  61.2 21.3 %collective-permute-start.14 = (bf16[1024,256]{1,0:T(8,128)(2,1)S(1)}, bf16[1024,256]{1,0:T(8,128)(2,1)S(1)}, u32[]{:S(2)}, u32[]{:S(2)}) collective-permute-start(bf16[1024,256]{1,0:T(8,128)(2,1)S(1)} %get-tuple-element.126.refs_0_), channel_id=1, source_target_pairs={{0,3},{1,0},{2,1},{3,2},{4,7},{5,4},{6,5},{7,6},{8,11},{9,8},{10,9... | collective-permute-start | bytes 1572872 | tf_op jit(solution)/shard_map/ppermute | solution.py:418
  61.5 21.1 %collective-permute-start.15 = (bf16[1024,256]{1,0:T(8,128)(2,1)S(1)}, bf16[1024,256]{1,0:T(8,128)(2,1)S(1)}, u32[]{:S(2)}, u32[]{:S(2)}) collective-permute-start(bf16[1024,256]{1,0:T(8,128)(2,1)S(1)} %get-tuple-element.126.refs_0_), channel_id=1, source_target_pairs={{0,2},{1,3},{2,0},{3,1},{4,6},{5,7},{6,4},{7,5},{8,10},{9,11},{10,... | collective-permute-start | bytes 1572872 | tf_op jit(solution)/shard_map/ppermute | solution.py:418
  62.5 20.6 %collective-permute-start.16 = (bf16[1024,256]{1,0:T(8,128)(2,1)S(1)}, bf16[1024,256]{1,0:T(8,128)(2,1)S(1)}, u32[]{:S(2)}, u32[]{:S(2)}) collective-permute-start(bf16[1024,256]{1,0:T(8,128)(2,1)S(1)} %get-tuple-element.126.refs_0_), channel_id=1, source_target_pairs={{0,1},{1,2},{2,3},{3,0},{4,5},{5,6},{6,7},{7,4},{8,9},{9,10},{10,1... | collective-permute-start | bytes 1572872 | tf_op jit(solution)/shard_map/ppermute | solution.py:418
  71.9 12.6 %collective-permute-start.17 = (bf16[4,128,512]{2,1,0:T(8,128)(2,1)S(1)}, bf16[4,128,512]{2,1,0:T(8,128)(2,1)S(1)}, u32[]{:S(2)}, u32[]{:S(2)}) collective-permute-start(bf16[4,128,512]{2,1,0:T(8,128)(2,1)S(1)} %get-tuple-element.129), channel_id=1, source_target_pairs={{0,16},{16,0},{1,17},{17,1},{2,18},{18,2},{3,19},{19,3},{4,20},{20... | collective-permute-start | bytes 1572872 | tf_op jit(solution)/shard_map/ppermute | solution.py:422
  79.5 6.5 %collective-permute-start.18 = (bf16[4,128,512]{2,1,0:T(8,128)(2,1)S(1)}, bf16[4,128,512]{2,1,0:T(8,128)(2,1)S(1)}, u32[]{:S(2)}, u32[]{:S(2)}) collective-permute-start(bf16[4,128,512]{2,1,0:T(8,128)(2,1)S(1)} %get-tuple-element.130), channel_id=1, source_target_pairs={{0,16},{16,0},{1,17},{17,1},{2,18},{18,2},{3,19},{19,3},{4,20},{20... | collective-permute-start | bytes 1572872 | tf_op jit(solution)/shard_map/ppermute | solution.py:422
  87.3 28.8 %all-to-all-start = ((bf16[16,32,1280]{2,1,0:T(8,128)(2,1)}), bf16[16,32,1280]{2,1,0:T(8,128)(2,1)S(1)}, u32[]{:S(2)}, u32[]{:S(2)}) async-start(bf16[16,32,1280]{2,1,0:T(8,128)(2,1)} %bitcast.7), calls=%async_computation | async-start | bytes 2621440 | tf_op jit(solution)/shard_map/all_to_all | solution.py:511
  94.7 27.6 %collective-permute-start.20 = (bf16[256,1024]{1,0:T(8,128)(2,1)}, bf16[256,1024]{1,0:T(8,128)(2,1)S(1)}, u32[]{:S(2)}, u32[]{:S(2)}) collective-permute-start(bf16[256,1024]{1,0:T(8,128)(2,1)} %get-tuple-element.134), channel_id=1, source_target_pairs={{0,1},{1,2},{2,3},{3,0},{4,5},{5,6},{6,7},{7,4},{8,9},{9,10},{10,1... | collective-permute-start | bytes 1572872 | tf_op jit(solution)/shard_map/ppermute | solution.py:418
  96.5 26.0 %collective-permute-start.21 = (bf16[256,1024]{1,0:T(8,128)(2,1)}, bf16[256,1024]{1,0:T(8,128)(2,1)S(1)}, u32[]{:S(2)}, u32[]{:S(2)}) collective-permute-start(bf16[256,1024]{1,0:T(8,128)(2,1)} %copy-done.7), channel_id=1, source_target_pairs={{0,2},{1,3},{2,0},{3,1},{4,6},{5,7},{6,4},{7,5},{8,10},{9,11},{10,... | collective-permute-start | bytes 1572872 | tf_op jit(solution)/shard_map/ppermute | solution.py:418
  99.0 23.5 %collective-permute-start.22 = (bf16[256,1024]{1,0:T(8,128)(2,1)}, bf16[256,1024]{1,0:T(8,128)(2,1)}, u32[]{:S(2)}, u32[]{:S(2)}) collective-permute-start(bf16[256,1024]{1,0:T(8,128)(2,1)} %copy-done.6), channel_id=1, source_target_pairs={{0,3},{1,0},{2,1},{3,2},{4,7},{5,4},{6,5},{7,6},{8,11},{9,8},{10,9... | collective-permute-start | bytes 1572872 | tf_op jit(solution)/shard_map/ppermute | solution.py:418
  116.9 11.1 %all-to-all-start.1 = ((bf16[4,8,1280]{2,1,0:T(8,128)(2,1)}), bf16[4,8,1280]{2,1,0:T(8,128)(2,1)S(1)}, u32[]{:S(2)}, u32[]{:S(2)}) async-start(bf16[4,8,1280]{2,1,0:T(8,128)(2,1)} %bitcast.9), calls=%async_computation.1 | async-start | bytes 163840 | tf_op jit(solution)/shard_map/all_to_all | solution.py:517
  (9 other events, 42.7 us)

commit v17 on v15

--- a/solution.py
+++ b/solution.py
@@ -501,8 +501,15 @@
     sums = lax.all_to_all(mine.reshape(16, 32, 5 * BLK), ("x", "y"), 0, 0)
     total = call(add_xy_body, bf16((32, 5 * BLK)), 1, 1 << 20, 1 << 20, scalars=0)(sums)
     _, own_rows = lax.optimization_barrier((total, partial[0]))
-    grad_events = call(
-        add_rows_body, bf16((BLK, D)), 4, 1 << 20, 4 << 20, scalars=0
+    block = pl.BlockSpec((BLK // 4, D), lambda i: (i, 0))
+    grad_events = pl.pallas_call(
+        add_rows_body,
+        grid=(4,),
+        out_shape=bf16((BLK, D)),
+        in_specs=[block] * 4,
+        out_specs=block,
+        compiler_params=pltpu.CompilerParams(vmem_limit_bytes=20 * 1024 * 1024),
+        cost_estimate=pl.CostEstimate(flops=1 << 20, bytes_accessed=4 << 20, transcendentals=0),
     )(own_rows, *partial[1:])
     got = lax.all_to_all(total.reshape(4, 8, 5 * BLK), "z", 0, 0)
     grad_w_in, grad_w_out = call(

time: 131 us -> 129 us (0.985)
  starting transfers between devices: 48.5 us -> 46.3 us
    ppermute x3, starting transfers between devices: 2.92 us -> 0.73 us  [swap(): return lax.ppermute(x, 'c', [(0, 1), (1, 0)])]
  transfers between devices with their start and end apart: 25 -> 25, of which waited for: 12 -> 12; matrix products, arithmetic and copies ran while one was open for 1% -> 1% of each run, Pallas kernels for 28% -> 29%
where the time goes in v17:
time: 129 us; the launch traced here: 128 us
  starting transfers between devices  46.3 us (36%)
  Pallas kernels  41.2 us (32%)
  waiting for transfers between devices  35.4 us (27%)
  local copies, waits for them, and re-layouts  4.13 us (3%)
    ppermute x20, starting transfers between devices, along(): return lax.ppermute(x, axis, [(i, (i + d) % 4) for i in range(4)])  32.9 us
    ppermute x20, waiting for transfers between devices, along(): return lax.ppermute(x, axis, [(i, (i + d) % 4) for i in range(4)])  17.7 us
    all_to_all x1, waiting for transfers between devices, body(): sums = lax.all_to_all(mine.reshape(16, 32, 5 * BLK), ('x', 'y'), 0, 0)  14.2 us
    pallas_call x1, Pallas kernels, body(): call(backward_local_body, (bf16((GRP, BLK)), f32((GRP, 2 * BLK))), 8, 1 <...  8.18 us
    all_to_all x1, starting transfers between devices, body(): sums = lax.all_to_all(mine.reshape(16, 32, 5 * BLK), ('x', 'y'), 0, 0)  7.24 us
    pallas_call x3, Pallas kernels, body(): call(project_body, (bf16((n * BLK, 2 * BLK)), bf16((n * BLK, BLK)), bf16(...  6.22 us
    pallas_call x3, Pallas kernels, weights(): call(kernel, (bf16((4, 128, cols)), f32((4, 128, cols))), len(operands),...  6.21 us
    all_to_all x1, starting transfers between devices, body(): got = lax.all_to_all(total.reshape(4, 8, 5 * BLK), 'z', 0, 0)  5.45 us
  transfers between devices with their start and end apart: 25, of which 12 were waited for; matrix products, arithmetic and copies ran while one was open for 1% of the time, Pallas kernels for 29%

profile of v17, /device:TPU:0, one launch (start us, length us, event | category | flops | bytes accessed | tf_op | source)
XLA Modules:
  0.0 127.9 jit_solution(11417307771504710218)
XLA Ops:
  0.6 4.2 %collective-permute-start = (bf16[256,1024]{1,0:T(8,128)(2,1)}, bf16[256,1024]{1,0:T(8,128)(2,1)S(1)}, u32[]{:S(2)}, u32[]{:S(2)}) collective-permute-start(bf16[256,1024]{1,0:T(8,128)(2,1)} %bitcast.5.refs_0_), channel_id=1, source_target_pairs={{0,3},{1,0},{2,1},{3,2},{4,7},{5,4},{6,5},{7,6},{8,11},{9,8},{10,9... | collective-permute-start | bytes 1572872 | tf_op jit(solution)/shard_map/ppermute | solution.py:411
  5.6 3.4 %copy-done = bf16[1024,4096]{1,0:T(8,128)(2,1)S(1)} copy-done((bf16[1024,4096]{1,0:T(8,128)(2,1)S(1)}, bf16[1024,4096]{1,0:T(8,128)(2,1)}, u32[]{:S(2)}) %copy-start) | copy-done | bytes 8388632
  8.9 2.2 %shard_map.76 = (bf16[256,512]{1,0:T(8,128)(2,1)S(1)}, bf16[256,256]{1,0:T(8,128)(2,1)S(1)}, bf16[256,256]{1,0:T(8,128)(2,1)S(1)}, bf16[256,1024]{1,0:T(8,128)(2,1)S(1)}) custom-call(s32[12]{0:T(128)S(1)} %concatenate.3.info, bf16[256,1024]{1,0:T(8,128)(2,1)} %bitcast.5.refs_0_, bf16[1024,4096]{1,0:T(8,128)(2,1)S(1)} %copy-done), custom_call_target="tpu_custom_call" | custom-call | flops 1048576 | bytes 1048576 | tf_op jit(solution)/shard_map/pallas_call | solution.py:448
  11.2 5.1 %collective-permute-done.refs_0_.refs_1_ = bf16[256,1024]{1,0:T(8,128)(2,1)S(1)} collective-permute-done((bf16[256,1024]{1,0:T(8,128)(2,1)}, bf16[256,1024]{1,0:T(8,128)(2,1)S(1)}, u32[]{:S(2)}, u32[]{:S(2)}) %collective-permute-start) | collective-permute-done | bytes 524320 | tf_op jit(solution)/shard_map/ppermute | solution.py:411
  16.3 3.3 %collective-permute-done.1.refs_1_.refs_3_ = bf16[256,1024]{1,0:T(8,128)(2,1)S(1)} collective-permute-done((bf16[256,1024]{1,0:T(8,128)(2,1)}, bf16[256,1024]{1,0:T(8,128)(2,1)S(1)}, u32[]{:S(2)}, u32[]{:S(2)}) %collective-permute-start.1) | collective-permute-done | bytes 524320 | tf_op jit(solution)/shard_map/ppermute | solution.py:411
  21.3 2.4 %shard_map.77 = (bf16[512,512]{1,0:T(8,128)(2,1)S(1)}, bf16[512,256]{1,0:T(8,128)(2,1)S(1)}, bf16[512,256]{1,0:T(8,128)(2,1)S(1)}, bf16[256,1024]{1,0:T(8,128)(2,1)S(1)}, bf16[256,1024]{1,0:T(8,128)(2,1)S(1)}) custom-call(s32[12]{0:T(128)S(1)} %concatenate.3.info, bf16[256,1024]{1,0:T(8,128)(2,1)S(1)} %collective-permute-done.refs_0_.refs_1_, ...), custom_call_target="tpu_custom_call" | custom-call | flops 1048576 | bytes 1048576 | tf_op jit(solution)/shard_map/pallas_call | solution.py:448
  27.9 2.4 %collective-permute-start.5 = (bf16[256,512]{1,0:T(8,128)(2,1)S(1)}, bf16[256,512]{1,0:T(8,128)(2,1)S(1)}, u32[]{:S(2)}, u32[]{:S(2)}) collective-permute-start(bf16[256,512]{1,0:T(8,128)(2,1)S(1)} %get-tuple-element.81), channel_id=1, source_target_pairs={{0,2},{1,3},{2,0},{3,1},{4,6},{5,7},{6,4},{7,5},{8,10},{9,11},{10,... | collective-permute-start | bytes 786440 | tf_op jit(solution)/shard_map/ppermute | solution.py:411
  30.3 5.9 %collective-permute-done.2.refs_0_.refs_2_ = bf16[256,1024]{1,0:T(8,128)(2,1)S(1)} collective-permute-done((bf16[256,1024]{1,0:T(8,128)(2,1)}, bf16[256,1024]{1,0:T(8,128)(2,1)S(1)}, u32[]{:S(2)}, u32[]{:S(2)}) %collective-permute-start.2) | collective-permute-done | bytes 524320 | tf_op jit(solution)/shard_map/ppermute | solution.py:411
  39.8 5.1 %shard_map.79 = (bf16[1024,256]{1,0:T(8,128)(2,1)S(1)}, bf16[1024,512]{1,0:T(8,128)(2,1)S(1)}, f32[1024,256]{1,0:T(8,128)S(1)}) custom-call(s32[12]{0:T(128)S(1)} %concatenate.3.info, bf16[256,256]{1,0:T(8,128)(2,1)S(1)} %get-tuple-element.64.refs_0_, bf16[512,256]{1,0:T(8,128)(2,1)S(1)} %get-tuple-element.68.refs_1_, ...), custom_call_target="tpu_custom_call" | custom-call | flops 5368709120 | bytes 4194304 | tf_op jit(solution)/shard_map/pallas_call | solution.py:462
  48.2 3.1 %collective-permute-start.11 = (f32[8,1024]{1,0:T(8,128)S(1)}, f32[8,1024]{1,0:T(8,128)S(1)}, u32[]{:S(2)}, u32[]{:S(2)}) collective-permute-start(f32[8,1024]{1,0:T(8,128)S(1)} %get-tuple-element.89.refs_3_), channel_id=1, source_target_pairs={{0,2},{1,3},{2,0},{3,1},{4,6},{5,7},{6,4},{7,5},{8,10},{9,11},{10,... | collective-permute-start | bytes 98312 | tf_op jit(solution)/shard_map/ppermute | solution.py:411
  51.3 3.5 %collective-permute-start.3 = (bf16[1024,256]{1,0:T(8,128)(2,1)S(1)}, bf16[1024,256]{1,0:T(8,128)(2,1)S(1)}, u32[]{:S(2)}, u32[]{:S(2)}) collective-permute-start(bf16[1024,256]{1,0:T(8,128)(2,1)S(1)} %get-tuple-element.73.refs_0_), channel_id=1, source_target_pairs={{0,12},{4,0},{8,4},{12,8},{1,13},{5,1},{9,5},{13,9},{2,14},{6,2},{... | collective-permute-start | bytes 1572872 | tf_op jit(solution)/shard_map/ppermute | solution.py:411
  58.1 3.6 %collective-permute-start.13 = (bf16[1024,256]{1,0:T(8,128)(2,1)S(1)}, bf16[1024,256]{1,0:T(8,128)(2,1)S(1)}, u32[]{:S(2)}, u32[]{:S(2)}) collective-permute-start(bf16[1024,256]{1,0:T(8,128)(2,1)S(1)} %get-tuple-element.94.refs_1_), channel_id=1, source_target_pairs={{0,12},{4,0},{8,4},{12,8},{1,13},{5,1},{9,5},{13,9},{2,14},{6,2},{... | collective-permute-start | bytes 1572872 | tf_op jit(solution)/shard_map/ppermute | solution.py:411
  63.7 8.2 %shard_map.83 = (bf16[1024,256]{1,0:T(8,128)(2,1)S(1)}, f32[1024,512]{1,0:T(8,128)S(1)}) custom-call(s32[12]{0:T(128)S(1)} %concatenate.3.info, bf16[1024,256]{1,0:T(8,128)(2,1)S(1)} %get-tuple-element.73.refs_0_, bf16[1024,256]{1,0:T(8,128)(2,1)S(1)} %get-tuple-element.94.refs_1_, bf16[1024,512]{1,0:T(8,128)(2,1)S(1)} %get-tuple-element.96.refs_2_, ...), custom_call_target="tpu_custom_call" | custom-call | flops 1048576 | bytes 1048576 | tf_op jit(solution)/shard_map/pallas_call | solution.py:476
  71.9 2.5 %shard_map.84 = (bf16[4,128,512]{2,1,0:T(8,128)(2,1)S(1)}, f32[4,128,512]{2,1,0:T(8,128)S(1)}) custom-call(s32[12]{0:T(128)S(1)} %concatenate.3.info, bf16[256,1024]{1,0:T(8,128)(2,1)} %bitcast.5.refs_0_, bf16[256,1024]{1,0:T(8,128)(2,1)S(1)} %collective-permute-done.refs_0_.refs_1_, bf16[256,1024]{1,0:T(8,128)(2,1)S(1)} %collective-permute-done.2.refs_0_.refs_2_, ...), custom_call_target="tpu_custom_call" | custom-call | flops 1048576 | bytes 1048576 | tf_op jit(solution)/shard_map/pallas_call | solution.py:481
  74.5 1.8 %shard_map.85 = (bf16[256,1024]{1,0:T(8,128)(2,1)S(1)}, bf16[256,1024]{1,0:T(8,128)(2,1)S(1)}, bf16[256,1024]{1,0:T(8,128)(2,1)S(1)}, bf16[256,1024]{1,0:T(8,128)(2,1)S(1)}) custom-call(s32[12]{0:T(128)S(1)} %concatenate.3.info, bf16[1024,256]{1,0:T(8,128)(2,1)S(1)} %collective-permute-done.3.refs_0_, bf16[1024,256]{1,0:T(8,128)(2,1)S(1)} %collective-permute-done.13.refs_1_, ...), custom_call_target="tpu_custom_call" | custom-call | flops 5368709120 | bytes 4194304 | tf_op jit(solution)/shard_map/pallas_call | solution.py:488
  76.3 2.4 %shard_map.86 = (bf16[4,128,512]{2,1,0:T(8,128)(2,1)S(1)}, f32[4,128,512]{2,1,0:T(8,128)S(1)}) custom-call(s32[12]{0:T(128)S(1)} %concatenate.3.info, bf16[256,1024]{1,0:T(8,128)(2,1)} %bitcast.5.refs_0_, bf16[256,1024]{1,0:T(8,128)(2,1)S(1)} %collective-permute-done.refs_0_.refs_1_, bf16[256,1024]{1,0:T(8,128)(2,1)S(1)} %collective-permute-done.2.refs_0_.refs_2_, ...), custom_call_target="tpu_custom_call" | custom-call | flops 1048576 | bytes 1048576 | tf_op jit(solution)/shard_map/pallas_call | solution.py:481
  79.3 3.0 %shard_map.87 = (f32[256,1024]{1,0:T(8,128)S(1)}, bf16[256,1024]{1,0:T(8,128)(2,1)}, bf16[256,1024]{1,0:T(8,128)(2,1)S(1)}, bf16[256,1024]{1,0:T(8,128)(2,1)S(1)}) custom-call(s32[12]{0:T(128)S(1)} %concatenate.3.info, bf16[256,1024]{1,0:T(8,128)(2,1)S(1)} %get-tuple-element.105.refs_4_.refs_0_, bf16[256,1024]{1,0:T(8,128)(2,1)S(1)} %get-tuple-element.106.refs_5_.refs_1_, ...), custom_call_target="tpu_custom_call" | custom-call | flops 1048576 | bytes 1048576 | tf_op jit(solution)/shard_map/pallas_call | solution.py:492
  86.9 7.2 %all-to-all-start = ((bf16[16,32,1280]{2,1,0:T(8,128)(2,1)}), bf16[16,32,1280]{2,1,0:T(8,128)(2,1)S(1)}, u32[]{:S(2)}, u32[]{:S(2)}) async-start(bf16[16,32,1280]{2,1,0:T(8,128)(2,1)} %bitcast.7), calls=%async_computation | async-start | bytes 2621440 | tf_op jit(solution)/shard_map/all_to_all | solution.py:501
  95.9 2.6 %collective-permute-start.21 = (bf16[256,1024]{1,0:T(8,128)(2,1)}, bf16[256,1024]{1,0:T(8,128)(2,1)S(1)}, u32[]{:S(2)}, u32[]{:S(2)}) collective-permute-start(bf16[256,1024]{1,0:T(8,128)(2,1)} %copy-done.5), channel_id=1, source_target_pairs={{0,2},{1,3},{2,0},{3,1},{4,6},{5,7},{6,4},{7,5},{8,10},{9,11},{10,... | collective-permute-start | bytes 1572872 | tf_op jit(solution)/shard_map/ppermute | solution.py:411
  98.5 2.5 %collective-permute-start.22 = (bf16[256,1024]{1,0:T(8,128)(2,1)}, bf16[256,1024]{1,0:T(8,128)(2,1)}, u32[]{:S(2)}, u32[]{:S(2)}) collective-permute-start(bf16[256,1024]{1,0:T(8,128)(2,1)} %copy-done.4), channel_id=1, source_target_pairs={{0,3},{1,0},{2,1},{3,2},{4,7},{5,4},{6,5},{7,6},{8,11},{9,8},{10,9... | collective-permute-start | bytes 1572872 | tf_op jit(solution)/shard_map/ppermute | solution.py:411
  101.1 14.2 %all-to-all-done.got = bf16[16,32,1280]{2,1,0:T(8,128)(2,1)S(1)} async-done(((bf16[16,32,1280]{2,1,0:T(8,128)(2,1)}), bf16[16,32,1280]{2,1,0:T(8,128)(2,1)S(1)}, u32[]{:S(2)}, u32[]{:S(2)}) %all-to-all-start) | async-done | bytes 1310752 | tf_op jit(solution)/shard_map/all_to_all | solution.py:501
  116.1 5.4 %all-to-all-start.1 = ((bf16[4,8,1280]{2,1,0:T(8,128)(2,1)}), bf16[4,8,1280]{2,1,0:T(8,128)(2,1)S(1)}, u32[]{:S(2)}, u32[]{:S(2)}) async-start(bf16[4,8,1280]{2,1,0:T(8,128)(2,1)} %bitcast.9), calls=%async_computation.1 | async-start | bytes 163840 | tf_op jit(solution)/shard_map/all_to_all | solution.py:514
  122.0 3.2 %shard_map.91 = bf16[256,1024]{1,0:T(8,128)(2,1)} custom-call(f32[256,1024]{1,0:T(8,128)S(1)} %get-tuple-element.119.own, bf16[256,1024]{1,0:T(8,128)(2,1)S(1)} %collective-permute-done.20.got_1, bf16[256,1024]{1,0:T(8,128)(2,1)S(1)} %collective-permute-done.21.got_2, bf16[256,1024]{1,0:T(8,128)(2,1)} %collective-permute-done.22.got_3), custom_call_target="tpu_custom_call" | custom-call | flops 1048576 | bytes 4194304 | tf_op jit(solution)/shard_map/pallas_call | solution.py:505
  125.3 1.9 %all-to-all-done.1.got = bf16[4,8,1280]{2,1,0:T(8,128)(2,1)S(1)} async-done(((bf16[4,8,1280]{2,1,0:T(8,128)(2,1)}), bf16[4,8,1280]{2,1,0:T(8,128)(2,1)S(1)}, u32[]{:S(2)}, u32[]{:S(2)}) %all-to-all-start.1) | async-done | bytes 81952 | tf_op jit(solution)/shard_map/all_to_all | solution.py:514
  (56 shorter events, 27.6 us)
Async XLA Ops:
  0.6 15.7 %collective-permute-start = (bf16[256,1024]{1,0:T(8,128)(2,1)}, bf16[256,1024]{1,0:T(8,128)(2,1)S(1)}, u32[]{:S(2)}, u32[]{:S(2)}) collective-permute-start(bf16[256,1024]{1,0:T(8,128)(2,1)} %bitcast.5.refs_0_), channel_id=1, source_target_pairs={{0,3},{1,0},{2,1},{3,2},{4,7},{5,4},{6,5},{7,6},{8,11},{9,8},{10,9... | collective-permute-start | bytes 1572872 | tf_op jit(solution)/shard_map/ppermute | solution.py:411
  4.8 14.8 %collective-permute-start.1 = (bf16[256,1024]{1,0:T(8,128)(2,1)}, bf16[256,1024]{1,0:T(8,128)(2,1)S(1)}, u32[]{:S(2)}, u32[]{:S(2)}) collective-permute-start(bf16[256,1024]{1,0:T(8,128)(2,1)} %bitcast.5.refs_0_), channel_id=1, source_target_pairs={{0,1},{1,2},{2,3},{3,0},{4,5},{5,6},{6,7},{7,4},{8,9},{9,10},{10,1... | collective-permute-start | bytes 1572872 | tf_op jit(solution)/shard_map/ppermute | solution.py:411
  19.6 16.6 %collective-permute-start.2 = (bf16[256,1024]{1,0:T(8,128)(2,1)}, bf16[256,1024]{1,0:T(8,128)(2,1)S(1)}, u32[]{:S(2)}, u32[]{:S(2)}) collective-permute-start(bf16[256,1024]{1,0:T(8,128)(2,1)} %bitcast.5.refs_0_), channel_id=1, source_target_pairs={{0,2},{1,3},{2,0},{3,1},{4,6},{5,7},{6,4},{7,5},{8,10},{9,11},{10,... | collective-permute-start | bytes 1572872 | tf_op jit(solution)/shard_map/ppermute | solution.py:411
  19.6 18.5 %collective-permute-start.7 = (bf16[256,512]{1,0:T(8,128)(2,1)S(1)}, bf16[256,512]{1,0:T(8,128)(2,1)S(1)}, u32[]{:S(2)}, u32[]{:S(2)}) collective-permute-start(bf16[256,512]{1,0:T(8,128)(2,1)S(1)} %get-tuple-element.65.refs_3_), channel_id=1, source_target_pairs={{0,4},{4,8},{8,12},{12,0},{1,5},{5,9},{9,13},{13,1},{2,6},{6,10},{... | collective-permute-start | bytes 786440 | tf_op jit(solution)/shard_map/ppermute | solution.py:411
  23.7 21.4 %collective-permute-start.8 = (bf16[512,512]{1,0:T(8,128)(2,1)S(1)}, bf16[512,512]{1,0:T(8,128)(2,1)S(1)}, u32[]{:S(2)}, u32[]{:S(2)}) collective-permute-start(bf16[512,512]{1,0:T(8,128)(2,1)S(1)} %get-tuple-element.71.refs_4_), channel_id=1, source_target_pairs={{0,4},{4,8},{8,12},{12,0},{1,5},{5,9},{9,13},{13,1},{2,6},{6,10},{... | collective-permute-start | bytes 1572872 | tf_op jit(solution)/shard_map/ppermute | solution.py:411
  26.7 18.2 %collective-permute-start.4 = (bf16[256,512]{1,0:T(8,128)(2,1)S(1)}, bf16[256,512]{1,0:T(8,128)(2,1)S(1)}, u32[]{:S(2)}, u32[]{:S(2)}) collective-permute-start(bf16[256,512]{1,0:T(8,128)(2,1)S(1)} %get-tuple-element.80), channel_id=1, source_target_pairs={{0,1},{1,2},{2,3},{3,0},{4,5},{5,6},{6,7},{7,4},{8,9},{9,10},{10,1... | collective-permute-start | bytes 786440 | tf_op jit(solution)/shard_map/ppermute | solution.py:411
  27.9 17.2 %collective-permute-start.5 = (bf16[256,512]{1,0:T(8,128)(2,1)S(1)}, bf16[256,512]{1,0:T(8,128)(2,1)S(1)}, u32[]{:S(2)}, u32[]{:S(2)}) collective-permute-start(bf16[256,512]{1,0:T(8,128)(2,1)S(1)} %get-tuple-element.81), channel_id=1, source_target_pairs={{0,2},{1,3},{2,0},{3,1},{4,6},{5,7},{6,4},{7,5},{8,10},{9,11},{10,... | collective-permute-start | bytes 786440 | tf_op jit(solution)/shard_map/ppermute | solution.py:411
  36.2 8.9 %collective-permute-start.6 = (bf16[256,512]{1,0:T(8,128)(2,1)S(1)}, bf16[256,512]{1,0:T(8,128)(2,1)S(1)}, u32[]{:S(2)}, u32[]{:S(2)}) collective-permute-start(bf16[256,512]{1,0:T(8,128)(2,1)S(1)} %get-tuple-element.82), channel_id=1, source_target_pairs={{0,3},{1,0},{2,1},{3,2},{4,7},{5,4},{6,5},{7,6},{8,11},{9,8},{10,9... | collective-permute-start | bytes 786440 | tf_op jit(solution)/shard_map/ppermute | solution.py:411
  38.2 7.7 %collective-permute-start.9 = (bf16[256,512]{1,0:T(8,128)(2,1)S(1)}, bf16[256,512]{1,0:T(8,128)(2,1)S(1)}, u32[]{:S(2)}, u32[]{:S(2)}) collective-permute-start(bf16[256,512]{1,0:T(8,128)(2,1)S(1)} %get-tuple-element.72.refs_5_), channel_id=1, source_target_pairs={{0,4},{4,8},{8,12},{12,0},{1,5},{5,9},{9,13},{13,1},{2,6},{6,10},{... | collective-permute-start | bytes 786440 | tf_op jit(solution)/shard_map/ppermute | solution.py:411
  47.5 7.4 %collective-permute-start.10 = (f32[8,1024]{1,0:T(8,128)S(1)}, f32[8,1024]{1,0:T(8,128)S(1)}, u32[]{:S(2)}, u32[]{:S(2)}) collective-permute-start(f32[8,1024]{1,0:T(8,128)S(1)} %get-tuple-element.89.refs_3_), channel_id=1, source_target_pairs={{0,3},{1,0},{2,1},{3,2},{4,7},{5,4},{6,5},{7,6},{8,11},{9,8},{10,9... | collective-permute-start | bytes 98312 | tf_op jit(solution)/shard_map/ppermute | solution.py:411
  48.2 6.7 %collective-permute-start.11 = (f32[8,1024]{1,0:T(8,128)S(1)}, f32[8,1024]{1,0:T(8,128)S(1)}, u32[]{:S(2)}, u32[]{:S(2)}) collective-permute-start(f32[8,1024]{1,0:T(8,128)S(1)} %get-tuple-element.89.refs_3_), channel_id=1, source_target_pairs={{0,2},{1,3},{2,0},{3,1},{4,6},{5,7},{6,4},{7,5},{8,10},{9,11},{10,... | collective-permute-start | bytes 98312 | tf_op jit(solution)/shard_map/ppermute | solution.py:411
  51.3 5.1 %collective-permute-start.12 = (f32[8,1024]{1,0:T(8,128)S(1)}, f32[8,1024]{1,0:T(8,128)S(1)}, u32[]{:S(2)}, u32[]{:S(2)}) collective-permute-start(f32[8,1024]{1,0:T(8,128)S(1)} %get-tuple-element.89.refs_3_), channel_id=1, source_target_pairs={{0,1},{1,2},{2,3},{3,0},{4,5},{5,6},{6,7},{7,4},{8,9},{9,10},{10,1... | collective-permute-start | bytes 98312 | tf_op jit(solution)/shard_map/ppermute | solution.py:411
  51.3 23.1 %collective-permute-start.3 = (bf16[1024,256]{1,0:T(8,128)(2,1)S(1)}, bf16[1024,256]{1,0:T(8,128)(2,1)S(1)}, u32[]{:S(2)}, u32[]{:S(2)}) collective-permute-start(bf16[1024,256]{1,0:T(8,128)(2,1)S(1)} %get-tuple-element.73.refs_0_), channel_id=1, source_target_pairs={{0,12},{4,0},{8,4},{12,8},{1,13},{5,1},{9,5},{13,9},{2,14},{6,2},{... | collective-permute-start | bytes 1572872 | tf_op jit(solution)/shard_map/ppermute | solution.py:411
  58.1 16.4 %collective-permute-start.13 = (bf16[1024,256]{1,0:T(8,128)(2,1)S(1)}, bf16[1024,256]{1,0:T(8,128)(2,1)S(1)}, u32[]{:S(2)}, u32[]{:S(2)}) collective-permute-start(bf16[1024,256]{1,0:T(8,128)(2,1)S(1)} %get-tuple-element.94.refs_1_), channel_id=1, source_target_pairs={{0,12},{4,0},{8,4},{12,8},{1,13},{5,1},{9,5},{13,9},{2,14},{6,2},{... | collective-permute-start | bytes 1572872 | tf_op jit(solution)/shard_map/ppermute | solution.py:411
  61.7 20.6 %collective-permute-start.14 = (bf16[1024,256]{1,0:T(8,128)(2,1)S(1)}, bf16[1024,256]{1,0:T(8,128)(2,1)S(1)}, u32[]{:S(2)}, u32[]{:S(2)}) collective-permute-start(bf16[1024,256]{1,0:T(8,128)(2,1)S(1)} %get-tuple-element.112.refs_0_), channel_id=1, source_target_pairs={{0,3},{1,0},{2,1},{3,2},{4,7},{5,4},{6,5},{7,6},{8,11},{9,8},{10,9... | collective-permute-start | bytes 1572872 | tf_op jit(solution)/shard_map/ppermute | solution.py:411
  62.0 20.3 %collective-permute-start.15 = (bf16[1024,256]{1,0:T(8,128)(2,1)S(1)}, bf16[1024,256]{1,0:T(8,128)(2,1)S(1)}, u32[]{:S(2)}, u32[]{:S(2)}) collective-permute-start(bf16[1024,256]{1,0:T(8,128)(2,1)S(1)} %get-tuple-element.112.refs_0_), channel_id=1, source_target_pairs={{0,2},{1,3},{2,0},{3,1},{4,6},{5,7},{6,4},{7,5},{8,10},{9,11},{10,... | collective-permute-start | bytes 1572872 | tf_op jit(solution)/shard_map/ppermute | solution.py:411
  62.9 19.8 %collective-permute-start.16 = (bf16[1024,256]{1,0:T(8,128)(2,1)S(1)}, bf16[1024,256]{1,0:T(8,128)(2,1)S(1)}, u32[]{:S(2)}, u32[]{:S(2)}) collective-permute-start(bf16[1024,256]{1,0:T(8,128)(2,1)S(1)} %get-tuple-element.112.refs_0_), channel_id=1, source_target_pairs={{0,1},{1,2},{2,3},{3,0},{4,5},{5,6},{6,7},{7,4},{8,9},{9,10},{10,1... | collective-permute-start | bytes 1572872 | tf_op jit(solution)/shard_map/ppermute | solution.py:411
  74.4 9.6 %collective-permute-start.17 = (bf16[4,128,512]{2,1,0:T(8,128)(2,1)S(1)}, bf16[4,128,512]{2,1,0:T(8,128)(2,1)S(1)}, u32[]{:S(2)}, u32[]{:S(2)}) collective-permute-start(bf16[4,128,512]{2,1,0:T(8,128)(2,1)S(1)} %get-tuple-element.115), channel_id=1, source_target_pairs={{0,16},{16,0},{1,17},{17,1},{2,18},{18,2},{3,19},{19,3},{4,20},{20... | collective-permute-start | bytes 1572872 | tf_op jit(solution)/shard_map/ppermute | solution.py:415
  78.8 6.8 %collective-permute-start.18 = (bf16[4,128,512]{2,1,0:T(8,128)(2,1)S(1)}, bf16[4,128,512]{2,1,0:T(8,128)(2,1)S(1)}, u32[]{:S(2)}, u32[]{:S(2)}) collective-permute-start(bf16[4,128,512]{2,1,0:T(8,128)(2,1)S(1)} %get-tuple-element.116), channel_id=1, source_target_pairs={{0,16},{16,0},{1,17},{17,1},{2,18},{18,2},{3,19},{19,3},{4,20},{20... | collective-permute-start | bytes 1572872 | tf_op jit(solution)/shard_map/ppermute | solution.py:415
  86.9 28.3 %all-to-all-start = ((bf16[16,32,1280]{2,1,0:T(8,128)(2,1)}), bf16[16,32,1280]{2,1,0:T(8,128)(2,1)S(1)}, u32[]{:S(2)}, u32[]{:S(2)}) async-start(bf16[16,32,1280]{2,1,0:T(8,128)(2,1)} %bitcast.7), calls=%async_computation | async-start | bytes 2621440 | tf_op jit(solution)/shard_map/all_to_all | solution.py:501
  94.2 27.3 %collective-permute-start.20 = (bf16[256,1024]{1,0:T(8,128)(2,1)}, bf16[256,1024]{1,0:T(8,128)(2,1)S(1)}, u32[]{:S(2)}, u32[]{:S(2)}) collective-permute-start(bf16[256,1024]{1,0:T(8,128)(2,1)} %get-tuple-element.120), channel_id=1, source_target_pairs={{0,1},{1,2},{2,3},{3,0},{4,5},{5,6},{6,7},{7,4},{8,9},{9,10},{10,1... | collective-permute-start | bytes 1572872 | tf_op jit(solution)/shard_map/ppermute | solution.py:411
  95.9 25.9 %collective-permute-start.21 = (bf16[256,1024]{1,0:T(8,128)(2,1)}, bf16[256,1024]{1,0:T(8,128)(2,1)S(1)}, u32[]{:S(2)}, u32[]{:S(2)}) collective-permute-start(bf16[256,1024]{1,0:T(8,128)(2,1)} %copy-done.5), channel_id=1, source_target_pairs={{0,2},{1,3},{2,0},{3,1},{4,6},{5,7},{6,4},{7,5},{8,10},{9,11},{10,... | collective-permute-start | bytes 1572872 | tf_op jit(solution)/shard_map/ppermute | solution.py:411
  98.5 23.5 %collective-permute-start.22 = (bf16[256,1024]{1,0:T(8,128)(2,1)}, bf16[256,1024]{1,0:T(8,128)(2,1)}, u32[]{:S(2)}, u32[]{:S(2)}) collective-permute-start(bf16[256,1024]{1,0:T(8,128)(2,1)} %copy-done.4), channel_id=1, source_target_pairs={{0,3},{1,0},{2,1},{3,2},{4,7},{5,4},{6,5},{7,6},{8,11},{9,8},{10,9... | collective-permute-start | bytes 1572872 | tf_op jit(solution)/shard_map/ppermute | solution.py:411
  116.1 11.2 %all-to-all-start.1 = ((bf16[4,8,1280]{2,1,0:T(8,128)(2,1)}), bf16[4,8,1280]{2,1,0:T(8,128)(2,1)S(1)}, u32[]{:S(2)}, u32[]{:S(2)}) async-start(bf16[4,8,1280]{2,1,0:T(8,128)(2,1)} %bitcast.9), calls=%async_computation.1 | async-start | bytes 163840 | tf_op jit(solution)/shard_map/all_to_all | solution.py:514
  (7 other events, 38.1 us)
